TPU v7x, 32 devices: a whole 2x2x4 slice. The times are simulated.
32 devices in a mesh: groups: 2 (over x), row: 4 (over y, core), col: 4 (over z).
Axes of the slice: x: 2, y: 2, z: 4, core: 2. Of those that a mesh axis runs over, the one named last changes fastest.
Arguments:
- pair_act: bfloat16 [1536, 768, 128], P(('groups', 'row'), 'col'), parts along dimension 0, may hold values from -6 to 6
- ln_gain: float32 [128], replicated, may hold values from 0.1 to 1.9
- ln_bias: float32 [128], replicated, may hold values from -3 to 3
- w_proj: bfloat16 [128, 512], replicated, may hold values from -0.5 to 0.5
- w_gate: bfloat16 [128, 128], replicated, may hold values from -0.5 to 0.5
- out_gain: float32 [128], replicated, may hold values from 0.1 to 1.9
- out_bias: float32 [128], replicated, may hold values from -3 to 3
- w_out: bfloat16 [128, 128], replicated, may hold values from -0.5 to 0.5
Outputs:
- update: bfloat16 [1536, 768, 128], P(('groups', 'row'), 'col'), parts along dimension 0
There are 2 independent parts, one for each index of `groups`. A program takes and returns all parts, laid end to end along the dimension named above; an argument that names none is the same for every part. Nothing has to cross between parts.
All inputs are finite; a program needn't handle non-finite values.
Results may differ from a plain program's by a relative error of at most 0.013.
Values may be sent and summed in bfloat16 or wider, within the bound.
No kernel may reach another device: no remote copies, remote signals or barrier semaphores. Data moves between devices by JAX's collectives and lax.ppermute only.
A program may use at most 192 MiB of HBM per device.

v0:
```python
import jax
import jax.numpy as jnp
from jax import lax
from jax.sharding import PartitionSpec as P


def layer_norm(values, scale_gain, shift_bias):
    average = jnp.mean(values, axis=-1, keepdims=True)
    centred = values - average
    variance = jnp.mean(centred * centred, axis=-1, keepdims=True)
    return centred * lax.rsqrt(variance + 1e-05) * scale_gain + shift_bias


def on_device(pair_act, ln_gain, ln_bias, w_proj, w_gate, out_gain, out_bias, w_out):
    tile_rows, tile_cols, channels = pair_act.shape
    hidden_width = w_proj.shape[1] // 4
    normed = layer_norm(pair_act.astype(jnp.float32), ln_gain, ln_bias).astype(jnp.bfloat16)
    flattened = normed.reshape(tile_rows * tile_cols, channels)
    projected = jnp.dot(flattened, w_proj, preferred_element_type=jnp.float32)
    left_side = (
        jax.nn.sigmoid(projected[:, :hidden_width]) * projected[:, hidden_width : 2 * hidden_width]
    ).astype(jnp.bfloat16)
    right_side = (
        jax.nn.sigmoid(projected[:, 2 * hidden_width : 3 * hidden_width])
        * projected[:, 3 * hidden_width :]
    ).astype(jnp.bfloat16)
    left_side = left_side.reshape(tile_rows, tile_cols, hidden_width)
    right_side = right_side.reshape(tile_rows, tile_cols, hidden_width)
    gated = jax.nn.sigmoid(jnp.dot(flattened, w_gate, preferred_element_type=jnp.float32)).astype(
        jnp.bfloat16
    )
    gating = gated.reshape(tile_rows, tile_cols, channels)
    partial_sum = jnp.einsum(
        "jkh,ikh->jih",
        lax.all_gather(right_side, "row", axis=0, tiled=True),
        left_side,
        preferred_element_type=jnp.float32,
    )
    tri_sum = lax.psum_scatter(
        partial_sum.astype(jnp.bfloat16), "col", scatter_dimension=0, tiled=True
    ).astype(jnp.float32)
    out_normed = layer_norm(tri_sum, out_gain, out_bias).astype(jnp.bfloat16)
    result = jnp.dot(
        out_normed.reshape(tile_cols * tile_rows, hidden_width),
        w_out,
        preferred_element_type=jnp.float32,
    )
    result = jnp.swapaxes(result.reshape(tile_cols, tile_rows, channels), 0, 1)
    return (result * gating.astype(jnp.float32)).astype(jnp.bfloat16)


def solution(mesh):
    in_specs = (P(("groups", "row"), "col", None), P(), P(), P(), P(), P(), P(), P())
    out_specs = P(("groups", "row"), "col", None)
    return jax.shard_map(
        on_device, mesh=mesh, in_specs=in_specs, out_specs=out_specs, check_vma=False
    )
```

profile of v0, /device:TPU:0, one launch (start us, length us, event | category | flops | bytes accessed | tf_op | source)
XLA Modules:
  0.0 1194.4 jit_solution(3863674304336193467)
XLA Ops:
  6.5 7.2 convert_reduce_fusion.1
  13.8 13.9 %fusion.12 = f32[192,192]{1,0:T(8,128)S(1)} fusion(bf16[192,192,128]{2,1,0:T(8,128)(2,1)} %param.8, f32[192,192]{1,0:T(8,128)S(1)} %broadcast_multiply_fusion.1), kind=kLoop, calls=%fused_computation.18 | loop fusion | flops 18837504 | bytes 9732096 | tf_op jit(solution)/shard_map/reduce_sum | solution.py:10
  27.8 0.0 copy-done.5
  27.8 0.0 copy-done.6
  27.8 13.7 %fusion.15 = bf16[192,192,128]{2,1,0:T(8,128)(2,1)} fusion(bf16[192,192,128]{2,1,0:T(8,128)(2,1)} %param.8, f32[128]{0:T(128)S(1)} %copy-done.5, f32[128]{0:T(128)S(1)} %copy-done.6, f32[192,192]{1,0:T(8,128)S(1)} %add_rsqrt_fusion.1, f32[192,192]{1,0:T(8,128)S(1)} %broadcast_multiply_fusion.1), kind=kLoop, calls=%fused_computation.21 | loop fusion | flops 28311552 | bytes 19170304 | tf_op jit(solution)/shard_map/convert_element_type | solution.py:17
  41.5 29.9 %fusion.34 = f32[36864,512]{1,0:T(8,128)} fusion(bf16[36864,128]{1,0:T(8,128)(2,1)} %bitcast.20, bf16[128,512]{1,0:T(8,128)(2,1)S(1)} %copy-done), kind=kOutput, calls=%fused_computation.46 | convolution fusion | flops 4831838208 | bytes 85065728 | tf_op jit(solution)/shard_map/dot_general | solution.py:19
  71.4 32.2 %fusion.16 = (bf16[36864,128]{1,0:T(8,128)(2,1)}, bf16[36864,128]{1,0:T(8,128)(2,1)}) fusion(f32[36864,512]{1,0:T(8,128)} %fusion.34), kind=kLoop, calls=%fused_computation.23 | loop fusion | flops 47185920 | bytes 94371840 | tf_op jit(solution)/shard_map/convert_element_type | solution.py:26
  103.5 17.4 %copy.16 = bf16[192,192,128]{1,0,2:T(8,128)(2,1)} copy(bf16[192,192,128]{2,1,0:T(8,128)(2,1)} %bitcast.23) | data formatting | bytes 18874368 | tf_op jit(solution)/shard_map/reshape | solution.py:28
  121.0 0.0 all-gather.2.cloned.1.call-update
  121.0 0.2 reduce-scatter.2.cloned.1.call-start
  121.2 18.0 %copy.17 = bf16[192,192,128]{1,0,2:T(8,128)(2,1)} copy(bf16[192,192,128]{2,1,0:T(8,128)(2,1)} %bitcast.22) | data formatting | bytes 18874368 | tf_op jit(solution)/shard_map/reshape | solution.py:27
  139.2 284.1 %all-gather.2.cloned.1.call-done = bf16[768,192,128]{1,0,2:T(8,128)(2,1)} async-done(((bf16[192,192,128]{1,0,2:T(8,128)(2,1)}), bf16[768,192,128]{1,0,2:T(8,128)(2,1)}) %all-gather.2.cloned.1.call-update) | async-done | bytes 37748752 | tf_op jit(solution)/shard_map/all_gather | solution.py:35
  423.3 37.8 %convert_bitcast_fusion = bf16[768,192,128]{0,1,2:T(8,128)(2,1)} fusion(bf16[192,192,128]{1,0,2:T(8,128)(2,1)} %copy.17, bf16[768,192,128]{1,0,2:T(8,128)(2,1)} %all-gather.2.cloned.1.call-done), kind=kOutput, calls=%fused_computation.5 | convolution fusion | flops 7266631680 | bytes 84934656 | tf_op jit(solution)/shard_map/jkh,ikh->jih/dot_general | solution.py:33
  461.1 52.4 %copy.18 = bf16[768,192,128]{2,1,0:T(8,128)(2,1)} copy(bf16[768,192,128]{0,1,2:T(8,128)(2,1)} %convert_bitcast_fusion) | data formatting | bytes 75497472 | tf_op jit(solution)/shard_map/convert_element_type | solution.py:40
  513.4 0.0 reduce-scatter.2.cloned.1.call-update
  513.4 0.7 copy-done.7
  514.2 9.7 fusion.3
  523.9 12.2 %convert.1 = f32[192,192,128]{2,1,0:T(8,128)} convert(bf16[192,192,128]{2,1,0:T(8,128)(2,1)} %bitcast.24) | non-fusion elementwise | flops 4718592 | bytes 28311552 | tf_op jit(solution)/shard_map/convert_element_type | solution.py:49
  536.1 596.7 %reduce-scatter.2.cloned.1.call-done = bf16[192,192,128]{2,1,0:T(8,128)(2,1)} async-done(((bf16[768,192,128]{2,1,0:T(8,128)(2,1)}), bf16[192,192,128]{2,1,0:T(8,128)(2,1)}) %reduce-scatter.2.cloned.1.call-update) | async-done | bytes 9437200 | tf_op jit(solution)/shard_map/reduce_scatter | solution.py:39
  1132.8 7.2 convert_reduce_fusion
  1140.0 13.9 %fusion.8 = f32[192,192]{1,0:T(8,128)S(1)} fusion(bf16[192,192,128]{2,1,0:T(8,128)(2,1)} %reduce-scatter.2.cloned.1.call-done, f32[192,192]{1,0:T(8,128)S(1)} %broadcast_multiply_fusion), kind=kLoop, calls=%fused_computation.14 | loop fusion | flops 18837504 | bytes 9732096 | tf_op jit(solution)/shard_map/reduce_sum | solution.py:10
  1154.0 0.0 copy-start.1
  1154.0 20.1 %fusion.24 = bf16[192,192,128]{2,0,1:T(8,128)(2,1)} fusion(f32[192,192,128]{2,1,0:T(8,128)} %convert.1, bf16[192,192,128]{2,1,0:T(8,128)(2,1)} %reduce-scatter.2.cloned.1.call-done, f32[128]{0:T(128)S(1)} %copy-done.3, f32[128]{0:T(128)S(1)} %copy-done.4, f32[192,192]{1,0:T(8,128)S(1)} %add_rsqrt_fusion, f32[192,192]{1,0:T(8,128)S(1)} %broadcast_multiply_fusion, ...), kind=kOutput, calls=%fused_computation.35 | convolution fusion | flops 1245708288 | bytes 38077440 | tf_op jit(solution)/shard_map/dot_general | solution.py:43
  1174.1 13.5 %copy.20 = bf16[192,192,128]{2,1,0:T(8,128)(2,1)} copy(bf16[192,192,128]{2,0,1:T(8,128)(2,1)} %fusion.24) | data formatting | bytes 18874368 | tf_op jit(solution)/shard_map/convert_element_type | solution.py:49
  (17 shorter events, 0.1 us)
Async XLA Ops:
  6.5 34.9 %copy-start = (bf16[128,512]{1,0:T(8,128)(2,1)S(1)}, bf16[128,512]{1,0:T(8,128)(2,1)}, u32[]{:S(2)}) copy-start(bf16[128,512]{1,0:T(8,128)(2,1)} %param.11) | copy-start | bytes 393220
  6.5 21.2 %copy-start.5 = (f32[128]{0:T(128)S(1)}, f32[128]{0:T(128)}, u32[]{:S(2)}) copy-start(f32[128]{0:T(128)} %param.10) | copy-start | bytes 1540
  6.5 21.2 %copy-start.6 = (f32[128]{0:T(128)S(1)}, f32[128]{0:T(128)}, u32[]{:S(2)}) copy-start(f32[128]{0:T(128)} %param.9) | copy-start | bytes 1540
  6.5 416.8 %all-gather.2.cloned.1.call-start = ((), (), s32[]{:S(2)}) async-start(), calls=%async_computation.1 | async-start | bytes 62914560 | tf_op jit(solution)/shard_map/all_gather | solution.py:35
  121.0 1011.8 %reduce-scatter.2.cloned.1.call-start = ((), (), s32[]{:S(2)}) async-start(), calls=%async_computation.2 | async-start | bytes 47185920 | tf_op jit(solution)/shard_map/reduce_scatter | solution.py:39
  513.4 0.8 copy-start.7
  523.9 630.1 %copy-start.2 = (bf16[128,128]{1,0:T(8,128)(2,1)S(1)}, bf16[128,128]{1,0:T(8,128)(2,1)}, u32[]{:S(2)}) copy-start(bf16[128,128]{1,0:T(8,128)(2,1)} %param.15) | copy-start | bytes 98308
  523.9 630.1 %copy-start.3 = (f32[128]{0:T(128)S(1)}, f32[128]{0:T(128)}, u32[]{:S(2)}) copy-start(f32[128]{0:T(128)} %param.14) | copy-start | bytes 1540
  523.9 630.1 %copy-start.4 = (f32[128]{0:T(128)S(1)}, f32[128]{0:T(128)}, u32[]{:S(2)}) copy-start(f32[128]{0:T(128)} %param.13) | copy-start | bytes 1540
  1154.0 33.6 %copy-start.1 = (bf16[128,512]{1,0:T(8,128)(2,1)S(1)}, bf16[128,512]{1,0:T(8,128)(2,1)}, u32[]{:S(2)}) copy-start(bf16[128,512]{1,0:T(8,128)(2,1)} %param.11) | copy-start | bytes 393220
Sparse Core Ops, SparseCore 0:
  121.1 302.1 all-gather.1
  513.6 619.1 reduce-scatter.1
where the time goes:
time: 1200 us; the launch traced here: 1190 us
  waiting for transfers between devices  881 us (73%)
  local copies, waits for them, and re-layouts  102 us (8%)
  other arithmetic  100 us (8%)
  matrix products  97.4 us (8%)
  between operations  13.5 us (1%)
    reduce_scatter x1, waiting for transfers between devices, on_device(): lax.psum_scatter(partial_sum.astype(jnp.bfloat16), 'col', scatter_dimensi...  597 us
    all_gather x1, waiting for transfers between devices, on_device(): lax.all_gather(right_side, 'row', axis=0, tiled=True)  284 us
    convert_element_type x1, local copies, waits for them, and re-layouts, on_device(): partial_sum.astype(jnp.bfloat16)  52.4 us
    dot_general x1, matrix products, on_device(): jnp.einsum('jkh,ikh->jih', lax.all_gather(right_side, 'row', axis=0, tile...  37.8 us
    convert_element_type x1, other arithmetic, on_device(): right_side = (jax.nn.sigmoid(projected[:, 2 * hidden_width:3 * hidden_wid...  32.2 us
    dot_general x1, matrix products, on_device(): projected = jnp.dot(flattened, w_proj, preferred_element_type=jnp.float32)  29.9 us
    reduce_sum x2, other arithmetic, layer_norm(): variance = jnp.mean(centred * centred, axis=-1, keepdims=True)  27.8 us
  transfers between devices with their start and end apart: 2, of which 2 were waited for; matrix products, arithmetic and copies ran while one was open for 3% of the time, Pallas kernels for 0%

commit v1 on v0

v1 whole, which is shorter than its diff:
```python
import functools
import math

import jax
import jax.numpy as jnp
from jax import lax
from jax.experimental import pallas as pl
from jax.experimental.pallas import tpu as pltpu
from jax.sharding import PartitionSpec as P

CHUNKS = 3
EPS = 1e-05
F32, BF16 = jnp.float32, jnp.bfloat16
PARAMS = pltpu.CompilerParams(vmem_limit_bytes=52 * 1024 * 1024)


def contract(left, right, left_dim, right_dim):
    return lax.dot_general(
        left, right, (((left_dim,), (right_dim,)), ((), ())), preferred_element_type=F32
    )


def project_kernel(n_pieces, *refs):
    pieces, (weights, centre, gain, bias, left_out, right_out, left_rows, right_rows) = (
        refs[:n_pieces],
        refs[n_pieces:],
    )
    hidden, rows, depth = left_out.shape

    def one_row(i, carry):
        values = jnp.concatenate([piece[i] for piece in pieces], axis=0)
        centred = contract(centre[...], values, 1, 1)
        variance = jnp.mean(centred * centred, axis=0, keepdims=True)
        normed = centred * lax.rsqrt(variance + EPS) * gain[...] + bias[...]
        halved = contract(weights[...], normed.astype(BF16), 1, 0)
        for first, held in ((0, left_rows), (2 * hidden, right_rows)):
            gate, value = halved[first : first + hidden], halved[first + hidden : first + 2 * hidden]
            side = value + value * jnp.tanh(gate)
            for n in range(depth // 128):
                held[n, pl.ds(i, hidden, stride=rows), :] = side[:, n * 128 : (n + 1) * 128]
        return carry

    lax.fori_loop(0, rows, one_row, 0, unroll=2)
    for held, out in ((left_rows, left_out), (right_rows, right_out)):
        for n in range(depth // 128):
            out[:, :, n * 128 : (n + 1) * 128] = held[n].reshape(hidden, rows, 128).astype(BF16)


def project(pieces, firsts, count, weights, centre, gain, bias):
    rows = 16
    hidden = weights.shape[0] // 4
    channels = weights.shape[1]
    depth = sum(piece.shape[1] for piece in pieces)
    whole = lambda x: pl.BlockSpec(x.shape, lambda i: (0,) * x.ndim)
    in_specs = [
        pl.BlockSpec((rows, piece.shape[1], channels), functools.partial(lambda f, i: (i + f, 0, 0), first // rows))
        for piece, first in zip(pieces, firsts)
    ] + [whole(x) for x in (weights, centre, gain, bias)]
    shape = jax.ShapeDtypeStruct((hidden, count, depth), BF16)
    return pl.pallas_call(
        functools.partial(project_kernel, len(pieces)),
        grid=(count // rows,),
        in_specs=in_specs,
        out_specs=[pl.BlockSpec((hidden, rows, depth), lambda i: (0, i, 0))] * 2,
        out_shape=[shape, shape],
        scratch_shapes=[pltpu.VMEM((depth // 128, hidden * rows, 128), F32)] * 2,
        compiler_params=PARAMS,
        name="project",
    )(*pieces, weights, centre, gain, bias)


def triangle_kernel(n_sides, group, which, left, *refs):
    sides, out = refs[:n_sides], refs[n_sides]

    def go(side):
        for first in range(0, left.shape[0], group):
            parts = [contract(left[h], side[h], 1, 1) for h in range(first, first + group)]
            out[first // group] = jnp.concatenate(parts, axis=-1).astype(BF16)

    for n, side in enumerate(sides):
        pl.when(which[0] == n)(functools.partial(go, side))


def group_of(columns):
    return 128 // math.gcd(columns, 128)


def triangle(left, sides, which):
    hidden, rows, depth = left.shape
    columns = sides[0].shape[1]
    group = group_of(columns)
    step = max(16, group)

    def side_spec(n):
        return pl.BlockSpec((step, columns, depth), lambda h, which: (jnp.where(which[0] == n, h, 0), 0, 0))

    return pl.pallas_call(
        functools.partial(triangle_kernel, len(sides), group),
        grid_spec=pltpu.PrefetchScalarGridSpec(
            num_scalar_prefetch=1,
            grid=(hidden // step,),
            in_specs=[pl.BlockSpec((step, rows, depth), lambda h, which: (h, 0, 0))]
            + [side_spec(n) for n in range(len(sides))],
            out_specs=pl.BlockSpec((step // group, rows, group * columns), lambda h, which: (h, 0, 0)),
        ),
        out_shape=jax.ShapeDtypeStruct((hidden // group, rows, group * columns), BF16),
        compiler_params=PARAMS,
        name="triangle",
    )(which, left, *sides)


def gate_kernel(pair, centre, mean, gain, bias, weights, out):
    rows, columns, channels = pair.shape
    values = pair[...].reshape(rows * columns, channels)
    centred = contract(values, centre[...], 1, 0)
    square = centred * centred
    high = square.astype(BF16)
    low = (square - high.astype(F32)).astype(BF16)
    variance = contract(jnp.concatenate([high, low], axis=1), mean[...], 1, 0)
    normed = (centred * lax.rsqrt(variance + EPS) * gain[...] + bias[...]).astype(BF16)
    gate = 0.5 + 0.5 * jnp.tanh(contract(normed, weights[...], 1, 0))
    out[...] = gate.astype(BF16).reshape(rows, columns, channels)


def gate_of(pair, centre, mean, gain, bias, weights):
    rows = 8
    count, columns, channels = pair.shape
    whole = lambda x: pl.BlockSpec(x.shape, lambda i: (0,) * x.ndim)
    block = pl.BlockSpec((rows, columns, channels), lambda i: (i, 0, 0))
    return pl.pallas_call(
        gate_kernel,
        grid=(count // rows,),
        in_specs=[block] + [whole(x) for x in (centre, mean, gain, bias, weights)],
        out_specs=block,
        out_shape=jax.ShapeDtypeStruct(pair.shape, BF16),
        compiler_params=PARAMS,
        name="gate",
    )(pair, centre, mean, gain, bias, weights)


def finish_kernel(n_parts, group, hidden, *refs):
    own, sent = refs[:n_parts], refs[n_parts : 2 * n_parts]
    gate, weights, gain, bias, _, out, rows_of = refs[2 * n_parts :]
    packed, rows, lanes = own[0].shape
    columns = lanes // group

    def over_hidden(x):
        total = jnp.sum(x, axis=0)
        shift = columns
        while shift < lanes:
            total = total + pltpu.roll(total, shift, 1)
            shift *= 2
        return total * (1.0 / hidden)

    for n in range(n_parts):
        total = own[n][...].astype(F32) + sent[n][...].astype(F32)
        centred = total - over_hidden(total)[None]
        scale = lax.rsqrt(over_hidden(centred * centred) + EPS)
        normed = centred * scale[None] * gain[...] + bias[...]
        rows_of[n] = normed.reshape(packed * rows, lanes)
    for i in range(rows):
        parts = []
        for n in range(n_parts):
            held = rows_of[n, pl.ds(i, packed, stride=rows), :]
            parts.append(
                jnp.concatenate([held[:, g * columns : (g + 1) * columns] for g in range(group)], axis=0)
            )
        normed = jnp.concatenate(parts, axis=1).astype(BF16)
        result = contract(normed, weights[...], 0, 0)
        out[i] = (result * gate[i].astype(F32)).astype(BF16)


def finish(own, sent, gate, first, weights, gain, bias, held):
    rows = 8
    packed, count, lanes = own[0].shape
    hidden = weights.shape[0]
    group = hidden // packed
    whole = lambda x: pl.BlockSpec(x.shape, lambda i: (0,) * x.ndim)
    part = pl.BlockSpec((packed, rows, lanes), lambda i: (0, i, 0))
    block = pl.BlockSpec((rows,) + gate.shape[1:], lambda i: (i + first // rows, 0, 0))
    n_parts = len(own)
    return pl.pallas_call(
        functools.partial(finish_kernel, n_parts, group, hidden),
        grid=(count // rows,),
        in_specs=[part] * (2 * n_parts)
        + [block, whole(weights), whole(gain), whole(bias), pl.BlockSpec(memory_space=pl.ANY)],
        out_specs=block,
        out_shape=jax.ShapeDtypeStruct(gate.shape, BF16),
        scratch_shapes=[pltpu.VMEM((n_parts, packed * rows, lanes), F32)],
        input_output_aliases={2 * n_parts + 4: 0},
        compiler_params=PARAMS,
        name="finish",
    )(*own, *sent, gate, weights, gain, bias, held)


def after(value, *others):
    return lax.optimization_barrier((value,) + others)[0]


def on_device(n_row, n_col, pair_act, ln_gain, ln_bias, w_proj, w_gate, out_gain, out_bias, w_out):
    tile_rows, tile_cols, channels = pair_act.shape
    hidden = w_proj.shape[1] // 4
    half = n_col // 2
    top = n_row // 2
    share = n_row // n_col
    row, col = lax.axis_index("row"), lax.axis_index("col")
    axes = ("row", "col")
    place = lambda r, c: r * n_col + c
    step = tile_rows // CHUNKS
    group = group_of(step)
    packed = hidden // group

    halves = (w_proj * 0.5).astype(BF16).T
    centre = (jnp.eye(channels, dtype=F32) - 1.0 / channels).astype(BF16)
    mean = jnp.full((2 * channels, channels), 1.0 / channels, BF16)
    half_gate = (w_gate * 0.5).astype(BF16)
    by_hidden = lambda v: jnp.repeat(v.reshape(packed, group), step, axis=1)[:, None, :]
    gain_out, bias_out = by_hidden(out_gain), by_hidden(out_bias)
    w_last = w_out.reshape(packed, group, channels).swapaxes(0, 1).reshape(hidden, channels)

    def holds(r, c):
        return (r // share) % half == c % half

    def spread(near):
        far = lax.ppermute(
            near,
            axes,
            [(place(r, c), place(r ^ top, c)) for r in range(n_row) for c in range(n_col) if holds(r, c)],
        )
        bit = top // 2
        while bit >= share:
            alike = (bit * 2 - 1) & ~(share - 1)
            sends = [
                (place(r, c), place(r ^ bit, c))
                for r in range(n_row)
                for c in range(n_col)
                if (r ^ (c * share)) & alike == 0
            ]
            near_in, far_in = lax.ppermute(near, axes, sends), lax.ppermute(far, axes, sends)
            keep = ((row ^ (col * share)) & bit) == 0
            if bit == 1:
                return [near, near_in, far, far_in], jnp.where(keep, 0, 1)
            near, far = jnp.where(keep, near, near_in), jnp.where(keep, far, far_in)
            bit //= 2
        sides = [[near], [far]]
        while bit >= 1:
            swap = [(r, r ^ bit) for r in range(n_row)]
            first = (row & bit) == 0
            for n in range(2):
                others = [lax.ppermute(x, "row", swap) for x in sides[n]]
                sides[n] = [jnp.where(first, a, b) for a, b in zip(sides[n] + others, others + sides[n])]
            bit //= 2
        return sides, jnp.int32(0)

    near_is_own = (row // top) == (col // half)
    swap_half = [(c, c ^ half) for c in range(n_col)]
    lefts, spreads, sent = [], [], {}

    def product(i, j, s, own):
        sides, choice = spreads[j]
        take_near = near_is_own if own else jnp.logical_not(near_is_own)
        if share == 1:
            which = jnp.where(take_near, choice, choice + len(sides) // 2)
            return triangle(lefts[i], sides, which.astype(jnp.int32).reshape(1))
        which = jnp.where(take_near, 0, 1)
        return triangle(lefts[i], [sides[0][s], sides[1][s]], which.astype(jnp.int32).reshape(1))

    blocks = [pair_act[t * step : (t + 1) * step] for t in range(CHUNKS)]
    last = None
    for t in range(CHUNKS):
        block = blocks[t] if last is None else after(blocks[t], last)
        pieces = [block]
        for offset in range(1, half):
            pieces.append(lax.ppermute(block, "col", [(c, c ^ offset) for c in range(n_col)]))
        last = pieces[-1]
        left, right = project(
            [pair_act] + pieces[1:],
            [t * step] + [0] * (half - 1),
            step,
            halves,
            centre,
            ln_gain[:, None],
            ln_bias[:, None],
        )
        lefts.append(left)
        spreads.append(spread(right))
        for i, j in [(a, t) for a in range(t)] + [(t, b) for b in range(t + 1)]:
            for s in range(share):
                sent[i, j, s] = lax.ppermute(product(i, j, s, False), "col", swap_half)

    gate = gate_of(pair_act, centre, mean, ln_gain[None], ln_bias[None], half_gate)
    order = [(j, s) for s in range(share) for j in range(CHUNKS)]
    out = jnp.zeros(pair_act.shape, BF16)
    for i in range(CHUNKS):
        own = [product(i, j, s, True) for j, s in order]
        out = finish(own, [sent[i, j, s] for j, s in order], gate, i * step, w_last, gain_out, bias_out, out)
    return out


def solution(mesh):
    n_row, n_col = mesh.shape["row"], mesh.shape["col"]
    in_specs = (P(("groups", "row"), "col", None), P(), P(), P(), P(), P(), P(), P())
    out_specs = P(("groups", "row"), "col", None)
    return jax.shard_map(
        functools.partial(on_device, n_row, n_col),
        mesh=mesh,
        in_specs=in_specs,
        out_specs=out_specs,
        check_vma=False,
    )
```

time: 1200 us -> 827 us (0.69)
  waiting for transfers between devices: 881 us -> 419 us
  Pallas kernels: 0 us -> 333 us
  other arithmetic: 100 us -> 0.04 us
  matrix products: 97.4 us -> 0 us
  local copies, waits for them, and re-layouts: 102 us -> 18.7 us
  starting transfers between devices: 0.22 us -> 47.9 us
  between operations: 13.5 us -> 0.93 us
    reduce_scatter x1 -> x0, waiting for transfers between devices: 597 us -> none  [on_device(): lax.psum_scatter(partial_sum.astype(jnp.bfloat16), 'col', scatter_dimensi...]
    ppermute x0 -> x21, waiting for transfers between devices: none -> 419 us  [the longest x9 176 us: on_device(): sent[i, j, s] = lax.ppermute(product(i, j, s, False), 'col', swap_half)]
    pallas_call x0 -> x25, Pallas kernels: none -> 333 us  [the longest x18 168 us: triangle(): pl.pallas_call(functools.partial(triangle_kernel, len(sides), group), gri...]
    all_gather x1 -> x0, waiting for transfers between devices: 284 us -> none  [on_device(): lax.all_gather(right_side, 'row', axis=0, tiled=True)]
    dot_general x4 -> x0, matrix products: 97.4 us -> none  [the longest x1 37.8 us: on_device(): jnp.einsum('jkh,ikh->jih', lax.all_gather(right_side, 'row', axis=0, tile...]
    convert_element_type x2 -> x0, local copies, waits for them, and re-layouts: 65.8 us -> none  [the longest x1 52.4 us: on_device(): partial_sum.astype(jnp.bfloat16)]
    convert_element_type x3 -> x1, other arithmetic: 58.1 us -> 0.02 us  [on_device(): centre = (jnp.eye(channels, dtype=F32) - 1.0 / channels).astype(BF16)]
    ppermute x0 -> x21, starting transfers between devices: none -> 47.9 us  [the longest x3 12 us: spread(): lax.ppermute(far, axes, sends)]
  transfers between devices with their start and end apart: 2 -> 21, of which waited for: 2 -> 8; matrix products, arithmetic and copies ran while one was open for 3% -> 1% of each run, Pallas kernels for 0% -> 39%
where the time goes in v1:
time: 827 us; the launch traced here: 820 us
  waiting for transfers between devices  419 us (51%)
  Pallas kernels  333 us (40%)
  starting transfers between devices  47.9 us (6%)
  local copies, waits for them, and re-layouts  18.7 us (2%)
    ppermute x9, waiting for transfers between devices, on_device(): sent[i, j, s] = lax.ppermute(product(i, j, s, False), 'col', swap_half)  176 us
    pallas_call x18, Pallas kernels, triangle(): pl.pallas_call(functools.partial(triangle_kernel, len(sides), group), gri...  168 us
    ppermute x3, waiting for transfers between devices, on_device(): lax.ppermute(block, 'col', [(c, c ^ offset) for c in range(n_col)])  136 us
    ppermute x3, waiting for transfers between devices, spread(): lax.ppermute(near, axes, [(place(r, c), place(r ^ top, c)) for r in range...  108 us
    pallas_call x3, Pallas kernels, project(): pl.pallas_call(functools.partial(project_kernel, len(pieces)), grid=(coun...  107 us
    pallas_call x3, Pallas kernels, finish(): pl.pallas_call(functools.partial(finish_kernel, n_parts, group, hidden),...  33.5 us
    pallas_call x1, Pallas kernels, gate_of(): pl.pallas_call(gate_kernel, grid=(count // rows,), in_specs=[block] + [wh...  25.1 us
  transfers between devices with their start and end apart: 21, of which 8 were waited for; matrix products, arithmetic and copies ran while one was open for 1% of the time, Pallas kernels for 39%

profile of v1, /device:TPU:0, one launch (start us, length us, event | category | flops | bytes accessed | tf_op | source)
XLA Modules:
  0.0 820.0 jit_solution(150401172131504449)
XLA Ops:
  8.4 68.1 %collective-permute-done.refs_1_ = bf16[64,192,128]{2,1,0:T(8,128)(2,1)S(1)} collective-permute-done((bf16[64,192,128]{2,1,0:T(8,128)(2,1)S(1)}, bf16[64,192,128]{2,1,0:T(8,128)(2,1)S(1)}, u32[]{:S(2)}, u32[]{:S(2)}) %collective-permute-start) | collective-permute-done | bytes 3145760 | tf_op jit(solution)/shard_map/ppermute | solution.py:274
  78.2 67.5 %collective-permute-done.1.refs_1_ = bf16[64,192,128]{2,1,0:T(8,128)(2,1)S(1)} collective-permute-done((bf16[64,192,128]{2,1,0:T(8,128)(2,1)S(1)}, bf16[64,192,128]{2,1,0:T(8,128)(2,1)S(1)}, u32[]{:S(2)}, u32[]{:S(2)}) %collective-permute-start.1) | collective-permute-done | bytes 3145760 | tf_op jit(solution)/shard_map/ppermute | solution.py:274
  147.9 35.6 %project.4 = (bf16[128,64,384]{2,1,0:T(8,128)(2,1)}, bf16[128,64,384]{2,1,0:T(8,128)(2,1)}) custom-call(bf16[192,192,128]{2,1,0:T(8,128)(2,1)} %pair.1, bf16[64,192,128]{2,1,0:T(8,128)(2,1)} %copy-done.9, bf16[512,128]{1,0:T(8,128)(2,1)S(1)} %multiply_bitcast_fusion.refs_2_, bf16[128,128]{1,0:T(8,128)(2,1)S(1)} %add_convert_fusion.refs_3_.centre, ...), custom_call_target="tpu_custom_call" | custom-call | tf_op jit(solution)/shard_map/project/pallas_call | solution.py:60
  190.7 35.6 %project.5 = (bf16[128,64,384]{2,1,0:T(8,128)(2,1)}, bf16[128,64,384]{2,1,0:T(8,128)(2,1)}) custom-call(bf16[192,192,128]{2,1,0:T(8,128)(2,1)} %pair.1, bf16[64,192,128]{2,1,0:T(8,128)(2,1)} %copy-done.8, bf16[512,128]{1,0:T(8,128)(2,1)S(1)} %multiply_bitcast_fusion.refs_2_, bf16[128,128]{1,0:T(8,128)(2,1)S(1)} %add_convert_fusion.refs_3_.centre, ...), custom_call_target="tpu_custom_call" | custom-call | tf_op jit(solution)/shard_map/project/pallas_call | solution.py:60
  228.9 35.5 %project.3 = (bf16[128,64,384]{2,1,0:T(8,128)(2,1)}, bf16[128,64,384]{2,1,0:T(8,128)(2,1)}) custom-call(bf16[192,192,128]{2,1,0:T(8,128)(2,1)} %pair.1, bf16[64,192,128]{2,1,0:T(8,128)(2,1)} %collective-permute-done.2.refs_1_, bf16[512,128]{1,0:T(8,128)(2,1)S(1)} %multiply_bitcast_fusion.refs_2_, bf16[128,128]{1,0:T(8,128)(2,1)S(1)} %add_convert_fusion.refs_3_.centre, ...), custom_call_target="tpu_custom_call" | custom-call | tf_op jit(solution)/shard_map/project/pallas_call | solution.py:60
  275.7 48.3 %collective-permute-done.7.refs_2_ = bf16[128,64,384]{2,1,0:T(8,128)(2,1)} collective-permute-done((bf16[128,64,384]{2,1,0:T(8,128)(2,1)}, bf16[128,64,384]{2,1,0:T(8,128)(2,1)}, u32[]{:S(2)}, u32[]{:S(2)}) %collective-permute-start.7) | collective-permute-done | bytes 6291488 | tf_op jit(solution)/shard_map/ppermute | solution.py:225
  331.8 59.7 %collective-permute-done.10.refs_2_ = bf16[128,64,384]{2,1,0:T(8,128)(2,1)} collective-permute-done((bf16[128,64,384]{2,1,0:T(8,128)(2,1)}, bf16[128,64,384]{2,1,0:T(8,128)(2,1)}, u32[]{:S(2)}, u32[]{:S(2)}) %collective-permute-start.10) | collective-permute-done | bytes 6291488 | tf_op jit(solution)/shard_map/ppermute | solution.py:225
  450.4 9.9 %triangle.28 = bf16[64,64,128]{2,1,0:T(8,128)(2,1)} custom-call(s32[1]{0:T(128)} %bitcast.4.which, bf16[128,64,384]{2,1,0:T(8,128)(2,1)} %get-tuple-element.19.left, bf16[128,64,384]{2,1,0:T(8,128)(2,1)} %get-tuple-element.17.refs_0_, bf16[128,64,384]{2,1,0:T(8,128)(2,1)} %collective-permute-done.6.refs_1_, ...), custom_call_target="tpu_custom_call" | custom-call | tf_op jit(solution)/shard_map/triangle/pallas_call | solution.py:97
  469.5 9.4 %triangle.23 = bf16[64,64,128]{2,1,0:T(8,128)(2,1)S(1)} custom-call(s32[1]{0:T(128)} %bitcast.4.which, bf16[128,64,384]{2,1,0:T(8,128)(2,1)} %get-tuple-element.15.left, bf16[128,64,384]{2,1,0:T(8,128)(2,1)} %get-tuple-element.18.refs_0_, bf16[128,64,384]{2,1,0:T(8,128)(2,1)} %collective-permute-done.9.refs_1_, ...), custom_call_target="tpu_custom_call" | custom-call | tf_op jit(solution)/shard_map/triangle/pallas_call | solution.py:97
  479.0 10.0 %triangle.29 = bf16[64,64,128]{2,1,0:T(8,128)(2,1)} custom-call(s32[1]{0:T(128)} %bitcast.4.which, bf16[128,64,384]{2,1,0:T(8,128)(2,1)} %get-tuple-element.19.left, bf16[128,64,384]{2,1,0:T(8,128)(2,1)} %get-tuple-element.18.refs_0_, bf16[128,64,384]{2,1,0:T(8,128)(2,1)} %collective-permute-done.9.refs_1_, ...), custom_call_target="tpu_custom_call" | custom-call | tf_op jit(solution)/shard_map/triangle/pallas_call | solution.py:97
  488.9 51.9 %collective-permute-done.15.refs_3_ = bf16[64,64,128]{2,1,0:T(8,128)(2,1)S(1)} collective-permute-done((bf16[64,64,128]{2,1,0:T(8,128)(2,1)S(1)}, bf16[64,64,128]{2,1,0:T(8,128)(2,1)S(1)}, u32[]{:S(2)}, u32[]{:S(2)}) %collective-permute-start.15) | collective-permute-done | bytes 1048608 | tf_op jit(solution)/shard_map/ppermute | solution.py:289
  540.9 44.9 %collective-permute-done.18.refs_3_ = bf16[64,64,128]{2,1,0:T(8,128)(2,1)S(1)} collective-permute-done((bf16[64,64,128]{2,1,0:T(8,128)(2,1)S(1)}, bf16[64,64,128]{2,1,0:T(8,128)(2,1)S(1)}, u32[]{:S(2)}, u32[]{:S(2)}) %collective-permute-start.18) | collective-permute-done | bytes 1048608 | tf_op jit(solution)/shard_map/ppermute | solution.py:289
  585.8 44.9 %collective-permute-done.19.refs_4_ = bf16[64,64,128]{2,1,0:T(8,128)(2,1)S(1)} collective-permute-done((bf16[64,64,128]{2,1,0:T(8,128)(2,1)S(1)}, bf16[64,64,128]{2,1,0:T(8,128)(2,1)S(1)}, u32[]{:S(2)}, u32[]{:S(2)}) %collective-permute-start.19) | collective-permute-done | bytes 1048608 | tf_op jit(solution)/shard_map/ppermute | solution.py:289
  630.8 33.8 %collective-permute-done.20.refs_5_ = bf16[64,64,128]{2,1,0:T(8,128)(2,1)} collective-permute-done((bf16[64,64,128]{2,1,0:T(8,128)(2,1)S(1)}, bf16[64,64,128]{2,1,0:T(8,128)(2,1)}, u32[]{:S(2)}, u32[]{:S(2)}) %collective-permute-start.20) | collective-permute-done | bytes 1048608 | tf_op jit(solution)/shard_map/ppermute | solution.py:289
  665.5 25.1 %gate.1.refs_6_ = bf16[192,192,128]{2,1,0:T(8,128)(2,1)} custom-call(bf16[192,192,128]{2,1,0:T(8,128)(2,1)} %pair.1, bf16[128,128]{1,0:T(8,128)(2,1)S(1)} %add_convert_fusion.refs_3_.centre, bf16[256,128]{1,0:T(8,128)(2,1)S(1)} %broadcast_in_dim.30.mean, f32[1,128]{1,0:T(1,128)S(1)} %bitcast.16, f32[1,128]{1,0:T(1,128)S(1)} %bitcast.18, ...), custom_call_target="tpu_custom_call" | custom-call | tf_op jit(solution)/shard_map/gate/pallas_call | solution.py:130
  690.6 9.2 %triangle.30.refs_0_ = bf16[64,64,128]{2,1,0:T(8,128)(2,1)S(1)} custom-call(s32[1]{0:T(128)} %bitcast.which, bf16[128,64,384]{2,1,0:T(8,128)(2,1)} %get-tuple-element.20.left, bf16[128,64,384]{2,1,0:T(8,128)(2,1)} %get-tuple-element.16.refs_0_, bf16[128,64,384]{2,1,0:T(8,128)(2,1)} %collective-permute-done.3.refs_1_, ...), custom_call_target="tpu_custom_call" | custom-call | tf_op jit(solution)/shard_map/triangle/pallas_call | solution.py:97
  699.8 9.3 %triangle.24.refs_0_ = bf16[64,64,128]{2,1,0:T(8,128)(2,1)S(1)} custom-call(s32[1]{0:T(128)} %bitcast.which, bf16[128,64,384]{2,1,0:T(8,128)(2,1)} %get-tuple-element.19.left, bf16[128,64,384]{2,1,0:T(8,128)(2,1)} %get-tuple-element.16.refs_0_, bf16[128,64,384]{2,1,0:T(8,128)(2,1)} %collective-permute-done.3.refs_1_, ...), custom_call_target="tpu_custom_call" | custom-call | tf_op jit(solution)/shard_map/triangle/pallas_call | solution.py:97
  709.1 9.3 %triangle.18.refs_0_ = bf16[64,64,128]{2,1,0:T(8,128)(2,1)S(1)} custom-call(s32[1]{0:T(128)} %bitcast.which, bf16[128,64,384]{2,1,0:T(8,128)(2,1)} %get-tuple-element.15.left, bf16[128,64,384]{2,1,0:T(8,128)(2,1)} %get-tuple-element.16.refs_0_, bf16[128,64,384]{2,1,0:T(8,128)(2,1)} %collective-permute-done.3.refs_1_, ...), custom_call_target="tpu_custom_call" | custom-call | tf_op jit(solution)/shard_map/triangle/pallas_call | solution.py:97
  718.3 9.3 %triangle.25.refs_1_ = bf16[64,64,128]{2,1,0:T(8,128)(2,1)S(1)} custom-call(s32[1]{0:T(128)} %bitcast.which, bf16[128,64,384]{2,1,0:T(8,128)(2,1)} %get-tuple-element.19.left, bf16[128,64,384]{2,1,0:T(8,128)(2,1)} %get-tuple-element.17.refs_0_, bf16[128,64,384]{2,1,0:T(8,128)(2,1)} %collective-permute-done.6.refs_1_, ...), custom_call_target="tpu_custom_call" | custom-call | tf_op jit(solution)/shard_map/triangle/pallas_call | solution.py:97
  728.6 9.2 %triangle.19.refs_1_ = bf16[64,64,128]{2,1,0:T(8,128)(2,1)S(1)} custom-call(s32[1]{0:T(128)} %bitcast.which, bf16[128,64,384]{2,1,0:T(8,128)(2,1)} %get-tuple-element.15.left, bf16[128,64,384]{2,1,0:T(8,128)(2,1)} %get-tuple-element.17.refs_0_, bf16[128,64,384]{2,1,0:T(8,128)(2,1)} %collective-permute-done.6.refs_1_, ...), custom_call_target="tpu_custom_call" | custom-call | tf_op jit(solution)/shard_map/triangle/pallas_call | solution.py:97
  738.8 9.5 %triangle.31.refs_1_ = bf16[64,64,128]{2,1,0:T(8,128)(2,1)S(1)} custom-call(s32[1]{0:T(128)} %bitcast.which, bf16[128,64,384]{2,1,0:T(8,128)(2,1)} %get-tuple-element.20.left, bf16[128,64,384]{2,1,0:T(8,128)(2,1)} %get-tuple-element.17.refs_0_, bf16[128,64,384]{2,1,0:T(8,128)(2,1)} %collective-permute-done.6.refs_1_, ...), custom_call_target="tpu_custom_call" | custom-call | tf_op jit(solution)/shard_map/triangle/pallas_call | solution.py:97
  786.0 11.2 %finish.3.refs_10_ = bf16[192,192,128]{2,1,0:T(8,128)(2,1)} custom-call(bf16[64,64,128]{2,1,0:T(8,128)(2,1)S(1)} %triangle.30.refs_0_, bf16[64,64,128]{2,1,0:T(8,128)(2,1)} %copy-done.4, bf16[64,64,128]{2,1,0:T(8,128)(2,1)} %copy-done.5, bf16[64,64,128]{2,1,0:T(8,128)(2,1)} %copy-done.11, ...), custom_call_target="tpu_custom_call", output_to_operand_aliasing={{}: (10, {})} | custom-call | tf_op jit(solution)/shard_map/finish/pallas_call | solution.py:182
  797.2 11.2 %finish.4.refs_10_ = bf16[192,192,128]{2,1,0:T(8,128)(2,1)} custom-call(bf16[64,64,128]{2,1,0:T(8,128)(2,1)S(1)} %triangle.24.refs_0_, bf16[64,64,128]{2,1,0:T(8,128)(2,1)} %copy-done.2, bf16[64,64,128]{2,1,0:T(8,128)(2,1)} %copy-done.3, bf16[64,64,128]{2,1,0:T(8,128)(2,1)} %copy-done.10, ...), custom_call_target="tpu_custom_call", output_to_operand_aliasing={{}: (10, {})} | custom-call | tf_op jit(solution)/shard_map/finish/pallas_call | solution.py:182
  808.4 11.2 %finish.5 = bf16[192,192,128]{2,1,0:T(8,128)(2,1)} custom-call(bf16[64,64,128]{2,1,0:T(8,128)(2,1)S(1)} %triangle.18.refs_0_, bf16[64,64,128]{2,1,0:T(8,128)(2,1)} %copy-done, bf16[64,64,128]{2,1,0:T(8,128)(2,1)} %copy-done.1, bf16[64,64,128]{2,1,0:T(8,128)(2,1)} %collective-permute-done.12.refs_3_, ...), custom_call_target="tpu_custom_call", output_to_operand_aliasing={{}: (10, {})} | custom-call | tf_op jit(solution)/shard_map/finish/pallas_call | solution.py:182
  (95 shorter events, 149.6 us)
Async XLA Ops:
  5.4 71.1 %collective-permute-start = (bf16[64,192,128]{2,1,0:T(8,128)(2,1)S(1)}, bf16[64,192,128]{2,1,0:T(8,128)(2,1)S(1)}, u32[]{:S(2)}, u32[]{:S(2)}) collective-permute-start(bf16[64,192,128]{2,1,0:T(8,128)(2,1)S(1)} %get-tuple-element.21), channel_id=1, source_target_pairs={{0,1},{1,0},{2,3},{3,2},{4,5},{5,4},{6,7},{7,6},{8,9},{9,8},{10,11... | collective-permute-start | bytes 9437192 | tf_op jit(solution)/shard_map/ppermute | solution.py:274
  76.5 69.3 %collective-permute-start.1 = (bf16[64,192,128]{2,1,0:T(8,128)(2,1)S(1)}, bf16[64,192,128]{2,1,0:T(8,128)(2,1)S(1)}, u32[]{:S(2)}, u32[]{:S(2)}) collective-permute-start(bf16[64,192,128]{2,1,0:T(8,128)(2,1)S(1)} %get-tuple-element.13), channel_id=1, source_target_pairs={{0,1},{1,0},{2,3},{3,2},{4,5},{5,4},{6,7},{7,6},{8,9},{9,8},{10,11... | collective-permute-start | bytes 9437192 | tf_op jit(solution)/shard_map/ppermute | solution.py:274
  145.8 83.1 %collective-permute-start.2 = (bf16[64,192,128]{2,1,0:T(8,128)(2,1)}, bf16[64,192,128]{2,1,0:T(8,128)(2,1)}, u32[]{:S(2)}, u32[]{:S(2)}) collective-permute-start(bf16[64,192,128]{2,1,0:T(8,128)(2,1)} %get-tuple-element.14), channel_id=1, source_target_pairs={{0,1},{1,0},{2,3},{3,2},{4,5},{5,4},{6,7},{7,6},{8,9},{9,8},{10,11... | collective-permute-start | bytes 9437192 | tf_op jit(solution)/shard_map/ppermute | solution.py:274
  183.4 84.3 %collective-permute-start.4 = (bf16[128,64,384]{2,1,0:T(8,128)(2,1)}, bf16[128,64,384]{2,1,0:T(8,128)(2,1)}, u32[]{:S(2)}, u32[]{:S(2)}) collective-permute-start(bf16[128,64,384]{2,1,0:T(8,128)(2,1)} %get-tuple-element.16.refs_0_), channel_id=1, source_target_pairs={{0,8},{2,10},{5,13},{7,15},{8,0},{10,2},{13,5},{15,7},{16,24},{18,... | collective-permute-start | bytes 18874376 | tf_op jit(solution)/shard_map/ppermute | solution.py:225
  186.7 141.2 %collective-permute-start.3 = (bf16[128,64,384]{2,1,0:T(8,128)(2,1)}, bf16[128,64,384]{2,1,0:T(8,128)(2,1)}, u32[]{:S(2)}, u32[]{:S(2)}) collective-permute-start(bf16[128,64,384]{2,1,0:T(8,128)(2,1)} %get-tuple-element.16.refs_0_), channel_id=1, source_target_pairs={{0,4},{2,6},{5,1},{7,3},{8,12},{10,14},{13,9},{15,11},{16,20},{18,... | collective-permute-start | bytes 18874376 | tf_op jit(solution)/shard_map/ppermute | solution.py:239
  226.3 97.7 %collective-permute-start.7 = (bf16[128,64,384]{2,1,0:T(8,128)(2,1)}, bf16[128,64,384]{2,1,0:T(8,128)(2,1)}, u32[]{:S(2)}, u32[]{:S(2)}) collective-permute-start(bf16[128,64,384]{2,1,0:T(8,128)(2,1)} %get-tuple-element.17.refs_0_), channel_id=1, source_target_pairs={{0,8},{2,10},{5,13},{7,15},{8,0},{10,2},{13,5},{15,7},{16,24},{18,... | collective-permute-start | bytes 18874376 | tf_op jit(solution)/shard_map/ppermute | solution.py:225
  264.4 127.0 %collective-permute-start.10 = (bf16[128,64,384]{2,1,0:T(8,128)(2,1)}, bf16[128,64,384]{2,1,0:T(8,128)(2,1)}, u32[]{:S(2)}, u32[]{:S(2)}) collective-permute-start(bf16[128,64,384]{2,1,0:T(8,128)(2,1)} %get-tuple-element.18.refs_0_), channel_id=1, source_target_pairs={{0,8},{2,10},{5,13},{7,15},{8,0},{10,2},{13,5},{15,7},{16,24},{18,... | collective-permute-start | bytes 18874376 | tf_op jit(solution)/shard_map/ppermute | solution.py:225
  267.7 127.9 %collective-permute-start.5 = (bf16[128,64,384]{2,1,0:T(8,128)(2,1)}, bf16[128,64,384]{2,1,0:T(8,128)(2,1)}, u32[]{:S(2)}, u32[]{:S(2)}) collective-permute-start(bf16[128,64,384]{2,1,0:T(8,128)(2,1)} %collective-permute-done.4.refs_2_), channel_id=1, source_target_pairs={{0,4},{2,6},{5,1},{7,3},{8,12},{10,14},{13,9},{15,11},{16,20},{18,... | collective-permute-start | bytes 18874376 | tf_op jit(solution)/shard_map/ppermute | solution.py:239
  271.8 144.8 %collective-permute-start.6 = (bf16[128,64,384]{2,1,0:T(8,128)(2,1)}, bf16[128,64,384]{2,1,0:T(8,128)(2,1)}, u32[]{:S(2)}, u32[]{:S(2)}) collective-permute-start(bf16[128,64,384]{2,1,0:T(8,128)(2,1)} %get-tuple-element.17.refs_0_), channel_id=1, source_target_pairs={{0,4},{2,6},{5,1},{7,3},{8,12},{10,14},{13,9},{15,11},{16,20},{18,... | collective-permute-start | bytes 18874376 | tf_op jit(solution)/shard_map/ppermute | solution.py:239
  324.0 93.1 %collective-permute-start.8 = (bf16[128,64,384]{2,1,0:T(8,128)(2,1)}, bf16[128,64,384]{2,1,0:T(8,128)(2,1)}, u32[]{:S(2)}, u32[]{:S(2)}) collective-permute-start(bf16[128,64,384]{2,1,0:T(8,128)(2,1)} %collective-permute-done.7.refs_2_), channel_id=1, source_target_pairs={{0,4},{2,6},{5,1},{7,3},{8,12},{10,14},{13,9},{15,11},{16,20},{18,... | collective-permute-start | bytes 18874376 | tf_op jit(solution)/shard_map/ppermute | solution.py:239
  327.9 101.0 %collective-permute-start.9 = (bf16[128,64,384]{2,1,0:T(8,128)(2,1)}, bf16[128,64,384]{2,1,0:T(8,128)(2,1)}, u32[]{:S(2)}, u32[]{:S(2)}) collective-permute-start(bf16[128,64,384]{2,1,0:T(8,128)(2,1)} %get-tuple-element.18.refs_0_), channel_id=1, source_target_pairs={{0,4},{2,6},{5,1},{7,3},{8,12},{10,14},{13,9},{15,11},{16,20},{18,... | collective-permute-start | bytes 18874376 | tf_op jit(solution)/shard_map/ppermute | solution.py:239
  391.4 37.4 %collective-permute-start.11 = (bf16[128,64,384]{2,1,0:T(8,128)(2,1)}, bf16[128,64,384]{2,1,0:T(8,128)(2,1)}, u32[]{:S(2)}, u32[]{:S(2)}) collective-permute-start(bf16[128,64,384]{2,1,0:T(8,128)(2,1)} %collective-permute-done.10.refs_2_), channel_id=1, source_target_pairs={{0,4},{2,6},{5,1},{7,3},{8,12},{10,14},{13,9},{15,11},{16,20},{18,... | collective-permute-start | bytes 18874376 | tf_op jit(solution)/shard_map/ppermute | solution.py:239
  404.8 136.0 %collective-permute-start.15 = (bf16[64,64,128]{2,1,0:T(8,128)(2,1)S(1)}, bf16[64,64,128]{2,1,0:T(8,128)(2,1)S(1)}, u32[]{:S(2)}, u32[]{:S(2)}) collective-permute-start(bf16[64,64,128]{2,1,0:T(8,128)(2,1)S(1)} %triangle.27), channel_id=1, source_target_pairs={{0,2},{1,3},{2,0},{3,1},{4,6},{5,7},{6,4},{7,5},{8,10},{9,11},{10,... | collective-permute-start | bytes 3145736 | tf_op jit(solution)/shard_map/ppermute | solution.py:289
  416.6 169.2 %collective-permute-start.18 = (bf16[64,64,128]{2,1,0:T(8,128)(2,1)S(1)}, bf16[64,64,128]{2,1,0:T(8,128)(2,1)S(1)}, u32[]{:S(2)}, u32[]{:S(2)}) collective-permute-start(bf16[64,64,128]{2,1,0:T(8,128)(2,1)S(1)} %triangle.33), channel_id=1, source_target_pairs={{0,2},{1,3},{2,0},{3,1},{4,6},{5,7},{6,4},{7,5},{8,10},{9,11},{10,... | collective-permute-start | bytes 3145736 | tf_op jit(solution)/shard_map/ppermute | solution.py:289
  426.3 204.4 %collective-permute-start.19 = (bf16[64,64,128]{2,1,0:T(8,128)(2,1)S(1)}, bf16[64,64,128]{2,1,0:T(8,128)(2,1)S(1)}, u32[]{:S(2)}, u32[]{:S(2)}) collective-permute-start(bf16[64,64,128]{2,1,0:T(8,128)(2,1)S(1)} %triangle.34), channel_id=1, source_target_pairs={{0,2},{1,3},{2,0},{3,1},{4,6},{5,7},{6,4},{7,5},{8,10},{9,11},{10,... | collective-permute-start | bytes 3145736 | tf_op jit(solution)/shard_map/ppermute | solution.py:289
  438.1 226.5 %collective-permute-start.20 = (bf16[64,64,128]{2,1,0:T(8,128)(2,1)S(1)}, bf16[64,64,128]{2,1,0:T(8,128)(2,1)}, u32[]{:S(2)}, u32[]{:S(2)}) collective-permute-start(bf16[64,64,128]{2,1,0:T(8,128)(2,1)S(1)} %triangle.35), channel_id=1, source_target_pairs={{0,2},{1,3},{2,0},{3,1},{4,6},{5,7},{6,4},{7,5},{8,10},{9,11},{10,... | collective-permute-start | bytes 3145736 | tf_op jit(solution)/shard_map/ppermute | solution.py:289
  447.8 360.6 %collective-permute-start.12 = (bf16[64,64,128]{2,1,0:T(8,128)(2,1)S(1)}, bf16[64,64,128]{2,1,0:T(8,128)(2,1)}, u32[]{:S(2)}, u32[]{:S(2)}) collective-permute-start(bf16[64,64,128]{2,1,0:T(8,128)(2,1)S(1)} %triangle.21), channel_id=1, source_target_pairs={{0,2},{1,3},{2,0},{3,1},{4,6},{5,7},{6,4},{7,5},{8,10},{9,11},{10,... | collective-permute-start | bytes 3145736 | tf_op jit(solution)/shard_map/ppermute | solution.py:289
  478.9 186.1 %copy-start.17 = (f32[128]{0:T(128)S(1)}, f32[128]{0:T(128)}, u32[]{:S(2)}) copy-start(f32[128]{0:T(128)} %param.14) | copy-start | bytes 1540
  479.0 186.5 %copy-start.14 = (bf16[128,128]{1,0:T(8,128)(2,1)S(1)}, bf16[128,128]{1,0:T(8,128)(2,1)}, u32[]{:S(2)}) copy-start(bf16[128,128]{1,0:T(8,128)(2,1)} %param.15) | copy-start | bytes 98308
  479.0 186.5 %copy-start.15 = (bf16[128,128]{1,0:T(8,128)(2,1)S(1)}, bf16[128,128]{1,0:T(8,128)(2,1)}, u32[]{:S(2)}) copy-start(bf16[128,128]{1,0:T(8,128)(2,1)} %param.12) | copy-start | bytes 98308
  540.9 256.3 %collective-permute-start.16 = (bf16[64,64,128]{2,1,0:T(8,128)(2,1)}, bf16[64,64,128]{2,1,0:T(8,128)(2,1)}, u32[]{:S(2)}, u32[]{:S(2)}) collective-permute-start(bf16[64,64,128]{2,1,0:T(8,128)(2,1)} %triangle.28), channel_id=1, source_target_pairs={{0,2},{1,3},{2,0},{3,1},{4,6},{5,7},{6,4},{7,5},{8,10},{9,11},{10,... | collective-permute-start | bytes 3145736 | tf_op jit(solution)/shard_map/ppermute | solution.py:289
  585.8 211.4 %collective-permute-start.17 = (bf16[64,64,128]{2,1,0:T(8,128)(2,1)}, bf16[64,64,128]{2,1,0:T(8,128)(2,1)}, u32[]{:S(2)}, u32[]{:S(2)}) collective-permute-start(bf16[64,64,128]{2,1,0:T(8,128)(2,1)} %triangle.29), channel_id=1, source_target_pairs={{0,2},{1,3},{2,0},{3,1},{4,6},{5,7},{6,4},{7,5},{8,10},{9,11},{10,... | collective-permute-start | bytes 3145736 | tf_op jit(solution)/shard_map/ppermute | solution.py:289
  630.7 177.7 %collective-permute-start.13 = (bf16[64,64,128]{2,1,0:T(8,128)(2,1)S(1)}, bf16[64,64,128]{2,1,0:T(8,128)(2,1)}, u32[]{:S(2)}, u32[]{:S(2)}) collective-permute-start(bf16[64,64,128]{2,1,0:T(8,128)(2,1)S(1)} %triangle.22), channel_id=1, source_target_pairs={{0,2},{1,3},{2,0},{3,1},{4,6},{5,7},{6,4},{7,5},{8,10},{9,11},{10,... | collective-permute-start | bytes 3145736 | tf_op jit(solution)/shard_map/ppermute | solution.py:289
  664.6 143.8 %collective-permute-start.14 = (bf16[64,64,128]{2,1,0:T(8,128)(2,1)S(1)}, bf16[64,64,128]{2,1,0:T(8,128)(2,1)}, u32[]{:S(2)}, u32[]{:S(2)}) collective-permute-start(bf16[64,64,128]{2,1,0:T(8,128)(2,1)S(1)} %triangle.23), channel_id=1, source_target_pairs={{0,2},{1,3},{2,0},{3,1},{4,6},{5,7},{6,4},{7,5},{8,10},{9,11},{10,... | collective-permute-start | bytes 3145736 | tf_op jit(solution)/shard_map/ppermute | solution.py:289
  (15 other events, 943.0 us)

commit v2 on v1

--- a/solution.py
+++ b/solution.py
@@ -8,7 +8,7 @@
 from jax.experimental.pallas import tpu as pltpu
 from jax.sharding import PartitionSpec as P
 
-CHUNKS = 3
+CHUNKS = 6
 EPS = 1e-05
 F32, BF16 = jnp.float32, jnp.bfloat16
 PARAMS = pltpu.CompilerParams(vmem_limit_bytes=52 * 1024 * 1024)
@@ -17,6 +17,14 @@
 def contract(left, right, left_dim, right_dim):
     return lax.dot_general(
         left, right, (((left_dim,), (right_dim,)), ((), ())), preferred_element_type=F32
+    )
+
+
+def at_least(macs, transcendentals, *arrays):
+    return pl.CostEstimate(
+        flops=2 * macs,
+        transcendentals=transcendentals,
+        bytes_accessed=sum(math.prod(x.shape) * x.dtype.itemsize for x in arrays),
     )
 
 
@@ -40,7 +48,7 @@
                 held[n, pl.ds(i, hidden, stride=rows), :] = side[:, n * 128 : (n + 1) * 128]
         return carry
 
-    lax.fori_loop(0, rows, one_row, 0, unroll=2)
+    lax.fori_loop(0, rows, one_row, 0, unroll=8)
     for held, out in ((left_rows, left_out), (right_rows, right_out)):
         for n in range(depth // 128):
             out[:, :, n * 128 : (n + 1) * 128] = held[n].reshape(hidden, rows, 128).astype(BF16)
@@ -65,48 +73,62 @@
         out_shape=[shape, shape],
         scratch_shapes=[pltpu.VMEM((depth // 128, hidden * rows, 128), F32)] * 2,
         compiler_params=PARAMS,
+        cost_estimate=at_least(
+            count * depth * channels * (channels + 4 * hidden), 2 * count * depth * hidden, shape, shape
+        ),
         name="project",
     )(*pieces, weights, centre, gain, bias)
 
 
-def triangle_kernel(n_sides, group, which, left, *refs):
-    sides, out = refs[:n_sides], refs[n_sides]
-
-    def go(side):
-        for first in range(0, left.shape[0], group):
-            parts = [contract(left[h], side[h], 1, 1) for h in range(first, first + group)]
-            out[first // group] = jnp.concatenate(parts, axis=-1).astype(BF16)
-
-    for n, side in enumerate(sides):
-        pl.when(which[0] == n)(functools.partial(go, side))
+def triangle_kernel(n_left, n_sides, group, pairs, which, *refs):
+    lefts, out = refs[:n_left], refs[-1]
+    sides = refs[n_left:-1]
+    step = lefts[0].shape[0]
+
+    def go(choice):
+        for first in range(0, step, group):
+            for n, (i, j) in enumerate(pairs):
+                side = sides[j * n_sides + choice]
+                parts = [contract(lefts[i][h], side[h], 1, 1) for h in range(first, first + group)]
+                out[n, first // group] = jnp.concatenate(parts, axis=-1).astype(BF16)
+
+    for n in range(n_sides):
+        pl.when(which[0] == n)(functools.partial(go, n))
 
 
 def group_of(columns):
     return 128 // math.gcd(columns, 128)
 
 
-def triangle(left, sides, which):
-    hidden, rows, depth = left.shape
-    columns = sides[0].shape[1]
+def triangle(lefts, rights, pairs, which):
+    hidden, rows, depth = lefts[0].shape
+    columns = rights[0][0].shape[1]
+    n_sides = len(rights[0])
     group = group_of(columns)
-    step = max(16, group)
+    step = max(8, group)
+    shape = jax.ShapeDtypeStruct((len(pairs), hidden // group, rows, group * columns), BF16)
 
     def side_spec(n):
         return pl.BlockSpec((step, columns, depth), lambda h, which: (jnp.where(which[0] == n, h, 0), 0, 0))
 
     return pl.pallas_call(
-        functools.partial(triangle_kernel, len(sides), group),
+        functools.partial(triangle_kernel, len(lefts), n_sides, group, pairs),
         grid_spec=pltpu.PrefetchScalarGridSpec(
             num_scalar_prefetch=1,
             grid=(hidden // step,),
-            in_specs=[pl.BlockSpec((step, rows, depth), lambda h, which: (h, 0, 0))]
-            + [side_spec(n) for n in range(len(sides))],
-            out_specs=pl.BlockSpec((step // group, rows, group * columns), lambda h, which: (h, 0, 0)),
-        ),
-        out_shape=jax.ShapeDtypeStruct((hidden // group, rows, group * columns), BF16),
+            in_specs=[pl.BlockSpec((step, rows, depth), lambda h, which: (h, 0, 0))] * len(lefts)
+            + [side_spec(n) for _ in rights for n in range(n_sides)],
+            out_specs=pl.BlockSpec(
+                (len(pairs), step // group, rows, group * columns), lambda h, which: (0, h, 0, 0)
+            ),
+        ),
+        out_shape=shape,
         compiler_params=PARAMS,
+        cost_estimate=at_least(
+            len(pairs) * hidden * rows * columns * depth, 0, shape, *lefts, *[side[0] for side in rights]
+        ),
         name="triangle",
-    )(which, left, *sides)
+    )(which, *lefts, *[x for side in rights for x in side])
 
 
 def gate_kernel(pair, centre, mean, gain, bias, weights, out):
@@ -134,13 +156,17 @@
         out_specs=block,
         out_shape=jax.ShapeDtypeStruct(pair.shape, BF16),
         compiler_params=PARAMS,
+        cost_estimate=at_least(
+            count * columns * channels * 4 * channels, count * columns * channels, pair, pair
+        ),
         name="gate",
     )(pair, centre, mean, gain, bias, weights)
 
 
 def finish_kernel(n_parts, group, hidden, *refs):
     own, sent = refs[:n_parts], refs[n_parts : 2 * n_parts]
-    gate, weights, gain, bias, _, out, rows_of = refs[2 * n_parts :]
+    gate, weights, gain, bias = refs[2 * n_parts : 2 * n_parts + 4]
+    out, rows_of = refs[-2:]
     packed, rows, lanes = own[0].shape
     columns = lanes // group
 
@@ -171,26 +197,34 @@
 
 
 def finish(own, sent, gate, first, weights, gain, bias, held):
-    rows = 8
-    packed, count, lanes = own[0].shape
+    rows = 16
+    _, packed, count, lanes = own[0][0].shape
     hidden = weights.shape[0]
     group = hidden // packed
     whole = lambda x: pl.BlockSpec(x.shape, lambda i: (0,) * x.ndim)
-    part = pl.BlockSpec((packed, rows, lanes), lambda i: (0, i, 0))
+    part = lambda n: pl.BlockSpec((None, packed, rows, lanes), lambda i: (n, 0, i, 0))
     block = pl.BlockSpec((rows,) + gate.shape[1:], lambda i: (i + first // rows, 0, 0))
     n_parts = len(own)
+    parts = own + sent
+    earlier = [] if held is None else [held]
     return pl.pallas_call(
         functools.partial(finish_kernel, n_parts, group, hidden),
         grid=(count // rows,),
-        in_specs=[part] * (2 * n_parts)
-        + [block, whole(weights), whole(gain), whole(bias), pl.BlockSpec(memory_space=pl.ANY)],
+        in_specs=[part(n) for _, n in parts]
+        + [block, whole(weights), whole(gain), whole(bias)]
+        + [pl.BlockSpec(memory_space=pl.ANY)] * len(earlier),
         out_specs=block,
         out_shape=jax.ShapeDtypeStruct(gate.shape, BF16),
         scratch_shapes=[pltpu.VMEM((n_parts, packed * rows, lanes), F32)],
-        input_output_aliases={2 * n_parts + 4: 0},
+        input_output_aliases={2 * n_parts + 4: 0} if earlier else {},
         compiler_params=PARAMS,
+        cost_estimate=at_least(
+            count * gate.shape[1] * hidden * gate.shape[2],
+            count * gate.shape[1],
+            *[jax.ShapeDtypeStruct(x.shape[1:], x.dtype) for x, _ in parts],
+        ),
         name="finish",
-    )(*own, *sent, gate, weights, gain, bias, held)
+    )(*[x for x, _ in parts], gate, weights, gain, bias, *earlier)
 
 
 def after(value, *others):
@@ -206,7 +240,8 @@
     row, col = lax.axis_index("row"), lax.axis_index("col")
     axes = ("row", "col")
     place = lambda r, c: r * n_col + c
-    step = tile_rows // CHUNKS
+    chunks = min(CHUNKS, tile_rows // 16)
+    step = tile_rows // chunks
     group = group_of(step)
     packed = hidden // group
 
@@ -221,12 +256,11 @@
     def holds(r, c):
         return (r // share) % half == c % half
 
-    def spread(near):
-        far = lax.ppermute(
-            near,
-            axes,
-            [(place(r, c), place(r ^ top, c)) for r in range(n_row) for c in range(n_col) if holds(r, c)],
-        )
+    def across_top(near):
+        pairs = [(place(r, c), place(r ^ top, c)) for r in range(n_row) for c in range(n_col) if holds(r, c)]
+        return lax.ppermute(near, axes, pairs)
+
+    def to_all_rows(held):
         bit = top // 2
         while bit >= share:
             alike = (bit * 2 - 1) & ~(share - 1)
@@ -236,64 +270,117 @@
                 for c in range(n_col)
                 if (r ^ (c * share)) & alike == 0
             ]
-            near_in, far_in = lax.ppermute(near, axes, sends), lax.ppermute(far, axes, sends)
-            keep = ((row ^ (col * share)) & bit) == 0
+            came = lax.ppermute(held, axes, sends)
             if bit == 1:
-                return [near, near_in, far, far_in], jnp.where(keep, 0, 1)
-            near, far = jnp.where(keep, near, near_in), jnp.where(keep, far, far_in)
+                return [[held, came]]
+            held = jnp.where(((row ^ (col * share)) & bit) == 0, held, came)
             bit //= 2
-        sides = [[near], [far]]
+        slabs = [held]
         while bit >= 1:
             swap = [(r, r ^ bit) for r in range(n_row)]
-            first = (row & bit) == 0
-            for n in range(2):
-                others = [lax.ppermute(x, "row", swap) for x in sides[n]]
-                sides[n] = [jnp.where(first, a, b) for a, b in zip(sides[n] + others, others + sides[n])]
+            others = [lax.ppermute(x, "row", swap) for x in slabs]
+            slabs = [jnp.where((row & bit) == 0, a, b) for a, b in zip(slabs + others, others + slabs)]
             bit //= 2
-        return sides, jnp.int32(0)
+        return [[x] for x in slabs]
 
     near_is_own = (row // top) == (col // half)
     swap_half = [(c, c ^ half) for c in range(n_col)]
-    lefts, spreads, sent = [], [], {}
-
-    def product(i, j, s, own):
-        sides, choice = spreads[j]
+    lefts, nears, fars, units = [], [], [], []
+
+    def product(pairs, own):
         take_near = near_is_own if own else jnp.logical_not(near_is_own)
-        if share == 1:
-            which = jnp.where(take_near, choice, choice + len(sides) // 2)
-            return triangle(lefts[i], sides, which.astype(jnp.int32).reshape(1))
-        which = jnp.where(take_near, 0, 1)
-        return triangle(lefts[i], [sides[0][s], sides[1][s]], which.astype(jnp.int32).reshape(1))
-
-    blocks = [pair_act[t * step : (t + 1) * step] for t in range(CHUNKS)]
-    last = None
-    for t in range(CHUNKS):
-        block = blocks[t] if last is None else after(blocks[t], last)
-        pieces = [block]
-        for offset in range(1, half):
-            pieces.append(lax.ppermute(block, "col", [(c, c ^ offset) for c in range(n_col)]))
-        last = pieces[-1]
+        which = jnp.where(take_near, 0, len(nears[0][0]))
+        if share == 1 and top > 1:
+            which = which + ((row ^ col) & 1)
+        used_left = sorted({i for i, _, _ in pairs})
+        used_right = sorted({(j, s) for _, j, s in pairs})
+        return triangle(
+            [lefts[i] for i in used_left],
+            [units[j][s] for j, s in used_right],
+            [(used_left.index(i), used_right.index((j, s))) for i, j, s in pairs],
+            which.astype(jnp.int32).reshape(1),
+        )
+
+    wide = lambda v: jnp.broadcast_to(v[:, None], (channels, half * tile_cols))
+    gain_in, bias_in = wide(ln_gain), wide(ln_bias)
+    shards = range(share)
+    waves = []
+    for t in range(chunks):
+        by_column = [(i, t, s) for i in range(t) for s in shards]
+        by_row = [(t, j, s) for j in range(t + 1) for s in shards]
+        waves.append([by_column, by_row] if t == chunks - 1 and t else [by_column + by_row])
+
+    exchanged, arrived, own_parts, sent_parts = [], {}, {}, {}
+
+    def exchange(t):
+        block = pair_act[t * step : (t + 1) * step]
+        if exchanged:
+            block = after(block, exchanged[-1][-1])
+        exchanged.append([lax.ppermute(block, "col", [(c, c ^ o) for c in range(n_col)]) for o in range(1, half)])
+
+    def prepare(t, *held):
+        exchange(t)
+        scale = after(gain_in, *held) if held else gain_in
         left, right = project(
-            [pair_act] + pieces[1:],
+            [pair_act] + exchanged[t],
             [t * step] + [0] * (half - 1),
             step,
             halves,
             centre,
-            ln_gain[:, None],
-            ln_bias[:, None],
+            scale,
+            bias_in,
         )
         lefts.append(left)
-        spreads.append(spread(right))
-        for i, j in [(a, t) for a in range(t)] + [(t, b) for b in range(t + 1)]:
-            for s in range(share):
-                sent[i, j, s] = lax.ppermute(product(i, j, s, False), "col", swap_half)
-
-    gate = gate_of(pair_act, centre, mean, ln_gain[None], ln_bias[None], half_gate)
-    order = [(j, s) for s in range(share) for j in range(CHUNKS)]
-    out = jnp.zeros(pair_act.shape, BF16)
-    for i in range(CHUNKS):
-        own = [product(i, j, s, True) for j, s in order]
-        out = finish(own, [sent[i, j, s] for j, s in order], gate, i * step, w_last, gain_out, bias_out, out)
+        fars.append(across_top(right))
+        nears.append(to_all_rows(right))
+        return left
+
+    def complete(t):
+        waits = nears[t + 1][-1][-1:] if t + 1 < len(nears) else []
+        far = to_all_rows(after(fars[t], *waits))
+        units.append([a + b for a, b in zip(nears[t], far)])
+
+    ahead = 2
+    token = []
+    moved = []
+    for t in range(min(ahead, chunks)):
+        token = [prepare(t, *token)]
+    for t in range(chunks):
+        complete(t)
+        for pairs in waves[t]:
+            lefts[t] = after(lefts[t], *token)
+            made = product(pairs, False)
+            token = [made]
+            moved.append(lax.ppermute(made, "col", swap_half))
+            for n, pair in enumerate(pairs):
+                sent_parts[pair] = (moved[-1], n)
+        if t + ahead < chunks:
+            token = [prepare(t + ahead, *token, *(moved[t - 1 : t] if t in (1, 2) else []))]
+    for t in range(chunks):
+        pairs = [pair for part in waves[t] for pair in part]
+        if t == 0 and chunks > 3:
+            token = token + [moved[chunks - 3]]
+        if t == chunks // 2:
+            token = token + [moved[chunks - 2]]
+        lefts[t] = after(lefts[t], *token)
+        made = product(pairs, True)
+        token = [made]
+        for n, pair in enumerate(pairs):
+            own_parts[pair] = (made, n)
+    gate = gate_of(pair_act, centre, mean, after(ln_gain[None], *token), ln_bias[None], half_gate)
+    out = None
+    for i in range(chunks):
+        pairs = [(i, j, s) for s in shards for j in range(chunks)]
+        out = finish(
+            [own_parts[pair] for pair in pairs],
+            [sent_parts[pair] for pair in pairs],
+            gate,
+            i * step,
+            w_last,
+            gain_out,
+            bias_out,
+            out,
+        )
     return out
 
 

time: 827 us -> 902 us (1.091)
  Pallas kernels: 333 us -> 418 us
  waiting for transfers between devices: 419 us -> 378 us
  starting transfers between devices: 47.9 us -> 72.5 us
    pallas_call x18 -> x13, Pallas kernels: 168 us -> 236 us  [triangle(): pl.pallas_call(functools.partial(triangle_kernel, len(lefts), n_sides, gr...]
    ppermute x21 -> x31, waiting for transfers between devices: 419 us -> 378 us  [the longest x7 246 us: on_device(): moved.append(lax.ppermute(made, 'col', swap_half))]
    ppermute x21 -> x31, starting transfers between devices: 47.9 us -> 72.5 us  [the longest x12 31.7 us: to_all_rows(): came = lax.ppermute(held, axes, sends)]
    pallas_call x3 -> x6, Pallas kernels: 33.5 us -> 55.6 us  [finish(): pl.pallas_call(functools.partial(finish_kernel, n_parts, group, hidden),...]
    pallas_call x3 -> x6, Pallas kernels: 107 us -> 102 us  [project(): pl.pallas_call(functools.partial(project_kernel, len(pieces)), grid=(coun...]
  transfers between devices with their start and end apart: 21 -> 31, of which waited for: 8 -> 17; matrix products, arithmetic and copies ran while one was open for 1% -> 0% of each run, Pallas kernels for 39% -> 46%
where the time goes in v2:
time: 902 us; the launch traced here: 889 us
  Pallas kernels  418 us (46%)
  waiting for transfers between devices  378 us (42%)
  starting transfers between devices  72.5 us (8%)
  local copies, waits for them, and re-layouts  18.9 us (2%)
    ppermute x7, waiting for transfers between devices, on_device(): moved.append(lax.ppermute(made, 'col', swap_half))  246 us
    pallas_call x13, Pallas kernels, triangle(): pl.pallas_call(functools.partial(triangle_kernel, len(lefts), n_sides, gr...  236 us
    pallas_call x6, Pallas kernels, project(): pl.pallas_call(functools.partial(project_kernel, len(pieces)), grid=(coun...  102 us
    ppermute x6, waiting for transfers between devices, exchange(): lax.ppermute(block, 'col', [(c, c ^ o) for c in range(n_col)])  80.8 us
    pallas_call x6, Pallas kernels, finish(): pl.pallas_call(functools.partial(finish_kernel, n_parts, group, hidden),...  55.6 us
    ppermute x6, waiting for transfers between devices, across_top(): return lax.ppermute(near, axes, pairs)  31.7 us
    ppermute x12, starting transfers between devices, to_all_rows(): came = lax.ppermute(held, axes, sends)  31.7 us
    pallas_call x1, Pallas kernels, gate_of(): pl.pallas_call(gate_kernel, grid=(count // rows,), in_specs=[block] + [wh...  25.1 us
  transfers between devices with their start and end apart: 31, of which 17 were waited for; matrix products, arithmetic and copies ran while one was open for 0% of the time, Pallas kernels for 46%

profile of v2, /device:TPU:0, one launch (start us, length us, event | category | flops | bytes accessed | tf_op | source)
XLA Modules:
  0.0 888.9 jit_solution(1354236516563433561)
XLA Ops:
  9.6 34.4 %collective-permute-done.refs_1_ = bf16[32,192,128]{2,1,0:T(8,128)(2,1)S(1)} collective-permute-done((bf16[32,192,128]{2,1,0:T(8,128)(2,1)S(1)}, bf16[32,192,128]{2,1,0:T(8,128)(2,1)S(1)}, u32[]{:S(2)}, u32[]{:S(2)}) %collective-permute-start) | collective-permute-done | bytes 1572896 | tf_op jit(solution)/shard_map/ppermute | solution.py:319
  47.3 17.0 %project.6 = (bf16[128,32,384]{2,1,0:T(8,128)(2,1)}, bf16[128,32,384]{2,1,0:T(8,128)(2,1)}) custom-call(bf16[192,192,128]{2,1,0:T(8,128)(2,1)} %pair.1, bf16[32,192,128]{2,1,0:T(8,128)(2,1)} %copy-done.23, bf16[512,128]{1,0:T(8,128)(2,1)S(1)} %multiply_bitcast_fusion.refs_2_, bf16[128,128]{1,0:T(8,128)(2,1)S(1)} %add_convert_fusion.refs_3_.centre, ...), custom_call_target="tpu_custom_call" | custom-call | flops 2013265920 | bytes 6291456 | tf_op jit(solution)/shard_map/project/pallas_call | solution.py:68
  81.1 17.0 %project.7 = (bf16[128,32,384]{2,1,0:T(8,128)(2,1)}, bf16[128,32,384]{2,1,0:T(8,128)(2,1)}) custom-call(bf16[192,192,128]{2,1,0:T(8,128)(2,1)} %pair.1, bf16[32,192,128]{2,1,0:T(8,128)(2,1)} %collective-permute-done.1.refs_1_, bf16[512,128]{1,0:T(8,128)(2,1)S(1)} %multiply_bitcast_fusion.refs_2_, bf16[128,128]{1,0:T(8,128)(2,1)S(1)} %add_convert_fusion.refs_3_.centre, ...), custom_call_target="tpu_custom_call" | custom-call | flops 2013265920 | bytes 6291456 | tf_op jit(solution)/shard_map/project/pallas_call | solution.py:68
  125.3 21.0 %collective-permute-done.2.refs_1_ = bf16[32,192,128]{2,1,0:T(8,128)(2,1)} collective-permute-done((bf16[32,192,128]{2,1,0:T(8,128)(2,1)}, bf16[32,192,128]{2,1,0:T(8,128)(2,1)}, u32[]{:S(2)}, u32[]{:S(2)}) %collective-permute-start.2) | collective-permute-done | bytes 1572896 | tf_op jit(solution)/shard_map/ppermute | solution.py:319
  146.3 17.0 %project.8 = (bf16[128,32,384]{2,1,0:T(8,128)(2,1)}, bf16[128,32,384]{2,1,0:T(8,128)(2,1)}) custom-call(bf16[192,192,128]{2,1,0:T(8,128)(2,1)} %pair.1, bf16[32,192,128]{2,1,0:T(8,128)(2,1)} %collective-permute-done.2.refs_1_, bf16[512,128]{1,0:T(8,128)(2,1)S(1)} %multiply_bitcast_fusion.refs_2_, bf16[128,128]{1,0:T(8,128)(2,1)S(1)} %add_convert_fusion.refs_3_.centre, ...), custom_call_target="tpu_custom_call" | custom-call | flops 2013265920 | bytes 6291456 | tf_op jit(solution)/shard_map/project/pallas_call | solution.py:68
  181.8 13.9 %triangle.14 = bf16[3,32,32,128]{3,2,1,0:T(8,128)(2,1)S(1)} custom-call(s32[1]{0:T(128)} %bitcast.2.which, bf16[128,32,384]{2,1,0:T(8,128)(2,1)} %get-tuple-element.80.refs_0_, bf16[128,32,384]{2,1,0:T(8,128)(2,1)} %get-tuple-element.81.refs_1_, bf16[128,32,384]{2,1,0:T(8,128)(2,1)} %get-tuple-element.55.refs_1_.refs_2_.refs_3_.refs_4_.refs_5_.refs_6_, ...), custom_call_target="tpu_custom_call" | custom-call | flops 301989888 | bytes 13369344 | tf_op jit(solution)/shard_map/triangle/pallas_call | solution.py:114
  195.7 17.2 %collective-permute-done.13.refs_6_ = bf16[1,32,32,128]{3,2,1,0:T(8,128)(2,1)S(1)} collective-permute-done((bf16[1,32,32,128]{3,2,1,0:T(8,128)(2,1)S(1)}, bf16[1,32,32,128]{3,2,1,0:T(8,128)(2,1)S(1)}, u32[]{:S(2)}, u32[]{:S(2)}) %collective-permute-start.13) | collective-permute-done | bytes 262176 | tf_op jit(solution)/shard_map/ppermute | solution.py:354
  214.5 17.1 %project.9 = (bf16[128,32,384]{2,1,0:T(8,128)(2,1)}, bf16[128,32,384]{2,1,0:T(8,128)(2,1)}) custom-call(bf16[192,192,128]{2,1,0:T(8,128)(2,1)} %pair.1, bf16[32,192,128]{2,1,0:T(8,128)(2,1)} %collective-permute-done.3.refs_1_, bf16[512,128]{1,0:T(8,128)(2,1)S(1)} %multiply_bitcast_fusion.refs_2_, bf16[128,128]{1,0:T(8,128)(2,1)S(1)} %add_convert_fusion.refs_3_.centre, ...), custom_call_target="tpu_custom_call" | custom-call | flops 2013265920 | bytes 6291456 | tf_op jit(solution)/shard_map/project/pallas_call | solution.py:68
  249.4 17.7 %triangle.15 = bf16[5,32,32,128]{3,2,1,0:T(8,128)(2,1)} custom-call(s32[1]{0:T(128)} %bitcast.2.which, bf16[128,32,384]{2,1,0:T(8,128)(2,1)} %get-tuple-element.80.refs_0_, bf16[128,32,384]{2,1,0:T(8,128)(2,1)} %get-tuple-element.81.refs_1_, bf16[128,32,384]{2,1,0:T(8,128)(2,1)} %get-tuple-element.82.refs_2_, ...), custom_call_target="tpu_custom_call" | custom-call | flops 503316480 | bytes 20185088 | tf_op jit(solution)/shard_map/triangle/pallas_call | solution.py:114
  267.1 27.7 %collective-permute-done.17.refs_7_.refs_6_ = bf16[3,32,32,128]{3,2,1,0:T(8,128)(2,1)S(1)} collective-permute-done((bf16[3,32,32,128]{3,2,1,0:T(8,128)(2,1)S(1)}, bf16[3,32,32,128]{3,2,1,0:T(8,128)(2,1)S(1)}, u32[]{:S(2)}, u32[]{:S(2)}) %collective-permute-start.17) | collective-permute-done | bytes 786464 | tf_op jit(solution)/shard_map/ppermute | solution.py:354
  295.1 17.0 %project.10 = (bf16[128,32,384]{2,1,0:T(8,128)(2,1)}, bf16[128,32,384]{2,1,0:T(8,128)(2,1)}) custom-call(bf16[192,192,128]{2,1,0:T(8,128)(2,1)} %pair.1, bf16[32,192,128]{2,1,0:T(8,128)(2,1)} %collective-permute-done.4.refs_1_, bf16[512,128]{1,0:T(8,128)(2,1)S(1)} %multiply_bitcast_fusion.refs_2_, bf16[128,128]{1,0:T(8,128)(2,1)S(1)} %add_convert_fusion.refs_3_.centre, ...), custom_call_target="tpu_custom_call" | custom-call | flops 2013265920 | bytes 6291456 | tf_op jit(solution)/shard_map/project/pallas_call | solution.py:68
  329.2 19.8 %triangle.16 = bf16[7,32,32,128]{3,2,1,0:T(8,128)(2,1)S(1)} custom-call(s32[1]{0:T(128)} %bitcast.2.which, bf16[128,32,384]{2,1,0:T(8,128)(2,1)} %get-tuple-element.80.refs_0_, bf16[128,32,384]{2,1,0:T(8,128)(2,1)} %get-tuple-element.81.refs_1_, bf16[128,32,384]{2,1,0:T(8,128)(2,1)} %get-tuple-element.82.refs_2_, ...), custom_call_target="tpu_custom_call" | custom-call | flops 704643072 | bytes 27000832 | tf_op jit(solution)/shard_map/triangle/pallas_call | solution.py:114
  360.5 17.0 %project.11 = (bf16[128,32,384]{2,1,0:T(8,128)(2,1)}, bf16[128,32,384]{2,1,0:T(8,128)(2,1)}) custom-call(bf16[192,192,128]{2,1,0:T(8,128)(2,1)} %pair.1, bf16[32,192,128]{2,1,0:T(8,128)(2,1)} %copy-done.22, bf16[512,128]{1,0:T(8,128)(2,1)S(1)} %multiply_bitcast_fusion.refs_2_, bf16[128,128]{1,0:T(8,128)(2,1)S(1)} %add_convert_fusion.refs_3_.centre, ...), custom_call_target="tpu_custom_call" | custom-call | flops 2013265920 | bytes 6291456 | tf_op jit(solution)/shard_map/project/pallas_call | solution.py:68
  386.9 31.7 %collective-permute-done.24.refs_7_.refs_23_.refs_28_ = bf16[128,32,384]{2,1,0:T(8,128)(2,1)} collective-permute-done((bf16[128,32,384]{2,1,0:T(8,128)(2,1)}, bf16[128,32,384]{2,1,0:T(8,128)(2,1)}, u32[]{:S(2)}, u32[]{:S(2)}) %collective-permute-start.24) | collective-permute-done | bytes 3145760 | tf_op jit(solution)/shard_map/ppermute | solution.py:261
  423.3 23.2 %triangle.17 = bf16[9,32,32,128]{3,2,1,0:T(8,128)(2,1)} custom-call(s32[1]{0:T(128)} %bitcast.2.which, bf16[128,32,384]{2,1,0:T(8,128)(2,1)} %get-tuple-element.80.refs_0_, bf16[128,32,384]{2,1,0:T(8,128)(2,1)} %get-tuple-element.81.refs_1_, bf16[128,32,384]{2,1,0:T(8,128)(2,1)} %get-tuple-element.82.refs_2_, ...), custom_call_target="tpu_custom_call" | custom-call | flops 905969664 | bytes 33816576 | tf_op jit(solution)/shard_map/triangle/pallas_call | solution.py:114
  449.4 16.7 %triangle.18 = bf16[5,32,32,128]{3,2,1,0:T(8,128)(2,1)} custom-call(s32[1]{0:T(128)} %bitcast.2.which, bf16[128,32,384]{2,1,0:T(8,128)(2,1)} %get-tuple-element.80.refs_0_, bf16[128,32,384]{2,1,0:T(8,128)(2,1)} %get-tuple-element.81.refs_1_, bf16[128,32,384]{2,1,0:T(8,128)(2,1)} %get-tuple-element.82.refs_2_, ...), custom_call_target="tpu_custom_call" | custom-call | flops 503316480 | bytes 20185088 | tf_op jit(solution)/shard_map/triangle/pallas_call | solution.py:114
  466.2 20.3 %triangle.19 = bf16[6,32,32,128]{3,2,1,0:T(8,128)(2,1)} custom-call(s32[1]{0:T(128)} %bitcast.2.which, bf16[128,32,384]{2,1,0:T(8,128)(2,1)} %get-tuple-element.85.refs_0_.refs_5_, bf16[128,32,384]{2,1,0:T(8,128)(2,1)} %get-tuple-element.55.refs_1_.refs_2_.refs_3_.refs_4_.refs_5_.refs_6_, ...), custom_call_target="tpu_custom_call" | custom-call | flops 603979776 | bytes 23592960 | tf_op jit(solution)/shard_map/triangle/pallas_call | solution.py:114
  492.3 200.7 %collective-permute-done.26.refs_9_.refs_6_.refs_7_.refs_8_ = bf16[7,32,32,128]{3,2,1,0:T(8,128)(2,1)} collective-permute-done((bf16[7,32,32,128]{3,2,1,0:T(8,128)(2,1)S(1)}, bf16[7,32,32,128]{3,2,1,0:T(8,128)(2,1)}, u32[]{:S(2)}, u32[]{:S(2)}) %collective-permute-start.26) | collective-permute-done | bytes 1835040 | tf_op jit(solution)/shard_map/ppermute | solution.py:354
  704.4 14.1 %triangle.21.refs_1_.refs_0_ = bf16[3,32,32,128]{3,2,1,0:T(8,128)(2,1)S(1)} custom-call(s32[1]{0:T(128)} %bitcast.which, bf16[128,32,384]{2,1,0:T(8,128)(2,1)} %get-tuple-element.80.refs_0_, bf16[128,32,384]{2,1,0:T(8,128)(2,1)} %get-tuple-element.81.refs_1_, bf16[128,32,384]{2,1,0:T(8,128)(2,1)} %get-tuple-element.55.refs_1_.refs_2_.refs_3_.refs_4_.refs_5_.refs_6_, ...), custom_call_target="tpu_custom_call" | custom-call | flops 301989888 | bytes 13369344 | tf_op jit(solution)/shard_map/triangle/pallas_call | solution.py:114
  718.5 17.3 %triangle.22.refs_2_.refs_0_.refs_1_ = bf16[5,32,32,128]{3,2,1,0:T(8,128)(2,1)S(1)} custom-call(s32[1]{0:T(128)} %bitcast.which, bf16[128,32,384]{2,1,0:T(8,128)(2,1)} %get-tuple-element.80.refs_0_, bf16[128,32,384]{2,1,0:T(8,128)(2,1)} %get-tuple-element.81.refs_1_, bf16[128,32,384]{2,1,0:T(8,128)(2,1)} %get-tuple-element.82.refs_2_, ...), custom_call_target="tpu_custom_call" | custom-call | flops 503316480 | bytes 20185088 | tf_op jit(solution)/shard_map/triangle/pallas_call | solution.py:114
  736.9 20.1 %triangle.23.refs_3_.refs_0_.refs_1_.refs_2_ = bf16[7,32,32,128]{3,2,1,0:T(8,128)(2,1)S(1)} custom-call(s32[1]{0:T(128)} %bitcast.which, bf16[128,32,384]{2,1,0:T(8,128)(2,1)} %get-tuple-element.80.refs_0_, bf16[128,32,384]{2,1,0:T(8,128)(2,1)} %get-tuple-element.81.refs_1_, bf16[128,32,384]{2,1,0:T(8,128)(2,1)} %get-tuple-element.82.refs_2_, ...), custom_call_target="tpu_custom_call" | custom-call | flops 704643072 | bytes 27000832 | tf_op jit(solution)/shard_map/triangle/pallas_call | solution.py:114
  757.1 23.6 %triangle.24.refs_4_.refs_0_.refs_1_.refs_2_.refs_3_ = bf16[9,32,32,128]{3,2,1,0:T(8,128)(2,1)} custom-call(s32[1]{0:T(128)} %bitcast.which, bf16[128,32,384]{2,1,0:T(8,128)(2,1)} %get-tuple-element.80.refs_0_, bf16[128,32,384]{2,1,0:T(8,128)(2,1)} %get-tuple-element.81.refs_1_, bf16[128,32,384]{2,1,0:T(8,128)(2,1)} %get-tuple-element.82.refs_2_, ...), custom_call_target="tpu_custom_call" | custom-call | flops 905969664 | bytes 33816576 | tf_op jit(solution)/shard_map/triangle/pallas_call | solution.py:114
  780.7 26.1 %triangle.25.refs_5_.refs_0_.refs_1_.refs_2_.refs_3_.refs_4_ = bf16[11,32,32,128]{3,2,1,0:T(8,128)(2,1)} custom-call(s32[1]{0:T(128)} %bitcast.which, bf16[128,32,384]{2,1,0:T(8,128)(2,1)} %get-tuple-element.80.refs_0_, bf16[128,32,384]{2,1,0:T(8,128)(2,1)} %get-tuple-element.81.refs_1_, bf16[128,32,384]{2,1,0:T(8,128)(2,1)} %get-tuple-element.82.refs_2_, ...), custom_call_target="tpu_custom_call" | custom-call | flops 1107296256 | bytes 40632320 | tf_op jit(solution)/shard_map/triangle/pallas_call | solution.py:114
  806.9 25.1 %gate.1.refs_12_ = bf16[192,192,128]{2,1,0:T(8,128)(2,1)} custom-call(bf16[192,192,128]{2,1,0:T(8,128)(2,1)} %pair.1, bf16[128,128]{1,0:T(8,128)(2,1)S(1)} %add_convert_fusion.refs_3_.centre, bf16[256,128]{1,0:T(8,128)(2,1)S(1)} %broadcast_in_dim.29.mean, f32[1,128]{1,0:T(1,128)S(1)} %bitcast.16, f32[1,128]{1,0:T(1,128)S(1)} %bitcast.17, ...), custom_call_target="tpu_custom_call" | custom-call | flops 4831838208 | bytes 18874368 | tf_op jit(solution)/shard_map/gate/pallas_call | solution.py:152
  (137 shorter events, 215.5 us)
Async XLA Ops:
  6.6 37.4 %collective-permute-start = (bf16[32,192,128]{2,1,0:T(8,128)(2,1)S(1)}, bf16[32,192,128]{2,1,0:T(8,128)(2,1)S(1)}, u32[]{:S(2)}, u32[]{:S(2)}) collective-permute-start(bf16[32,192,128]{2,1,0:T(8,128)(2,1)S(1)} %get-tuple-element.92), channel_id=1, source_target_pairs={{0,1},{1,0},{2,3},{3,2},{4,5},{5,4},{6,7},{7,6},{8,9},{9,8},{10,11... | collective-permute-start | bytes 4718600 | tf_op jit(solution)/shard_map/ppermute | solution.py:319
  45.2 35.9 %collective-permute-start.1 = (bf16[32,192,128]{2,1,0:T(8,128)(2,1)}, bf16[32,192,128]{2,1,0:T(8,128)(2,1)}, u32[]{:S(2)}, u32[]{:S(2)}) collective-permute-start(bf16[32,192,128]{2,1,0:T(8,128)(2,1)} %get-tuple-element.47), channel_id=1, source_target_pairs={{0,1},{1,0},{2,3},{3,2},{4,5},{5,4},{6,7},{7,6},{8,9},{9,8},{10,11... | collective-permute-start | bytes 4718600 | tf_op jit(solution)/shard_map/ppermute | solution.py:319
  64.3 39.7 %collective-permute-start.7 = (bf16[128,32,384]{2,1,0:T(8,128)(2,1)}, bf16[128,32,384]{2,1,0:T(8,128)(2,1)}, u32[]{:S(2)}, u32[]{:S(2)}) collective-permute-start(bf16[128,32,384]{2,1,0:T(8,128)(2,1)} %get-tuple-element.55.refs_1_.refs_2_.refs_3_.refs_4_.refs_5_.refs_6_), channel_id=1, source_target_pairs={{0,8},{2,10},{5,13},{7,15},{8,0},{10,2},{13,5},{15,7},{16,24},{18,... | collective-permute-start | bytes 9437192 | tf_op jit(solution)/shard_map/ppermute | solution.py:261
  101.0 11.1 %collective-permute-start.6 = (bf16[128,32,384]{2,1,0:T(8,128)(2,1)}, bf16[128,32,384]{2,1,0:T(8,128)(2,1)}, u32[]{:S(2)}, u32[]{:S(2)}) collective-permute-start(bf16[128,32,384]{2,1,0:T(8,128)(2,1)} %get-tuple-element.55.refs_1_.refs_2_.refs_3_.refs_4_.refs_5_.refs_6_), channel_id=1, source_target_pairs={{0,4},{2,6},{5,1},{7,3},{8,12},{10,14},{13,9},{15,11},{16,20},{18,... | collective-permute-start | bytes 9437192 | tf_op jit(solution)/shard_map/ppermute | solution.py:273
  108.9 37.4 %collective-permute-start.2 = (bf16[32,192,128]{2,1,0:T(8,128)(2,1)}, bf16[32,192,128]{2,1,0:T(8,128)(2,1)}, u32[]{:S(2)}, u32[]{:S(2)}) collective-permute-start(bf16[32,192,128]{2,1,0:T(8,128)(2,1)} %get-tuple-element.51), channel_id=1, source_target_pairs={{0,1},{1,0},{2,3},{3,2},{4,5},{5,4},{6,7},{7,6},{8,9},{9,8},{10,11... | collective-permute-start | bytes 4718600 | tf_op jit(solution)/shard_map/ppermute | solution.py:319
  108.9 57.9 %collective-permute-start.10 = (bf16[128,32,384]{2,1,0:T(8,128)(2,1)}, bf16[128,32,384]{2,1,0:T(8,128)(2,1)S(1)}, u32[]{:S(2)}, u32[]{:S(2)}) collective-permute-start(bf16[128,32,384]{2,1,0:T(8,128)(2,1)} %get-tuple-element.56.refs_6_.refs_7_.refs_8_.refs_9_.refs_5_.refs_10_), channel_id=1, source_target_pairs={{0,8},{2,10},{5,13},{7,15},{8,0},{10,2},{13,5},{15,7},{16,24},{18,... | collective-permute-start | bytes 9437192 | tf_op jit(solution)/shard_map/ppermute | solution.py:261
  170.8 9.3 %collective-permute-start.12 = (bf16[128,32,384]{2,1,0:T(8,128)(2,1)S(1)}, bf16[128,32,384]{2,1,0:T(8,128)(2,1)S(1)}, u32[]{:S(2)}, u32[]{:S(2)}) collective-permute-start(bf16[128,32,384]{2,1,0:T(8,128)(2,1)S(1)} %collective-permute-done.10.refs_8_.refs_9_.refs_10_.refs_11_.refs_7_.refs_12_), channel_id=1, source_target_pairs={{0,4},{2,6},{5,1},{7,3},{8,12},{10,14},{13,9},{15,11},{16,20},{18,... | collective-permute-start | bytes 9437192 | tf_op jit(solution)/shard_map/ppermute | solution.py:273
  173.3 41.3 %collective-permute-start.3 = (bf16[32,192,128]{2,1,0:T(8,128)(2,1)S(1)}, bf16[32,192,128]{2,1,0:T(8,128)(2,1)}, u32[]{:S(2)}, u32[]{:S(2)}) collective-permute-start(bf16[32,192,128]{2,1,0:T(8,128)(2,1)S(1)} %copy-done.21), channel_id=1, source_target_pairs={{0,1},{1,0},{2,3},{3,2},{4,5},{5,4},{6,7},{7,6},{8,9},{9,8},{10,11... | collective-permute-start | bytes 4718600 | tf_op jit(solution)/shard_map/ppermute | solution.py:319
  173.3 39.5 %collective-permute-start.13 = (bf16[1,32,32,128]{3,2,1,0:T(8,128)(2,1)S(1)}, bf16[1,32,32,128]{3,2,1,0:T(8,128)(2,1)S(1)}, u32[]{:S(2)}, u32[]{:S(2)}) collective-permute-start(bf16[1,32,32,128]{3,2,1,0:T(8,128)(2,1)S(1)} %triangle.13), channel_id=1, source_target_pairs={{0,2},{1,3},{2,0},{3,1},{4,6},{5,7},{6,4},{7,5},{8,10},{9,11},{10,... | collective-permute-start | bytes 786440 | tf_op jit(solution)/shard_map/ppermute | solution.py:354
  176.1 56.9 %collective-permute-start.14 = (bf16[128,32,384]{2,1,0:T(8,128)(2,1)}, bf16[128,32,384]{2,1,0:T(8,128)(2,1)}, u32[]{:S(2)}, u32[]{:S(2)}) collective-permute-start(bf16[128,32,384]{2,1,0:T(8,128)(2,1)} %get-tuple-element.61.refs_11_.refs_12_.refs_13_.refs_9_.refs_14_), channel_id=1, source_target_pairs={{0,8},{2,10},{5,13},{7,15},{8,0},{10,2},{13,5},{15,7},{16,24},{18,... | collective-permute-start | bytes 9437192 | tf_op jit(solution)/shard_map/ppermute | solution.py:261
  238.4 9.3 %collective-permute-start.16 = (bf16[128,32,384]{2,1,0:T(8,128)(2,1)}, bf16[128,32,384]{2,1,0:T(8,128)(2,1)S(1)}, u32[]{:S(2)}, u32[]{:S(2)}) collective-permute-start(bf16[128,32,384]{2,1,0:T(8,128)(2,1)} %collective-permute-done.14.refs_13_.refs_14_.refs_15_.refs_11_.refs_16_), channel_id=1, source_target_pairs={{0,4},{2,6},{5,1},{7,3},{8,12},{10,14},{13,9},{15,11},{16,20},{18,... | collective-permute-start | bytes 9437192 | tf_op jit(solution)/shard_map/ppermute | solution.py:273
  240.8 54.2 %collective-permute-start.4 = (bf16[32,192,128]{2,1,0:T(8,128)(2,1)S(1)}, bf16[32,192,128]{2,1,0:T(8,128)(2,1)}, u32[]{:S(2)}, u32[]{:S(2)}) collective-permute-start(bf16[32,192,128]{2,1,0:T(8,128)(2,1)S(1)} %get-tuple-element.53), channel_id=1, source_target_pairs={{0,1},{1,0},{2,3},{3,2},{4,5},{5,4},{6,7},{7,6},{8,9},{9,8},{10,11... | collective-permute-start | bytes 4718600 | tf_op jit(solution)/shard_map/ppermute | solution.py:319
  243.4 51.4 %collective-permute-start.17 = (bf16[3,32,32,128]{3,2,1,0:T(8,128)(2,1)S(1)}, bf16[3,32,32,128]{3,2,1,0:T(8,128)(2,1)S(1)}, u32[]{:S(2)}, u32[]{:S(2)}) collective-permute-start(bf16[3,32,32,128]{3,2,1,0:T(8,128)(2,1)S(1)} %triangle.14), channel_id=1, source_target_pairs={{0,2},{1,3},{2,0},{3,1},{4,6},{5,7},{6,4},{7,5},{8,10},{9,11},{10,... | collective-permute-start | bytes 2359304 | tf_op jit(solution)/shard_map/ppermute | solution.py:354
  244.2 70.4 %collective-permute-start.18 = (bf16[128,32,384]{2,1,0:T(8,128)(2,1)}, bf16[128,32,384]{2,1,0:T(8,128)(2,1)}, u32[]{:S(2)}, u32[]{:S(2)}) collective-permute-start(bf16[128,32,384]{2,1,0:T(8,128)(2,1)} %get-tuple-element.66.refs_16_.refs_17_.refs_13_.refs_18_), channel_id=1, source_target_pairs={{0,8},{2,10},{5,13},{7,15},{8,0},{10,2},{13,5},{15,7},{16,24},{18,... | collective-permute-start | bytes 9437192 | tf_op jit(solution)/shard_map/ppermute | solution.py:261
  322.3 36.9 %collective-permute-start.5 = (bf16[32,192,128]{2,1,0:T(8,128)(2,1)}, bf16[32,192,128]{2,1,0:T(8,128)(2,1)S(1)}, u32[]{:S(2)}, u32[]{:S(2)}) collective-permute-start(bf16[32,192,128]{2,1,0:T(8,128)(2,1)} %get-tuple-element.54), channel_id=1, source_target_pairs={{0,1},{1,0},{2,3},{3,2},{4,5},{5,4},{6,7},{7,6},{8,9},{9,8},{10,11... | collective-permute-start | bytes 4718600 | tf_op jit(solution)/shard_map/ppermute | solution.py:319
  323.1 59.5 %collective-permute-start.21 = (bf16[128,32,384]{2,1,0:T(8,128)(2,1)}, bf16[128,32,384]{2,1,0:T(8,128)(2,1)}, u32[]{:S(2)}, u32[]{:S(2)}) collective-permute-start(bf16[128,32,384]{2,1,0:T(8,128)(2,1)} %get-tuple-element.71.refs_21_.refs_17_.refs_22_), channel_id=1, source_target_pairs={{0,8},{2,10},{5,13},{7,15},{8,0},{10,2},{13,5},{15,7},{16,24},{18,... | collective-permute-start | bytes 9437192 | tf_op jit(solution)/shard_map/ppermute | solution.py:261
  379.1 39.5 %collective-permute-start.24 = (bf16[128,32,384]{2,1,0:T(8,128)(2,1)}, bf16[128,32,384]{2,1,0:T(8,128)(2,1)}, u32[]{:S(2)}, u32[]{:S(2)}) collective-permute-start(bf16[128,32,384]{2,1,0:T(8,128)(2,1)} %get-tuple-element.76.refs_5_.refs_21_.refs_26_), channel_id=1, source_target_pairs={{0,8},{2,10},{5,13},{7,15},{8,0},{10,2},{13,5},{15,7},{16,24},{18,... | collective-permute-start | bytes 9437192 | tf_op jit(solution)/shard_map/ppermute | solution.py:261
  384.4 37.1 %collective-permute-start.23 = (bf16[128,32,384]{2,1,0:T(8,128)(2,1)}, bf16[128,32,384]{2,1,0:T(8,128)(2,1)S(1)}, u32[]{:S(2)}, u32[]{:S(2)}) collective-permute-start(bf16[128,32,384]{2,1,0:T(8,128)(2,1)} %collective-permute-done.21.refs_23_.refs_19_.refs_24_), channel_id=1, source_target_pairs={{0,4},{2,6},{5,1},{7,3},{8,12},{10,14},{13,9},{15,11},{16,20},{18,... | collective-permute-start | bytes 9437192 | tf_op jit(solution)/shard_map/ppermute | solution.py:273
  418.6 30.8 %collective-permute-start.25 = (bf16[128,32,384]{2,1,0:T(8,128)(2,1)}, bf16[128,32,384]{2,1,0:T(8,128)(2,1)}, u32[]{:S(2)}, u32[]{:S(2)}) collective-permute-start(bf16[128,32,384]{2,1,0:T(8,128)(2,1)} %collective-permute-done.24.refs_7_.refs_23_.refs_28_), channel_id=1, source_target_pairs={{0,4},{2,6},{5,1},{7,3},{8,12},{10,14},{13,9},{15,11},{16,20},{18,... | collective-permute-start | bytes 9437192 | tf_op jit(solution)/shard_map/ppermute | solution.py:273
  446.5 290.5 %collective-permute-start.27 = (bf16[9,32,32,128]{3,2,1,0:T(8,128)(2,1)}, bf16[9,32,32,128]{3,2,1,0:T(8,128)(2,1)}, u32[]{:S(2)}, u32[]{:S(2)}) collective-permute-start(bf16[9,32,32,128]{3,2,1,0:T(8,128)(2,1)} %triangle.17), channel_id=1, source_target_pairs={{0,2},{1,3},{2,0},{3,1},{4,6},{5,7},{6,4},{7,5},{8,10},{9,11},{10,... | collective-permute-start | bytes 7077896 | tf_op jit(solution)/shard_map/ppermute | solution.py:354
  448.4 244.6 %collective-permute-start.26 = (bf16[7,32,32,128]{3,2,1,0:T(8,128)(2,1)S(1)}, bf16[7,32,32,128]{3,2,1,0:T(8,128)(2,1)}, u32[]{:S(2)}, u32[]{:S(2)}) collective-permute-start(bf16[7,32,32,128]{3,2,1,0:T(8,128)(2,1)S(1)} %triangle.16), channel_id=1, source_target_pairs={{0,2},{1,3},{2,0},{3,1},{4,6},{5,7},{6,4},{7,5},{8,10},{9,11},{10,... | collective-permute-start | bytes 5505032 | tf_op jit(solution)/shard_map/ppermute | solution.py:354
  486.5 393.0 %collective-permute-start.28 = (bf16[6,32,32,128]{3,2,1,0:T(8,128)(2,1)}, bf16[6,32,32,128]{3,2,1,0:T(8,128)(2,1)}, u32[]{:S(2)}, u32[]{:S(2)}) collective-permute-start(bf16[6,32,32,128]{3,2,1,0:T(8,128)(2,1)} %triangle.19), channel_id=1, source_target_pairs={{0,2},{1,3},{2,0},{3,1},{4,6},{5,7},{6,4},{7,5},{8,10},{9,11},{10,... | collective-permute-start | bytes 4718600 | tf_op jit(solution)/shard_map/ppermute | solution.py:354
  488.7 343.3 %collective-permute-start.30 = (bf16[5,32,32,128]{3,2,1,0:T(8,128)(2,1)}, bf16[5,32,32,128]{3,2,1,0:T(8,128)(2,1)}, u32[]{:S(2)}, u32[]{:S(2)}) collective-permute-start(bf16[5,32,32,128]{3,2,1,0:T(8,128)(2,1)} %triangle.15), channel_id=1, source_target_pairs={{0,2},{1,3},{2,0},{3,1},{4,6},{5,7},{6,4},{7,5},{8,10},{9,11},{10,... | collective-permute-start | bytes 3932168 | tf_op jit(solution)/shard_map/ppermute | solution.py:354
  489.5 342.5 %collective-permute-start.29 = (bf16[5,32,32,128]{3,2,1,0:T(8,128)(2,1)}, bf16[5,32,32,128]{3,2,1,0:T(8,128)(2,1)S(1)}, u32[]{:S(2)}, u32[]{:S(2)}) collective-permute-start(bf16[5,32,32,128]{3,2,1,0:T(8,128)(2,1)} %triangle.18), channel_id=1, source_target_pairs={{0,2},{1,3},{2,0},{3,1},{4,6},{5,7},{6,4},{7,5},{8,10},{9,11},{10,... | collective-permute-start | bytes 3932168 | tf_op jit(solution)/shard_map/ppermute | solution.py:354
  (36 other events, 655.8 us)

commit v3 on v2

--- a/solution.py
+++ b/solution.py
@@ -28,12 +28,27 @@
     )
 
 
+def swap_eight(arrays):
+    place = lax.broadcasted_iota(jnp.int32, arrays[0].shape, 1)
+    for shift in (4, 2, 1):
+        low = (place & shift) == 0
+        swapped = list(arrays)
+        for n in range(8):
+            if n & shift == 0:
+                one, two = arrays[n], arrays[n + shift]
+                swapped[n] = jnp.where(low, one, pltpu.roll(two, shift, 1))
+                swapped[n + shift] = jnp.where(low, pltpu.roll(one, 8 - shift, 1), two)
+        arrays = swapped
+    return arrays
+
+
 def project_kernel(n_pieces, *refs):
     pieces, (weights, centre, gain, bias, left_out, right_out, left_rows, right_rows) = (
         refs[:n_pieces],
         refs[n_pieces:],
     )
-    hidden, rows, depth = left_out.shape
+    eights, _, rows, depth = left_out.shape
+    hidden = eights * 8
 
     def one_row(i, carry):
         values = jnp.concatenate([piece[i] for piece in pieces], axis=0)
@@ -43,15 +58,24 @@
         halved = contract(weights[...], normed.astype(BF16), 1, 0)
         for first, held in ((0, left_rows), (2 * hidden, right_rows)):
             gate, value = halved[first : first + hidden], halved[first + hidden : first + 2 * hidden]
-            side = value + value * jnp.tanh(gate)
+            held[i] = value + value * jnp.tanh(gate)
+        return carry
+
+    lax.fori_loop(0, rows, one_row, 0, unroll=4)
+
+    def one_group(e, carry):
+        at = pl.ds(pl.multiple_of(e * 8, 8), 8)
+        for held, out in ((left_rows, left_out), (right_rows, right_out)):
             for n in range(depth // 128):
-                held[n, pl.ds(i, hidden, stride=rows), :] = side[:, n * 128 : (n + 1) * 128]
+                lanes = slice(n * 128, (n + 1) * 128)
+                halves = [
+                    swap_eight([held[first + i, at, lanes][None] for i in range(8)]) for first in range(0, rows, 8)
+                ]
+                for h in range(8):
+                    out[e, h, :, lanes] = jnp.concatenate([half[h][0] for half in halves], axis=0).astype(BF16)
         return carry
 
-    lax.fori_loop(0, rows, one_row, 0, unroll=8)
-    for held, out in ((left_rows, left_out), (right_rows, right_out)):
-        for n in range(depth // 128):
-            out[:, :, n * 128 : (n + 1) * 128] = held[n].reshape(hidden, rows, 128).astype(BF16)
+    lax.fori_loop(0, eights, one_group, 0, unroll=2)
 
 
 def project(pieces, firsts, count, weights, centre, gain, bias):
@@ -64,20 +88,21 @@
         pl.BlockSpec((rows, piece.shape[1], channels), functools.partial(lambda f, i: (i + f, 0, 0), first // rows))
         for piece, first in zip(pieces, firsts)
     ] + [whole(x) for x in (weights, centre, gain, bias)]
-    shape = jax.ShapeDtypeStruct((hidden, count, depth), BF16)
-    return pl.pallas_call(
+    shape = jax.ShapeDtypeStruct((hidden // 8, 8, count, depth), BF16)
+    left, right = pl.pallas_call(
         functools.partial(project_kernel, len(pieces)),
         grid=(count // rows,),
         in_specs=in_specs,
-        out_specs=[pl.BlockSpec((hidden, rows, depth), lambda i: (0, i, 0))] * 2,
+        out_specs=[pl.BlockSpec((hidden // 8, 8, rows, depth), lambda i: (0, 0, i, 0))] * 2,
         out_shape=[shape, shape],
-        scratch_shapes=[pltpu.VMEM((depth // 128, hidden * rows, 128), F32)] * 2,
+        scratch_shapes=[pltpu.VMEM((rows, hidden, depth), F32)] * 2,
         compiler_params=PARAMS,
         cost_estimate=at_least(
             count * depth * channels * (channels + 4 * hidden), 2 * count * depth * hidden, shape, shape
         ),
         name="project",
     )(*pieces, weights, centre, gain, bias)
+    return left.reshape(hidden, count, depth), right.reshape(hidden, count, depth)
 
 
 def triangle_kernel(n_left, n_sides, group, pairs, which, *refs):
@@ -285,13 +310,29 @@
 
     near_is_own = (row // top) == (col // half)
     swap_half = [(c, c ^ half) for c in range(n_col)]
-    lefts, nears, fars, units = [], [], [], []
+    two_chips = share == 1 and top == 2
+    holder = ((row ^ col) & 1) == 0
+    lefts, rights, fars, units = [], [], [], []
+
+    def first_step(right):
+        if not two_chips:
+            return across_top(right)
+        pairs = [(place(r, c), place(r ^ top ^ 1, c)) for r in range(n_row) for c in range(n_col) if holds(r, c)]
+        return lax.ppermute(right, axes, pairs)
+
+    def second_step(right, far, *waits):
+        if not two_chips:
+            return [a + b for a, b in zip(to_all_rows(right), to_all_rows(far))]
+        given = jnp.where(holder, right, after(far, *waits))
+        got = lax.ppermute(given, "row", [(r, r ^ 1) for r in range(n_row)])
+        return [[right, got, far]]
 
     def product(pairs, own):
         take_near = near_is_own if own else jnp.logical_not(near_is_own)
-        which = jnp.where(take_near, 0, len(nears[0][0]))
-        if share == 1 and top > 1:
-            which = which + ((row ^ col) & 1)
+        if two_chips:
+            which = jnp.where(holder, 0, 1) + jnp.where(take_near, 0, 1)
+        else:
+            which = jnp.where(take_near, 0, 1)
         used_left = sorted({i for i, _, _ in pairs})
         used_right = sorted({(j, s) for _, j, s in pairs})
         return triangle(
@@ -312,56 +353,50 @@
 
     exchanged, arrived, own_parts, sent_parts = [], {}, {}, {}
 
-    def exchange(t):
-        block = pair_act[t * step : (t + 1) * step]
-        if exchanged:
-            block = after(block, exchanged[-1][-1])
-        exchanged.append([lax.ppermute(block, "col", [(c, c ^ o) for c in range(n_col)]) for o in range(1, half)])
-
     def prepare(t, *held):
-        exchange(t)
-        scale = after(gain_in, *held) if held else gain_in
         left, right = project(
             [pair_act] + exchanged[t],
             [t * step] + [0] * (half - 1),
             step,
             halves,
             centre,
-            scale,
+            after(gain_in, *held) if held else gain_in,
             bias_in,
         )
         lefts.append(left)
-        fars.append(across_top(right))
-        nears.append(to_all_rows(right))
+        rights.append(right)
         return left
 
-    def complete(t):
-        waits = nears[t + 1][-1][-1:] if t + 1 < len(nears) else []
-        far = to_all_rows(after(fars[t], *waits))
-        units.append([a + b for a, b in zip(nears[t], far)])
-
-    ahead = 2
+    def exchange(n, *waits):
+        block = pair_act[n * step : (n + 1) * step]
+        block = after(block, *waits) if waits else block
+        exchanged.append([lax.ppermute(block, "col", [(c, c ^ o) for c in range(n_col)]) for o in range(1, half)])
+
+    exchange(0)
     token = []
     moved = []
-    for t in range(min(ahead, chunks)):
-        token = [prepare(t, *token)]
-    for t in range(chunks):
-        complete(t)
-        for pairs in waves[t]:
-            lefts[t] = after(lefts[t], *token)
-            made = product(pairs, False)
-            token = [made]
-            moved.append(lax.ppermute(made, "col", swap_half))
-            for n, pair in enumerate(pairs):
-                sent_parts[pair] = (moved[-1], n)
-        if t + ahead < chunks:
-            token = [prepare(t + ahead, *token, *(moved[t - 1 : t] if t in (1, 2) else []))]
+    for n in range(chunks + 2):
+        waits = token + (exchanged[n][-1:] if n < chunks else []) + (moved[n - 4 : n - 3] if n >= 4 else [])
+        if n + 1 < chunks:
+            exchange(n + 1, *waits)
+        if 0 < n <= chunks:
+            fars.append(first_step(after(rights[n - 1], *waits)))
+        if n >= 2:
+            units.append(second_step(rights[n - 2], fars[n - 2], *waits))
+        if n < chunks:
+            token = [prepare(n, *token)]
+        if n >= 2:
+            t = n - 2
+            for pairs in waves[t]:
+                lefts[t] = after(lefts[t], *token)
+                made = product(pairs, False)
+                token = [made]
+                waits = moved[t - 1 : t] if t < chunks - 1 else []
+                moved.append(lax.ppermute(after(made, *waits) if waits else made, "col", swap_half))
+                for p, pair in enumerate(pairs):
+                    sent_parts[pair] = (moved[-1], p)
     for t in range(chunks):
         pairs = [pair for part in waves[t] for pair in part]
-        if t == 0 and chunks > 3:
-            token = token + [moved[chunks - 3]]
-        if t == chunks // 2:
-            token = token + [moved[chunks - 2]]
         lefts[t] = after(lefts[t], *token)
         made = product(pairs, True)
         token = [made]

time: 902 us -> 734 us (0.81)
  waiting for transfers between devices: 378 us -> 229 us
  starting transfers between devices: 72.5 us -> 40.7 us
  other arithmetic: 0.04 us -> 21.8 us
    ppermute x25 -> x19, waiting for transfers between devices: 297 us -> 145 us  [the longest x7 137 us: on_device(): lax.ppermute(after(made, *waits) if waits else made, 'col', swap_half)]
    ppermute x25 -> x19, starting transfers between devices: 64.3 us -> 35.2 us  [the longest x6 21.1 us: first_step(): return lax.ppermute(right, axes, pairs)]
    select_n x0 -> x6, other arithmetic: none -> 21.8 us  [second_step(): given = jnp.where(holder, right, after(far, *waits))]
  transfers between devices with their start and end apart: 31 -> 25, of which waited for: 17 -> 13; matrix products, arithmetic and copies ran while one was open for 0% -> 0% of each run, Pallas kernels for 46% -> 56%
where the time goes in v3:
time: 734 us; the launch traced here: 722 us
  Pallas kernels  410 us (56%)
  waiting for transfers between devices  229 us (31%)
  starting transfers between devices  40.7 us (6%)
  other arithmetic  21.8 us (3%)
  local copies, waits for them, and re-layouts  19.4 us (3%)
    pallas_call x13, Pallas kernels, triangle(): pl.pallas_call(functools.partial(triangle_kernel, len(lefts), n_sides, gr...  228 us
    ppermute x7, waiting for transfers between devices, on_device(): lax.ppermute(after(made, *waits) if waits else made, 'col', swap_half)  137 us
    pallas_call x6, Pallas kernels, project(): pl.pallas_call(functools.partial(project_kernel, len(pieces)), grid=(coun...  101 us
    ppermute x6, waiting for transfers between devices, exchange(): lax.ppermute(block, 'col', [(c, c ^ o) for c in range(n_col)])  83.9 us
    pallas_call x6, Pallas kernels, finish(): pl.pallas_call(functools.partial(finish_kernel, n_parts, group, hidden),...  55.1 us
    pallas_call x1, Pallas kernels, gate_of(): pl.pallas_call(gate_kernel, grid=(count // rows,), in_specs=[block] + [wh...  25.1 us
    select_n x6, other arithmetic, second_step(): given = jnp.where(holder, right, after(far, *waits))  21.8 us
    ppermute x6, starting transfers between devices, first_step(): return lax.ppermute(right, axes, pairs)  21.1 us
  transfers between devices with their start and end apart: 25, of which 13 were waited for; matrix products, arithmetic and copies ran while one was open for 0% of the time, Pallas kernels for 56%

profile of v3, /device:TPU:0, one launch (start us, length us, event | category | flops | bytes accessed | tf_op | source)
XLA Modules:
  0.0 721.6 jit_solution(9346792067303908316)
XLA Ops:
  9.6 34.4 %collective-permute-done.refs_1_ = bf16[32,192,128]{2,1,0:T(8,128)(2,1)S(1)} collective-permute-done((bf16[32,192,128]{2,1,0:T(8,128)(2,1)S(1)}, bf16[32,192,128]{2,1,0:T(8,128)(2,1)S(1)}, u32[]{:S(2)}, u32[]{:S(2)}) %collective-permute-start) | collective-permute-done | bytes 1572896 | tf_op jit(solution)/shard_map/ppermute | solution.py:373
  47.2 16.8 %project.6 = (bf16[16,8,32,384]{3,2,1,0:T(8,128)(2,1)}, bf16[16,8,32,384]{3,2,1,0:T(8,128)(2,1)}) custom-call(bf16[192,192,128]{2,1,0:T(8,128)(2,1)} %pair.1, bf16[32,192,128]{2,1,0:T(8,128)(2,1)} %copy-done.25, bf16[512,128]{1,0:T(8,128)(2,1)S(1)} %multiply_bitcast_fusion.refs_2_, bf16[128,128]{1,0:T(8,128)(2,1)S(1)} %add_convert_fusion.refs_3_.centre, ...), custom_call_target="tpu_custom_call" | custom-call | flops 2013265920 | bytes 6291456 | tf_op jit(solution)/shard_map/project/pallas_call | solution.py:92
  64.1 16.9 %collective-permute-done.1.refs_1_ = bf16[32,192,128]{2,1,0:T(8,128)(2,1)} collective-permute-done((bf16[32,192,128]{2,1,0:T(8,128)(2,1)}, bf16[32,192,128]{2,1,0:T(8,128)(2,1)}, u32[]{:S(2)}, u32[]{:S(2)}) %collective-permute-start.1) | collective-permute-done | bytes 1572896 | tf_op jit(solution)/shard_map/ppermute | solution.py:373
  84.0 17.0 %project.7 = (bf16[16,8,32,384]{3,2,1,0:T(8,128)(2,1)}, bf16[16,8,32,384]{3,2,1,0:T(8,128)(2,1)}) custom-call(bf16[192,192,128]{2,1,0:T(8,128)(2,1)} %pair.1, bf16[32,192,128]{2,1,0:T(8,128)(2,1)} %collective-permute-done.1.refs_1_, bf16[512,128]{1,0:T(8,128)(2,1)S(1)} %multiply_bitcast_fusion.refs_2_, bf16[128,128]{1,0:T(8,128)(2,1)S(1)} %add_convert_fusion.refs_3_.centre, ...), custom_call_target="tpu_custom_call" | custom-call | flops 2013265920 | bytes 6291456 | tf_op jit(solution)/shard_map/project/pallas_call | solution.py:92
  101.0 19.6 %collective-permute-done.2.refs_1_ = bf16[32,192,128]{2,1,0:T(8,128)(2,1)} collective-permute-done((bf16[32,192,128]{2,1,0:T(8,128)(2,1)}, bf16[32,192,128]{2,1,0:T(8,128)(2,1)}, u32[]{:S(2)}, u32[]{:S(2)}) %collective-permute-start.2) | collective-permute-done | bytes 1572896 | tf_op jit(solution)/shard_map/ppermute | solution.py:373
  130.0 17.1 %project.8 = (bf16[16,8,32,384]{3,2,1,0:T(8,128)(2,1)}, bf16[16,8,32,384]{3,2,1,0:T(8,128)(2,1)}) custom-call(bf16[192,192,128]{2,1,0:T(8,128)(2,1)} %pair.1, bf16[32,192,128]{2,1,0:T(8,128)(2,1)} %collective-permute-done.2.refs_1_, bf16[512,128]{1,0:T(8,128)(2,1)S(1)} %multiply_bitcast_fusion.refs_2_, bf16[128,128]{1,0:T(8,128)(2,1)S(1)} %add_convert_fusion.refs_3_.centre, ...), custom_call_target="tpu_custom_call" | custom-call | flops 2013265920 | bytes 6291456 | tf_op jit(solution)/shard_map/project/pallas_call | solution.py:92
  176.4 16.8 %project.9 = (bf16[16,8,32,384]{3,2,1,0:T(8,128)(2,1)}, bf16[16,8,32,384]{3,2,1,0:T(8,128)(2,1)}) custom-call(bf16[192,192,128]{2,1,0:T(8,128)(2,1)} %pair.1, bf16[32,192,128]{2,1,0:T(8,128)(2,1)} %collective-permute-done.3.refs_1_, bf16[512,128]{1,0:T(8,128)(2,1)S(1)} %multiply_bitcast_fusion.refs_2_, bf16[128,128]{1,0:T(8,128)(2,1)S(1)} %add_convert_fusion.refs_3_.centre, ...), custom_call_target="tpu_custom_call" | custom-call | flops 2013265920 | bytes 6291456 | tf_op jit(solution)/shard_map/project/pallas_call | solution.py:92
  225.6 16.9 %project.10 = (bf16[16,8,32,384]{3,2,1,0:T(8,128)(2,1)}, bf16[16,8,32,384]{3,2,1,0:T(8,128)(2,1)}) custom-call(bf16[192,192,128]{2,1,0:T(8,128)(2,1)} %pair.1, bf16[32,192,128]{2,1,0:T(8,128)(2,1)} %copy-done.24, bf16[512,128]{1,0:T(8,128)(2,1)S(1)} %multiply_bitcast_fusion.refs_2_, bf16[128,128]{1,0:T(8,128)(2,1)S(1)} %add_convert_fusion.refs_3_.centre, ...), custom_call_target="tpu_custom_call" | custom-call | flops 2013265920 | bytes 6291456 | tf_op jit(solution)/shard_map/project/pallas_call | solution.py:92
  244.2 16.6 %triangle.15 = bf16[5,32,32,128]{3,2,1,0:T(8,128)(2,1)S(1)} custom-call(s32[1]{0:T(128)} %bitcast.5.which, bf16[128,32,384]{2,1,0:T(8,128)(2,1)} %bitcast.51, bf16[128,32,384]{2,1,0:T(8,128)(2,1)} %bitcast.62, bf16[128,32,384]{2,1,0:T(8,128)(2,1)} %bitcast.80, bf16[128,32,384]{2,1,0:T(8,128)(2,1)} %bitcast.39, ...), custom_call_target="tpu_custom_call" | custom-call | flops 503316480 | bytes 20185088 | tf_op jit(solution)/shard_map/triangle/pallas_call | solution.py:139
  260.8 14.9 %collective-permute-done.14.refs_7_.refs_6_ = bf16[3,32,32,128]{3,2,1,0:T(8,128)(2,1)S(1)} collective-permute-done((bf16[3,32,32,128]{3,2,1,0:T(8,128)(2,1)S(1)}, bf16[3,32,32,128]{3,2,1,0:T(8,128)(2,1)S(1)}, u32[]{:S(2)}, u32[]{:S(2)}) %collective-permute-start.14) | collective-permute-done | bytes 786464 | tf_op jit(solution)/shard_map/ppermute | solution.py:395
  289.6 16.8 %project.11 = (bf16[16,8,32,384]{3,2,1,0:T(8,128)(2,1)}, bf16[16,8,32,384]{3,2,1,0:T(8,128)(2,1)}) custom-call(bf16[192,192,128]{2,1,0:T(8,128)(2,1)} %pair.1, bf16[32,192,128]{2,1,0:T(8,128)(2,1)} %collective-permute-done.10.refs_1_, bf16[512,128]{1,0:T(8,128)(2,1)S(1)} %multiply_bitcast_fusion.refs_2_, ...), custom_call_target="tpu_custom_call" | custom-call | flops 2013265920 | bytes 6291456 | tf_op jit(solution)/shard_map/project/pallas_call | solution.py:92
  308.1 19.3 %triangle.16 = bf16[7,32,32,128]{3,2,1,0:T(8,128)(2,1)S(1)} custom-call(s32[1]{0:T(128)} %bitcast.5.which, bf16[128,32,384]{2,1,0:T(8,128)(2,1)} %bitcast.52, bf16[128,32,384]{2,1,0:T(8,128)(2,1)} %bitcast.63, bf16[128,32,384]{2,1,0:T(8,128)(2,1)} %bitcast.81, bf16[128,32,384]{2,1,0:T(8,128)(2,1)} %bitcast.88, bf16[128,32,384]{2,1,0:T(8,128)(2,1)} %bitcast.40, ...), custom_call_target="tpu_custom_call" | custom-call | flops 704643072 | bytes 27000832 | tf_op jit(solution)/shard_map/triangle/pallas_call | solution.py:139
  327.4 18.4 %collective-permute-done.17.refs_8_.refs_6_.refs_7_ = bf16[5,32,32,128]{3,2,1,0:T(8,128)(2,1)} collective-permute-done((bf16[5,32,32,128]{3,2,1,0:T(8,128)(2,1)S(1)}, bf16[5,32,32,128]{3,2,1,0:T(8,128)(2,1)}, u32[]{:S(2)}, u32[]{:S(2)}) %collective-permute-start.17) | collective-permute-done | bytes 1310752 | tf_op jit(solution)/shard_map/ppermute | solution.py:395
  356.8 22.2 %triangle.17 = bf16[9,32,32,128]{3,2,1,0:T(8,128)(2,1)} custom-call(s32[1]{0:T(128)} %bitcast.5.which, bf16[128,32,384]{2,1,0:T(8,128)(2,1)} %bitcast.53, bf16[128,32,384]{2,1,0:T(8,128)(2,1)} %bitcast.64, bf16[128,32,384]{2,1,0:T(8,128)(2,1)} %bitcast.82, bf16[128,32,384]{2,1,0:T(8,128)(2,1)} %bitcast.89, bf16[128,32,384]{2,1,0:T(8,128)(2,1)} %bitcast.94, ...), custom_call_target="tpu_custom_call" | custom-call | flops 905969664 | bytes 33816576 | tf_op jit(solution)/shard_map/triangle/pallas_call | solution.py:139
  379.1 52.7 %collective-permute-done.20.refs_9_.refs_6_.refs_7_.refs_8_ = bf16[7,32,32,128]{3,2,1,0:T(8,128)(2,1)S(1)} collective-permute-done((bf16[7,32,32,128]{3,2,1,0:T(8,128)(2,1)S(1)}, bf16[7,32,32,128]{3,2,1,0:T(8,128)(2,1)S(1)}, u32[]{:S(2)}, u32[]{:S(2)}) %collective-permute-start.20) | collective-permute-done | bytes 1835040 | tf_op jit(solution)/shard_map/ppermute | solution.py:395
  443.5 16.6 %triangle.18 = bf16[5,32,32,128]{3,2,1,0:T(8,128)(2,1)} custom-call(s32[1]{0:T(128)} %bitcast.5.which, bf16[128,32,384]{2,1,0:T(8,128)(2,1)} %bitcast.54, bf16[128,32,384]{2,1,0:T(8,128)(2,1)} %bitcast.65, bf16[128,32,384]{2,1,0:T(8,128)(2,1)} %bitcast.83, bf16[128,32,384]{2,1,0:T(8,128)(2,1)} %bitcast.90, bf16[128,32,384]{2,1,0:T(8,128)(2,1)} %bitcast.95, ...), custom_call_target="tpu_custom_call" | custom-call | flops 503316480 | bytes 20185088 | tf_op jit(solution)/shard_map/triangle/pallas_call | solution.py:139
  460.1 19.5 %triangle.19 = bf16[6,32,32,128]{3,2,1,0:T(8,128)(2,1)} custom-call(s32[1]{0:T(128)} %bitcast.5.which, bf16[128,32,384]{2,1,0:T(8,128)(2,1)} %bitcast.98, bf16[128,32,384]{2,1,0:T(8,128)(2,1)} %bitcast.42, bf16[128,32,384]{2,1,0:T(8,128)(2,1)} %collective-permute-done.5.refs_2_.refs_3_.refs_4_.refs_5_.refs_6_.refs_7_, ...), custom_call_target="tpu_custom_call" | custom-call | flops 603979776 | bytes 23592960 | tf_op jit(solution)/shard_map/triangle/pallas_call | solution.py:139
  494.6 14.0 %triangle.21.refs_1_.refs_0_ = bf16[3,32,32,128]{3,2,1,0:T(8,128)(2,1)S(1)} custom-call(s32[1]{0:T(128)} %bitcast.which, bf16[128,32,384]{2,1,0:T(8,128)(2,1)} %bitcast.56, bf16[128,32,384]{2,1,0:T(8,128)(2,1)} %bitcast.66, bf16[128,32,384]{2,1,0:T(8,128)(2,1)} %bitcast.44, ...), custom_call_target="tpu_custom_call" | custom-call | flops 301989888 | bytes 13369344 | tf_op jit(solution)/shard_map/triangle/pallas_call | solution.py:139
  508.5 16.7 %triangle.22.refs_2_.refs_0_.refs_1_ = bf16[5,32,32,128]{3,2,1,0:T(8,128)(2,1)S(1)} custom-call(s32[1]{0:T(128)} %bitcast.which, bf16[128,32,384]{2,1,0:T(8,128)(2,1)} %bitcast.57, bf16[128,32,384]{2,1,0:T(8,128)(2,1)} %bitcast.67, bf16[128,32,384]{2,1,0:T(8,128)(2,1)} %bitcast.84, bf16[128,32,384]{2,1,0:T(8,128)(2,1)} %bitcast.45, ...), custom_call_target="tpu_custom_call" | custom-call | flops 503316480 | bytes 20185088 | tf_op jit(solution)/shard_map/triangle/pallas_call | solution.py:139
  526.3 19.3 %triangle.23.refs_3_.refs_0_.refs_1_.refs_2_ = bf16[7,32,32,128]{3,2,1,0:T(8,128)(2,1)S(1)} custom-call(s32[1]{0:T(128)} %bitcast.which, bf16[128,32,384]{2,1,0:T(8,128)(2,1)} %bitcast.58, bf16[128,32,384]{2,1,0:T(8,128)(2,1)} %bitcast.68, bf16[128,32,384]{2,1,0:T(8,128)(2,1)} %bitcast.85, bf16[128,32,384]{2,1,0:T(8,128)(2,1)} %bitcast.91, ...), custom_call_target="tpu_custom_call" | custom-call | flops 704643072 | bytes 27000832 | tf_op jit(solution)/shard_map/triangle/pallas_call | solution.py:139
  545.6 22.8 %triangle.24.refs_4_.refs_0_.refs_1_.refs_2_.refs_3_ = bf16[9,32,32,128]{3,2,1,0:T(8,128)(2,1)} custom-call(s32[1]{0:T(128)} %bitcast.which, bf16[128,32,384]{2,1,0:T(8,128)(2,1)} %bitcast.59, bf16[128,32,384]{2,1,0:T(8,128)(2,1)} %bitcast.69, bf16[128,32,384]{2,1,0:T(8,128)(2,1)} %bitcast.86, bf16[128,32,384]{2,1,0:T(8,128)(2,1)} %bitcast.92, ...), custom_call_target="tpu_custom_call" | custom-call | flops 905969664 | bytes 33816576 | tf_op jit(solution)/shard_map/triangle/pallas_call | solution.py:139
  568.5 24.8 %triangle.25.refs_5_.refs_0_.refs_1_.refs_2_.refs_3_.refs_4_ = bf16[11,32,32,128]{3,2,1,0:T(8,128)(2,1)} custom-call(s32[1]{0:T(128)} %bitcast.which, bf16[128,32,384]{2,1,0:T(8,128)(2,1)} %bitcast.60, bf16[128,32,384]{2,1,0:T(8,128)(2,1)} %bitcast.70, bf16[128,32,384]{2,1,0:T(8,128)(2,1)} %bitcast.87, bf16[128,32,384]{2,1,0:T(8,128)(2,1)} %bitcast.93, ...), custom_call_target="tpu_custom_call" | custom-call | flops 1107296256 | bytes 40632320 | tf_op jit(solution)/shard_map/triangle/pallas_call | solution.py:139
  593.4 25.1 %gate.1.refs_12_ = bf16[192,192,128]{2,1,0:T(8,128)(2,1)} custom-call(bf16[192,192,128]{2,1,0:T(8,128)(2,1)} %pair.1, bf16[128,128]{1,0:T(8,128)(2,1)S(1)} %add_convert_fusion.refs_3_.centre, bf16[256,128]{1,0:T(8,128)(2,1)S(1)} %broadcast_in_dim.29.mean, f32[1,128]{1,0:T(1,128)S(1)} %bitcast.34, f32[1,128]{1,0:T(1,128)S(1)} %bitcast.35, ...), custom_call_target="tpu_custom_call" | custom-call | flops 4831838208 | bytes 18874368 | tf_op jit(solution)/shard_map/gate/pallas_call | solution.py:177
  618.5 46.5 %collective-permute-done.24.refs_11_ = bf16[5,32,32,128]{3,2,1,0:T(8,128)(2,1)S(1)} collective-permute-done((bf16[5,32,32,128]{3,2,1,0:T(8,128)(2,1)}, bf16[5,32,32,128]{3,2,1,0:T(8,128)(2,1)S(1)}, u32[]{:S(2)}, u32[]{:S(2)}) %collective-permute-start.24) | collective-permute-done | bytes 1310752 | tf_op jit(solution)/shard_map/ppermute | solution.py:395
  (135 shorter events, 199.0 us)
Async XLA Ops:
  6.5 37.4 %collective-permute-start = (bf16[32,192,128]{2,1,0:T(8,128)(2,1)S(1)}, bf16[32,192,128]{2,1,0:T(8,128)(2,1)S(1)}, u32[]{:S(2)}, u32[]{:S(2)}) collective-permute-start(bf16[32,192,128]{2,1,0:T(8,128)(2,1)S(1)} %get-tuple-element.114), channel_id=1, source_target_pairs={{0,1},{1,0},{2,3},{3,2},{4,5},{5,4},{6,7},{7,6},{8,9},{9,8},{10,11... | collective-permute-start | bytes 4718600 | tf_op jit(solution)/shard_map/ppermute | solution.py:373
  45.1 35.9 %collective-permute-start.1 = (bf16[32,192,128]{2,1,0:T(8,128)(2,1)}, bf16[32,192,128]{2,1,0:T(8,128)(2,1)}, u32[]{:S(2)}, u32[]{:S(2)}) collective-permute-start(bf16[32,192,128]{2,1,0:T(8,128)(2,1)} %get-tuple-element.58), channel_id=1, source_target_pairs={{0,1},{1,0},{2,3},{3,2},{4,5},{5,4},{6,7},{7,6},{8,9},{9,8},{10,11... | collective-permute-start | bytes 4718600 | tf_op jit(solution)/shard_map/ppermute | solution.py:373
  81.0 39.6 %collective-permute-start.4 = (bf16[128,32,384]{2,1,0:T(8,128)(2,1)}, bf16[128,32,384]{2,1,0:T(8,128)(2,1)}, u32[]{:S(2)}, u32[]{:S(2)}) collective-permute-start(bf16[128,32,384]{2,1,0:T(8,128)(2,1)} %bitcast.36), channel_id=1, source_target_pairs={{0,12},{2,14},{5,9},{7,11},{8,4},{10,6},{13,1},{15,3},{16,28},{18,... | collective-permute-start | bytes 9437192 | tf_op jit(solution)/shard_map/ppermute | solution.py:321
  84.0 36.6 %collective-permute-start.2 = (bf16[32,192,128]{2,1,0:T(8,128)(2,1)}, bf16[32,192,128]{2,1,0:T(8,128)(2,1)}, u32[]{:S(2)}, u32[]{:S(2)}) collective-permute-start(bf16[32,192,128]{2,1,0:T(8,128)(2,1)} %get-tuple-element.59), channel_id=1, source_target_pairs={{0,1},{1,0},{2,3},{3,2},{4,5},{5,4},{6,7},{7,6},{8,9},{9,8},{10,11... | collective-permute-start | bytes 4718600 | tf_op jit(solution)/shard_map/ppermute | solution.py:373
  122.9 24.2 %collective-permute-start.5 = (bf16[128,32,384]{2,1,0:T(8,128)(2,1)}, bf16[128,32,384]{2,1,0:T(8,128)(2,1)}, u32[]{:S(2)}, u32[]{:S(2)}) collective-permute-start(bf16[128,32,384]{2,1,0:T(8,128)(2,1)} %broadcast_select_fusion.5), channel_id=1, source_target_pairs={{0,4},{4,0},{8,12},{12,8},{1,5},{5,1},{9,13},{13,9},{2,6},{6,2},{1... | collective-permute-start | bytes 9437192 | tf_op jit(solution)/shard_map/ppermute | solution.py:327
  125.3 39.8 %collective-permute-start.6 = (bf16[128,32,384]{2,1,0:T(8,128)(2,1)}, bf16[128,32,384]{2,1,0:T(8,128)(2,1)}, u32[]{:S(2)}, u32[]{:S(2)}) collective-permute-start(bf16[128,32,384]{2,1,0:T(8,128)(2,1)} %bitcast.8.refs_5_.refs_6_.refs_7_.refs_8_.refs_4_.refs_9_), channel_id=1, source_target_pairs={{0,12},{2,14},{5,9},{7,11},{8,4},{10,6},{13,1},{15,3},{16,28},{18,... | collective-permute-start | bytes 9437192 | tf_op jit(solution)/shard_map/ppermute | solution.py:321
  130.0 35.1 %collective-permute-start.3 = (bf16[32,192,128]{2,1,0:T(8,128)(2,1)S(1)}, bf16[32,192,128]{2,1,0:T(8,128)(2,1)}, u32[]{:S(2)}, u32[]{:S(2)}) collective-permute-start(bf16[32,192,128]{2,1,0:T(8,128)(2,1)S(1)} %get-tuple-element.65), channel_id=1, source_target_pairs={{0,1},{1,0},{2,3},{3,2},{4,5},{5,4},{6,7},{7,6},{8,9},{9,8},{10,11... | collective-permute-start | bytes 4718600 | tf_op jit(solution)/shard_map/ppermute | solution.py:373
  169.1 24.2 %collective-permute-start.7 = (bf16[128,32,384]{2,1,0:T(8,128)(2,1)}, bf16[128,32,384]{2,1,0:T(8,128)(2,1)S(1)}, u32[]{:S(2)}, u32[]{:S(2)}) collective-permute-start(bf16[128,32,384]{2,1,0:T(8,128)(2,1)} %broadcast_select_fusion.4), channel_id=1, source_target_pairs={{0,4},{4,0},{8,12},{12,8},{1,5},{5,1},{9,13},{13,9},{2,6},{6,2},{1... | collective-permute-start | bytes 9437192 | tf_op jit(solution)/shard_map/ppermute | solution.py:327
  169.4 46.9 %collective-permute-start.11 = (bf16[128,32,384]{2,1,0:T(8,128)(2,1)S(1)}, bf16[128,32,384]{2,1,0:T(8,128)(2,1)}, u32[]{:S(2)}, u32[]{:S(2)}) collective-permute-start(bf16[128,32,384]{2,1,0:T(8,128)(2,1)S(1)} %bitcast.79), channel_id=1, source_target_pairs={{0,12},{2,14},{5,9},{7,11},{8,4},{10,6},{13,1},{15,3},{16,28},{18,... | collective-permute-start | bytes 9437192 | tf_op jit(solution)/shard_map/ppermute | solution.py:321
  173.8 42.5 %collective-permute-start.8 = (bf16[32,192,128]{2,1,0:T(8,128)(2,1)}, bf16[32,192,128]{2,1,0:T(8,128)(2,1)S(1)}, u32[]{:S(2)}, u32[]{:S(2)}) collective-permute-start(bf16[32,192,128]{2,1,0:T(8,128)(2,1)} %get-tuple-element.75), channel_id=1, source_target_pairs={{0,1},{1,0},{2,3},{3,2},{4,5},{5,4},{6,7},{7,6},{8,9},{9,8},{10,11... | collective-permute-start | bytes 4718600 | tf_op jit(solution)/shard_map/ppermute | solution.py:373
  173.8 39.4 %collective-permute-start.9 = (bf16[1,32,32,128]{3,2,1,0:T(8,128)(2,1)S(1)}, bf16[1,32,32,128]{3,2,1,0:T(8,128)(2,1)S(1)}, u32[]{:S(2)}, u32[]{:S(2)}) collective-permute-start(bf16[1,32,32,128]{3,2,1,0:T(8,128)(2,1)S(1)} %triangle.13), channel_id=1, source_target_pairs={{0,2},{1,3},{2,0},{3,1},{4,6},{5,7},{6,4},{7,5},{8,10},{9,11},{10,... | collective-permute-start | bytes 786440 | tf_op jit(solution)/shard_map/ppermute | solution.py:395
  218.7 23.7 %collective-permute-start.12 = (bf16[128,32,384]{2,1,0:T(8,128)(2,1)}, bf16[128,32,384]{2,1,0:T(8,128)(2,1)S(1)}, u32[]{:S(2)}, u32[]{:S(2)}) collective-permute-start(bf16[128,32,384]{2,1,0:T(8,128)(2,1)} %broadcast_select_fusion.3), channel_id=1, source_target_pairs={{0,4},{4,0},{8,12},{12,8},{1,5},{5,1},{9,13},{13,9},{2,6},{6,2},{1... | collective-permute-start | bytes 9437192 | tf_op jit(solution)/shard_map/ppermute | solution.py:327
  220.5 58.4 %collective-permute-start.13 = (bf16[128,32,384]{2,1,0:T(8,128)(2,1)}, bf16[128,32,384]{2,1,0:T(8,128)(2,1)S(1)}, u32[]{:S(2)}, u32[]{:S(2)}) collective-permute-start(bf16[128,32,384]{2,1,0:T(8,128)(2,1)} %bitcast.12.refs_13_.refs_14_.refs_10_.refs_15_), channel_id=1, source_target_pairs={{0,12},{2,14},{5,9},{7,11},{8,4},{10,6},{13,1},{15,3},{16,28},{18,... | collective-permute-start | bytes 9437192 | tf_op jit(solution)/shard_map/ppermute | solution.py:321
  224.7 54.2 %collective-permute-start.10 = (bf16[32,192,128]{2,1,0:T(8,128)(2,1)}, bf16[32,192,128]{2,1,0:T(8,128)(2,1)}, u32[]{:S(2)}, u32[]{:S(2)}) collective-permute-start(bf16[32,192,128]{2,1,0:T(8,128)(2,1)} %get-tuple-element.76), channel_id=1, source_target_pairs={{0,1},{1,0},{2,3},{3,2},{4,5},{5,4},{6,7},{7,6},{8,9},{9,8},{10,11... | collective-permute-start | bytes 4718600 | tf_op jit(solution)/shard_map/ppermute | solution.py:373
  225.4 50.3 %collective-permute-start.14 = (bf16[3,32,32,128]{3,2,1,0:T(8,128)(2,1)S(1)}, bf16[3,32,32,128]{3,2,1,0:T(8,128)(2,1)S(1)}, u32[]{:S(2)}, u32[]{:S(2)}) collective-permute-start(bf16[3,32,32,128]{3,2,1,0:T(8,128)(2,1)S(1)} %triangle.14), channel_id=1, source_target_pairs={{0,2},{1,3},{2,0},{3,1},{4,6},{5,7},{6,4},{7,5},{8,10},{9,11},{10,... | collective-permute-start | bytes 2359304 | tf_op jit(solution)/shard_map/ppermute | solution.py:395
  284.2 22.3 %collective-permute-start.15 = (bf16[128,32,384]{2,1,0:T(8,128)(2,1)}, bf16[128,32,384]{2,1,0:T(8,128)(2,1)S(1)}, u32[]{:S(2)}, u32[]{:S(2)}) collective-permute-start(bf16[128,32,384]{2,1,0:T(8,128)(2,1)} %broadcast_select_fusion.2), channel_id=1, source_target_pairs={{0,4},{4,0},{8,12},{12,8},{1,5},{5,1},{9,13},{13,9},{2,6},{6,2},{1... | collective-permute-start | bytes 9437192 | tf_op jit(solution)/shard_map/ppermute | solution.py:327
  284.3 61.5 %collective-permute-start.16 = (bf16[128,32,384]{2,1,0:T(8,128)(2,1)}, bf16[128,32,384]{2,1,0:T(8,128)(2,1)S(1)}, u32[]{:S(2)}, u32[]{:S(2)}) collective-permute-start(bf16[128,32,384]{2,1,0:T(8,128)(2,1)} %bitcast.13.refs_17_.refs_13_.refs_18_), channel_id=1, source_target_pairs={{0,12},{2,14},{5,9},{7,11},{8,4},{10,6},{13,1},{15,3},{16,28},{18,... | collective-permute-start | bytes 9437192 | tf_op jit(solution)/shard_map/ppermute | solution.py:321
  286.2 59.6 %collective-permute-start.17 = (bf16[5,32,32,128]{3,2,1,0:T(8,128)(2,1)S(1)}, bf16[5,32,32,128]{3,2,1,0:T(8,128)(2,1)}, u32[]{:S(2)}, u32[]{:S(2)}) collective-permute-start(bf16[5,32,32,128]{3,2,1,0:T(8,128)(2,1)S(1)} %triangle.15), channel_id=1, source_target_pairs={{0,2},{1,3},{2,0},{3,1},{4,6},{5,7},{6,4},{7,5},{8,10},{9,11},{10,... | collective-permute-start | bytes 3932168 | tf_op jit(solution)/shard_map/ppermute | solution.py:395
  349.4 5.7 collective-permute-start.18
  349.5 82.3 %collective-permute-start.19 = (bf16[128,32,384]{2,1,0:T(8,128)(2,1)}, bf16[128,32,384]{2,1,0:T(8,128)(2,1)S(1)}, u32[]{:S(2)}, u32[]{:S(2)}) collective-permute-start(bf16[128,32,384]{2,1,0:T(8,128)(2,1)} %bitcast.14.refs_5_.refs_16_.refs_21_), channel_id=1, source_target_pairs={{0,12},{2,14},{5,9},{7,11},{8,4},{10,6},{13,1},{15,3},{16,28},{18,... | collective-permute-start | bytes 9437192 | tf_op jit(solution)/shard_map/ppermute | solution.py:321
  352.4 79.4 %collective-permute-start.20 = (bf16[7,32,32,128]{3,2,1,0:T(8,128)(2,1)S(1)}, bf16[7,32,32,128]{3,2,1,0:T(8,128)(2,1)S(1)}, u32[]{:S(2)}, u32[]{:S(2)}) collective-permute-start(bf16[7,32,32,128]{3,2,1,0:T(8,128)(2,1)S(1)} %triangle.16), channel_id=1, source_target_pairs={{0,2},{1,3},{2,0},{3,1},{4,6},{5,7},{6,4},{7,5},{8,10},{9,11},{10,... | collective-permute-start | bytes 5505032 | tf_op jit(solution)/shard_map/ppermute | solution.py:395
  436.1 182.4 %collective-permute-start.23 = (bf16[9,32,32,128]{3,2,1,0:T(8,128)(2,1)}, bf16[9,32,32,128]{3,2,1,0:T(8,128)(2,1)}, u32[]{:S(2)}, u32[]{:S(2)}) collective-permute-start(bf16[9,32,32,128]{3,2,1,0:T(8,128)(2,1)} %triangle.17), channel_id=1, source_target_pairs={{0,2},{1,3},{2,0},{3,1},{4,6},{5,7},{6,4},{7,5},{8,10},{9,11},{10,... | collective-permute-start | bytes 7077896 | tf_op jit(solution)/shard_map/ppermute | solution.py:395
  479.6 232.7 %collective-permute-start.22 = (bf16[6,32,32,128]{3,2,1,0:T(8,128)(2,1)}, bf16[6,32,32,128]{3,2,1,0:T(8,128)(2,1)S(1)}, u32[]{:S(2)}, u32[]{:S(2)}) collective-permute-start(bf16[6,32,32,128]{3,2,1,0:T(8,128)(2,1)} %triangle.19), channel_id=1, source_target_pairs={{0,2},{1,3},{2,0},{3,1},{4,6},{5,7},{6,4},{7,5},{8,10},{9,11},{10,... | collective-permute-start | bytes 4718600 | tf_op jit(solution)/shard_map/ppermute | solution.py:395
  479.6 185.4 %collective-permute-start.24 = (bf16[5,32,32,128]{3,2,1,0:T(8,128)(2,1)}, bf16[5,32,32,128]{3,2,1,0:T(8,128)(2,1)S(1)}, u32[]{:S(2)}, u32[]{:S(2)}) collective-permute-start(bf16[5,32,32,128]{3,2,1,0:T(8,128)(2,1)} %triangle.18), channel_id=1, source_target_pairs={{0,2},{1,3},{2,0},{3,1},{4,6},{5,7},{6,4},{7,5},{8,10},{9,11},{10,... | collective-permute-start | bytes 3932168 | tf_op jit(solution)/shard_map/ppermute | solution.py:395
  (32 other events, 504.7 us)

commit v4 on v3

--- a/solution.py
+++ b/solution.py
@@ -12,6 +12,10 @@
 EPS = 1e-05
 F32, BF16 = jnp.float32, jnp.bfloat16
 PARAMS = pltpu.CompilerParams(vmem_limit_bytes=52 * 1024 * 1024)
+
+
+def sigmoid(x):
+    return pl.reciprocal(1.0 + jnp.exp(-x), approx=True)
 
 
 def contract(left, right, left_dim, right_dim):
@@ -55,10 +59,10 @@
         centred = contract(centre[...], values, 1, 1)
         variance = jnp.mean(centred * centred, axis=0, keepdims=True)
         normed = centred * lax.rsqrt(variance + EPS) * gain[...] + bias[...]
-        halved = contract(weights[...], normed.astype(BF16), 1, 0)
+        projected = contract(weights[...], normed.astype(BF16), 1, 0)
         for first, held in ((0, left_rows), (2 * hidden, right_rows)):
-            gate, value = halved[first : first + hidden], halved[first + hidden : first + 2 * hidden]
-            held[i] = value + value * jnp.tanh(gate)
+            gate = projected[first : first + hidden]
+            held[i] = sigmoid(gate) * projected[first + hidden : first + 2 * hidden]
         return carry
 
     lax.fori_loop(0, rows, one_row, 0, unroll=4)
@@ -111,11 +115,14 @@
     step = lefts[0].shape[0]
 
     def go(choice):
-        for first in range(0, step, group):
+        def one_group(g, carry):
             for n, (i, j) in enumerate(pairs):
                 side = sides[j * n_sides + choice]
-                parts = [contract(lefts[i][h], side[h], 1, 1) for h in range(first, first + group)]
-                out[n, first // group] = jnp.concatenate(parts, axis=-1).astype(BF16)
+                parts = [contract(lefts[i][g * group + h], side[g * group + h], 1, 1) for h in range(group)]
+                out[n, g] = jnp.concatenate(parts, axis=-1).astype(BF16)
+            return carry
+
+        lax.fori_loop(0, step // group, one_group, 0, unroll=2)
 
     for n in range(n_sides):
         pl.when(which[0] == n)(functools.partial(go, n))
@@ -130,7 +137,7 @@
     columns = rights[0][0].shape[1]
     n_sides = len(rights[0])
     group = group_of(columns)
-    step = max(8, group)
+    step = max(16 if len(rights) > 3 else 32, group)
     shape = jax.ShapeDtypeStruct((len(pairs), hidden // group, rows, group * columns), BF16)
 
     def side_spec(n):
@@ -165,7 +172,7 @@
     low = (square - high.astype(F32)).astype(BF16)
     variance = contract(jnp.concatenate([high, low], axis=1), mean[...], 1, 0)
     normed = (centred * lax.rsqrt(variance + EPS) * gain[...] + bias[...]).astype(BF16)
-    gate = 0.5 + 0.5 * jnp.tanh(contract(normed, weights[...], 1, 0))
+    gate = sigmoid(contract(normed, weights[...], 1, 0))
     out[...] = gate.astype(BF16).reshape(rows, columns, channels)
 
 
@@ -188,11 +195,9 @@
     )(pair, centre, mean, gain, bias, weights)
 
 
-def finish_kernel(n_parts, group, hidden, *refs):
-    own, sent = refs[:n_parts], refs[n_parts : 2 * n_parts]
-    gate, weights, gain, bias = refs[2 * n_parts : 2 * n_parts + 4]
+def finish_kernel(group, hidden, own, sent, gate, weights, gain, bias, *refs):
     out, rows_of = refs[-2:]
-    packed, rows, lanes = own[0].shape
+    packed, rows, lanes = own.shape
     columns = lanes // group
 
     def over_hidden(x):
@@ -203,53 +208,52 @@
             shift *= 2
         return total * (1.0 / hidden)
 
-    for n in range(n_parts):
-        total = own[n][...].astype(F32) + sent[n][...].astype(F32)
-        centred = total - over_hidden(total)[None]
-        scale = lax.rsqrt(over_hidden(centred * centred) + EPS)
-        normed = centred * scale[None] * gain[...] + bias[...]
-        rows_of[n] = normed.reshape(packed * rows, lanes)
+    total = own[...].astype(F32) + sent[...].astype(F32)
+    centred = total - over_hidden(total)[None]
+    scale = lax.rsqrt(over_hidden(centred * centred) + EPS)
+    normed = centred * scale[None] * gain[...] + bias[...]
+    rows_of[...] = normed.reshape(packed * rows, lanes)
     for i in range(rows):
-        parts = []
-        for n in range(n_parts):
-            held = rows_of[n, pl.ds(i, packed, stride=rows), :]
-            parts.append(
-                jnp.concatenate([held[:, g * columns : (g + 1) * columns] for g in range(group)], axis=0)
-            )
-        normed = jnp.concatenate(parts, axis=1).astype(BF16)
-        result = contract(normed, weights[...], 0, 0)
+        held = rows_of[pl.ds(i, packed, stride=rows), :]
+        parts = [held[:, g * columns : (g + 1) * columns] for g in range(group)]
+        result = contract(jnp.concatenate(parts, axis=0).astype(BF16), weights[...], 0, 0)
         out[i] = (result * gate[i].astype(F32)).astype(BF16)
 
 
-def finish(own, sent, gate, first, weights, gain, bias, held):
+def finish(own, sent, gate, t, chunks, share, weights, gain, bias, held):
     rows = 16
-    _, packed, count, lanes = own[0][0].shape
-    hidden = weights.shape[0]
+    pieces, packed, count, lanes = own.shape
+    hidden, channels = weights.shape
     group = hidden // packed
-    whole = lambda x: pl.BlockSpec(x.shape, lambda i: (0,) * x.ndim)
-    part = lambda n: pl.BlockSpec((None, packed, rows, lanes), lambda i: (n, 0, i, 0))
-    block = pl.BlockSpec((rows,) + gate.shape[1:], lambda i: (i + first // rows, 0, 0))
-    n_parts = len(own)
-    parts = own + sent
+    steps = count // rows
+    before = t * share
+
+    def row_of(p):
+        return jnp.where(p < before, p // share, t)
+
+    def column_of(p):
+        of_row = p - before
+        return jnp.where(p < before, (p % share) * chunks + t, (of_row % share) * chunks + of_row // share)
+
+    whole = lambda x: pl.BlockSpec(x.shape, lambda p, r: (0,) * x.ndim)
+    part = pl.BlockSpec((None, packed, rows, lanes), lambda p, r: (p, 0, r, 0))
+    block = pl.BlockSpec((rows, lanes // group, channels), lambda p, r: (row_of(p) * steps + r, column_of(p), 0))
     earlier = [] if held is None else [held]
     return pl.pallas_call(
-        functools.partial(finish_kernel, n_parts, group, hidden),
-        grid=(count // rows,),
-        in_specs=[part(n) for _, n in parts]
-        + [block, whole(weights), whole(gain), whole(bias)]
+        functools.partial(finish_kernel, group, hidden),
+        grid=(pieces, steps),
+        in_specs=[part, part, block, whole(weights), whole(gain), whole(bias)]
         + [pl.BlockSpec(memory_space=pl.ANY)] * len(earlier),
         out_specs=block,
         out_shape=jax.ShapeDtypeStruct(gate.shape, BF16),
-        scratch_shapes=[pltpu.VMEM((n_parts, packed * rows, lanes), F32)],
-        input_output_aliases={2 * n_parts + 4: 0} if earlier else {},
+        scratch_shapes=[pltpu.VMEM((packed * rows, lanes), F32)],
+        input_output_aliases={6: 0} if earlier else {},
         compiler_params=PARAMS,
         cost_estimate=at_least(
-            count * gate.shape[1] * hidden * gate.shape[2],
-            count * gate.shape[1],
-            *[jax.ShapeDtypeStruct(x.shape[1:], x.dtype) for x, _ in parts],
+            pieces * count * (lanes // group) * hidden * channels, pieces * count * (lanes // group), own, sent
         ),
         name="finish",
-    )(*[x for x, _ in parts], gate, weights, gain, bias, *earlier)
+    )(own, sent, gate, weights, gain, bias, *earlier)
 
 
 def after(value, *others):
@@ -270,10 +274,9 @@
     group = group_of(step)
     packed = hidden // group
 
-    halves = (w_proj * 0.5).astype(BF16).T
+    w_sides = w_proj.T
     centre = (jnp.eye(channels, dtype=F32) - 1.0 / channels).astype(BF16)
     mean = jnp.full((2 * channels, channels), 1.0 / channels, BF16)
-    half_gate = (w_gate * 0.5).astype(BF16)
     by_hidden = lambda v: jnp.repeat(v.reshape(packed, group), step, axis=1)[:, None, :]
     gain_out, bias_out = by_hidden(out_gain), by_hidden(out_bias)
     w_last = w_out.reshape(packed, group, channels).swapaxes(0, 1).reshape(hidden, channels)
@@ -349,16 +352,16 @@
     for t in range(chunks):
         by_column = [(i, t, s) for i in range(t) for s in shards]
         by_row = [(t, j, s) for j in range(t + 1) for s in shards]
-        waves.append([by_column, by_row] if t == chunks - 1 and t else [by_column + by_row])
-
-    exchanged, arrived, own_parts, sent_parts = [], {}, {}, {}
+        waves.append(by_column + by_row)
+
+    exchanged = []
 
     def prepare(t, *held):
         left, right = project(
             [pair_act] + exchanged[t],
             [t * step] + [0] * (half - 1),
             step,
-            halves,
+            w_sides,
             centre,
             after(gain_in, *held) if held else gain_in,
             bias_in,
@@ -368,13 +371,17 @@
         return left
 
     def exchange(n, *waits):
-        block = pair_act[n * step : (n + 1) * step]
-        block = after(block, *waits) if waits else block
+        block = (after(pair_act, *waits) if waits else pair_act)[n * step : (n + 1) * step]
         exchanged.append([lax.ppermute(block, "col", [(c, c ^ o) for c in range(n_col)]) for o in range(1, half)])
 
+    def keep_own():
+        t = len(own)
+        lefts[t] = after(lefts[t], *token)
+        own.append(product(waves[t], True))
+        token[:] = own[-1:]
+
     exchange(0)
-    token = []
-    moved = []
+    token, moved, own = [], [], []
     for n in range(chunks + 2):
         waits = token + (exchanged[n][-1:] if n < chunks else []) + (moved[n - 4 : n - 3] if n >= 4 else [])
         if n + 1 < chunks:
@@ -387,35 +394,20 @@
             token = [prepare(n, *token)]
         if n >= 2:
             t = n - 2
-            for pairs in waves[t]:
-                lefts[t] = after(lefts[t], *token)
-                made = product(pairs, False)
-                token = [made]
-                waits = moved[t - 1 : t] if t < chunks - 1 else []
-                moved.append(lax.ppermute(after(made, *waits) if waits else made, "col", swap_half))
-                for p, pair in enumerate(pairs):
-                    sent_parts[pair] = (moved[-1], p)
+            if t == chunks - 1:
+                while len(own) < t - 1:
+                    keep_own()
+            lefts[t] = after(lefts[t], *token)
+            made = product(waves[t], False)
+            token = [made]
+            waits = moved[t - 1 : t]
+            moved.append(lax.ppermute(after(made, *waits) if waits else made, "col", swap_half))
+    while len(own) < chunks:
+        keep_own()
+    gate = gate_of(pair_act, centre, mean, after(ln_gain[None], *token), ln_bias[None], w_gate)
+    out = None
     for t in range(chunks):
-        pairs = [pair for part in waves[t] for pair in part]
-        lefts[t] = after(lefts[t], *token)
-        made = product(pairs, True)
-        token = [made]
-        for n, pair in enumerate(pairs):
-            own_parts[pair] = (made, n)
-    gate = gate_of(pair_act, centre, mean, after(ln_gain[None], *token), ln_bias[None], half_gate)
-    out = None
-    for i in range(chunks):
-        pairs = [(i, j, s) for s in shards for j in range(chunks)]
-        out = finish(
-            [own_parts[pair] for pair in pairs],
-            [sent_parts[pair] for pair in pairs],
-            gate,
-            i * step,
-            w_last,
-            gain_out,
-            bias_out,
-            out,
-        )
+        out = finish(own[t], moved[t], gate, t, chunks, share, w_last, gain_out, bias_out, out)
     return out
 
 

time: 734 us -> 705 us (0.960)
  Pallas kernels: 410 us -> 379 us
    pallas_call x13 -> x12, Pallas kernels: 228 us -> 174 us  [triangle(): pl.pallas_call(functools.partial(triangle_kernel, len(lefts), n_sides, gr...]
    pallas_call x6, Pallas kernels: 55.1 us -> 77.2 us  [finish(): pl.pallas_call(functools.partial(finish_kernel, group, hidden), grid=(pie...]
    ppermute x7 -> x6, waiting for transfers between devices: 137 us -> 143 us  [on_device(): lax.ppermute(after(made, *waits) if waits else made, 'col', swap_half)]
  transfers between devices with their start and end apart: 25 -> 24, of which waited for: 13 -> 13; matrix products, arithmetic and copies ran while one was open for 0% -> 1% of each run, Pallas kernels for 56% -> 51%
where the time goes in v4:
time: 705 us; the launch traced here: 694 us
  Pallas kernels  379 us (54%)
  waiting for transfers between devices  235 us (33%)
  starting transfers between devices  36.3 us (5%)
  other arithmetic  22.8 us (3%)
  local copies, waits for them, and re-layouts  19.9 us (3%)
    pallas_call x12, Pallas kernels, triangle(): pl.pallas_call(functools.partial(triangle_kernel, len(lefts), n_sides, gr...  174 us
    ppermute x6, waiting for transfers between devices, on_device(): lax.ppermute(after(made, *waits) if waits else made, 'col', swap_half)  143 us
    pallas_call x6, Pallas kernels, project(): pl.pallas_call(functools.partial(project_kernel, len(pieces)), grid=(coun...  102 us
    ppermute x6, waiting for transfers between devices, exchange(): lax.ppermute(block, 'col', [(c, c ^ o) for c in range(n_col)])  88.7 us
    pallas_call x6, Pallas kernels, finish(): pl.pallas_call(functools.partial(finish_kernel, group, hidden), grid=(pie...  77.2 us
    pallas_call x1, Pallas kernels, gate_of(): pl.pallas_call(gate_kernel, grid=(count // rows,), in_specs=[block] + [wh...  25.2 us
    select_n x6, other arithmetic, second_step(): given = jnp.where(holder, right, after(far, *waits))  22.7 us
    ppermute x6, starting transfers between devices, first_step(): return lax.ppermute(right, axes, pairs)  21.2 us
  transfers between devices with their start and end apart: 24, of which 13 were waited for; matrix products, arithmetic and copies ran while one was open for 1% of the time, Pallas kernels for 51%

profile of v4, /device:TPU:0, one launch (start us, length us, event | category | flops | bytes accessed | tf_op | source)
XLA Modules:
  0.0 693.5 jit_solution(15050081175700448209)
XLA Ops:
  4.7 34.5 %collective-permute-done.refs_1_ = bf16[32,192,128]{2,1,0:T(8,128)(2,1)} collective-permute-done((bf16[32,192,128]{2,1,0:T(8,128)(2,1)S(1)}, bf16[32,192,128]{2,1,0:T(8,128)(2,1)}, u32[]{:S(2)}, u32[]{:S(2)}) %collective-permute-start) | collective-permute-done | bytes 1572896 | tf_op jit(solution)/shard_map/ppermute | solution.py:375
  42.8 16.9 %project.6 = (bf16[16,8,32,384]{3,2,1,0:T(8,128)(2,1)}, bf16[16,8,32,384]{3,2,1,0:T(8,128)(2,1)}) custom-call(bf16[192,192,128]{2,1,0:T(8,128)(2,1)} %pair.1, bf16[32,192,128]{2,1,0:T(8,128)(2,1)} %collective-permute-done.refs_1_, bf16[512,128]{1,0:T(8,128)(2,1)S(1)} %bitcast.27, bf16[128,128]{1,0:T(8,128)(2,1)S(1)} %add_convert_fusion.refs_3_.centre, ...), custom_call_target="tpu_custom_call" | custom-call | flops 2013265920 | bytes 6291456 | tf_op jit(solution)/shard_map/project/pallas_call | solution.py:96
  59.7 16.7 %collective-permute-done.1.refs_1_ = bf16[32,192,128]{2,1,0:T(8,128)(2,1)} collective-permute-done((bf16[32,192,128]{2,1,0:T(8,128)(2,1)S(1)}, bf16[32,192,128]{2,1,0:T(8,128)(2,1)}, u32[]{:S(2)}, u32[]{:S(2)}) %collective-permute-start.1) | collective-permute-done | bytes 1572896 | tf_op jit(solution)/shard_map/ppermute | solution.py:375
  81.0 17.1 %project.7 = (bf16[16,8,32,384]{3,2,1,0:T(8,128)(2,1)}, bf16[16,8,32,384]{3,2,1,0:T(8,128)(2,1)}) custom-call(bf16[192,192,128]{2,1,0:T(8,128)(2,1)} %pair.1, bf16[32,192,128]{2,1,0:T(8,128)(2,1)} %collective-permute-done.1.refs_1_, bf16[512,128]{1,0:T(8,128)(2,1)S(1)} %bitcast.28, bf16[128,128]{1,0:T(8,128)(2,1)S(1)} %add_convert_fusion.refs_3_.centre, ...), custom_call_target="tpu_custom_call" | custom-call | flops 2013265920 | bytes 6291456 | tf_op jit(solution)/shard_map/project/pallas_call | solution.py:96
  98.1 19.3 %collective-permute-done.2.refs_1_ = bf16[32,192,128]{2,1,0:T(8,128)(2,1)} collective-permute-done((bf16[32,192,128]{2,1,0:T(8,128)(2,1)S(1)}, bf16[32,192,128]{2,1,0:T(8,128)(2,1)}, u32[]{:S(2)}, u32[]{:S(2)}) %collective-permute-start.2) | collective-permute-done | bytes 1572896 | tf_op jit(solution)/shard_map/ppermute | solution.py:375
  128.4 17.1 %project.8 = (bf16[16,8,32,384]{3,2,1,0:T(8,128)(2,1)}, bf16[16,8,32,384]{3,2,1,0:T(8,128)(2,1)}) custom-call(bf16[192,192,128]{2,1,0:T(8,128)(2,1)} %pair.1, bf16[32,192,128]{2,1,0:T(8,128)(2,1)} %collective-permute-done.2.refs_1_, bf16[512,128]{1,0:T(8,128)(2,1)S(1)} %bitcast.29, bf16[128,128]{1,0:T(8,128)(2,1)S(1)} %add_convert_fusion.refs_3_.centre, ...), custom_call_target="tpu_custom_call" | custom-call | flops 2013265920 | bytes 6291456 | tf_op jit(solution)/shard_map/project/pallas_call | solution.py:96
  175.1 16.9 %project.9 = (bf16[16,8,32,384]{3,2,1,0:T(8,128)(2,1)}, bf16[16,8,32,384]{3,2,1,0:T(8,128)(2,1)}) custom-call(bf16[192,192,128]{2,1,0:T(8,128)(2,1)} %pair.1, bf16[32,192,128]{2,1,0:T(8,128)(2,1)} %collective-permute-done.3.refs_1_, bf16[512,128]{1,0:T(8,128)(2,1)S(1)} %bitcast.30, bf16[128,128]{1,0:T(8,128)(2,1)S(1)} %add_convert_fusion.refs_3_.centre, ...), custom_call_target="tpu_custom_call" | custom-call | flops 2013265920 | bytes 6291456 | tf_op jit(solution)/shard_map/project/pallas_call | solution.py:96
  226.4 17.0 %project.10 = (bf16[16,8,32,384]{3,2,1,0:T(8,128)(2,1)}, bf16[16,8,32,384]{3,2,1,0:T(8,128)(2,1)}) custom-call(bf16[192,192,128]{2,1,0:T(8,128)(2,1)} %pair.1, bf16[32,192,128]{2,1,0:T(8,128)(2,1)} %collective-permute-done.6.refs_1_, bf16[512,128]{1,0:T(8,128)(2,1)S(1)} %bitcast.31, bf16[128,128]{1,0:T(8,128)(2,1)S(1)} %add_convert_fusion.refs_3_.centre, ...), custom_call_target="tpu_custom_call" | custom-call | flops 2013265920 | bytes 6291456 | tf_op jit(solution)/shard_map/project/pallas_call | solution.py:96
  258.1 17.3 %collective-permute-done.14.sent = bf16[3,32,32,128]{3,2,1,0:T(8,128)(2,1)S(1)} collective-permute-done((bf16[3,32,32,128]{3,2,1,0:T(8,128)(2,1)S(1)}, bf16[3,32,32,128]{3,2,1,0:T(8,128)(2,1)S(1)}, u32[]{:S(2)}, u32[]{:S(2)}) %collective-permute-start.14) | collective-permute-done | bytes 786464 | tf_op jit(solution)/shard_map/ppermute | solution.py:404
  290.6 16.9 %project.11 = (bf16[16,8,32,384]{3,2,1,0:T(8,128)(2,1)}, bf16[16,8,32,384]{3,2,1,0:T(8,128)(2,1)}) custom-call(bf16[192,192,128]{2,1,0:T(8,128)(2,1)} %pair.1, bf16[32,192,128]{2,1,0:T(8,128)(2,1)} %collective-permute-done.10.refs_1_, bf16[512,128]{1,0:T(8,128)(2,1)S(1)} %bitcast.32, bf16[128,128]{1,0:T(8,128)(2,1)S(1)} %add_convert_fusion.refs_3_.centre, ...), custom_call_target="tpu_custom_call" | custom-call | flops 2013265920 | bytes 6291456 | tf_op jit(solution)/shard_map/project/pallas_call | solution.py:96
  309.2 16.0 %triangle.15 = bf16[7,32,32,128]{3,2,1,0:T(8,128)(2,1)S(1)} custom-call(s32[1]{0:T(128)} %bitcast.5.which, bf16[128,32,384]{2,1,0:T(8,128)(2,1)} %bitcast.57, bf16[128,32,384]{2,1,0:T(8,128)(2,1)} %bitcast.68, bf16[128,32,384]{2,1,0:T(8,128)(2,1)} %bitcast.86, bf16[128,32,384]{2,1,0:T(8,128)(2,1)} %bitcast.93, bf16[128,32,384]{2,1,0:T(8,128)(2,1)} %bitcast.45, ...), custom_call_target="tpu_custom_call" | custom-call | flops 704643072 | bytes 27000832 | tf_op jit(solution)/shard_map/triangle/pallas_call | solution.py:146
  325.2 21.5 %collective-permute-done.17.sent = bf16[5,32,32,128]{3,2,1,0:T(8,128)(2,1)S(1)} collective-permute-done((bf16[5,32,32,128]{3,2,1,0:T(8,128)(2,1)S(1)}, bf16[5,32,32,128]{3,2,1,0:T(8,128)(2,1)S(1)}, u32[]{:S(2)}, u32[]{:S(2)}) %collective-permute-start.17) | collective-permute-done | bytes 1310752 | tf_op jit(solution)/shard_map/ppermute | solution.py:404
  358.6 19.2 %triangle.16 = bf16[9,32,32,128]{3,2,1,0:T(8,128)(2,1)} custom-call(s32[1]{0:T(128)} %bitcast.5.which, bf16[128,32,384]{2,1,0:T(8,128)(2,1)} %bitcast.58, bf16[128,32,384]{2,1,0:T(8,128)(2,1)} %bitcast.69, bf16[128,32,384]{2,1,0:T(8,128)(2,1)} %bitcast.87, bf16[128,32,384]{2,1,0:T(8,128)(2,1)} %bitcast.94, bf16[128,32,384]{2,1,0:T(8,128)(2,1)} %bitcast.99, ...), custom_call_target="tpu_custom_call" | custom-call | flops 905969664 | bytes 33816576 | tf_op jit(solution)/shard_map/triangle/pallas_call | solution.py:146
  377.8 55.9 %collective-permute-done.20.sent = bf16[7,32,32,128]{3,2,1,0:T(8,128)(2,1)} collective-permute-done((bf16[7,32,32,128]{3,2,1,0:T(8,128)(2,1)S(1)}, bf16[7,32,32,128]{3,2,1,0:T(8,128)(2,1)}, u32[]{:S(2)}, u32[]{:S(2)}) %collective-permute-start.20) | collective-permute-done | bytes 1835040 | tf_op jit(solution)/shard_map/ppermute | solution.py:404
  455.4 13.3 %triangle.19.own = bf16[5,32,32,128]{3,2,1,0:T(8,128)(2,1)S(1)} custom-call(s32[1]{0:T(128)} %bitcast.which, bf16[128,32,384]{2,1,0:T(8,128)(2,1)} %bitcast.61, bf16[128,32,384]{2,1,0:T(8,128)(2,1)} %bitcast.71, bf16[128,32,384]{2,1,0:T(8,128)(2,1)} %bitcast.88, bf16[128,32,384]{2,1,0:T(8,128)(2,1)} %bitcast.49, ...), custom_call_target="tpu_custom_call" | custom-call | flops 503316480 | bytes 20185088 | tf_op jit(solution)/shard_map/triangle/pallas_call | solution.py:146
  468.7 16.0 %triangle.20.own = bf16[7,32,32,128]{3,2,1,0:T(8,128)(2,1)S(1)} custom-call(s32[1]{0:T(128)} %bitcast.which, bf16[128,32,384]{2,1,0:T(8,128)(2,1)} %bitcast.62, bf16[128,32,384]{2,1,0:T(8,128)(2,1)} %bitcast.72, bf16[128,32,384]{2,1,0:T(8,128)(2,1)} %bitcast.89, bf16[128,32,384]{2,1,0:T(8,128)(2,1)} %bitcast.95, bf16[128,32,384]{2,1,0:T(8,128)(2,1)} %bitcast.50, ...), custom_call_target="tpu_custom_call" | custom-call | flops 704643072 | bytes 27000832 | tf_op jit(solution)/shard_map/triangle/pallas_call | solution.py:146
  484.8 22.3 %triangle.21 = bf16[11,32,32,128]{3,2,1,0:T(8,128)(2,1)} custom-call(s32[1]{0:T(128)} %bitcast.5.which, bf16[128,32,384]{2,1,0:T(8,128)(2,1)} %bitcast.63, bf16[128,32,384]{2,1,0:T(8,128)(2,1)} %bitcast.73, bf16[128,32,384]{2,1,0:T(8,128)(2,1)} %bitcast.90, bf16[128,32,384]{2,1,0:T(8,128)(2,1)} %bitcast.96, bf16[128,32,384]{2,1,0:T(8,128)(2,1)} %bitcast.100, ...), custom_call_target="tpu_custom_call" | custom-call | flops 1107296256 | bytes 40632320 | tf_op jit(solution)/shard_map/triangle/pallas_call | solution.py:146
  507.0 37.3 %collective-permute-done.22.sent = bf16[9,32,32,128]{3,2,1,0:T(8,128)(2,1)} collective-permute-done((bf16[9,32,32,128]{3,2,1,0:T(8,128)(2,1)}, bf16[9,32,32,128]{3,2,1,0:T(8,128)(2,1)}, u32[]{:S(2)}, u32[]{:S(2)}) %collective-permute-start.22) | collective-permute-done | bytes 2359328 | tf_op jit(solution)/shard_map/ppermute | solution.py:404
  545.8 19.5 %triangle.22.own = bf16[9,32,32,128]{3,2,1,0:T(8,128)(2,1)} custom-call(s32[1]{0:T(128)} %bitcast.which, bf16[128,32,384]{2,1,0:T(8,128)(2,1)} %bitcast.64, bf16[128,32,384]{2,1,0:T(8,128)(2,1)} %bitcast.74, bf16[128,32,384]{2,1,0:T(8,128)(2,1)} %bitcast.91, bf16[128,32,384]{2,1,0:T(8,128)(2,1)} %bitcast.97, bf16[128,32,384]{2,1,0:T(8,128)(2,1)} %bitcast.101, ...), custom_call_target="tpu_custom_call" | custom-call | flops 905969664 | bytes 33816576 | tf_op jit(solution)/shard_map/triangle/pallas_call | solution.py:146
  565.3 22.3 %triangle.23.own = bf16[11,32,32,128]{3,2,1,0:T(8,128)(2,1)} custom-call(s32[1]{0:T(128)} %bitcast.which, bf16[128,32,384]{2,1,0:T(8,128)(2,1)} %bitcast.65, bf16[128,32,384]{2,1,0:T(8,128)(2,1)} %bitcast.75, bf16[128,32,384]{2,1,0:T(8,128)(2,1)} %bitcast.92, bf16[128,32,384]{2,1,0:T(8,128)(2,1)} %bitcast.98, bf16[128,32,384]{2,1,0:T(8,128)(2,1)} %bitcast.102, ...), custom_call_target="tpu_custom_call" | custom-call | flops 1107296256 | bytes 40632320 | tf_op jit(solution)/shard_map/triangle/pallas_call | solution.py:146
  587.7 25.2 %gate.1 = bf16[192,192,128]{2,1,0:T(8,128)(2,1)} custom-call(bf16[192,192,128]{2,1,0:T(8,128)(2,1)} %pair.1, bf16[128,128]{1,0:T(8,128)(2,1)S(1)} %add_convert_fusion.refs_3_.centre, bf16[256,128]{1,0:T(8,128)(2,1)S(1)} %broadcast_in_dim.29.mean, f32[1,128]{1,0:T(1,128)S(1)} %bitcast.39, f32[1,128]{1,0:T(1,128)S(1)} %bitcast.40, bf16[128,128]{1,0:T(8,128)(2,1)S(1)} %copy-done.6), custom_call_target="tpu_custom_call" | custom-call | flops 4831838208 | bytes 18874368 | tf_op jit(solution)/shard_map/gate/pallas_call | solution.py:184
  634.1 14.6 %finish.9.refs_0_ = bf16[192,192,128]{2,1,0:T(8,128)(2,1)} custom-call(bf16[7,32,32,128]{3,2,1,0:T(8,128)(2,1)S(1)} %triangle.20.own, bf16[7,32,32,128]{3,2,1,0:T(8,128)(2,1)} %collective-permute-done.20.sent, bf16[192,192,128]{2,1,0:T(8,128)(2,1)} %gate.1, bf16[128,128]{1,0:T(8,128)(2,1)S(1)} %bitcast.36, ...), custom_call_target="tpu_custom_call", output_to_operand_aliasing={{}: (6, {})} | custom-call | flops 234881024 | bytes 3670016 | tf_op jit(solution)/shard_map/finish/pallas_call | solution.py:242
  648.7 18.8 %finish.10.refs_0_ = bf16[192,192,128]{2,1,0:T(8,128)(2,1)} custom-call(bf16[9,32,32,128]{3,2,1,0:T(8,128)(2,1)} %triangle.22.own, bf16[9,32,32,128]{3,2,1,0:T(8,128)(2,1)} %collective-permute-done.22.sent, bf16[192,192,128]{2,1,0:T(8,128)(2,1)} %gate.1, bf16[128,128]{1,0:T(8,128)(2,1)S(1)} %bitcast.37, ...), custom_call_target="tpu_custom_call", output_to_operand_aliasing={{}: (6, {})} | custom-call | flops 301989888 | bytes 4718592 | tf_op jit(solution)/shard_map/finish/pallas_call | solution.py:242
  670.4 22.7 %finish.11 = bf16[192,192,128]{2,1,0:T(8,128)(2,1)} custom-call(bf16[11,32,32,128]{3,2,1,0:T(8,128)(2,1)} %triangle.23.own, bf16[11,32,32,128]{3,2,1,0:T(8,128)(2,1)} %collective-permute-done.23.sent, bf16[192,192,128]{2,1,0:T(8,128)(2,1)} %gate.1, bf16[128,128]{1,0:T(8,128)(2,1)S(1)} %bitcast.38, ...), custom_call_target="tpu_custom_call", output_to_operand_aliasing={{}: (6, {})} | custom-call | flops 369098752 | bytes 5767168 | tf_op jit(solution)/shard_map/finish/pallas_call | solution.py:242
  (121 shorter events, 178.3 us)
Async XLA Ops:
  1.6 37.6 %collective-permute-start = (bf16[32,192,128]{2,1,0:T(8,128)(2,1)S(1)}, bf16[32,192,128]{2,1,0:T(8,128)(2,1)}, u32[]{:S(2)}, u32[]{:S(2)}) collective-permute-start(bf16[32,192,128]{2,1,0:T(8,128)(2,1)S(1)} %slice.18), channel_id=1, source_target_pairs={{0,1},{1,0},{2,3},{3,2},{4,5},{5,4},{6,7},{7,6},{8,9},{9,8},{10,11... | collective-permute-start | bytes 4718600 | tf_op jit(solution)/shard_map/ppermute | solution.py:375
  40.7 35.8 %collective-permute-start.1 = (bf16[32,192,128]{2,1,0:T(8,128)(2,1)S(1)}, bf16[32,192,128]{2,1,0:T(8,128)(2,1)}, u32[]{:S(2)}, u32[]{:S(2)}) collective-permute-start(bf16[32,192,128]{2,1,0:T(8,128)(2,1)S(1)} %slice.19), channel_id=1, source_target_pairs={{0,1},{1,0},{2,3},{3,2},{4,5},{5,4},{6,7},{7,6},{8,9},{9,8},{10,11... | collective-permute-start | bytes 4718600 | tf_op jit(solution)/shard_map/ppermute | solution.py:375
  76.4 41.0 %collective-permute-start.4 = (bf16[128,32,384]{2,1,0:T(8,128)(2,1)}, bf16[128,32,384]{2,1,0:T(8,128)(2,1)}, u32[]{:S(2)}, u32[]{:S(2)}) collective-permute-start(bf16[128,32,384]{2,1,0:T(8,128)(2,1)} %bitcast.41), channel_id=1, source_target_pairs={{0,12},{2,14},{5,9},{7,11},{8,4},{10,6},{13,1},{15,3},{16,28},{18,... | collective-permute-start | bytes 9437192 | tf_op jit(solution)/shard_map/ppermute | solution.py:324
  80.9 36.5 %collective-permute-start.2 = (bf16[32,192,128]{2,1,0:T(8,128)(2,1)S(1)}, bf16[32,192,128]{2,1,0:T(8,128)(2,1)}, u32[]{:S(2)}, u32[]{:S(2)}) collective-permute-start(bf16[32,192,128]{2,1,0:T(8,128)(2,1)S(1)} %slice.20), channel_id=1, source_target_pairs={{0,1},{1,0},{2,3},{3,2},{4,5},{5,4},{6,7},{7,6},{8,9},{9,8},{10,11... | collective-permute-start | bytes 4718600 | tf_op jit(solution)/shard_map/ppermute | solution.py:375
  119.7 25.8 %collective-permute-start.5 = (bf16[128,32,384]{2,1,0:T(8,128)(2,1)}, bf16[128,32,384]{2,1,0:T(8,128)(2,1)}, u32[]{:S(2)}, u32[]{:S(2)}) collective-permute-start(bf16[128,32,384]{2,1,0:T(8,128)(2,1)} %broadcast_select_fusion.5), channel_id=1, source_target_pairs={{0,4},{4,0},{8,12},{12,8},{1,5},{5,1},{9,13},{13,9},{2,6},{6,2},{1... | collective-permute-start | bytes 9437192 | tf_op jit(solution)/shard_map/ppermute | solution.py:330
  122.0 40.8 %collective-permute-start.7 = (bf16[128,32,384]{2,1,0:T(8,128)(2,1)}, bf16[128,32,384]{2,1,0:T(8,128)(2,1)}, u32[]{:S(2)}, u32[]{:S(2)}) collective-permute-start(bf16[128,32,384]{2,1,0:T(8,128)(2,1)} %bitcast.8.refs_5_.refs_6_.refs_7_.refs_8_.refs_9_), channel_id=1, source_target_pairs={{0,12},{2,14},{5,9},{7,11},{8,4},{10,6},{13,1},{15,3},{16,28},{18,... | collective-permute-start | bytes 9437192 | tf_op jit(solution)/shard_map/ppermute | solution.py:324
  128.3 34.6 %collective-permute-start.3 = (bf16[32,192,128]{2,1,0:T(8,128)(2,1)S(1)}, bf16[32,192,128]{2,1,0:T(8,128)(2,1)}, u32[]{:S(2)}, u32[]{:S(2)}) collective-permute-start(bf16[32,192,128]{2,1,0:T(8,128)(2,1)S(1)} %slice.21), channel_id=1, source_target_pairs={{0,1},{1,0},{2,3},{3,2},{4,5},{5,4},{6,7},{7,6},{8,9},{9,8},{10,11... | collective-permute-start | bytes 4718600 | tf_op jit(solution)/shard_map/ppermute | solution.py:375
  166.8 25.1 %collective-permute-start.8 = (bf16[128,32,384]{2,1,0:T(8,128)(2,1)}, bf16[128,32,384]{2,1,0:T(8,128)(2,1)S(1)}, u32[]{:S(2)}, u32[]{:S(2)}) collective-permute-start(bf16[128,32,384]{2,1,0:T(8,128)(2,1)} %broadcast_select_fusion.4), channel_id=1, source_target_pairs={{0,4},{4,0},{8,12},{12,8},{1,5},{5,1},{9,13},{13,9},{2,6},{6,2},{1... | collective-permute-start | bytes 9437192 | tf_op jit(solution)/shard_map/ppermute | solution.py:330
  166.8 48.0 %collective-permute-start.11 = (bf16[128,32,384]{2,1,0:T(8,128)(2,1)S(1)}, bf16[128,32,384]{2,1,0:T(8,128)(2,1)}, u32[]{:S(2)}, u32[]{:S(2)}) collective-permute-start(bf16[128,32,384]{2,1,0:T(8,128)(2,1)S(1)} %bitcast.84), channel_id=1, source_target_pairs={{0,12},{2,14},{5,9},{7,11},{8,4},{10,6},{13,1},{15,3},{16,28},{18,... | collective-permute-start | bytes 9437192 | tf_op jit(solution)/shard_map/ppermute | solution.py:324
  172.3 42.5 %collective-permute-start.6 = (bf16[32,192,128]{2,1,0:T(8,128)(2,1)S(1)}, bf16[32,192,128]{2,1,0:T(8,128)(2,1)}, u32[]{:S(2)}, u32[]{:S(2)}) collective-permute-start(bf16[32,192,128]{2,1,0:T(8,128)(2,1)S(1)} %slice.22), channel_id=1, source_target_pairs={{0,1},{1,0},{2,3},{3,2},{4,5},{5,4},{6,7},{7,6},{8,9},{9,8},{10,11... | collective-permute-start | bytes 4718600 | tf_op jit(solution)/shard_map/ppermute | solution.py:375
  172.4 39.2 %collective-permute-start.9 = (bf16[1,32,32,128]{3,2,1,0:T(8,128)(2,1)S(1)}, bf16[1,32,32,128]{3,2,1,0:T(8,128)(2,1)S(1)}, u32[]{:S(2)}, u32[]{:S(2)}) collective-permute-start(bf16[1,32,32,128]{3,2,1,0:T(8,128)(2,1)S(1)} %triangle.12), channel_id=1, source_target_pairs={{0,2},{1,3},{2,0},{3,1},{4,6},{5,7},{6,4},{7,5},{8,10},{9,11},{10,... | collective-permute-start | bytes 786440 | tf_op jit(solution)/shard_map/ppermute | solution.py:404
  217.3 26.1 %collective-permute-start.12 = (bf16[128,32,384]{2,1,0:T(8,128)(2,1)}, bf16[128,32,384]{2,1,0:T(8,128)(2,1)S(1)}, u32[]{:S(2)}, u32[]{:S(2)}) collective-permute-start(bf16[128,32,384]{2,1,0:T(8,128)(2,1)} %broadcast_select_fusion.3), channel_id=1, source_target_pairs={{0,4},{4,0},{8,12},{12,8},{1,5},{5,1},{9,13},{13,9},{2,6},{6,2},{1... | collective-permute-start | bytes 9437192 | tf_op jit(solution)/shard_map/ppermute | solution.py:330
  218.4 61.5 %collective-permute-start.13 = (bf16[128,32,384]{2,1,0:T(8,128)(2,1)}, bf16[128,32,384]{2,1,0:T(8,128)(2,1)S(1)}, u32[]{:S(2)}, u32[]{:S(2)}) collective-permute-start(bf16[128,32,384]{2,1,0:T(8,128)(2,1)} %bitcast.12.refs_13_.refs_14_.refs_15_), channel_id=1, source_target_pairs={{0,12},{2,14},{5,9},{7,11},{8,4},{10,6},{13,1},{15,3},{16,28},{18,... | collective-permute-start | bytes 9437192 | tf_op jit(solution)/shard_map/ppermute | solution.py:324
  225.7 54.1 %collective-permute-start.10 = (bf16[32,192,128]{2,1,0:T(8,128)(2,1)}, bf16[32,192,128]{2,1,0:T(8,128)(2,1)}, u32[]{:S(2)}, u32[]{:S(2)}) collective-permute-start(bf16[32,192,128]{2,1,0:T(8,128)(2,1)} %slice.23), channel_id=1, source_target_pairs={{0,1},{1,0},{2,3},{3,2},{4,5},{5,4},{6,7},{7,6},{8,9},{9,8},{10,11... | collective-permute-start | bytes 4718600 | tf_op jit(solution)/shard_map/ppermute | solution.py:375
  225.7 49.8 %collective-permute-start.14 = (bf16[3,32,32,128]{3,2,1,0:T(8,128)(2,1)S(1)}, bf16[3,32,32,128]{3,2,1,0:T(8,128)(2,1)S(1)}, u32[]{:S(2)}, u32[]{:S(2)}) collective-permute-start(bf16[3,32,32,128]{3,2,1,0:T(8,128)(2,1)S(1)} %triangle.13), channel_id=1, source_target_pairs={{0,2},{1,3},{2,0},{3,1},{4,6},{5,7},{6,4},{7,5},{8,10},{9,11},{10,... | collective-permute-start | bytes 2359304 | tf_op jit(solution)/shard_map/ppermute | solution.py:404
  285.1 22.4 %collective-permute-start.15 = (bf16[128,32,384]{2,1,0:T(8,128)(2,1)}, bf16[128,32,384]{2,1,0:T(8,128)(2,1)S(1)}, u32[]{:S(2)}, u32[]{:S(2)}) collective-permute-start(bf16[128,32,384]{2,1,0:T(8,128)(2,1)} %broadcast_select_fusion.2), channel_id=1, source_target_pairs={{0,4},{4,0},{8,12},{12,8},{1,5},{5,1},{9,13},{13,9},{2,6},{6,2},{1... | collective-permute-start | bytes 9437192 | tf_op jit(solution)/shard_map/ppermute | solution.py:330
  285.2 62.5 %collective-permute-start.16 = (bf16[128,32,384]{2,1,0:T(8,128)(2,1)}, bf16[128,32,384]{2,1,0:T(8,128)(2,1)S(1)}, u32[]{:S(2)}, u32[]{:S(2)}) collective-permute-start(bf16[128,32,384]{2,1,0:T(8,128)(2,1)} %bitcast.13.refs_17_.refs_18_), channel_id=1, source_target_pairs={{0,12},{2,14},{5,9},{7,11},{8,4},{10,6},{13,1},{15,3},{16,28},{18,... | collective-permute-start | bytes 9437192 | tf_op jit(solution)/shard_map/ppermute | solution.py:324
  287.7 59.0 %collective-permute-start.17 = (bf16[5,32,32,128]{3,2,1,0:T(8,128)(2,1)S(1)}, bf16[5,32,32,128]{3,2,1,0:T(8,128)(2,1)S(1)}, u32[]{:S(2)}, u32[]{:S(2)}) collective-permute-start(bf16[5,32,32,128]{3,2,1,0:T(8,128)(2,1)S(1)} %triangle.14), channel_id=1, source_target_pairs={{0,2},{1,3},{2,0},{3,1},{4,6},{5,7},{6,4},{7,5},{8,10},{9,11},{10,... | collective-permute-start | bytes 3932168 | tf_op jit(solution)/shard_map/ppermute | solution.py:404
  351.3 5.7 collective-permute-start.18
  351.4 82.4 %collective-permute-start.19 = (bf16[128,32,384]{2,1,0:T(8,128)(2,1)}, bf16[128,32,384]{2,1,0:T(8,128)(2,1)S(1)}, u32[]{:S(2)}, u32[]{:S(2)}) collective-permute-start(bf16[128,32,384]{2,1,0:T(8,128)(2,1)} %bitcast.14.refs_21_), channel_id=1, source_target_pairs={{0,12},{2,14},{5,9},{7,11},{8,4},{10,6},{13,1},{15,3},{16,28},{18,... | collective-permute-start | bytes 9437192 | tf_op jit(solution)/shard_map/ppermute | solution.py:324
  353.8 79.9 %collective-permute-start.20 = (bf16[7,32,32,128]{3,2,1,0:T(8,128)(2,1)S(1)}, bf16[7,32,32,128]{3,2,1,0:T(8,128)(2,1)}, u32[]{:S(2)}, u32[]{:S(2)}) collective-permute-start(bf16[7,32,32,128]{3,2,1,0:T(8,128)(2,1)S(1)} %triangle.15), channel_id=1, source_target_pairs={{0,2},{1,3},{2,0},{3,1},{4,6},{5,7},{6,4},{7,5},{8,10},{9,11},{10,... | collective-permute-start | bytes 5505032 | tf_op jit(solution)/shard_map/ppermute | solution.py:404
  439.0 45.8 %collective-permute-start.21 = (bf16[128,32,384]{2,1,0:T(8,128)(2,1)}, bf16[128,32,384]{2,1,0:T(8,128)(2,1)}, u32[]{:S(2)}, u32[]{:S(2)}) collective-permute-start(bf16[128,32,384]{2,1,0:T(8,128)(2,1)} %broadcast_select_fusion), channel_id=1, source_target_pairs={{0,4},{4,0},{8,12},{12,8},{1,5},{5,1},{9,13},{13,9},{2,6},{6,2},{1... | collective-permute-start | bytes 9437192 | tf_op jit(solution)/shard_map/ppermute | solution.py:330
  439.0 105.4 %collective-permute-start.22 = (bf16[9,32,32,128]{3,2,1,0:T(8,128)(2,1)}, bf16[9,32,32,128]{3,2,1,0:T(8,128)(2,1)}, u32[]{:S(2)}, u32[]{:S(2)}) collective-permute-start(bf16[9,32,32,128]{3,2,1,0:T(8,128)(2,1)} %triangle.16), channel_id=1, source_target_pairs={{0,2},{1,3},{2,0},{3,1},{4,6},{5,7},{6,4},{7,5},{8,10},{9,11},{10,... | collective-permute-start | bytes 7077896 | tf_op jit(solution)/shard_map/ppermute | solution.py:404
  544.3 126.0 %collective-permute-start.23 = (bf16[11,32,32,128]{3,2,1,0:T(8,128)(2,1)}, bf16[11,32,32,128]{3,2,1,0:T(8,128)(2,1)}, u32[]{:S(2)}, u32[]{:S(2)}) collective-permute-start(bf16[11,32,32,128]{3,2,1,0:T(8,128)(2,1)} %triangle.21), channel_id=1, source_target_pairs={{0,2},{1,3},{2,0},{3,1},{4,6},{5,7},{6,4},{7,5},{8,10},{9,11},{10,... | collective-permute-start | bytes 8650760 | tf_op jit(solution)/shard_map/ppermute | solution.py:404
  (24 other events, 448.0 us)

commit v5 on v4

--- a/solution.py
+++ b/solution.py
@@ -54,18 +54,20 @@
     eights, _, rows, depth = left_out.shape
     hidden = eights * 8
 
-    def one_row(i, carry):
-        values = jnp.concatenate([piece[i] for piece in pieces], axis=0)
+    def two_rows(n, carry):
+        values = jnp.concatenate([piece[2 * n + i] for i in range(2) for piece in pieces], axis=0)
         centred = contract(centre[...], values, 1, 1)
         variance = jnp.mean(centred * centred, axis=0, keepdims=True)
         normed = centred * lax.rsqrt(variance + EPS) * gain[...] + bias[...]
         projected = contract(weights[...], normed.astype(BF16), 1, 0)
         for first, held in ((0, left_rows), (2 * hidden, right_rows)):
             gate = projected[first : first + hidden]
-            held[i] = sigmoid(gate) * projected[first + hidden : first + 2 * hidden]
+            side = sigmoid(gate) * projected[first + hidden : first + 2 * hidden]
+            held[2 * n] = side[:, :depth]
+            held[2 * n + 1] = side[:, depth:]
         return carry
 
-    lax.fori_loop(0, rows, one_row, 0, unroll=4)
+    lax.fori_loop(0, rows // 2, two_rows, 0, unroll=2)
 
     def one_group(e, carry):
         at = pl.ds(pl.multiple_of(e * 8, 8), 8)
@@ -221,8 +223,8 @@
 
 
 def finish(own, sent, gate, t, chunks, share, weights, gain, bias, held):
-    rows = 16
     pieces, packed, count, lanes = own.shape
+    rows = count if count <= 32 else 16
     hidden, channels = weights.shape
     group = hidden // packed
     steps = count // rows
@@ -326,14 +328,16 @@
     def second_step(right, far, *waits):
         if not two_chips:
             return [a + b for a, b in zip(to_all_rows(right), to_all_rows(far))]
-        given = jnp.where(holder, right, after(far, *waits))
-        got = lax.ppermute(given, "row", [(r, r ^ 1) for r in range(n_row)])
-        return [[right, got, far]]
+        near, far = after(right, *waits), after(far, *waits)
+        cells = [(r, c, holds(r, c)) for r in range(n_row) for c in range(n_col)]
+        near_in = lax.ppermute(near, axes, [(place(r, c), place(r ^ 1, c)) for r, c, held in cells if held])
+        far_in = lax.ppermute(far, axes, [(place(r, c), place(r ^ 1, c)) for r, c, held in cells if not held])
+        return [[right, near_in, far, far_in]]
 
     def product(pairs, own):
         take_near = near_is_own if own else jnp.logical_not(near_is_own)
         if two_chips:
-            which = jnp.where(holder, 0, 1) + jnp.where(take_near, 0, 1)
+            which = jnp.where(take_near, jnp.where(holder, 0, 1), jnp.where(holder, 3, 2))
         else:
             which = jnp.where(take_near, 0, 1)
         used_left = sorted({i for i, _, _ in pairs})
@@ -345,7 +349,7 @@
             which.astype(jnp.int32).reshape(1),
         )
 
-    wide = lambda v: jnp.broadcast_to(v[:, None], (channels, half * tile_cols))
+    wide = lambda v: jnp.broadcast_to(v[:, None], (channels, 2 * half * tile_cols))
     gain_in, bias_in = wide(ln_gain), wide(ln_bias)
     shards = range(share)
     waves = []
@@ -371,7 +375,7 @@
         return left
 
     def exchange(n, *waits):
-        block = (after(pair_act, *waits) if waits else pair_act)[n * step : (n + 1) * step]
+        block = after(slabs[n], *waits) if waits else slabs[n]
         exchanged.append([lax.ppermute(block, "col", [(c, c ^ o) for c in range(n_col)]) for o in range(1, half)])
 
     def keep_own():
@@ -380,6 +384,12 @@
         own.append(product(waves[t], True))
         token[:] = own[-1:]
 
+    def slab(n, *waits):
+        return (after(pair_act, *waits) if waits else pair_act)[n * step : (n + 1) * step]
+
+    slabs = [slab(0)]
+    if chunks > 1:
+        slabs.append(slab(1, slabs[0]))
     exchange(0)
     token, moved, own = [], [], []
     for n in range(chunks + 2):
@@ -390,21 +400,27 @@
             fars.append(first_step(after(rights[n - 1], *waits)))
         if n >= 2:
             units.append(second_step(rights[n - 2], fars[n - 2], *waits))
+        if n + 2 < chunks:
+            slabs.append(slab(n + 2, *waits))
         if n < chunks:
-            token = [prepare(n, *token)]
+            token = [prepare(n, *token, *slabs[n + 2 : n + 3])]
         if n >= 2:
             t = n - 2
             if t == chunks - 1:
-                while len(own) < t - 1:
+                while len(own) < t:
                     keep_own()
             lefts[t] = after(lefts[t], *token)
             made = product(waves[t], False)
             token = [made]
             waits = moved[t - 1 : t]
             moved.append(lax.ppermute(after(made, *waits) if waits else made, "col", swap_half))
+            if t == chunks - 2:
+                while len(own) < t // 2:
+                    keep_own()
+                gate = gate_of(pair_act, centre, mean, after(ln_gain[None], *token), ln_bias[None], w_gate)
+                token = [gate]
     while len(own) < chunks:
         keep_own()
-    gate = gate_of(pair_act, centre, mean, after(ln_gain[None], *token), ln_bias[None], w_gate)
     out = None
     for t in range(chunks):
         out = finish(own[t], moved[t], gate, t, chunks, share, w_last, gain_out, bias_out, out)

time: 705 us -> 704 us (level)
  starting transfers between devices: 36.3 us -> 75.4 us
  Pallas kernels: 379 us -> 353 us
  other arithmetic: 22.8 us -> 0.02 us
  waiting for transfers between devices: 235 us -> 247 us
    ppermute x6 -> x12, starting transfers between devices: 3.73 us -> 27.8 us  [the longest x6 19.9 us: second_step(): lax.ppermute(near, axes, [(place(r, c), place(r ^ 1, c)) for r, c, held i...]
    select_n x6 -> x0, other arithmetic: 22.7 us -> none  [second_step(): given = jnp.where(holder, right, after(far, *waits))]
    pallas_call x6, Pallas kernels: 102 us -> 80.7 us  [project(): pl.pallas_call(functools.partial(project_kernel, len(pieces)), grid=(coun...]
    ppermute x6, starting transfers between devices: 21.2 us -> 37.9 us  [first_step(): return lax.ppermute(right, axes, pairs)]
    pallas_call x6, Pallas kernels: 77.2 us -> 61.3 us  [finish(): pl.pallas_call(functools.partial(finish_kernel, group, hidden), grid=(pie...]
    pallas_call x12, Pallas kernels: 174 us -> 185 us  [triangle(): pl.pallas_call(functools.partial(triangle_kernel, len(lefts), n_sides, gr...]
    ppermute x6, waiting for transfers between devices: 143 us -> 153 us  [on_device(): lax.ppermute(after(made, *waits) if waits else made, 'col', swap_half)]
  transfers between devices with their start and end apart: 24 -> 30, of which waited for: 13 -> 12; matrix products, arithmetic and copies ran while one was open for 1% -> 1% of each run, Pallas kernels for 51% -> 48%
where the time goes in v5:
time: 704 us; the launch traced here: 693 us
  Pallas kernels  353 us (50%)
  waiting for transfers between devices  247 us (35%)
  starting transfers between devices  75.4 us (11%)
  local copies, waits for them, and re-layouts  17.7 us (3%)
    pallas_call x12, Pallas kernels, triangle(): pl.pallas_call(functools.partial(triangle_kernel, len(lefts), n_sides, gr...  185 us
    ppermute x6, waiting for transfers between devices, on_device(): lax.ppermute(after(made, *waits) if waits else made, 'col', swap_half)  153 us
    ppermute x6, waiting for transfers between devices, exchange(): lax.ppermute(block, 'col', [(c, c ^ o) for c in range(n_col)])  93.5 us
    pallas_call x6, Pallas kernels, project(): pl.pallas_call(functools.partial(project_kernel, len(pieces)), grid=(coun...  80.7 us
    pallas_call x6, Pallas kernels, finish(): pl.pallas_call(functools.partial(finish_kernel, group, hidden), grid=(pie...  61.3 us
    ppermute x6, starting transfers between devices, first_step(): return lax.ppermute(right, axes, pairs)  37.9 us
    pallas_call x1, Pallas kernels, gate_of(): pl.pallas_call(gate_kernel, grid=(count // rows,), in_specs=[block] + [wh...  25.2 us
    ppermute x6, starting transfers between devices, second_step(): lax.ppermute(near, axes, [(place(r, c), place(r ^ 1, c)) for r, c, held i...  19.9 us
  transfers between devices with their start and end apart: 30, of which 12 were waited for; matrix products, arithmetic and copies ran while one was open for 1% of the time, Pallas kernels for 48%

profile of v5, /device:TPU:0, one launch (start us, length us, event | category | flops | bytes accessed | tf_op | source)
XLA Modules:
  0.0 693.5 jit_solution(9209407784212325470)
XLA Ops:
  6.2 32.9 %collective-permute-done.refs_1_ = bf16[32,192,128]{2,1,0:T(8,128)(2,1)S(1)} collective-permute-done((bf16[32,192,128]{2,1,0:T(8,128)(2,1)S(1)}, bf16[32,192,128]{2,1,0:T(8,128)(2,1)S(1)}, u32[]{:S(2)}, u32[]{:S(2)}) %collective-permute-start) | collective-permute-done | bytes 1572896 | tf_op jit(solution)/shard_map/ppermute | solution.py:379
  43.8 13.5 %project.6 = (bf16[16,8,32,384]{3,2,1,0:T(8,128)(2,1)}, bf16[16,8,32,384]{3,2,1,0:T(8,128)(2,1)}) custom-call(bf16[192,192,128]{2,1,0:T(8,128)(2,1)} %pair.1, bf16[32,192,128]{2,1,0:T(8,128)(2,1)} %copy-done.17, bf16[512,128]{1,0:T(8,128)(2,1)S(1)} %bitcast.21, bf16[128,128]{1,0:T(8,128)(2,1)S(1)} %add_convert_fusion.refs_3_.centre, ...), custom_call_target="tpu_custom_call" | custom-call | flops 2013265920 | bytes 6291456 | tf_op jit(solution)/shard_map/project/pallas_call | solution.py:98
  57.3 18.6 %collective-permute-done.1.refs_1_ = bf16[32,192,128]{2,1,0:T(8,128)(2,1)} collective-permute-done((bf16[32,192,128]{2,1,0:T(8,128)(2,1)S(1)}, bf16[32,192,128]{2,1,0:T(8,128)(2,1)}, u32[]{:S(2)}, u32[]{:S(2)}) %collective-permute-start.1) | collective-permute-done | bytes 1572896 | tf_op jit(solution)/shard_map/ppermute | solution.py:379
  80.4 13.5 %project.7 = (bf16[16,8,32,384]{3,2,1,0:T(8,128)(2,1)}, bf16[16,8,32,384]{3,2,1,0:T(8,128)(2,1)}) custom-call(bf16[192,192,128]{2,1,0:T(8,128)(2,1)} %pair.1, bf16[32,192,128]{2,1,0:T(8,128)(2,1)} %collective-permute-done.1.refs_1_, bf16[512,128]{1,0:T(8,128)(2,1)S(1)} %bitcast.22, bf16[128,128]{1,0:T(8,128)(2,1)S(1)} %add_convert_fusion.refs_3_.centre, ...), custom_call_target="tpu_custom_call" | custom-call | flops 2013265920 | bytes 6291456 | tf_op jit(solution)/shard_map/project/pallas_call | solution.py:98
  93.9 21.3 %collective-permute-done.2.refs_1_ = bf16[32,192,128]{2,1,0:T(8,128)(2,1)S(1)} collective-permute-done((bf16[32,192,128]{2,1,0:T(8,128)(2,1)S(1)}, bf16[32,192,128]{2,1,0:T(8,128)(2,1)S(1)}, u32[]{:S(2)}, u32[]{:S(2)}) %collective-permute-start.2) | collective-permute-done | bytes 1572896 | tf_op jit(solution)/shard_map/ppermute | solution.py:379
  129.8 13.4 %project.8 = (bf16[16,8,32,384]{3,2,1,0:T(8,128)(2,1)}, bf16[16,8,32,384]{3,2,1,0:T(8,128)(2,1)}) custom-call(bf16[192,192,128]{2,1,0:T(8,128)(2,1)} %pair.1, bf16[32,192,128]{2,1,0:T(8,128)(2,1)} %copy-done.15, bf16[512,128]{1,0:T(8,128)(2,1)S(1)} %bitcast.23, bf16[128,128]{1,0:T(8,128)(2,1)S(1)} %add_convert_fusion.refs_3_.centre, ...), custom_call_target="tpu_custom_call" | custom-call | flops 2013265920 | bytes 6291456 | tf_op jit(solution)/shard_map/project/pallas_call | solution.py:98
  177.8 13.5 %project.9 = (bf16[16,8,32,384]{3,2,1,0:T(8,128)(2,1)}, bf16[16,8,32,384]{3,2,1,0:T(8,128)(2,1)}) custom-call(bf16[192,192,128]{2,1,0:T(8,128)(2,1)} %pair.1, bf16[32,192,128]{2,1,0:T(8,128)(2,1)} %collective-permute-done.3.refs_1_, bf16[512,128]{1,0:T(8,128)(2,1)S(1)} %bitcast.24, bf16[128,128]{1,0:T(8,128)(2,1)S(1)} %add_convert_fusion.refs_3_.centre, ...), custom_call_target="tpu_custom_call" | custom-call | flops 2013265920 | bytes 6291456 | tf_op jit(solution)/shard_map/project/pallas_call | solution.py:98
  229.6 13.5 %project.10 = (bf16[16,8,32,384]{3,2,1,0:T(8,128)(2,1)}, bf16[16,8,32,384]{3,2,1,0:T(8,128)(2,1)}) custom-call(bf16[192,192,128]{2,1,0:T(8,128)(2,1)} %pair.1, bf16[32,192,128]{2,1,0:T(8,128)(2,1)} %copy-done.16, bf16[512,128]{1,0:T(8,128)(2,1)S(1)} %bitcast.25, bf16[128,128]{1,0:T(8,128)(2,1)S(1)} %add_convert_fusion.refs_3_.centre, ...), custom_call_target="tpu_custom_call" | custom-call | flops 2013265920 | bytes 6291456 | tf_op jit(solution)/shard_map/project/pallas_call | solution.py:98
  243.1 14.2 %triangle.14 = bf16[5,32,32,128]{3,2,1,0:T(8,128)(2,1)S(1)} custom-call(s32[1]{0:T(128)} %bitcast.5.which, bf16[128,32,384]{2,1,0:T(8,128)(2,1)} %bitcast.37, bf16[128,32,384]{2,1,0:T(8,128)(2,1)} %bitcast.48, bf16[128,32,384]{2,1,0:T(8,128)(2,1)} %bitcast.69, bf16[128,32,384]{2,1,0:T(8,128)(2,1)} %bitcast.6.refs_1_.refs_2_.refs_3_.refs_4_.refs_5_.refs_6_, ...), custom_call_target="tpu_custom_call" | custom-call | flops 503316480 | bytes 20185088 | tf_op jit(solution)/shard_map/triangle/pallas_call | solution.py:148
  257.3 21.0 %collective-permute-done.16.sent = bf16[3,32,32,128]{3,2,1,0:T(8,128)(2,1)S(1)} collective-permute-done((bf16[3,32,32,128]{3,2,1,0:T(8,128)(2,1)S(1)}, bf16[3,32,32,128]{3,2,1,0:T(8,128)(2,1)S(1)}, u32[]{:S(2)}, u32[]{:S(2)}) %collective-permute-start.16) | collective-permute-done | bytes 786464 | tf_op jit(solution)/shard_map/ppermute | solution.py:416
  309.0 16.7 %triangle.15 = bf16[7,32,32,128]{3,2,1,0:T(8,128)(2,1)S(1)} custom-call(s32[1]{0:T(128)} %bitcast.5.which, bf16[128,32,384]{2,1,0:T(8,128)(2,1)} %bitcast.38, bf16[128,32,384]{2,1,0:T(8,128)(2,1)} %bitcast.49, bf16[128,32,384]{2,1,0:T(8,128)(2,1)} %bitcast.70, bf16[128,32,384]{2,1,0:T(8,128)(2,1)} %bitcast.87, ...), custom_call_target="tpu_custom_call" | custom-call | flops 704643072 | bytes 27000832 | tf_op jit(solution)/shard_map/triangle/pallas_call | solution.py:148
  325.7 26.1 %collective-permute-done.20.sent = bf16[5,32,32,128]{3,2,1,0:T(8,128)(2,1)S(1)} collective-permute-done((bf16[5,32,32,128]{3,2,1,0:T(8,128)(2,1)S(1)}, bf16[5,32,32,128]{3,2,1,0:T(8,128)(2,1)S(1)}, u32[]{:S(2)}, u32[]{:S(2)}) %collective-permute-start.20) | collective-permute-done | bytes 1310752 | tf_op jit(solution)/shard_map/ppermute | solution.py:416
  363.1 20.5 %triangle.16 = bf16[9,32,32,128]{3,2,1,0:T(8,128)(2,1)} custom-call(s32[1]{0:T(128)} %bitcast.5.which, bf16[128,32,384]{2,1,0:T(8,128)(2,1)} %bitcast.39, bf16[128,32,384]{2,1,0:T(8,128)(2,1)} %bitcast.50, bf16[128,32,384]{2,1,0:T(8,128)(2,1)} %bitcast.71, bf16[128,32,384]{2,1,0:T(8,128)(2,1)} %bitcast.88, bf16[128,32,384]{2,1,0:T(8,128)(2,1)} %bitcast.101, ...), custom_call_target="tpu_custom_call" | custom-call | flops 905969664 | bytes 33816576 | tf_op jit(solution)/shard_map/triangle/pallas_call | solution.py:148
  401.8 25.2 %gate.1 = bf16[192,192,128]{2,1,0:T(8,128)(2,1)} custom-call(bf16[192,192,128]{2,1,0:T(8,128)(2,1)} %pair.1, bf16[128,128]{1,0:T(8,128)(2,1)S(1)} %add_convert_fusion.refs_3_.centre, bf16[256,128]{1,0:T(8,128)(2,1)S(1)} %broadcast_in_dim.29.mean, f32[1,128]{1,0:T(1,128)S(1)} %bitcast.33, f32[1,128]{1,0:T(1,128)S(1)} %bitcast.34, bf16[128,128]{1,0:T(8,128)(2,1)S(1)} %copy-done.6), custom_call_target="tpu_custom_call" | custom-call | flops 4831838208 | bytes 18874368 | tf_op jit(solution)/shard_map/gate/pallas_call | solution.py:186
  427.0 13.5 %collective-permute-done.24.sent = bf16[7,32,32,128]{3,2,1,0:T(8,128)(2,1)} collective-permute-done((bf16[7,32,32,128]{3,2,1,0:T(8,128)(2,1)S(1)}, bf16[7,32,32,128]{3,2,1,0:T(8,128)(2,1)}, u32[]{:S(2)}, u32[]{:S(2)}) %collective-permute-start.24) | collective-permute-done | bytes 1835040 | tf_op jit(solution)/shard_map/ppermute | solution.py:416
  444.2 14.1 %triangle.19.own = bf16[5,32,32,128]{3,2,1,0:T(8,128)(2,1)S(1)} custom-call(s32[1]{0:T(128)} %bitcast.which, bf16[128,32,384]{2,1,0:T(8,128)(2,1)} %bitcast.42, bf16[128,32,384]{2,1,0:T(8,128)(2,1)} %bitcast.52, bf16[128,32,384]{2,1,0:T(8,128)(2,1)} %bitcast.72, bf16[128,32,384]{2,1,0:T(8,128)(2,1)} %bitcast.6.refs_1_.refs_2_.refs_3_.refs_4_.refs_5_.refs_6_, ...), custom_call_target="tpu_custom_call" | custom-call | flops 503316480 | bytes 20185088 | tf_op jit(solution)/shard_map/triangle/pallas_call | solution.py:148
  458.3 16.8 %triangle.20.own = bf16[7,32,32,128]{3,2,1,0:T(8,128)(2,1)S(1)} custom-call(s32[1]{0:T(128)} %bitcast.which, bf16[128,32,384]{2,1,0:T(8,128)(2,1)} %bitcast.43, bf16[128,32,384]{2,1,0:T(8,128)(2,1)} %bitcast.53, bf16[128,32,384]{2,1,0:T(8,128)(2,1)} %bitcast.73, bf16[128,32,384]{2,1,0:T(8,128)(2,1)} %bitcast.89, ...), custom_call_target="tpu_custom_call" | custom-call | flops 704643072 | bytes 27000832 | tf_op jit(solution)/shard_map/triangle/pallas_call | solution.py:148
  475.0 20.5 %triangle.21.own = bf16[9,32,32,128]{3,2,1,0:T(8,128)(2,1)} custom-call(s32[1]{0:T(128)} %bitcast.which, bf16[128,32,384]{2,1,0:T(8,128)(2,1)} %bitcast.44, bf16[128,32,384]{2,1,0:T(8,128)(2,1)} %bitcast.54, bf16[128,32,384]{2,1,0:T(8,128)(2,1)} %bitcast.74, bf16[128,32,384]{2,1,0:T(8,128)(2,1)} %bitcast.90, bf16[128,32,384]{2,1,0:T(8,128)(2,1)} %bitcast.102, ...), custom_call_target="tpu_custom_call" | custom-call | flops 905969664 | bytes 33816576 | tf_op jit(solution)/shard_map/triangle/pallas_call | solution.py:148
  498.9 24.1 %triangle.22 = bf16[11,32,32,128]{3,2,1,0:T(8,128)(2,1)} custom-call(s32[1]{0:T(128)} %bitcast.5.which, bf16[128,32,384]{2,1,0:T(8,128)(2,1)} %bitcast.45, bf16[128,32,384]{2,1,0:T(8,128)(2,1)} %bitcast.55, bf16[128,32,384]{2,1,0:T(8,128)(2,1)} %bitcast.75, bf16[128,32,384]{2,1,0:T(8,128)(2,1)} %bitcast.91, bf16[128,32,384]{2,1,0:T(8,128)(2,1)} %bitcast.103, ...), custom_call_target="tpu_custom_call" | custom-call | flops 1107296256 | bytes 40632320 | tf_op jit(solution)/shard_map/triangle/pallas_call | solution.py:148
  523.0 26.2 %collective-permute-done.28.sent = bf16[9,32,32,128]{3,2,1,0:T(8,128)(2,1)S(1)} collective-permute-done((bf16[9,32,32,128]{3,2,1,0:T(8,128)(2,1)}, bf16[9,32,32,128]{3,2,1,0:T(8,128)(2,1)S(1)}, u32[]{:S(2)}, u32[]{:S(2)}) %collective-permute-start.28) | collective-permute-done | bytes 2359328 | tf_op jit(solution)/shard_map/ppermute | solution.py:416
  581.7 14.5 %finish.10.refs_0_ = bf16[192,192,128]{2,1,0:T(8,128)(2,1)} custom-call(bf16[9,32,32,128]{3,2,1,0:T(8,128)(2,1)} %triangle.21.own, bf16[9,32,32,128]{3,2,1,0:T(8,128)(2,1)} %copy-done.14, bf16[192,192,128]{2,1,0:T(8,128)(2,1)} %gate.1, bf16[128,128]{1,0:T(8,128)(2,1)S(1)} %bitcast.31, ...), custom_call_target="tpu_custom_call", output_to_operand_aliasing={{}: (6, {})} | custom-call | flops 301989888 | bytes 4718592 | tf_op jit(solution)/shard_map/finish/pallas_call | solution.py:244
  596.2 23.8 %triangle.23.own = bf16[11,32,32,128]{3,2,1,0:T(8,128)(2,1)} custom-call(s32[1]{0:T(128)} %bitcast.which, bf16[128,32,384]{2,1,0:T(8,128)(2,1)} %bitcast.46, bf16[128,32,384]{2,1,0:T(8,128)(2,1)} %bitcast.56, bf16[128,32,384]{2,1,0:T(8,128)(2,1)} %bitcast.76, bf16[128,32,384]{2,1,0:T(8,128)(2,1)} %bitcast.92, bf16[128,32,384]{2,1,0:T(8,128)(2,1)} %bitcast.104, ...), custom_call_target="tpu_custom_call" | custom-call | flops 1107296256 | bytes 40632320 | tf_op jit(solution)/shard_map/triangle/pallas_call | solution.py:148
  620.0 55.7 %collective-permute-done.29.sent = bf16[11,32,32,128]{3,2,1,0:T(8,128)(2,1)} collective-permute-done((bf16[11,32,32,128]{3,2,1,0:T(8,128)(2,1)}, bf16[11,32,32,128]{3,2,1,0:T(8,128)(2,1)}, u32[]{:S(2)}, u32[]{:S(2)}) %collective-permute-start.29) | collective-permute-done | bytes 2883616 | tf_op jit(solution)/shard_map/ppermute | solution.py:416
  675.7 17.3 %finish.11 = bf16[192,192,128]{2,1,0:T(8,128)(2,1)} custom-call(bf16[11,32,32,128]{3,2,1,0:T(8,128)(2,1)} %triangle.23.own, bf16[11,32,32,128]{3,2,1,0:T(8,128)(2,1)} %collective-permute-done.29.sent, bf16[192,192,128]{2,1,0:T(8,128)(2,1)} %gate.1, bf16[128,128]{1,0:T(8,128)(2,1)S(1)} %bitcast.32, ...), custom_call_target="tpu_custom_call", output_to_operand_aliasing={{}: (6, {})} | custom-call | flops 369098752 | bytes 5767168 | tf_op jit(solution)/shard_map/finish/pallas_call | solution.py:244
  (125 shorter events, 202.2 us)
Async XLA Ops:
  1.6 37.5 %collective-permute-start = (bf16[32,192,128]{2,1,0:T(8,128)(2,1)S(1)}, bf16[32,192,128]{2,1,0:T(8,128)(2,1)S(1)}, u32[]{:S(2)}, u32[]{:S(2)}) collective-permute-start(bf16[32,192,128]{2,1,0:T(8,128)(2,1)S(1)} %slice.18), channel_id=1, source_target_pairs={{0,1},{1,0},{2,3},{3,2},{4,5},{5,4},{6,7},{7,6},{8,9},{9,8},{10,11... | collective-permute-start | bytes 4718600 | tf_op jit(solution)/shard_map/ppermute | solution.py:379
  40.2 35.7 %collective-permute-start.1 = (bf16[32,192,128]{2,1,0:T(8,128)(2,1)S(1)}, bf16[32,192,128]{2,1,0:T(8,128)(2,1)}, u32[]{:S(2)}, u32[]{:S(2)}) collective-permute-start(bf16[32,192,128]{2,1,0:T(8,128)(2,1)S(1)} %slice.20), channel_id=1, source_target_pairs={{0,1},{1,0},{2,3},{3,2},{4,5},{5,4},{6,7},{7,6},{8,9},{9,8},{10,11... | collective-permute-start | bytes 4718600 | tf_op jit(solution)/shard_map/ppermute | solution.py:379
  75.9 43.6 %collective-permute-start.5 = (bf16[128,32,384]{2,1,0:T(8,128)(2,1)}, bf16[128,32,384]{2,1,0:T(8,128)(2,1)}, u32[]{:S(2)}, u32[]{:S(2)}) collective-permute-start(bf16[128,32,384]{2,1,0:T(8,128)(2,1)} %bitcast.6.refs_1_.refs_2_.refs_3_.refs_4_.refs_5_.refs_6_), channel_id=1, source_target_pairs={{0,12},{2,14},{5,9},{7,11},{8,4},{10,6},{13,1},{15,3},{16,28},{18,... | collective-permute-start | bytes 9437192 | tf_op jit(solution)/shard_map/ppermute | solution.py:326
  78.9 36.3 %collective-permute-start.2 = (bf16[32,192,128]{2,1,0:T(8,128)(2,1)S(1)}, bf16[32,192,128]{2,1,0:T(8,128)(2,1)S(1)}, u32[]{:S(2)}, u32[]{:S(2)}) collective-permute-start(bf16[32,192,128]{2,1,0:T(8,128)(2,1)S(1)} %slice.19), channel_id=1, source_target_pairs={{0,1},{1,0},{2,3},{3,2},{4,5},{5,4},{6,7},{7,6},{8,9},{9,8},{10,11... | collective-permute-start | bytes 4718600 | tf_op jit(solution)/shard_map/ppermute | solution.py:379
  115.2 28.0 %collective-permute-start.4 = (bf16[128,32,384]{2,1,0:T(8,128)(2,1)}, bf16[128,32,384]{2,1,0:T(8,128)(2,1)}, u32[]{:S(2)}, u32[]{:S(2)}) collective-permute-start(bf16[128,32,384]{2,1,0:T(8,128)(2,1)} %bitcast.6.refs_1_.refs_2_.refs_3_.refs_4_.refs_5_.refs_6_), channel_id=1, source_target_pairs={{0,4},{2,6},{5,1},{7,3},{8,12},{10,14},{13,9},{15,11},{16,20},{18,... | collective-permute-start | bytes 9437192 | tf_op jit(solution)/shard_map/ppermute | solution.py:333
  120.8 45.0 %collective-permute-start.9 = (bf16[128,32,384]{2,1,0:T(8,128)(2,1)}, bf16[128,32,384]{2,1,0:T(8,128)(2,1)}, u32[]{:S(2)}, u32[]{:S(2)}) collective-permute-start(bf16[128,32,384]{2,1,0:T(8,128)(2,1)} %bitcast.57), channel_id=1, source_target_pairs={{0,12},{2,14},{5,9},{7,11},{8,4},{10,6},{13,1},{15,3},{16,28},{18,... | collective-permute-start | bytes 9437192 | tf_op jit(solution)/shard_map/ppermute | solution.py:326
  128.3 34.6 %collective-permute-start.3 = (bf16[32,192,128]{2,1,0:T(8,128)(2,1)S(1)}, bf16[32,192,128]{2,1,0:T(8,128)(2,1)}, u32[]{:S(2)}, u32[]{:S(2)}) collective-permute-start(bf16[32,192,128]{2,1,0:T(8,128)(2,1)S(1)} %slice.21), channel_id=1, source_target_pairs={{0,1},{1,0},{2,3},{3,2},{4,5},{5,4},{6,7},{7,6},{8,9},{9,8},{10,11... | collective-permute-start | bytes 4718600 | tf_op jit(solution)/shard_map/ppermute | solution.py:379
  162.9 28.3 %collective-permute-start.8 = (bf16[128,32,384]{2,1,0:T(8,128)(2,1)S(1)}, bf16[128,32,384]{2,1,0:T(8,128)(2,1)}, u32[]{:S(2)}, u32[]{:S(2)}) collective-permute-start(bf16[128,32,384]{2,1,0:T(8,128)(2,1)S(1)} %bitcast.68), channel_id=1, source_target_pairs={{0,4},{2,6},{5,1},{7,3},{8,12},{10,14},{13,9},{15,11},{16,20},{18,... | collective-permute-start | bytes 9437192 | tf_op jit(solution)/shard_map/ppermute | solution.py:333
  167.1 52.7 %collective-permute-start.14 = (bf16[128,32,384]{2,1,0:T(8,128)(2,1)}, bf16[128,32,384]{2,1,0:T(8,128)(2,1)}, u32[]{:S(2)}, u32[]{:S(2)}) collective-permute-start(bf16[128,32,384]{2,1,0:T(8,128)(2,1)} %bitcast.77), channel_id=1, source_target_pairs={{0,12},{2,14},{5,9},{7,11},{8,4},{10,6},{13,1},{15,3},{16,28},{18,... | collective-permute-start | bytes 9437192 | tf_op jit(solution)/shard_map/ppermute | solution.py:326
  173.4 42.7 %collective-permute-start.7 = (bf16[32,192,128]{2,1,0:T(8,128)(2,1)S(1)}, bf16[32,192,128]{2,1,0:T(8,128)(2,1)S(1)}, u32[]{:S(2)}, u32[]{:S(2)}) collective-permute-start(bf16[32,192,128]{2,1,0:T(8,128)(2,1)S(1)} %slice.22), channel_id=1, source_target_pairs={{0,1},{1,0},{2,3},{3,2},{4,5},{5,4},{6,7},{7,6},{8,9},{9,8},{10,11... | collective-permute-start | bytes 4718600 | tf_op jit(solution)/shard_map/ppermute | solution.py:379
  173.7 38.7 %collective-permute-start.11 = (bf16[1,32,32,128]{3,2,1,0:T(8,128)(2,1)S(1)}, bf16[1,32,32,128]{3,2,1,0:T(8,128)(2,1)S(1)}, u32[]{:S(2)}, u32[]{:S(2)}) collective-permute-start(bf16[1,32,32,128]{3,2,1,0:T(8,128)(2,1)S(1)} %triangle.12), channel_id=1, source_target_pairs={{0,2},{1,3},{2,0},{3,1},{4,6},{5,7},{6,4},{7,5},{8,10},{9,11},{10,... | collective-permute-start | bytes 786440 | tf_op jit(solution)/shard_map/ppermute | solution.py:416
  216.1 27.0 %collective-permute-start.13 = (bf16[128,32,384]{2,1,0:T(8,128)(2,1)S(1)}, bf16[128,32,384]{2,1,0:T(8,128)(2,1)}, u32[]{:S(2)}, u32[]{:S(2)}) collective-permute-start(bf16[128,32,384]{2,1,0:T(8,128)(2,1)S(1)} %bitcast.86), channel_id=1, source_target_pairs={{0,4},{2,6},{5,1},{7,3},{8,12},{10,14},{13,9},{15,11},{16,20},{18,... | collective-permute-start | bytes 9437192 | tf_op jit(solution)/shard_map/ppermute | solution.py:333
  221.1 65.4 %collective-permute-start.18 = (bf16[128,32,384]{2,1,0:T(8,128)(2,1)}, bf16[128,32,384]{2,1,0:T(8,128)(2,1)}, u32[]{:S(2)}, u32[]{:S(2)}) collective-permute-start(bf16[128,32,384]{2,1,0:T(8,128)(2,1)} %bitcast.93), channel_id=1, source_target_pairs={{0,12},{2,14},{5,9},{7,11},{8,4},{10,6},{13,1},{15,3},{16,28},{18,... | collective-permute-start | bytes 9437192 | tf_op jit(solution)/shard_map/ppermute | solution.py:326
  228.8 53.9 %collective-permute-start.12 = (bf16[32,192,128]{2,1,0:T(8,128)(2,1)S(1)}, bf16[32,192,128]{2,1,0:T(8,128)(2,1)}, u32[]{:S(2)}, u32[]{:S(2)}) collective-permute-start(bf16[32,192,128]{2,1,0:T(8,128)(2,1)S(1)} %slice.23), channel_id=1, source_target_pairs={{0,1},{1,0},{2,3},{3,2},{4,5},{5,4},{6,7},{7,6},{8,9},{9,8},{10,11... | collective-permute-start | bytes 4718600 | tf_op jit(solution)/shard_map/ppermute | solution.py:379
  228.8 49.5 %collective-permute-start.16 = (bf16[3,32,32,128]{3,2,1,0:T(8,128)(2,1)S(1)}, bf16[3,32,32,128]{3,2,1,0:T(8,128)(2,1)S(1)}, u32[]{:S(2)}, u32[]{:S(2)}) collective-permute-start(bf16[3,32,32,128]{3,2,1,0:T(8,128)(2,1)S(1)} %triangle.13), channel_id=1, source_target_pairs={{0,2},{1,3},{2,0},{3,1},{4,6},{5,7},{6,4},{7,5},{8,10},{9,11},{10,... | collective-permute-start | bytes 2359304 | tf_op jit(solution)/shard_map/ppermute | solution.py:416
  282.7 26.2 %collective-permute-start.17 = (bf16[128,32,384]{2,1,0:T(8,128)(2,1)S(1)}, bf16[128,32,384]{2,1,0:T(8,128)(2,1)}, u32[]{:S(2)}, u32[]{:S(2)}) collective-permute-start(bf16[128,32,384]{2,1,0:T(8,128)(2,1)S(1)} %bitcast.100), channel_id=1, source_target_pairs={{0,4},{2,6},{5,1},{7,3},{8,12},{10,14},{13,9},{15,11},{16,20},{18,... | collective-permute-start | bytes 9437192 | tf_op jit(solution)/shard_map/ppermute | solution.py:333
  287.8 67.2 %collective-permute-start.22 = (bf16[128,32,384]{2,1,0:T(8,128)(2,1)}, bf16[128,32,384]{2,1,0:T(8,128)(2,1)}, u32[]{:S(2)}, u32[]{:S(2)}) collective-permute-start(bf16[128,32,384]{2,1,0:T(8,128)(2,1)} %bitcast.13.refs_21_.refs_22_), channel_id=1, source_target_pairs={{0,12},{2,14},{5,9},{7,11},{8,4},{10,6},{13,1},{15,3},{16,28},{18,... | collective-permute-start | bytes 9437192 | tf_op jit(solution)/shard_map/ppermute | solution.py:326
  294.4 57.4 %collective-permute-start.20 = (bf16[5,32,32,128]{3,2,1,0:T(8,128)(2,1)S(1)}, bf16[5,32,32,128]{3,2,1,0:T(8,128)(2,1)S(1)}, u32[]{:S(2)}, u32[]{:S(2)}) collective-permute-start(bf16[5,32,32,128]{3,2,1,0:T(8,128)(2,1)S(1)} %triangle.14), channel_id=1, source_target_pairs={{0,2},{1,3},{2,0},{3,1},{4,6},{5,7},{6,4},{7,5},{8,10},{9,11},{10,... | collective-permute-start | bytes 3932168 | tf_op jit(solution)/shard_map/ppermute | solution.py:416
  356.3 86.3 %collective-permute-start.26 = (bf16[128,32,384]{2,1,0:T(8,128)(2,1)}, bf16[128,32,384]{2,1,0:T(8,128)(2,1)}, u32[]{:S(2)}, u32[]{:S(2)}) collective-permute-start(bf16[128,32,384]{2,1,0:T(8,128)(2,1)} %bitcast.16.refs_26_), channel_id=1, source_target_pairs={{0,12},{2,14},{5,9},{7,11},{8,4},{10,6},{13,1},{15,3},{16,28},{18,... | collective-permute-start | bytes 9437192 | tf_op jit(solution)/shard_map/ppermute | solution.py:326
  363.1 77.4 %collective-permute-start.24 = (bf16[7,32,32,128]{3,2,1,0:T(8,128)(2,1)S(1)}, bf16[7,32,32,128]{3,2,1,0:T(8,128)(2,1)}, u32[]{:S(2)}, u32[]{:S(2)}) collective-permute-start(bf16[7,32,32,128]{3,2,1,0:T(8,128)(2,1)S(1)} %triangle.15), channel_id=1, source_target_pairs={{0,2},{1,3},{2,0},{3,1},{4,6},{5,7},{6,4},{7,5},{8,10},{9,11},{10,... | collective-permute-start | bytes 5505032 | tf_op jit(solution)/shard_map/ppermute | solution.py:416
  440.5 55.1 %collective-permute-start.25 = (bf16[128,32,384]{2,1,0:T(8,128)(2,1)}, bf16[128,32,384]{2,1,0:T(8,128)(2,1)S(1)}, u32[]{:S(2)}, u32[]{:S(2)}) collective-permute-start(bf16[128,32,384]{2,1,0:T(8,128)(2,1)} %bitcast.16.refs_26_), channel_id=1, source_target_pairs={{0,4},{2,6},{5,1},{7,3},{8,12},{10,14},{13,9},{15,11},{16,20},{18,... | collective-permute-start | bytes 9437192 | tf_op jit(solution)/shard_map/ppermute | solution.py:333
  442.6 53.0 %collective-permute-start.27 = (bf16[128,32,384]{2,1,0:T(8,128)(2,1)}, bf16[128,32,384]{2,1,0:T(8,128)(2,1)S(1)}, u32[]{:S(2)}, u32[]{:S(2)}) collective-permute-start(bf16[128,32,384]{2,1,0:T(8,128)(2,1)} %collective-permute-done.26.refs_28_), channel_id=1, source_target_pairs={{1,5},{3,7},{4,0},{6,2},{9,13},{11,15},{12,8},{14,10},{17,21},{19,... | collective-permute-start | bytes 9437192 | tf_op jit(solution)/shard_map/ppermute | solution.py:334
  444.1 105.0 %collective-permute-start.28 = (bf16[9,32,32,128]{3,2,1,0:T(8,128)(2,1)}, bf16[9,32,32,128]{3,2,1,0:T(8,128)(2,1)S(1)}, u32[]{:S(2)}, u32[]{:S(2)}) collective-permute-start(bf16[9,32,32,128]{3,2,1,0:T(8,128)(2,1)} %triangle.16), channel_id=1, source_target_pairs={{0,2},{1,3},{2,0},{3,1},{4,6},{5,7},{6,4},{7,5},{8,10},{9,11},{10,... | collective-permute-start | bytes 7077896 | tf_op jit(solution)/shard_map/ppermute | solution.py:416
  549.2 126.5 %collective-permute-start.29 = (bf16[11,32,32,128]{3,2,1,0:T(8,128)(2,1)}, bf16[11,32,32,128]{3,2,1,0:T(8,128)(2,1)}, u32[]{:S(2)}, u32[]{:S(2)}) collective-permute-start(bf16[11,32,32,128]{3,2,1,0:T(8,128)(2,1)} %triangle.22), channel_id=1, source_target_pairs={{0,2},{1,3},{2,0},{3,1},{4,6},{5,7},{6,4},{7,5},{8,10},{9,11},{10,... | collective-permute-start | bytes 8650760 | tf_op jit(solution)/shard_map/ppermute | solution.py:416
  (29 other events, 607.7 us)

commit v6 on v4

--- a/solution.py
+++ b/solution.py
@@ -46,67 +46,75 @@
     return arrays
 
 
-def project_kernel(n_pieces, *refs):
-    pieces, (weights, centre, gain, bias, left_out, right_out, left_rows, right_rows) = (
-        refs[:n_pieces],
-        refs[n_pieces:],
-    )
-    eights, _, rows, depth = left_out.shape
+def project_kernel(n_pieces, n_slabs, which, *refs):
+    pieces = refs[: n_pieces * n_slabs]
+    weights, centre, gain, bias, out, held = refs[n_pieces * n_slabs :]
+    eights, _, rows, depth = out.shape
     hidden = eights * 8
 
-    def one_row(i, carry):
-        values = jnp.concatenate([piece[i] for piece in pieces], axis=0)
-        centred = contract(centre[...], values, 1, 1)
-        variance = jnp.mean(centred * centred, axis=0, keepdims=True)
-        normed = centred * lax.rsqrt(variance + EPS) * gain[...] + bias[...]
-        projected = contract(weights[...], normed.astype(BF16), 1, 0)
-        for first, held in ((0, left_rows), (2 * hidden, right_rows)):
-            gate = projected[first : first + hidden]
-            held[i] = sigmoid(gate) * projected[first + hidden : first + 2 * hidden]
-        return carry
-
-    lax.fori_loop(0, rows, one_row, 0, unroll=4)
+    def go(first):
+        def two_rows(n, carry):
+            values = jnp.concatenate(
+                [piece[2 * n + i] for i in range(2) for piece in pieces[first : first + n_pieces]], axis=0
+            )
+            centred = contract(centre[...], values, 1, 1)
+            variance = jnp.mean(centred * centred, axis=0, keepdims=True)
+            normed = centred * lax.rsqrt(variance + EPS) * gain[...] + bias[...]
+            projected = contract(weights[...], normed.astype(BF16), 1, 0)
+            side = sigmoid(projected[:hidden]) * projected[hidden:]
+            held[2 * n] = side[:, :depth]
+            held[2 * n + 1] = side[:, depth:]
+            return carry
+
+        lax.fori_loop(0, rows // 2, two_rows, 0, unroll=2)
+
+    for n in range(n_slabs):
+        pl.when(which[0] == n)(functools.partial(go, n * n_pieces))
 
     def one_group(e, carry):
         at = pl.ds(pl.multiple_of(e * 8, 8), 8)
-        for held, out in ((left_rows, left_out), (right_rows, right_out)):
-            for n in range(depth // 128):
-                lanes = slice(n * 128, (n + 1) * 128)
-                halves = [
-                    swap_eight([held[first + i, at, lanes][None] for i in range(8)]) for first in range(0, rows, 8)
-                ]
-                for h in range(8):
-                    out[e, h, :, lanes] = jnp.concatenate([half[h][0] for half in halves], axis=0).astype(BF16)
+        for n in range(depth // 128):
+            lanes = slice(n * 128, (n + 1) * 128)
+            halves = [
+                swap_eight([held[first + i, at, lanes][None] for i in range(8)]) for first in range(0, rows, 8)
+            ]
+            for h in range(8):
+                out[e, h, :, lanes] = jnp.concatenate([half[h][0] for half in halves], axis=0).astype(BF16)
         return carry
 
     lax.fori_loop(0, eights, one_group, 0, unroll=2)
 
 
-def project(pieces, firsts, count, weights, centre, gain, bias):
+def project(slabs, which, n_pieces, weights, centre, gain, bias):
     rows = 16
-    hidden = weights.shape[0] // 4
-    channels = weights.shape[1]
-    depth = sum(piece.shape[1] for piece in pieces)
-    whole = lambda x: pl.BlockSpec(x.shape, lambda i: (0,) * x.ndim)
-    in_specs = [
-        pl.BlockSpec((rows, piece.shape[1], channels), functools.partial(lambda f, i: (i + f, 0, 0), first // rows))
-        for piece, first in zip(pieces, firsts)
-    ] + [whole(x) for x in (weights, centre, gain, bias)]
+    hidden, channels = weights.shape[0] // 2, weights.shape[1]
+    count, columns = slabs[0].shape[0] // n_pieces, slabs[0].shape[1]
+    depth = n_pieces * columns
+    steps = count // rows
+    whole = lambda x: pl.BlockSpec(x.shape, lambda i, which: (0,) * x.ndim)
+
+    def piece_spec(n, p):
+        return pl.BlockSpec(
+            (rows, columns, channels), lambda i, which: (p * steps + jnp.where(which[0] == n, i, 0), 0, 0)
+        )
+
     shape = jax.ShapeDtypeStruct((hidden // 8, 8, count, depth), BF16)
-    left, right = pl.pallas_call(
-        functools.partial(project_kernel, len(pieces)),
-        grid=(count // rows,),
-        in_specs=in_specs,
-        out_specs=[pl.BlockSpec((hidden // 8, 8, rows, depth), lambda i: (0, 0, i, 0))] * 2,
-        out_shape=[shape, shape],
-        scratch_shapes=[pltpu.VMEM((rows, hidden, depth), F32)] * 2,
+    side = pl.pallas_call(
+        functools.partial(project_kernel, n_pieces, len(slabs)),
+        grid_spec=pltpu.PrefetchScalarGridSpec(
+            num_scalar_prefetch=1,
+            grid=(steps,),
+            in_specs=[piece_spec(n, p) for n in range(len(slabs)) for p in range(n_pieces)]
+            + [whole(x) for x in (weights, centre, gain, bias)],
+            out_specs=pl.BlockSpec((hidden // 8, 8, rows, depth), lambda i, which: (0, 0, i, 0)),
+            scratch_shapes=[pltpu.VMEM((rows, hidden, depth), F32)],
+        ),
+        out_shape=shape,
         compiler_params=PARAMS,
-        cost_estimate=at_least(
-            count * depth * channels * (channels + 4 * hidden), 2 * count * depth * hidden, shape, shape
-        ),
+        cost_estimate=at_least(count * depth * channels * (channels + 2 * hidden), count * depth * hidden, shape),
         name="project",
-    )(*pieces, weights, centre, gain, bias)
-    return left.reshape(hidden, count, depth), right.reshape(hidden, count, depth)
+    )(which, *[slab for slab in slabs for _ in range(n_pieces)], weights, centre, gain, bias)
+    return side.reshape(hidden, count, depth)
 
 
 def triangle_kernel(n_left, n_sides, group, pairs, which, *refs):
@@ -221,8 +229,8 @@
 
 
 def finish(own, sent, gate, t, chunks, share, weights, gain, bias, held):
-    rows = 16
     pieces, packed, count, lanes = own.shape
+    rows = count if count <= 32 else 16
     hidden, channels = weights.shape
     group = hidden // packed
     steps = count // rows
@@ -274,7 +282,7 @@
     group = group_of(step)
     packed = hidden // group
 
-    w_sides = w_proj.T
+    w_left, w_right = w_proj.T[: 2 * hidden], w_proj.T[2 * hidden :]
     centre = (jnp.eye(channels, dtype=F32) - 1.0 / channels).astype(BF16)
     mean = jnp.full((2 * channels, channels), 1.0 / channels, BF16)
     by_hidden = lambda v: jnp.repeat(v.reshape(packed, group), step, axis=1)[:, None, :]
@@ -315,37 +323,34 @@
     swap_half = [(c, c ^ half) for c in range(n_col)]
     two_chips = share == 1 and top == 2
     holder = ((row ^ col) & 1) == 0
-    lefts, rights, fars, units = [], [], [], []
-
-    def first_step(right):
+    number = lambda x: jnp.asarray(x, jnp.int32).reshape(1)
+    slabs, firsts, lefts, units = [], [], [], []
+
+    def first_step(slab):
         if not two_chips:
-            return across_top(right)
+            return across_top(slab)
         pairs = [(place(r, c), place(r ^ top ^ 1, c)) for r in range(n_row) for c in range(n_col) if holds(r, c)]
-        return lax.ppermute(right, axes, pairs)
-
-    def second_step(right, far, *waits):
+        return lax.ppermute(slab, axes, pairs)
+
+    def second_step(slab, far, *waits):
         if not two_chips:
-            return [a + b for a, b in zip(to_all_rows(right), to_all_rows(far))]
-        given = jnp.where(holder, right, after(far, *waits))
+            return [[(x, 0 if len(x) == 1 else (row ^ col) & 1) for x in to_all_rows(held)] for held in (slab, far)]
+        given = jnp.where(holder, slab, after(far, *waits))
         got = lax.ppermute(given, "row", [(r, r ^ 1) for r in range(n_row)])
-        return [[right, got, far]]
+        return [[([slab, got], jnp.where(holder, 0, 1))], [([got, far], jnp.where(holder, 0, 1))]]
 
     def product(pairs, own):
         take_near = near_is_own if own else jnp.logical_not(near_is_own)
-        if two_chips:
-            which = jnp.where(holder, 0, 1) + jnp.where(take_near, 0, 1)
-        else:
-            which = jnp.where(take_near, 0, 1)
         used_left = sorted({i for i, _, _ in pairs})
         used_right = sorted({(j, s) for _, j, s in pairs})
         return triangle(
             [lefts[i] for i in used_left],
             [units[j][s] for j, s in used_right],
             [(used_left.index(i), used_right.index((j, s))) for i, j, s in pairs],
-            which.astype(jnp.int32).reshape(1),
+            number(jnp.where(take_near, 0, 1)),
         )
 
-    wide = lambda v: jnp.broadcast_to(v[:, None], (channels, half * tile_cols))
+    wide = lambda v: jnp.broadcast_to(v[:, None], (channels, 2 * half * tile_cols))
     gain_in, bias_in = wide(ln_gain), wide(ln_bias)
     shards = range(share)
     waves = []
@@ -354,25 +359,7 @@
         by_row = [(t, j, s) for j in range(t + 1) for s in shards]
         waves.append(by_column + by_row)
 
-    exchanged = []
-
-    def prepare(t, *held):
-        left, right = project(
-            [pair_act] + exchanged[t],
-            [t * step] + [0] * (half - 1),
-            step,
-            w_sides,
-            centre,
-            after(gain_in, *held) if held else gain_in,
-            bias_in,
-        )
-        lefts.append(left)
-        rights.append(right)
-        return left
-
-    def exchange(n, *waits):
-        block = (after(pair_act, *waits) if waits else pair_act)[n * step : (n + 1) * step]
-        exchanged.append([lax.ppermute(block, "col", [(c, c ^ o) for c in range(n_col)]) for o in range(1, half)])
+    token, moved, own, exchanged = [], [], [], []
 
     def keep_own():
         t = len(own)
@@ -380,31 +367,48 @@
         own.append(product(waves[t], True))
         token[:] = own[-1:]
 
+    def exchange(n, *waits):
+        block = (after(pair_act, *waits) if waits else pair_act)[n * step : (n + 1) * step]
+        exchanged.append([lax.ppermute(block, "col", [(c, c ^ o) for c in range(n_col)]) for o in range(1, half)])
+
+    def side(candidates, choice, weights):
+        made = project(candidates, number(choice), half, weights, centre, after(gain_in, *token), bias_in)
+        token[:] = [made]
+        return made
+
     exchange(0)
-    token, moved, own = [], [], []
-    for n in range(chunks + 2):
-        waits = token + (exchanged[n][-1:] if n < chunks else []) + (moved[n - 4 : n - 3] if n >= 4 else [])
+    gate = gate_of(pair_act, centre, mean, ln_gain[None], ln_bias[None], w_gate)
+    token[:] = [gate]
+    for n in range(chunks + 1):
+        waits = (token if n else []) + (exchanged[n][-1:] if n < chunks else [])
+        waits = waits + (moved[n - 3 : n - 2] if n >= 3 else [])
         if n + 1 < chunks:
             exchange(n + 1, *waits)
-        if 0 < n <= chunks:
-            fars.append(first_step(after(rights[n - 1], *waits)))
-        if n >= 2:
-            units.append(second_step(rights[n - 2], fars[n - 2], *waits))
         if n < chunks:
-            token = [prepare(n, *token)]
-        if n >= 2:
-            t = n - 2
-            if t == chunks - 1:
-                while len(own) < t - 1:
-                    keep_own()
-            lefts[t] = after(lefts[t], *token)
-            made = product(waves[t], False)
-            token = [made]
-            waits = moved[t - 1 : t]
-            moved.append(lax.ppermute(after(made, *waits) if waits else made, "col", swap_half))
+            block = after(pair_act, *waits)[n * step : (n + 1) * step]
+            slabs.append(jnp.concatenate([block] + exchanged[n], axis=0))
+            firsts.append(first_step(slabs[n]))
+        if n == 0:
+            continue
+        t = n - 1
+        near, far = second_step(slabs[t], firsts[t], *waits)
+        lefts.append(side([slabs[t]], 0, w_left))
+        units.append([])
+        for s in shards:
+            units[t].append([side(candidates, choice, w_right) for candidates, choice in (near[s], far[s])])
+        if t == chunks - 1:
+            while len(own) < t:
+                keep_own()
+        lefts[t] = after(lefts[t], *token)
+        made = product(waves[t], False)
+        token[:] = [made]
+        waits = moved[t - 1 : t]
+        moved.append(lax.ppermute(after(made, *waits) if waits else made, "col", swap_half))
+        if t == chunks - 2:
+            while len(own) < t // 2:
+                keep_own()
     while len(own) < chunks:
         keep_own()
-    gate = gate_of(pair_act, centre, mean, after(ln_gain[None], *token), ln_bias[None], w_gate)
     out = None
     for t in range(chunks):
         out = finish(own[t], moved[t], gate, t, chunks, share, w_last, gain_out, bias_out, out)

time: 705 us -> 707 us (level)
  waiting for transfers between devices: 235 us -> 139 us
  Pallas kernels: 379 us -> 449 us
  starting transfers between devices: 36.3 us -> 56.1 us
  other arithmetic: 22.8 us -> 29.9 us
    pallas_call x6 -> x18, Pallas kernels: 102 us -> 197 us  [project(): pl.pallas_call(functools.partial(project_kernel, n_pieces, len(slabs)), g...]
    ppermute x6, waiting for transfers between devices: 143 us -> 88.6 us  [on_device(): lax.ppermute(after(made, *waits) if waits else made, 'col', swap_half)]
    ppermute x6, waiting for transfers between devices: 88.7 us -> 50.6 us  [exchange(): lax.ppermute(block, 'col', [(c, c ^ o) for c in range(n_col)])]
    pallas_call x6, Pallas kernels: 77.2 us -> 61.3 us  [finish(): pl.pallas_call(functools.partial(finish_kernel, group, hidden), grid=(pie...]
    ppermute x6, starting transfers between devices: 21.2 us -> 36 us  [first_step(): return lax.ppermute(slab, axes, pairs)]
    concatenate x0 -> x6, other arithmetic: none -> 13.3 us  [on_device(): slabs.append(jnp.concatenate([block] + exchanged[n], axis=0))]
    pallas_call x12, Pallas kernels: 174 us -> 166 us  [triangle(): pl.pallas_call(functools.partial(triangle_kernel, len(lefts), n_sides, gr...]
  transfers between devices with their start and end apart: 24 -> 24, of which waited for: 13 -> 9; matrix products, arithmetic and copies ran while one was open for 1% -> 4% of each run, Pallas kernels for 51% -> 62%
where the time goes in v6:
time: 707 us; the launch traced here: 699 us
  Pallas kernels  449 us (64%)
  waiting for transfers between devices  139 us (20%)
  starting transfers between devices  56.1 us (8%)
  other arithmetic  29.9 us (4%)
  local copies, waits for them, and re-layouts  24.1 us (3%)
    pallas_call x18, Pallas kernels, project(): pl.pallas_call(functools.partial(project_kernel, n_pieces, len(slabs)), g...  197 us
    pallas_call x12, Pallas kernels, triangle(): pl.pallas_call(functools.partial(triangle_kernel, len(lefts), n_sides, gr...  166 us
    ppermute x6, waiting for transfers between devices, on_device(): lax.ppermute(after(made, *waits) if waits else made, 'col', swap_half)  88.6 us
    pallas_call x6, Pallas kernels, finish(): pl.pallas_call(functools.partial(finish_kernel, group, hidden), grid=(pie...  61.3 us
    ppermute x6, waiting for transfers between devices, exchange(): lax.ppermute(block, 'col', [(c, c ^ o) for c in range(n_col)])  50.6 us
    ppermute x6, starting transfers between devices, first_step(): return lax.ppermute(slab, axes, pairs)  36 us
    pallas_call x1, Pallas kernels, gate_of(): pl.pallas_call(gate_kernel, grid=(count // rows,), in_specs=[block] + [wh...  25.3 us
    slice x6, local copies, waits for them, and re-layouts, exchange(): (after(pair_act, *waits) if waits else pair_act)[n * step:(n + 1) * step]  17.2 us
  transfers between devices with their start and end apart: 24, of which 9 were waited for; matrix products, arithmetic and copies ran while one was open for 4% of the time, Pallas kernels for 62%

profile of v6, /device:TPU:0, one launch (start us, length us, event | category | flops | bytes accessed | tf_op | source)
XLA Modules:
  0.0 699.2 jit_solution(7550017730548828864)
XLA Ops:
  4.6 34.4 %collective-permute-done = bf16[32,192,128]{2,1,0:T(8,128)(2,1)S(1)} collective-permute-done((bf16[32,192,128]{2,1,0:T(8,128)(2,1)S(1)}, bf16[32,192,128]{2,1,0:T(8,128)(2,1)S(1)}, u32[]{:S(2)}, u32[]{:S(2)}) %collective-permute-start) | collective-permute-done | bytes 1572896 | tf_op jit(solution)/shard_map/ppermute | solution.py:372
  48.8 25.3 %gate.1 = bf16[192,192,128]{2,1,0:T(8,128)(2,1)} custom-call(bf16[192,192,128]{2,1,0:T(8,128)(2,1)} %pair.1, bf16[128,128]{1,0:T(8,128)(2,1)S(1)} %add_convert_fusion.centre.refs_3_.refs_5_, bf16[256,128]{1,0:T(8,128)(2,1)S(1)} %broadcast_in_dim.28.mean, f32[1,128]{1,0:T(1,128)S(1)} %bitcast.34, f32[1,128]{1,0:T(1,128)S(1)} %bitcast.35, ...), custom_call_target="tpu_custom_call" | custom-call | flops 4831838208 | bytes 18874368 | tf_op jit(solution)/shard_map/gate/pallas_call | solution.py:192
  74.1 11.9 %collective-permute-done.2 = bf16[32,192,128]{2,1,0:T(8,128)(2,1)} collective-permute-done((bf16[32,192,128]{2,1,0:T(8,128)(2,1)}, bf16[32,192,128]{2,1,0:T(8,128)(2,1)}, u32[]{:S(2)}, u32[]{:S(2)}) %collective-permute-start.2) | collective-permute-done | bytes 1572896 | tf_op jit(solution)/shard_map/ppermute | solution.py:372
  122.9 11.1 %project.20 = bf16[16,8,32,384]{3,2,1,0:T(8,128)(2,1)} custom-call(s32[1]{0:T(128)} %bitcast.5.which, bf16[64,192,128]{2,1,0:T(8,128)(2,1)} %collective-permute-done.3.refs_2_.refs_3_.refs_0_.refs_1_, bf16[64,192,128]{2,1,0:T(8,128)(2,1)} %collective-permute-done.3.refs_2_.refs_3_.refs_0_.refs_1_, ...), custom_call_target="tpu_custom_call" | custom-call | flops 1207959552 | bytes 3145728 | tf_op jit(solution)/shard_map/project/pallas_call | solution.py:102
  165.9 11.1 %project.22 = bf16[16,8,32,384]{3,2,1,0:T(8,128)(2,1)} custom-call(s32[1]{0:T(128)} %bitcast.5.which, bf16[64,192,128]{2,1,0:T(8,128)(2,1)} %pad_maximum_fusion.1.refs_0_.refs_1_, bf16[64,192,128]{2,1,0:T(8,128)(2,1)} %pad_maximum_fusion.1.refs_0_.refs_1_, bf16[64,192,128]{2,1,0:T(8,128)(2,1)} %collective-permute-done.6.refs_2_.refs_3_.refs_0_.refs_1_, ...), custom_call_target="tpu_custom_call" | custom-call | flops 1207959552 | bytes 3145728 | tf_op jit(solution)/shard_map/project/pallas_call | solution.py:102
  177.1 11.1 %project.23 = bf16[16,8,32,384]{3,2,1,0:T(8,128)(2,1)} custom-call(s32[1]{0:T(128)} %bitcast.5.which, bf16[64,192,128]{2,1,0:T(8,128)(2,1)} %collective-permute-done.6.refs_2_.refs_3_.refs_0_.refs_1_, bf16[64,192,128]{2,1,0:T(8,128)(2,1)} %collective-permute-done.6.refs_2_.refs_3_.refs_0_.refs_1_, ...), custom_call_target="tpu_custom_call" | custom-call | flops 1207959552 | bytes 3145728 | tf_op jit(solution)/shard_map/project/pallas_call | solution.py:102
  233.8 11.1 %project.26 = bf16[16,8,32,384]{3,2,1,0:T(8,128)(2,1)} custom-call(s32[1]{0:T(128)} %bitcast.5.which, bf16[64,192,128]{2,1,0:T(8,128)(2,1)} %collective-permute-done.10.refs_2_.refs_3_.refs_0_.refs_1_, bf16[64,192,128]{2,1,0:T(8,128)(2,1)} %collective-permute-done.10.refs_2_.refs_3_.refs_0_.refs_1_, ...), custom_call_target="tpu_custom_call" | custom-call | flops 1207959552 | bytes 3145728 | tf_op jit(solution)/shard_map/project/pallas_call | solution.py:102
  244.9 12.2 %triangle.14 = bf16[5,32,32,128]{3,2,1,0:T(8,128)(2,1)S(1)} custom-call(s32[1]{0:T(128)} %bitcast.8.which, bf16[128,32,384]{2,1,0:T(8,128)(2,1)} %bitcast.62, bf16[128,32,384]{2,1,0:T(8,128)(2,1)} %bitcast.93, bf16[128,32,384]{2,1,0:T(8,128)(2,1)} %bitcast.118, bf16[128,32,384]{2,1,0:T(8,128)(2,1)} %bitcast.38, bf16[128,32,384]{2,1,0:T(8,128)(2,1)} %bitcast.50, ...), custom_call_target="tpu_custom_call" | custom-call | flops 503316480 | bytes 20185088 | tf_op jit(solution)/shard_map/triangle/pallas_call | solution.py:154
  273.1 15.4 %collective-permute-start.15 = (bf16[64,192,128]{2,1,0:T(8,128)(2,1)S(1)}, bf16[64,192,128]{2,1,0:T(8,128)(2,1)}, u32[]{:S(2)}, u32[]{:S(2)}) collective-permute-start(bf16[64,192,128]{2,1,0:T(8,128)(2,1)S(1)} %pad_maximum_fusion.4.refs_0_.refs_1_), channel_id=1, source_target_pairs={{0,12},{2,14},{5,9},{7,11},{8,4},{10,6},{13,1},{15,3},{16,28},{18,... | collective-permute-start | bytes 9437192 | tf_op jit(solution)/shard_map/ppermute | solution.py:333
  304.2 11.1 %project.28 = bf16[16,8,32,384]{3,2,1,0:T(8,128)(2,1)} custom-call(s32[1]{0:T(128)} %bitcast.5.which, bf16[64,192,128]{2,1,0:T(8,128)(2,1)} %copy-done.10, bf16[64,192,128]{2,1,0:T(8,128)(2,1)} %copy-done.10, bf16[64,192,128]{2,1,0:T(8,128)(2,1)} %copy-done.12, bf16[64,192,128]{2,1,0:T(8,128)(2,1)} %copy-done.12, ...), custom_call_target="tpu_custom_call" | custom-call | flops 1207959552 | bytes 3145728 | tf_op jit(solution)/shard_map/project/pallas_call | solution.py:102
  315.4 11.1 %project.29 = bf16[16,8,32,384]{3,2,1,0:T(8,128)(2,1)} custom-call(s32[1]{0:T(128)} %bitcast.5.which, bf16[64,192,128]{2,1,0:T(8,128)(2,1)} %copy-done.12, bf16[64,192,128]{2,1,0:T(8,128)(2,1)} %copy-done.12, bf16[64,192,128]{2,1,0:T(8,128)(2,1)} %collective-permute-done.11.refs_2_.refs_3_, bf16[64,192,128]{2,1,0:T(8,128)(2,1)} %collective-permute-done.11.refs_2_.refs_3_, ...), custom_call_target="tpu_custom_call" | custom-call | flops 1207959552 | bytes 3145728 | tf_op jit(solution)/shard_map/project/pallas_call | solution.py:102
  326.5 15.3 %triangle.15 = bf16[7,32,32,128]{3,2,1,0:T(8,128)(2,1)S(1)} custom-call(s32[1]{0:T(128)} %bitcast.8.which, bf16[128,32,384]{2,1,0:T(8,128)(2,1)} %bitcast.63, bf16[128,32,384]{2,1,0:T(8,128)(2,1)} %bitcast.94, bf16[128,32,384]{2,1,0:T(8,128)(2,1)} %bitcast.119, bf16[128,32,384]{2,1,0:T(8,128)(2,1)} %bitcast.138, bf16[128,32,384]{2,1,0:T(8,128)(2,1)} %bitcast.39, ...), custom_call_target="tpu_custom_call" | custom-call | flops 704643072 | bytes 27000832 | tf_op jit(solution)/shard_map/triangle/pallas_call | solution.py:154
  380.6 11.2 %project.31 = bf16[16,8,32,384]{3,2,1,0:T(8,128)(2,1)} custom-call(s32[1]{0:T(128)} %bitcast.5.which, bf16[64,192,128]{2,1,0:T(8,128)(2,1)} %copy-done.11, bf16[64,192,128]{2,1,0:T(8,128)(2,1)} %copy-done.11, bf16[64,192,128]{2,1,0:T(8,128)(2,1)} %collective-permute-done.18.refs_2_.refs_3_.refs_0_.refs_1_, ...), custom_call_target="tpu_custom_call" | custom-call | flops 1207959552 | bytes 3145728 | tf_op jit(solution)/shard_map/project/pallas_call | solution.py:102
  402.8 18.5 %triangle.16 = bf16[9,32,32,128]{3,2,1,0:T(8,128)(2,1)} custom-call(s32[1]{0:T(128)} %bitcast.8.which, bf16[128,32,384]{2,1,0:T(8,128)(2,1)} %bitcast.64, bf16[128,32,384]{2,1,0:T(8,128)(2,1)} %bitcast.95, bf16[128,32,384]{2,1,0:T(8,128)(2,1)} %bitcast.120, bf16[128,32,384]{2,1,0:T(8,128)(2,1)} %bitcast.139, bf16[128,32,384]{2,1,0:T(8,128)(2,1)} %bitcast.152, ...), custom_call_target="tpu_custom_call" | custom-call | flops 905969664 | bytes 33816576 | tf_op jit(solution)/shard_map/triangle/pallas_call | solution.py:154
  472.4 11.1 %project.35 = bf16[16,8,32,384]{3,2,1,0:T(8,128)(2,1)} custom-call(s32[1]{0:T(128)} %bitcast.5.which, bf16[64,192,128]{2,1,0:T(8,128)(2,1)} %copy-done.13, bf16[64,192,128]{2,1,0:T(8,128)(2,1)} %copy-done.13, bf16[64,192,128]{2,1,0:T(8,128)(2,1)} %collective-permute-done.19.refs_2_.refs_3_, bf16[64,192,128]{2,1,0:T(8,128)(2,1)} %collective-permute-done.19.refs_2_.refs_3_, ...), custom_call_target="tpu_custom_call" | custom-call | flops 1207959552 | bytes 3145728 | tf_op jit(solution)/shard_map/project/pallas_call | solution.py:102
  483.5 12.1 %triangle.19.own = bf16[5,32,32,128]{3,2,1,0:T(8,128)(2,1)S(1)} custom-call(s32[1]{0:T(128)} %bitcast.which, bf16[128,32,384]{2,1,0:T(8,128)(2,1)} %bitcast.67, bf16[128,32,384]{2,1,0:T(8,128)(2,1)} %bitcast.97, bf16[128,32,384]{2,1,0:T(8,128)(2,1)} %bitcast.121, bf16[128,32,384]{2,1,0:T(8,128)(2,1)} %bitcast.43, bf16[128,32,384]{2,1,0:T(8,128)(2,1)} %bitcast.55, ...), custom_call_target="tpu_custom_call" | custom-call | flops 503316480 | bytes 20185088 | tf_op jit(solution)/shard_map/triangle/pallas_call | solution.py:154
  495.7 15.5 %triangle.20.own = bf16[7,32,32,128]{3,2,1,0:T(8,128)(2,1)S(1)} custom-call(s32[1]{0:T(128)} %bitcast.which, bf16[128,32,384]{2,1,0:T(8,128)(2,1)} %bitcast.68, bf16[128,32,384]{2,1,0:T(8,128)(2,1)} %bitcast.98, bf16[128,32,384]{2,1,0:T(8,128)(2,1)} %bitcast.122, bf16[128,32,384]{2,1,0:T(8,128)(2,1)} %bitcast.140, bf16[128,32,384]{2,1,0:T(8,128)(2,1)} %bitcast.44, ...), custom_call_target="tpu_custom_call" | custom-call | flops 704643072 | bytes 27000832 | tf_op jit(solution)/shard_map/triangle/pallas_call | solution.py:154
  511.2 18.5 %triangle.21.own = bf16[9,32,32,128]{3,2,1,0:T(8,128)(2,1)} custom-call(s32[1]{0:T(128)} %bitcast.which, bf16[128,32,384]{2,1,0:T(8,128)(2,1)} %bitcast.69, bf16[128,32,384]{2,1,0:T(8,128)(2,1)} %bitcast.99, bf16[128,32,384]{2,1,0:T(8,128)(2,1)} %bitcast.123, bf16[128,32,384]{2,1,0:T(8,128)(2,1)} %bitcast.141, bf16[128,32,384]{2,1,0:T(8,128)(2,1)} %bitcast.153, ...), custom_call_target="tpu_custom_call" | custom-call | flops 905969664 | bytes 33816576 | tf_op jit(solution)/shard_map/triangle/pallas_call | solution.py:154
  529.7 21.0 %triangle.22 = bf16[11,32,32,128]{3,2,1,0:T(8,128)(2,1)} custom-call(s32[1]{0:T(128)} %bitcast.8.which, bf16[128,32,384]{2,1,0:T(8,128)(2,1)} %bitcast.70, bf16[128,32,384]{2,1,0:T(8,128)(2,1)} %bitcast.100, bf16[128,32,384]{2,1,0:T(8,128)(2,1)} %bitcast.124, bf16[128,32,384]{2,1,0:T(8,128)(2,1)} %bitcast.142, bf16[128,32,384]{2,1,0:T(8,128)(2,1)} %bitcast.154, ...), custom_call_target="tpu_custom_call" | custom-call | flops 1107296256 | bytes 40632320 | tf_op jit(solution)/shard_map/triangle/pallas_call | solution.py:154
  573.9 11.6 %finish.9.refs_0_ = bf16[192,192,128]{2,1,0:T(8,128)(2,1)} custom-call(bf16[7,32,32,128]{3,2,1,0:T(8,128)(2,1)S(1)} %triangle.20.own, bf16[7,32,32,128]{3,2,1,0:T(8,128)(2,1)} %collective-permute-done.20.sent, bf16[192,192,128]{2,1,0:T(8,128)(2,1)} %gate.1, bf16[128,128]{1,0:T(8,128)(2,1)S(1)} %bitcast.31, ...), custom_call_target="tpu_custom_call", output_to_operand_aliasing={{}: (6, {})} | custom-call | flops 234881024 | bytes 3670016 | tf_op jit(solution)/shard_map/finish/pallas_call | solution.py:250
  585.5 14.5 %finish.10.refs_0_ = bf16[192,192,128]{2,1,0:T(8,128)(2,1)} custom-call(bf16[9,32,32,128]{3,2,1,0:T(8,128)(2,1)} %triangle.21.own, bf16[9,32,32,128]{3,2,1,0:T(8,128)(2,1)} %collective-permute-done.22.sent, bf16[192,192,128]{2,1,0:T(8,128)(2,1)} %gate.1, bf16[128,128]{1,0:T(8,128)(2,1)S(1)} %bitcast.32, ...), custom_call_target="tpu_custom_call", output_to_operand_aliasing={{}: (6, {})} | custom-call | flops 301989888 | bytes 4718592 | tf_op jit(solution)/shard_map/finish/pallas_call | solution.py:250
  600.0 21.2 %triangle.23.own = bf16[11,32,32,128]{3,2,1,0:T(8,128)(2,1)} custom-call(s32[1]{0:T(128)} %bitcast.which, bf16[128,32,384]{2,1,0:T(8,128)(2,1)} %bitcast.71, bf16[128,32,384]{2,1,0:T(8,128)(2,1)} %bitcast.101, bf16[128,32,384]{2,1,0:T(8,128)(2,1)} %bitcast.125, bf16[128,32,384]{2,1,0:T(8,128)(2,1)} %bitcast.143, bf16[128,32,384]{2,1,0:T(8,128)(2,1)} %bitcast.155, ...), custom_call_target="tpu_custom_call" | custom-call | flops 1107296256 | bytes 40632320 | tf_op jit(solution)/shard_map/triangle/pallas_call | solution.py:154
  621.2 60.2 %collective-permute-done.23.sent = bf16[11,32,32,128]{3,2,1,0:T(8,128)(2,1)} collective-permute-done((bf16[11,32,32,128]{3,2,1,0:T(8,128)(2,1)}, bf16[11,32,32,128]{3,2,1,0:T(8,128)(2,1)}, u32[]{:S(2)}, u32[]{:S(2)}) %collective-permute-start.23) | collective-permute-done | bytes 2883616 | tf_op jit(solution)/shard_map/ppermute | solution.py:406
  681.4 17.3 %finish.11 = bf16[192,192,128]{2,1,0:T(8,128)(2,1)} custom-call(bf16[11,32,32,128]{3,2,1,0:T(8,128)(2,1)} %triangle.23.own, bf16[11,32,32,128]{3,2,1,0:T(8,128)(2,1)} %collective-permute-done.23.sent, bf16[192,192,128]{2,1,0:T(8,128)(2,1)} %gate.1, bf16[128,128]{1,0:T(8,128)(2,1)S(1)} %bitcast.33, ...), custom_call_target="tpu_custom_call", output_to_operand_aliasing={{}: (6, {})} | custom-call | flops 369098752 | bytes 5767168 | tf_op jit(solution)/shard_map/finish/pallas_call | solution.py:250
  (141 shorter events, 284.3 us)
Async XLA Ops:
  1.5 37.5 %collective-permute-start = (bf16[32,192,128]{2,1,0:T(8,128)(2,1)S(1)}, bf16[32,192,128]{2,1,0:T(8,128)(2,1)S(1)}, u32[]{:S(2)}, u32[]{:S(2)}) collective-permute-start(bf16[32,192,128]{2,1,0:T(8,128)(2,1)S(1)} %slice.42), channel_id=1, source_target_pairs={{0,1},{1,0},{2,3},{3,2},{4,5},{5,4},{6,7},{7,6},{8,9},{9,8},{10,11... | collective-permute-start | bytes 4718600 | tf_op jit(solution)/shard_map/ppermute | solution.py:372
  44.9 41.1 %collective-permute-start.1 = (bf16[64,192,128]{2,1,0:T(8,128)(2,1)}, bf16[64,192,128]{2,1,0:T(8,128)(2,1)}, u32[]{:S(2)}, u32[]{:S(2)}) collective-permute-start(bf16[64,192,128]{2,1,0:T(8,128)(2,1)} %pad_maximum_fusion.refs_0_.refs_1_), channel_id=1, source_target_pairs={{0,12},{2,14},{5,9},{7,11},{8,4},{10,6},{13,1},{15,3},{16,28},{18,... | collective-permute-start | bytes 9437192 | tf_op jit(solution)/shard_map/ppermute | solution.py:333
  48.7 37.3 %collective-permute-start.2 = (bf16[32,192,128]{2,1,0:T(8,128)(2,1)}, bf16[32,192,128]{2,1,0:T(8,128)(2,1)}, u32[]{:S(2)}, u32[]{:S(2)}) collective-permute-start(bf16[32,192,128]{2,1,0:T(8,128)(2,1)} %get-tuple-element.107), channel_id=1, source_target_pairs={{0,1},{1,0},{2,3},{3,2},{4,5},{5,4},{6,7},{7,6},{8,9},{9,8},{10,11... | collective-permute-start | bytes 4718600 | tf_op jit(solution)/shard_map/ppermute | solution.py:372
  88.0 23.8 %collective-permute-start.3 = (bf16[64,192,128]{2,1,0:T(8,128)(2,1)}, bf16[64,192,128]{2,1,0:T(8,128)(2,1)}, u32[]{:S(2)}, u32[]{:S(2)}) collective-permute-start(bf16[64,192,128]{2,1,0:T(8,128)(2,1)} %broadcast_select_fusion.5), channel_id=1, source_target_pairs={{0,4},{4,0},{8,12},{12,8},{1,5},{5,1},{9,13},{13,9},{2,6},{6,2},{1... | collective-permute-start | bytes 9437192 | tf_op jit(solution)/shard_map/ppermute | solution.py:339
  96.6 43.7 %collective-permute-start.4 = (bf16[64,192,128]{2,1,0:T(8,128)(2,1)}, bf16[64,192,128]{2,1,0:T(8,128)(2,1)}, u32[]{:S(2)}, u32[]{:S(2)}) collective-permute-start(bf16[64,192,128]{2,1,0:T(8,128)(2,1)} %pad_maximum_fusion.1.refs_0_.refs_1_), channel_id=1, source_target_pairs={{0,12},{2,14},{5,9},{7,11},{8,4},{10,6},{13,1},{15,3},{16,28},{18,... | collective-permute-start | bytes 9437192 | tf_op jit(solution)/shard_map/ppermute | solution.py:333
  100.8 39.5 %collective-permute-start.5 = (bf16[32,192,128]{2,1,0:T(8,128)(2,1)}, bf16[32,192,128]{2,1,0:T(8,128)(2,1)}, u32[]{:S(2)}, u32[]{:S(2)}) collective-permute-start(bf16[32,192,128]{2,1,0:T(8,128)(2,1)} %get-tuple-element.105), channel_id=1, source_target_pairs={{0,1},{1,0},{2,3},{3,2},{4,5},{5,4},{6,7},{7,6},{8,9},{9,8},{10,11... | collective-permute-start | bytes 4718600 | tf_op jit(solution)/shard_map/ppermute | solution.py:372
  143.9 22.1 %collective-permute-start.6 = (bf16[64,192,128]{2,1,0:T(8,128)(2,1)}, bf16[64,192,128]{2,1,0:T(8,128)(2,1)}, u32[]{:S(2)}, u32[]{:S(2)}) collective-permute-start(bf16[64,192,128]{2,1,0:T(8,128)(2,1)} %broadcast_select_fusion.4), channel_id=1, source_target_pairs={{0,4},{4,0},{8,12},{12,8},{1,5},{5,1},{9,13},{13,9},{2,6},{6,2},{1... | collective-permute-start | bytes 9437192 | tf_op jit(solution)/shard_map/ppermute | solution.py:339
  148.7 48.8 %collective-permute-start.7 = (bf16[64,192,128]{2,1,0:T(8,128)(2,1)S(1)}, bf16[64,192,128]{2,1,0:T(8,128)(2,1)}, u32[]{:S(2)}, u32[]{:S(2)}) collective-permute-start(bf16[64,192,128]{2,1,0:T(8,128)(2,1)S(1)} %pad_maximum_fusion.2.refs_0_.refs_1_), channel_id=1, source_target_pairs={{0,12},{2,14},{5,9},{7,11},{8,4},{10,6},{13,1},{15,3},{16,28},{18,... | collective-permute-start | bytes 9437192 | tf_op jit(solution)/shard_map/ppermute | solution.py:333
  152.6 44.8 %collective-permute-start.8 = (bf16[32,192,128]{2,1,0:T(8,128)(2,1)S(1)}, bf16[32,192,128]{2,1,0:T(8,128)(2,1)S(1)}, u32[]{:S(2)}, u32[]{:S(2)}) collective-permute-start(bf16[32,192,128]{2,1,0:T(8,128)(2,1)S(1)} %get-tuple-element.103), channel_id=1, source_target_pairs={{0,1},{1,0},{2,3},{3,2},{4,5},{5,4},{6,7},{7,6},{8,9},{9,8},{10,11... | collective-permute-start | bytes 4718600 | tf_op jit(solution)/shard_map/ppermute | solution.py:372
  152.7 44.7 %collective-permute-start.9 = (bf16[1,32,32,128]{3,2,1,0:T(8,128)(2,1)S(1)}, bf16[1,32,32,128]{3,2,1,0:T(8,128)(2,1)S(1)}, u32[]{:S(2)}, u32[]{:S(2)}) collective-permute-start(bf16[1,32,32,128]{3,2,1,0:T(8,128)(2,1)S(1)} %triangle.12), channel_id=1, source_target_pairs={{0,2},{1,3},{2,0},{3,1},{4,6},{5,7},{6,4},{7,5},{8,10},{9,11},{10,... | collective-permute-start | bytes 786440 | tf_op jit(solution)/shard_map/ppermute | solution.py:406
  201.0 21.8 %collective-permute-start.10 = (bf16[64,192,128]{2,1,0:T(8,128)(2,1)}, bf16[64,192,128]{2,1,0:T(8,128)(2,1)}, u32[]{:S(2)}, u32[]{:S(2)}) collective-permute-start(bf16[64,192,128]{2,1,0:T(8,128)(2,1)} %broadcast_select_fusion.3), channel_id=1, source_target_pairs={{0,4},{4,0},{8,12},{12,8},{1,5},{5,1},{9,13},{13,9},{2,6},{6,2},{1... | collective-permute-start | bytes 9437192 | tf_op jit(solution)/shard_map/ppermute | solution.py:339
  207.7 56.6 %collective-permute-start.11 = (bf16[64,192,128]{2,1,0:T(8,128)(2,1)S(1)}, bf16[64,192,128]{2,1,0:T(8,128)(2,1)}, u32[]{:S(2)}, u32[]{:S(2)}) collective-permute-start(bf16[64,192,128]{2,1,0:T(8,128)(2,1)S(1)} %pad_maximum_fusion.3.refs_0_.refs_1_), channel_id=1, source_target_pairs={{0,12},{2,14},{5,9},{7,11},{8,4},{10,6},{13,1},{15,3},{16,28},{18,... | collective-permute-start | bytes 9437192 | tf_op jit(solution)/shard_map/ppermute | solution.py:333
  211.8 52.4 %collective-permute-start.12 = (bf16[32,192,128]{2,1,0:T(8,128)(2,1)}, bf16[32,192,128]{2,1,0:T(8,128)(2,1)}, u32[]{:S(2)}, u32[]{:S(2)}) collective-permute-start(bf16[32,192,128]{2,1,0:T(8,128)(2,1)} %get-tuple-element.101), channel_id=1, source_target_pairs={{0,1},{1,0},{2,3},{3,2},{4,5},{5,4},{6,7},{7,6},{8,9},{9,8},{10,11... | collective-permute-start | bytes 4718600 | tf_op jit(solution)/shard_map/ppermute | solution.py:372
  211.8 51.6 %collective-permute-start.13 = (bf16[3,32,32,128]{3,2,1,0:T(8,128)(2,1)S(1)}, bf16[3,32,32,128]{3,2,1,0:T(8,128)(2,1)S(1)}, u32[]{:S(2)}, u32[]{:S(2)}) collective-permute-start(bf16[3,32,32,128]{3,2,1,0:T(8,128)(2,1)S(1)} %triangle.13), channel_id=1, source_target_pairs={{0,2},{1,3},{2,0},{3,1},{4,6},{5,7},{6,4},{7,5},{8,10},{9,11},{10,... | collective-permute-start | bytes 2359304 | tf_op jit(solution)/shard_map/ppermute | solution.py:406
  266.4 36.2 %collective-permute-start.14 = (bf16[64,192,128]{2,1,0:T(8,128)(2,1)}, bf16[64,192,128]{2,1,0:T(8,128)(2,1)S(1)}, u32[]{:S(2)}, u32[]{:S(2)}) collective-permute-start(bf16[64,192,128]{2,1,0:T(8,128)(2,1)} %broadcast_select_fusion.2), channel_id=1, source_target_pairs={{0,4},{4,0},{8,12},{12,8},{1,5},{5,1},{9,13},{13,9},{2,6},{6,2},{1... | collective-permute-start | bytes 9437192 | tf_op jit(solution)/shard_map/ppermute | solution.py:339
  273.1 80.7 %collective-permute-start.15 = (bf16[64,192,128]{2,1,0:T(8,128)(2,1)S(1)}, bf16[64,192,128]{2,1,0:T(8,128)(2,1)}, u32[]{:S(2)}, u32[]{:S(2)}) collective-permute-start(bf16[64,192,128]{2,1,0:T(8,128)(2,1)S(1)} %pad_maximum_fusion.4.refs_0_.refs_1_), channel_id=1, source_target_pairs={{0,12},{2,14},{5,9},{7,11},{8,4},{10,6},{13,1},{15,3},{16,28},{18,... | collective-permute-start | bytes 9437192 | tf_op jit(solution)/shard_map/ppermute | solution.py:333
  288.4 65.3 %collective-permute-start.16 = (bf16[32,192,128]{2,1,0:T(8,128)(2,1)}, bf16[32,192,128]{2,1,0:T(8,128)(2,1)}, u32[]{:S(2)}, u32[]{:S(2)}) collective-permute-start(bf16[32,192,128]{2,1,0:T(8,128)(2,1)} %get-tuple-element.99), channel_id=1, source_target_pairs={{0,1},{1,0},{2,3},{3,2},{4,5},{5,4},{6,7},{7,6},{8,9},{9,8},{10,11... | collective-permute-start | bytes 4718600 | tf_op jit(solution)/shard_map/ppermute | solution.py:372
  288.5 61.7 %collective-permute-start.17 = (bf16[5,32,32,128]{3,2,1,0:T(8,128)(2,1)S(1)}, bf16[5,32,32,128]{3,2,1,0:T(8,128)(2,1)}, u32[]{:S(2)}, u32[]{:S(2)}) collective-permute-start(bf16[5,32,32,128]{3,2,1,0:T(8,128)(2,1)S(1)} %triangle.14), channel_id=1, source_target_pairs={{0,2},{1,3},{2,0},{3,1},{4,6},{5,7},{6,4},{7,5},{8,10},{9,11},{10,... | collective-permute-start | bytes 3932168 | tf_op jit(solution)/shard_map/ppermute | solution.py:406
  357.3 23.3 %collective-permute-start.18 = (bf16[64,192,128]{2,1,0:T(8,128)(2,1)}, bf16[64,192,128]{2,1,0:T(8,128)(2,1)}, u32[]{:S(2)}, u32[]{:S(2)}) collective-permute-start(bf16[64,192,128]{2,1,0:T(8,128)(2,1)} %broadcast_select_fusion.1), channel_id=1, source_target_pairs={{0,4},{4,0},{8,12},{12,8},{1,5},{5,1},{9,13},{13,9},{2,6},{6,2},{1... | collective-permute-start | bytes 9437192 | tf_op jit(solution)/shard_map/ppermute | solution.py:339
  363.5 83.6 %collective-permute-start.19 = (bf16[64,192,128]{2,1,0:T(8,128)(2,1)}, bf16[64,192,128]{2,1,0:T(8,128)(2,1)}, u32[]{:S(2)}, u32[]{:S(2)}) collective-permute-start(bf16[64,192,128]{2,1,0:T(8,128)(2,1)} %pad_maximum_fusion.5.refs_0_.refs_1_), channel_id=1, source_target_pairs={{0,12},{2,14},{5,9},{7,11},{8,4},{10,6},{13,1},{15,3},{16,28},{18,... | collective-permute-start | bytes 9437192 | tf_op jit(solution)/shard_map/ppermute | solution.py:333
  367.9 79.2 %collective-permute-start.20 = (bf16[7,32,32,128]{3,2,1,0:T(8,128)(2,1)S(1)}, bf16[7,32,32,128]{3,2,1,0:T(8,128)(2,1)}, u32[]{:S(2)}, u32[]{:S(2)}) collective-permute-start(bf16[7,32,32,128]{3,2,1,0:T(8,128)(2,1)S(1)} %triangle.15), channel_id=1, source_target_pairs={{0,2},{1,3},{2,0},{3,1},{4,6},{5,7},{6,4},{7,5},{8,10},{9,11},{10,... | collective-permute-start | bytes 5505032 | tf_op jit(solution)/shard_map/ppermute | solution.py:406
  448.9 10.8 %collective-permute-start.21 = (bf16[64,192,128]{2,1,0:T(8,128)(2,1)S(1)}, bf16[64,192,128]{2,1,0:T(8,128)(2,1)S(1)}, u32[]{:S(2)}, u32[]{:S(2)}) collective-permute-start(bf16[64,192,128]{2,1,0:T(8,128)(2,1)S(1)} %broadcast_select_fusion), channel_id=1, source_target_pairs={{0,4},{4,0},{8,12},{12,8},{1,5},{5,1},{9,13},{13,9},{2,6},{6,2},{1... | collective-permute-start | bytes 9437192 | tf_op jit(solution)/shard_map/ppermute | solution.py:339
  449.0 105.4 %collective-permute-start.22 = (bf16[9,32,32,128]{3,2,1,0:T(8,128)(2,1)}, bf16[9,32,32,128]{3,2,1,0:T(8,128)(2,1)}, u32[]{:S(2)}, u32[]{:S(2)}) collective-permute-start(bf16[9,32,32,128]{3,2,1,0:T(8,128)(2,1)} %triangle.16), channel_id=1, source_target_pairs={{0,2},{1,3},{2,0},{3,1},{4,6},{5,7},{6,4},{7,5},{8,10},{9,11},{10,... | collective-permute-start | bytes 7077896 | tf_op jit(solution)/shard_map/ppermute | solution.py:406
  554.4 127.0 %collective-permute-start.23 = (bf16[11,32,32,128]{3,2,1,0:T(8,128)(2,1)}, bf16[11,32,32,128]{3,2,1,0:T(8,128)(2,1)}, u32[]{:S(2)}, u32[]{:S(2)}) collective-permute-start(bf16[11,32,32,128]{3,2,1,0:T(8,128)(2,1)} %triangle.22), channel_id=1, source_target_pairs={{0,2},{1,3},{2,0},{3,1},{4,6},{5,7},{6,4},{7,5},{8,10},{9,11},{10,... | collective-permute-start | bytes 8650760 | tf_op jit(solution)/shard_map/ppermute | solution.py:406
  (24 other events, 284.4 us)

commit v7 on v6

--- a/solution.py
+++ b/solution.py
@@ -324,7 +324,7 @@
     two_chips = share == 1 and top == 2
     holder = ((row ^ col) & 1) == 0
     number = lambda x: jnp.asarray(x, jnp.int32).reshape(1)
-    slabs, firsts, lefts, units = [], [], [], []
+    payloads, firsts, lefts, spread, right_sent, right_own = [], [], [], {}, {}, {}
 
     def first_step(slab):
         if not two_chips:
@@ -334,20 +334,21 @@
 
     def second_step(slab, far, *waits):
         if not two_chips:
-            return [[(x, 0 if len(x) == 1 else (row ^ col) & 1) for x in to_all_rows(held)] for held in (slab, far)]
+            odd = (row ^ col) & 1
+            shards_of = zip(to_all_rows(slab), to_all_rows(far))
+            return [(a + b, odd if len(a) > 1 else 0, len(a) + (odd if len(a) > 1 else 0)) for a, b in shards_of]
         given = jnp.where(holder, slab, after(far, *waits))
         got = lax.ppermute(given, "row", [(r, r ^ 1) for r in range(n_row)])
-        return [[([slab, got], jnp.where(holder, 0, 1))], [([got, far], jnp.where(holder, 0, 1))]]
-
-    def product(pairs, own):
-        take_near = near_is_own if own else jnp.logical_not(near_is_own)
+        return [([slab, got, far], jnp.where(holder, 0, 1), jnp.where(holder, 1, 2))]
+
+    def product(pairs, rights):
         used_left = sorted({i for i, _, _ in pairs})
         used_right = sorted({(j, s) for _, j, s in pairs})
         return triangle(
             [lefts[i] for i in used_left],
-            [units[j][s] for j, s in used_right],
+            [[rights[key]] for key in used_right],
             [(used_left.index(i), used_right.index((j, s))) for i, j, s in pairs],
-            number(jnp.where(take_near, 0, 1)),
+            number(0),
         )
 
     wide = lambda v: jnp.broadcast_to(v[:, None], (channels, 2 * half * tile_cols))
@@ -361,46 +362,53 @@
 
     token, moved, own, exchanged = [], [], [], []
 
-    def keep_own():
-        t = len(own)
-        lefts[t] = after(lefts[t], *token)
-        own.append(product(waves[t], True))
-        token[:] = own[-1:]
-
-    def exchange(n, *waits):
-        block = (after(pair_act, *waits) if waits else pair_act)[n * step : (n + 1) * step]
-        exchanged.append([lax.ppermute(block, "col", [(c, c ^ o) for c in range(n_col)]) for o in range(1, half)])
-
     def side(candidates, choice, weights):
         made = project(candidates, number(choice), half, weights, centre, after(gain_in, *token), bias_in)
         token[:] = [made]
         return made
 
+    def right_of(key, own):
+        candidates, near, far = spread[key]
+        return side(candidates, jnp.where(near_is_own == own, near, far), w_right)
+
+    def keep_own():
+        t = len(own)
+        for s in shards:
+            right_own[t, s] = right_of((t, s), True)
+        lefts[t] = after(lefts[t], *token)
+        own.append(product(waves[t], right_own))
+        token[:] = own[-1:]
+
+    def exchange(n, *waits):
+        block = after(slabs[n], *waits) if waits else slabs[n]
+        exchanged.append([lax.ppermute(block, "col", [(c, c ^ o) for c in range(n_col)]) for o in range(1, half)])
+
+    slabs = [pair_act[:step]]
+    rest = after(pair_act, slabs[0])
+    slabs += [rest[n * step : (n + 1) * step] for n in range(1, chunks)]
     exchange(0)
-    gate = gate_of(pair_act, centre, mean, ln_gain[None], ln_bias[None], w_gate)
+    gate = gate_of(pair_act, centre, mean, after(ln_gain[None], *slabs), ln_bias[None], w_gate)
     token[:] = [gate]
     for n in range(chunks + 1):
-        waits = (token if n else []) + (exchanged[n][-1:] if n < chunks else [])
-        waits = waits + (moved[n - 3 : n - 2] if n >= 3 else [])
+        waits = token + (exchanged[n][-1:] if n < chunks else []) + (moved[n - 3 : n - 2] if 3 <= n < chunks else [])
         if n + 1 < chunks:
             exchange(n + 1, *waits)
         if n < chunks:
-            block = after(pair_act, *waits)[n * step : (n + 1) * step]
-            slabs.append(jnp.concatenate([block] + exchanged[n], axis=0))
-            firsts.append(first_step(slabs[n]))
+            payloads.append(jnp.concatenate([after(slabs[n], *waits)] + exchanged[n], axis=0))
+            firsts.append(first_step(payloads[n]))
         if n == 0:
             continue
         t = n - 1
-        near, far = second_step(slabs[t], firsts[t], *waits)
-        lefts.append(side([slabs[t]], 0, w_left))
-        units.append([])
+        for s, found in enumerate(second_step(payloads[t], firsts[t], *waits)):
+            spread[t, s] = found
+        lefts.append(side([payloads[t]], 0, w_left))
         for s in shards:
-            units[t].append([side(candidates, choice, w_right) for candidates, choice in (near[s], far[s])])
+            right_sent[t, s] = right_of((t, s), False)
         if t == chunks - 1:
-            while len(own) < t:
+            while len(own) < t - 1:
                 keep_own()
         lefts[t] = after(lefts[t], *token)
-        made = product(waves[t], False)
+        made = product(waves[t], right_sent)
         token[:] = [made]
         waits = moved[t - 1 : t]
         moved.append(lax.ppermute(after(made, *waits) if waits else made, "col", swap_half))

time: 707 us -> 682 us (0.965)
  starting transfers between devices: 56.1 us -> 39.5 us
  local copies, waits for them, and re-layouts: 24.1 us -> 38.3 us
  other arithmetic: 29.9 us -> 16.3 us
  waiting for transfers between devices: 139 us -> 128 us
    ppermute x6, waiting for transfers between devices: 88.6 us -> 72.5 us  [on_device(): lax.ppermute(after(made, *waits) if waits else made, 'col', swap_half)]
    concatenate x6 -> x0, other arithmetic: 13.3 us -> none  [on_device(): slabs.append(jnp.concatenate([block] + exchanged[n], axis=0))]
    slice x7 -> x2, local copies, waits for them, and re-layouts: 18.7 us -> 6.89 us  [the longest x1 5.38 us: on_device(): slabs += [rest[n * step:(n + 1) * step] for n in range(1, chunks)]]
    unnamed x49 -> x45, local copies, waits for them, and re-layouts: 4.51 us -> 15.8 us
    ppermute x6, starting transfers between devices: 36 us -> 25.3 us  [first_step(): return lax.ppermute(slab, axes, pairs)]
    concatenate x0 -> x6, local copies, waits for them, and re-layouts: none -> 8.61 us  [on_device(): jnp.concatenate([after(slabs[n], *waits)] + exchanged[n], axis=0)]
    pallas_call x12, Pallas kernels: 166 us -> 158 us  [triangle(): pl.pallas_call(functools.partial(triangle_kernel, len(lefts), n_sides, gr...]
  transfers between devices with their start and end apart: 24 -> 24, of which waited for: 9 -> 12; matrix products, arithmetic and copies ran while one was open for 4% -> 5% of each run, Pallas kernels for 62% -> 64%
where the time goes in v7:
time: 682 us; the launch traced here: 672 us
  Pallas kernels  448 us (66%)
  waiting for transfers between devices  128 us (19%)
  starting transfers between devices  39.5 us (6%)
  local copies, waits for them, and re-layouts  38.3 us (6%)
  other arithmetic  16.3 us (2%)
    pallas_call x18, Pallas kernels, project(): pl.pallas_call(functools.partial(project_kernel, n_pieces, len(slabs)), g...  204 us
    pallas_call x12, Pallas kernels, triangle(): pl.pallas_call(functools.partial(triangle_kernel, len(lefts), n_sides, gr...  158 us
    ppermute x6, waiting for transfers between devices, on_device(): lax.ppermute(after(made, *waits) if waits else made, 'col', swap_half)  72.5 us
    pallas_call x6, Pallas kernels, finish(): pl.pallas_call(functools.partial(finish_kernel, group, hidden), grid=(pie...  61.2 us
    ppermute x6, waiting for transfers between devices, exchange(): lax.ppermute(block, 'col', [(c, c ^ o) for c in range(n_col)])  55.8 us
    ppermute x6, starting transfers between devices, first_step(): return lax.ppermute(slab, axes, pairs)  25.3 us
    pallas_call x1, Pallas kernels, gate_of(): pl.pallas_call(gate_kernel, grid=(count // rows,), in_specs=[block] + [wh...  25.2 us
    select_n x6, other arithmetic, second_step(): given = jnp.where(holder, slab, after(far, *waits))  16.2 us
  transfers between devices with their start and end apart: 24, of which 12 were waited for; matrix products, arithmetic and copies ran while one was open for 5% of the time, Pallas kernels for 64%

profile of v7, /device:TPU:0, one launch (start us, length us, event | category | flops | bytes accessed | tf_op | source)
XLA Modules:
  0.0 671.7 jit_solution(17560268056793277613)
XLA Ops:
  10.1 25.2 %gate.1 = bf16[192,192,128]{2,1,0:T(8,128)(2,1)} custom-call(bf16[192,192,128]{2,1,0:T(8,128)(2,1)} %pair.1, bf16[128,128]{1,0:T(8,128)(2,1)S(1)} %add_convert_fusion.centre.refs_3_.refs_7_, bf16[256,128]{1,0:T(8,128)(2,1)S(1)} %broadcast_in_dim.27.mean, f32[1,128]{1,0:T(1,128)S(1)} %bitcast.33, f32[1,128]{1,0:T(1,128)S(1)} %bitcast.34, ...), custom_call_target="tpu_custom_call" | custom-call | flops 4831838208 | bytes 18874368 | tf_op jit(solution)/shard_map/gate/pallas_call | solution.py:192
  45.4 37.3 %collective-permute-done.2 = bf16[32,192,128]{2,1,0:T(8,128)(2,1)} collective-permute-done((bf16[32,192,128]{2,1,0:T(8,128)(2,1)}, bf16[32,192,128]{2,1,0:T(8,128)(2,1)}, u32[]{:S(2)}, u32[]{:S(2)}) %collective-permute-start.2) | collective-permute-done | bytes 1572896 | tf_op jit(solution)/shard_map/ppermute | solution.py:384
  107.5 11.6 %project.19 = bf16[16,8,32,384]{3,2,1,0:T(8,128)(2,1)} custom-call(s32[1]{0:T(128)} %bitcast.4.which, bf16[64,192,128]{2,1,0:T(8,128)(2,1)} %constant_dynamic-update-slice_fusion.refs_0_.refs_1_, bf16[64,192,128]{2,1,0:T(8,128)(2,1)} %constant_dynamic-update-slice_fusion.refs_0_.refs_1_, bf16[64,192,128]{2,1,0:T(8,128)(2,1)} %collective-permute-done.3.refs_2_.refs_3_, ...), custom_call_target="tpu_custom_call" | custom-call | flops 1207959552 | bytes 3145728 | tf_op jit(solution)/shard_map/project/pallas_call | solution.py:102
  155.1 11.6 %project.21 = bf16[16,8,32,384]{3,2,1,0:T(8,128)(2,1)} custom-call(s32[1]{0:T(128)} %bitcast.4.which, bf16[64,192,128]{2,1,0:T(8,128)(2,1)} %constant_dynamic-update-slice_fusion.2.refs_0_.refs_1_, bf16[64,192,128]{2,1,0:T(8,128)(2,1)} %constant_dynamic-update-slice_fusion.2.refs_0_.refs_1_, bf16[64,192,128]{2,1,0:T(8,128)(2,1)} %collective-permute-done.6.refs_2_.refs_3_, ...), custom_call_target="tpu_custom_call" | custom-call | flops 1207959552 | bytes 3145728 | tf_op jit(solution)/shard_map/project/pallas_call | solution.py:102
  207.1 11.7 %project.23 = bf16[16,8,32,384]{3,2,1,0:T(8,128)(2,1)} custom-call(s32[1]{0:T(128)} %bitcast.4.which, bf16[64,192,128]{2,1,0:T(8,128)(2,1)} %copy-done.12, bf16[64,192,128]{2,1,0:T(8,128)(2,1)} %copy-done.12, bf16[64,192,128]{2,1,0:T(8,128)(2,1)} %collective-permute-done.10.refs_2_.refs_3_, bf16[64,192,128]{2,1,0:T(8,128)(2,1)} %collective-permute-done.10.refs_2_.refs_3_, ...), custom_call_target="tpu_custom_call" | custom-call | flops 1207959552 | bytes 3145728 | tf_op jit(solution)/shard_map/project/pallas_call | solution.py:102
  230.1 15.4 %collective-permute-done.13.sent = bf16[3,32,32,128]{3,2,1,0:T(8,128)(2,1)S(1)} collective-permute-done((bf16[3,32,32,128]{3,2,1,0:T(8,128)(2,1)S(1)}, bf16[3,32,32,128]{3,2,1,0:T(8,128)(2,1)S(1)}, u32[]{:S(2)}, u32[]{:S(2)}) %collective-permute-start.13) | collective-permute-done | bytes 786464 | tf_op jit(solution)/shard_map/ppermute | solution.py:414
  271.1 11.6 %project.25 = bf16[16,8,32,384]{3,2,1,0:T(8,128)(2,1)} custom-call(s32[1]{0:T(128)} %bitcast.4.which, bf16[64,192,128]{2,1,0:T(8,128)(2,1)} %copy-done.13, bf16[64,192,128]{2,1,0:T(8,128)(2,1)} %copy-done.13, bf16[64,192,128]{2,1,0:T(8,128)(2,1)} %collective-permute-done.14.refs_2_.refs_3_, bf16[64,192,128]{2,1,0:T(8,128)(2,1)} %collective-permute-done.14.refs_2_.refs_3_, ...), custom_call_target="tpu_custom_call" | custom-call | flops 1207959552 | bytes 3145728 | tf_op jit(solution)/shard_map/project/pallas_call | solution.py:102
  282.7 15.4 %triangle.15 = bf16[7,32,32,128]{3,2,1,0:T(8,128)(2,1)} custom-call(s32[1]{0:T(128)} %constant.30.clone.1.which, bf16[128,32,384]{2,1,0:T(8,128)(2,1)} %bitcast.38, bf16[128,32,384]{2,1,0:T(8,128)(2,1)} %bitcast.49, bf16[128,32,384]{2,1,0:T(8,128)(2,1)} %bitcast.58, bf16[128,32,384]{2,1,0:T(8,128)(2,1)} %bitcast.77, bf16[128,32,384]{2,1,0:T(8,128)(2,1)} %bitcast.68, ...), custom_call_target="tpu_custom_call" | custom-call | flops 704643072 | bytes 27000832 | tf_op jit(solution)/shard_map/triangle/pallas_call | solution.py:154
  298.1 23.4 %collective-permute-done.17.sent = bf16[5,32,32,128]{3,2,1,0:T(8,128)(2,1)} collective-permute-done((bf16[5,32,32,128]{3,2,1,0:T(8,128)(2,1)S(1)}, bf16[5,32,32,128]{3,2,1,0:T(8,128)(2,1)}, u32[]{:S(2)}, u32[]{:S(2)}) %collective-permute-start.17) | collective-permute-done | bytes 1310752 | tf_op jit(solution)/shard_map/ppermute | solution.py:414
  346.9 11.6 %project.27 = bf16[16,8,32,384]{3,2,1,0:T(8,128)(2,1)} custom-call(s32[1]{0:T(128)} %bitcast.4.which, bf16[64,192,128]{2,1,0:T(8,128)(2,1)} %copy-done.14, bf16[64,192,128]{2,1,0:T(8,128)(2,1)} %copy-done.14, bf16[64,192,128]{2,1,0:T(8,128)(2,1)} %collective-permute-done.18.refs_2_.refs_3_, bf16[64,192,128]{2,1,0:T(8,128)(2,1)} %collective-permute-done.18.refs_2_.refs_3_, ...), custom_call_target="tpu_custom_call" | custom-call | flops 1207959552 | bytes 3145728 | tf_op jit(solution)/shard_map/project/pallas_call | solution.py:102
  358.5 17.9 %triangle.16 = bf16[9,32,32,128]{3,2,1,0:T(8,128)(2,1)} custom-call(s32[1]{0:T(128)} %constant.30.clone.1.which, bf16[128,32,384]{2,1,0:T(8,128)(2,1)} %bitcast.39, bf16[128,32,384]{2,1,0:T(8,128)(2,1)} %bitcast.50, bf16[128,32,384]{2,1,0:T(8,128)(2,1)} %bitcast.59, bf16[128,32,384]{2,1,0:T(8,128)(2,1)} %bitcast.78, bf16[128,32,384]{2,1,0:T(8,128)(2,1)} %bitcast.101, ...), custom_call_target="tpu_custom_call" | custom-call | flops 905969664 | bytes 33816576 | tf_op jit(solution)/shard_map/triangle/pallas_call | solution.py:154
  376.3 11.6 %project.28 = bf16[16,8,32,384]{3,2,1,0:T(8,128)(2,1)} custom-call(s32[1]{0:T(128)} %bitcast.6.which, bf16[64,192,128]{2,1,0:T(8,128)(2,1)} %constant_dynamic-update-slice_fusion.refs_0_.refs_1_, bf16[64,192,128]{2,1,0:T(8,128)(2,1)} %constant_dynamic-update-slice_fusion.refs_0_.refs_1_, bf16[64,192,128]{2,1,0:T(8,128)(2,1)} %collective-permute-done.3.refs_2_.refs_3_, ...), custom_call_target="tpu_custom_call" | custom-call | flops 1207959552 | bytes 3145728 | tf_op jit(solution)/shard_map/project/pallas_call | solution.py:102
  394.0 11.7 %project.29 = bf16[16,8,32,384]{3,2,1,0:T(8,128)(2,1)} custom-call(s32[1]{0:T(128)} %bitcast.6.which, bf16[64,192,128]{2,1,0:T(8,128)(2,1)} %constant_dynamic-update-slice_fusion.2.refs_0_.refs_1_, bf16[64,192,128]{2,1,0:T(8,128)(2,1)} %constant_dynamic-update-slice_fusion.2.refs_0_.refs_1_, bf16[64,192,128]{2,1,0:T(8,128)(2,1)} %collective-permute-done.6.refs_2_.refs_3_, ...), custom_call_target="tpu_custom_call" | custom-call | flops 1207959552 | bytes 3145728 | tf_op jit(solution)/shard_map/project/pallas_call | solution.py:102
  447.6 11.8 %project.32 = bf16[16,8,32,384]{3,2,1,0:T(8,128)(2,1)} custom-call(s32[1]{0:T(128)} %bitcast.6.which, bf16[64,192,128]{2,1,0:T(8,128)(2,1)} %copy-done.12, bf16[64,192,128]{2,1,0:T(8,128)(2,1)} %copy-done.12, bf16[64,192,128]{2,1,0:T(8,128)(2,1)} %collective-permute-done.10.refs_2_.refs_3_, bf16[64,192,128]{2,1,0:T(8,128)(2,1)} %collective-permute-done.10.refs_2_.refs_3_, ...), custom_call_target="tpu_custom_call" | custom-call | flops 1207959552 | bytes 3145728 | tf_op jit(solution)/shard_map/project/pallas_call | solution.py:102
  471.8 11.7 %project.33 = bf16[16,8,32,384]{3,2,1,0:T(8,128)(2,1)} custom-call(s32[1]{0:T(128)} %bitcast.6.which, bf16[64,192,128]{2,1,0:T(8,128)(2,1)} %copy-done.13, bf16[64,192,128]{2,1,0:T(8,128)(2,1)} %copy-done.13, bf16[64,192,128]{2,1,0:T(8,128)(2,1)} %collective-permute-done.14.refs_2_.refs_3_, bf16[64,192,128]{2,1,0:T(8,128)(2,1)} %collective-permute-done.14.refs_2_.refs_3_, ...), custom_call_target="tpu_custom_call" | custom-call | flops 1207959552 | bytes 3145728 | tf_op jit(solution)/shard_map/project/pallas_call | solution.py:102
  483.5 14.6 %triangle.20.own = bf16[7,32,32,128]{3,2,1,0:T(8,128)(2,1)S(1)} custom-call(s32[1]{0:T(128)} %constant.30.clone.1.which, bf16[128,32,384]{2,1,0:T(8,128)(2,1)} %bitcast.43, bf16[128,32,384]{2,1,0:T(8,128)(2,1)} %bitcast.53, bf16[128,32,384]{2,1,0:T(8,128)(2,1)} %bitcast.61, bf16[128,32,384]{2,1,0:T(8,128)(2,1)} %bitcast.79, bf16[128,32,384]{2,1,0:T(8,128)(2,1)} %bitcast.74, ...), custom_call_target="tpu_custom_call" | custom-call | flops 704643072 | bytes 27000832 | tf_op jit(solution)/shard_map/triangle/pallas_call | solution.py:154
  498.1 20.3 %triangle.21 = bf16[11,32,32,128]{3,2,1,0:T(8,128)(2,1)} custom-call(s32[1]{0:T(128)} %constant.30.clone.1.which, bf16[128,32,384]{2,1,0:T(8,128)(2,1)} %bitcast.44, bf16[128,32,384]{2,1,0:T(8,128)(2,1)} %bitcast.54, bf16[128,32,384]{2,1,0:T(8,128)(2,1)} %bitcast.62, bf16[128,32,384]{2,1,0:T(8,128)(2,1)} %bitcast.80, bf16[128,32,384]{2,1,0:T(8,128)(2,1)} %bitcast.102, ...), custom_call_target="tpu_custom_call" | custom-call | flops 1107296256 | bytes 40632320 | tf_op jit(solution)/shard_map/triangle/pallas_call | solution.py:154
  546.3 11.6 %project.34 = bf16[16,8,32,384]{3,2,1,0:T(8,128)(2,1)} custom-call(s32[1]{0:T(128)} %bitcast.6.which, bf16[64,192,128]{2,1,0:T(8,128)(2,1)} %copy-done.14, bf16[64,192,128]{2,1,0:T(8,128)(2,1)} %copy-done.14, bf16[64,192,128]{2,1,0:T(8,128)(2,1)} %collective-permute-done.18.refs_2_.refs_3_, bf16[64,192,128]{2,1,0:T(8,128)(2,1)} %collective-permute-done.18.refs_2_.refs_3_, ...), custom_call_target="tpu_custom_call" | custom-call | flops 1207959552 | bytes 3145728 | tf_op jit(solution)/shard_map/project/pallas_call | solution.py:102
  557.9 17.9 %triangle.22.own = bf16[9,32,32,128]{3,2,1,0:T(8,128)(2,1)} custom-call(s32[1]{0:T(128)} %constant.30.clone.1.which, bf16[128,32,384]{2,1,0:T(8,128)(2,1)} %bitcast.45, bf16[128,32,384]{2,1,0:T(8,128)(2,1)} %bitcast.55, bf16[128,32,384]{2,1,0:T(8,128)(2,1)} %bitcast.63, bf16[128,32,384]{2,1,0:T(8,128)(2,1)} %bitcast.81, bf16[128,32,384]{2,1,0:T(8,128)(2,1)} %bitcast.103, ...), custom_call_target="tpu_custom_call" | custom-call | flops 905969664 | bytes 33816576 | tf_op jit(solution)/shard_map/triangle/pallas_call | solution.py:154
  575.8 12.0 %project.35 = bf16[16,8,32,384]{3,2,1,0:T(8,128)(2,1)} custom-call(s32[1]{0:T(128)} %bitcast.6.which, bf16[64,192,128]{2,1,0:T(8,128)(2,1)} %constant_dynamic-update-slice_fusion.10.refs_0_.refs_1_, bf16[64,192,128]{2,1,0:T(8,128)(2,1)} %constant_dynamic-update-slice_fusion.10.refs_0_.refs_1_, bf16[64,192,128]{2,1,0:T(8,128)(2,1)} %copy-done.16, ...), custom_call_target="tpu_custom_call" | custom-call | flops 1207959552 | bytes 3145728 | tf_op jit(solution)/shard_map/project/pallas_call | solution.py:102
  596.6 11.6 %finish.9.refs_0_ = bf16[192,192,128]{2,1,0:T(8,128)(2,1)} custom-call(bf16[7,32,32,128]{3,2,1,0:T(8,128)(2,1)S(1)} %triangle.20.own, bf16[7,32,32,128]{3,2,1,0:T(8,128)(2,1)} %collective-permute-done.21.sent, bf16[192,192,128]{2,1,0:T(8,128)(2,1)} %gate.1, bf16[128,128]{1,0:T(8,128)(2,1)S(1)} %bitcast.30, ...), custom_call_target="tpu_custom_call", output_to_operand_aliasing={{}: (6, {})} | custom-call | flops 234881024 | bytes 3670016 | tf_op jit(solution)/shard_map/finish/pallas_call | solution.py:250
  608.2 14.5 %finish.10.refs_0_ = bf16[192,192,128]{2,1,0:T(8,128)(2,1)} custom-call(bf16[9,32,32,128]{3,2,1,0:T(8,128)(2,1)} %triangle.22.own, bf16[9,32,32,128]{3,2,1,0:T(8,128)(2,1)} %collective-permute-done.22.sent, bf16[192,192,128]{2,1,0:T(8,128)(2,1)} %gate.1, bf16[128,128]{1,0:T(8,128)(2,1)S(1)} %bitcast.31, ...), custom_call_target="tpu_custom_call", output_to_operand_aliasing={{}: (6, {})} | custom-call | flops 301989888 | bytes 4718592 | tf_op jit(solution)/shard_map/finish/pallas_call | solution.py:250
  622.7 20.3 %triangle.23.own = bf16[11,32,32,128]{3,2,1,0:T(8,128)(2,1)} custom-call(s32[1]{0:T(128)} %constant.30.clone.1.which, bf16[128,32,384]{2,1,0:T(8,128)(2,1)} %bitcast.46, bf16[128,32,384]{2,1,0:T(8,128)(2,1)} %bitcast.56, bf16[128,32,384]{2,1,0:T(8,128)(2,1)} %bitcast.64, bf16[128,32,384]{2,1,0:T(8,128)(2,1)} %bitcast.82, bf16[128,32,384]{2,1,0:T(8,128)(2,1)} %bitcast.104, ...), custom_call_target="tpu_custom_call" | custom-call | flops 1107296256 | bytes 40632320 | tf_op jit(solution)/shard_map/triangle/pallas_call | solution.py:154
  653.9 17.3 %finish.11 = bf16[192,192,128]{2,1,0:T(8,128)(2,1)} custom-call(bf16[11,32,32,128]{3,2,1,0:T(8,128)(2,1)} %triangle.23.own, bf16[11,32,32,128]{3,2,1,0:T(8,128)(2,1)} %collective-permute-done.23.sent, bf16[192,192,128]{2,1,0:T(8,128)(2,1)} %gate.1, bf16[128,128]{1,0:T(8,128)(2,1)S(1)} %bitcast.32, ...), custom_call_target="tpu_custom_call", output_to_operand_aliasing={{}: (6, {})} | custom-call | flops 369098752 | bytes 5767168 | tf_op jit(solution)/shard_map/finish/pallas_call | solution.py:250
  (132 shorter events, 291.2 us)
Async XLA Ops:
  1.6 37.5 %collective-permute-start = (bf16[32,192,128]{2,1,0:T(8,128)(2,1)S(1)}, bf16[32,192,128]{2,1,0:T(8,128)(2,1)S(1)}, u32[]{:S(2)}, u32[]{:S(2)}) collective-permute-start(bf16[32,192,128]{2,1,0:T(8,128)(2,1)S(1)} %slice.24), channel_id=1, source_target_pairs={{0,1},{1,0},{2,3},{3,2},{4,5},{5,4},{6,7},{7,6},{8,9},{9,8},{10,11... | collective-permute-start | bytes 4718600 | tf_op jit(solution)/shard_map/ppermute | solution.py:384
  41.5 43.8 %collective-permute-start.1 = (bf16[64,192,128]{2,1,0:T(8,128)(2,1)}, bf16[64,192,128]{2,1,0:T(8,128)(2,1)}, u32[]{:S(2)}, u32[]{:S(2)}) collective-permute-start(bf16[64,192,128]{2,1,0:T(8,128)(2,1)} %constant_dynamic-update-slice_fusion.refs_0_.refs_1_), channel_id=1, source_target_pairs={{0,12},{2,14},{5,9},{7,11},{8,4},{10,6},{13,1},{15,3},{16,28},{18,... | collective-permute-start | bytes 9437192 | tf_op jit(solution)/shard_map/ppermute | solution.py:333
  45.4 37.3 %collective-permute-start.2 = (bf16[32,192,128]{2,1,0:T(8,128)(2,1)}, bf16[32,192,128]{2,1,0:T(8,128)(2,1)}, u32[]{:S(2)}, u32[]{:S(2)}) collective-permute-start(bf16[32,192,128]{2,1,0:T(8,128)(2,1)} %get-tuple-element.67), channel_id=1, source_target_pairs={{0,1},{1,0},{2,3},{3,2},{4,5},{5,4},{6,7},{7,6},{8,9},{9,8},{10,11... | collective-permute-start | bytes 4718600 | tf_op jit(solution)/shard_map/ppermute | solution.py:384
  89.2 18.4 %collective-permute-start.3 = (bf16[64,192,128]{2,1,0:T(8,128)(2,1)}, bf16[64,192,128]{2,1,0:T(8,128)(2,1)}, u32[]{:S(2)}, u32[]{:S(2)}) collective-permute-start(bf16[64,192,128]{2,1,0:T(8,128)(2,1)} %broadcast_select_fusion.5), channel_id=1, source_target_pairs={{0,4},{4,0},{8,12},{12,8},{1,5},{5,1},{9,13},{13,9},{2,6},{6,2},{1... | collective-permute-start | bytes 9437192 | tf_op jit(solution)/shard_map/ppermute | solution.py:341
  92.0 39.6 %collective-permute-start.4 = (bf16[64,192,128]{2,1,0:T(8,128)(2,1)}, bf16[64,192,128]{2,1,0:T(8,128)(2,1)}, u32[]{:S(2)}, u32[]{:S(2)}) collective-permute-start(bf16[64,192,128]{2,1,0:T(8,128)(2,1)} %constant_dynamic-update-slice_fusion.2.refs_0_.refs_1_), channel_id=1, source_target_pairs={{0,12},{2,14},{5,9},{7,11},{8,4},{10,6},{13,1},{15,3},{16,28},{18,... | collective-permute-start | bytes 9437192 | tf_op jit(solution)/shard_map/ppermute | solution.py:333
  96.6 35.0 %collective-permute-start.5 = (bf16[32,192,128]{2,1,0:T(8,128)(2,1)}, bf16[32,192,128]{2,1,0:T(8,128)(2,1)}, u32[]{:S(2)}, u32[]{:S(2)}) collective-permute-start(bf16[32,192,128]{2,1,0:T(8,128)(2,1)} %get-tuple-element.73), channel_id=1, source_target_pairs={{0,1},{1,0},{2,3},{3,2},{4,5},{5,4},{6,7},{7,6},{8,9},{9,8},{10,11... | collective-permute-start | bytes 4718600 | tf_op jit(solution)/shard_map/ppermute | solution.py:384
  135.5 19.7 %collective-permute-start.6 = (bf16[64,192,128]{2,1,0:T(8,128)(2,1)}, bf16[64,192,128]{2,1,0:T(8,128)(2,1)}, u32[]{:S(2)}, u32[]{:S(2)}) collective-permute-start(bf16[64,192,128]{2,1,0:T(8,128)(2,1)} %broadcast_select_fusion.4), channel_id=1, source_target_pairs={{0,4},{4,0},{8,12},{12,8},{1,5},{5,1},{9,13},{13,9},{2,6},{6,2},{1... | collective-permute-start | bytes 9437192 | tf_op jit(solution)/shard_map/ppermute | solution.py:341
  138.6 45.5 %collective-permute-start.7 = (bf16[64,192,128]{2,1,0:T(8,128)(2,1)S(1)}, bf16[64,192,128]{2,1,0:T(8,128)(2,1)S(1)}, u32[]{:S(2)}, u32[]{:S(2)}) collective-permute-start(bf16[64,192,128]{2,1,0:T(8,128)(2,1)S(1)} %constant_dynamic-update-slice_fusion.4.refs_0_.refs_1_), channel_id=1, source_target_pairs={{0,12},{2,14},{5,9},{7,11},{8,4},{10,6},{13,1},{15,3},{16,28},{18,... | collective-permute-start | bytes 9437192 | tf_op jit(solution)/shard_map/ppermute | solution.py:333
  141.8 42.3 %collective-permute-start.8 = (bf16[32,192,128]{2,1,0:T(8,128)(2,1)}, bf16[32,192,128]{2,1,0:T(8,128)(2,1)}, u32[]{:S(2)}, u32[]{:S(2)}) collective-permute-start(bf16[32,192,128]{2,1,0:T(8,128)(2,1)} %get-tuple-element.79), channel_id=1, source_target_pairs={{0,1},{1,0},{2,3},{3,2},{4,5},{5,4},{6,7},{7,6},{8,9},{9,8},{10,11... | collective-permute-start | bytes 4718600 | tf_op jit(solution)/shard_map/ppermute | solution.py:384
  141.9 39.9 %collective-permute-start.9 = (bf16[1,32,32,128]{3,2,1,0:T(8,128)(2,1)S(1)}, bf16[1,32,32,128]{3,2,1,0:T(8,128)(2,1)S(1)}, u32[]{:S(2)}, u32[]{:S(2)}) collective-permute-start(bf16[1,32,32,128]{3,2,1,0:T(8,128)(2,1)S(1)} %triangle.12), channel_id=1, source_target_pairs={{0,2},{1,3},{2,0},{3,1},{4,6},{5,7},{6,4},{7,5},{8,10},{9,11},{10,... | collective-permute-start | bytes 786440 | tf_op jit(solution)/shard_map/ppermute | solution.py:414
  186.9 20.2 %collective-permute-start.10 = (bf16[64,192,128]{2,1,0:T(8,128)(2,1)}, bf16[64,192,128]{2,1,0:T(8,128)(2,1)}, u32[]{:S(2)}, u32[]{:S(2)}) collective-permute-start(bf16[64,192,128]{2,1,0:T(8,128)(2,1)} %broadcast_select_fusion.3), channel_id=1, source_target_pairs={{0,4},{4,0},{8,12},{12,8},{1,5},{5,1},{9,13},{13,9},{2,6},{6,2},{1... | collective-permute-start | bytes 9437192 | tf_op jit(solution)/shard_map/ppermute | solution.py:341
  190.1 59.4 %collective-permute-start.11 = (bf16[64,192,128]{2,1,0:T(8,128)(2,1)S(1)}, bf16[64,192,128]{2,1,0:T(8,128)(2,1)}, u32[]{:S(2)}, u32[]{:S(2)}) collective-permute-start(bf16[64,192,128]{2,1,0:T(8,128)(2,1)S(1)} %constant_dynamic-update-slice_fusion.6.refs_0_.refs_1_), channel_id=1, source_target_pairs={{0,12},{2,14},{5,9},{7,11},{8,4},{10,6},{13,1},{15,3},{16,28},{18,... | collective-permute-start | bytes 9437192 | tf_op jit(solution)/shard_map/ppermute | solution.py:333
  195.2 54.2 %collective-permute-start.12 = (bf16[32,192,128]{2,1,0:T(8,128)(2,1)}, bf16[32,192,128]{2,1,0:T(8,128)(2,1)S(1)}, u32[]{:S(2)}, u32[]{:S(2)}) collective-permute-start(bf16[32,192,128]{2,1,0:T(8,128)(2,1)} %get-tuple-element.86), channel_id=1, source_target_pairs={{0,1},{1,0},{2,3},{3,2},{4,5},{5,4},{6,7},{7,6},{8,9},{9,8},{10,11... | collective-permute-start | bytes 4718600 | tf_op jit(solution)/shard_map/ppermute | solution.py:384
  195.3 50.2 %collective-permute-start.13 = (bf16[3,32,32,128]{3,2,1,0:T(8,128)(2,1)S(1)}, bf16[3,32,32,128]{3,2,1,0:T(8,128)(2,1)S(1)}, u32[]{:S(2)}, u32[]{:S(2)}) collective-permute-start(bf16[3,32,32,128]{3,2,1,0:T(8,128)(2,1)S(1)} %triangle.13), channel_id=1, source_target_pairs={{0,2},{1,3},{2,0},{3,1},{4,6},{5,7},{6,4},{7,5},{8,10},{9,11},{10,... | collective-permute-start | bytes 2359304 | tf_op jit(solution)/shard_map/ppermute | solution.py:414
  251.4 19.6 %collective-permute-start.14 = (bf16[64,192,128]{2,1,0:T(8,128)(2,1)}, bf16[64,192,128]{2,1,0:T(8,128)(2,1)}, u32[]{:S(2)}, u32[]{:S(2)}) collective-permute-start(bf16[64,192,128]{2,1,0:T(8,128)(2,1)} %broadcast_select_fusion.2), channel_id=1, source_target_pairs={{0,4},{4,0},{8,12},{12,8},{1,5},{5,1},{9,13},{13,9},{2,6},{6,2},{1... | collective-permute-start | bytes 9437192 | tf_op jit(solution)/shard_map/ppermute | solution.py:341
  255.0 68.5 %collective-permute-start.15 = (bf16[64,192,128]{2,1,0:T(8,128)(2,1)S(1)}, bf16[64,192,128]{2,1,0:T(8,128)(2,1)}, u32[]{:S(2)}, u32[]{:S(2)}) collective-permute-start(bf16[64,192,128]{2,1,0:T(8,128)(2,1)S(1)} %constant_dynamic-update-slice_fusion.8.refs_0_.refs_1_), channel_id=1, source_target_pairs={{0,12},{2,14},{5,9},{7,11},{8,4},{10,6},{13,1},{15,3},{16,28},{18,... | collective-permute-start | bytes 9437192 | tf_op jit(solution)/shard_map/ppermute | solution.py:333
  259.2 64.3 %collective-permute-start.16 = (bf16[32,192,128]{2,1,0:T(8,128)(2,1)S(1)}, bf16[32,192,128]{2,1,0:T(8,128)(2,1)S(1)}, u32[]{:S(2)}, u32[]{:S(2)}) collective-permute-start(bf16[32,192,128]{2,1,0:T(8,128)(2,1)S(1)} %get-tuple-element.97), channel_id=1, source_target_pairs={{0,1},{1,0},{2,3},{3,2},{4,5},{5,4},{6,7},{7,6},{8,9},{9,8},{10,11... | collective-permute-start | bytes 4718600 | tf_op jit(solution)/shard_map/ppermute | solution.py:384
  259.2 62.2 %collective-permute-start.17 = (bf16[5,32,32,128]{3,2,1,0:T(8,128)(2,1)S(1)}, bf16[5,32,32,128]{3,2,1,0:T(8,128)(2,1)}, u32[]{:S(2)}, u32[]{:S(2)}) collective-permute-start(bf16[5,32,32,128]{3,2,1,0:T(8,128)(2,1)S(1)} %triangle.14), channel_id=1, source_target_pairs={{0,2},{1,3},{2,0},{3,1},{4,6},{5,7},{6,4},{7,5},{8,10},{9,11},{10,... | collective-permute-start | bytes 3932168 | tf_op jit(solution)/shard_map/ppermute | solution.py:414
  325.6 21.3 %collective-permute-start.18 = (bf16[64,192,128]{2,1,0:T(8,128)(2,1)}, bf16[64,192,128]{2,1,0:T(8,128)(2,1)}, u32[]{:S(2)}, u32[]{:S(2)}) collective-permute-start(bf16[64,192,128]{2,1,0:T(8,128)(2,1)} %broadcast_select_fusion.1), channel_id=1, source_target_pairs={{0,4},{4,0},{8,12},{12,8},{1,5},{5,1},{9,13},{13,9},{2,6},{6,2},{1... | collective-permute-start | bytes 9437192 | tf_op jit(solution)/shard_map/ppermute | solution.py:341
  329.1 85.3 %collective-permute-start.19 = (bf16[64,192,128]{2,1,0:T(8,128)(2,1)}, bf16[64,192,128]{2,1,0:T(8,128)(2,1)}, u32[]{:S(2)}, u32[]{:S(2)}) collective-permute-start(bf16[64,192,128]{2,1,0:T(8,128)(2,1)} %constant_dynamic-update-slice_fusion.10.refs_0_.refs_1_), channel_id=1, source_target_pairs={{0,12},{2,14},{5,9},{7,11},{8,4},{10,6},{13,1},{15,3},{16,28},{18,... | collective-permute-start | bytes 9437192 | tf_op jit(solution)/shard_map/ppermute | solution.py:333
  344.0 79.8 %collective-permute-start.21 = (bf16[7,32,32,128]{3,2,1,0:T(8,128)(2,1)}, bf16[7,32,32,128]{3,2,1,0:T(8,128)(2,1)}, u32[]{:S(2)}, u32[]{:S(2)}) collective-permute-start(bf16[7,32,32,128]{3,2,1,0:T(8,128)(2,1)} %triangle.15), channel_id=1, source_target_pairs={{0,2},{1,3},{2,0},{3,1},{4,6},{5,7},{6,4},{7,5},{8,10},{9,11},{10,... | collective-permute-start | bytes 5505032 | tf_op jit(solution)/shard_map/ppermute | solution.py:414
  416.7 17.7 %collective-permute-start.20 = (bf16[64,192,128]{2,1,0:T(8,128)(2,1)S(1)}, bf16[64,192,128]{2,1,0:T(8,128)(2,1)S(1)}, u32[]{:S(2)}, u32[]{:S(2)}) collective-permute-start(bf16[64,192,128]{2,1,0:T(8,128)(2,1)S(1)} %broadcast_select_fusion), channel_id=1, source_target_pairs={{0,4},{4,0},{8,12},{12,8},{1,5},{5,1},{9,13},{13,9},{2,6},{6,2},{1... | collective-permute-start | bytes 9437192 | tf_op jit(solution)/shard_map/ppermute | solution.py:341
  423.8 104.1 %collective-permute-start.22 = (bf16[9,32,32,128]{3,2,1,0:T(8,128)(2,1)}, bf16[9,32,32,128]{3,2,1,0:T(8,128)(2,1)}, u32[]{:S(2)}, u32[]{:S(2)}) collective-permute-start(bf16[9,32,32,128]{3,2,1,0:T(8,128)(2,1)} %triangle.16), channel_id=1, source_target_pairs={{0,2},{1,3},{2,0},{3,1},{4,6},{5,7},{6,4},{7,5},{8,10},{9,11},{10,... | collective-permute-start | bytes 7077896 | tf_op jit(solution)/shard_map/ppermute | solution.py:414
  527.9 126.0 %collective-permute-start.23 = (bf16[11,32,32,128]{3,2,1,0:T(8,128)(2,1)}, bf16[11,32,32,128]{3,2,1,0:T(8,128)(2,1)}, u32[]{:S(2)}, u32[]{:S(2)}) collective-permute-start(bf16[11,32,32,128]{3,2,1,0:T(8,128)(2,1)} %triangle.21), channel_id=1, source_target_pairs={{0,2},{1,3},{2,0},{3,1},{4,6},{5,7},{6,4},{7,5},{8,10},{9,11},{10,... | collective-permute-start | bytes 8650760 | tf_op jit(solution)/shard_map/ppermute | solution.py:414
  (19 other events, 281.9 us)

commit v8 on v7

--- a/solution.py
+++ b/solution.py
@@ -228,13 +228,12 @@
         out[i] = (result * gate[i].astype(F32)).astype(BF16)
 
 
-def finish(own, sent, gate, t, chunks, share, weights, gain, bias, held):
+def finish(own, sent, gate, t, before, chunks, share, weights, gain, bias, held):
     pieces, packed, count, lanes = own.shape
     rows = count if count <= 32 else 16
     hidden, channels = weights.shape
     group = hidden // packed
     steps = count // rows
-    before = t * share
 
     def row_of(p):
         return jnp.where(p < before, p // share, t)
@@ -358,7 +357,7 @@
     for t in range(chunks):
         by_column = [(i, t, s) for i in range(t) for s in shards]
         by_row = [(t, j, s) for j in range(t + 1) for s in shards]
-        waves.append(by_column + by_row)
+        waves.append([by_row, by_column] if t == chunks - 1 and t else [by_column + by_row])
 
     token, moved, own, exchanged = [], [], [], []
 
@@ -371,13 +370,19 @@
         candidates, near, far = spread[key]
         return side(candidates, jnp.where(near_is_own == own, near, far), w_right)
 
+    def multiply(t, rights):
+        made = []
+        for pairs in waves[t]:
+            lefts[t] = after(lefts[t], *token)
+            made.append(product(pairs, rights))
+            token[:] = made[-1:]
+        return made
+
     def keep_own():
         t = len(own)
         for s in shards:
             right_own[t, s] = right_of((t, s), True)
-        lefts[t] = after(lefts[t], *token)
-        own.append(product(waves[t], right_own))
-        token[:] = own[-1:]
+        own.append(multiply(t, right_own))
 
     def exchange(n, *waits):
         block = after(slabs[n], *waits) if waits else slabs[n]
@@ -387,31 +392,42 @@
     rest = after(pair_act, slabs[0])
     slabs += [rest[n * step : (n + 1) * step] for n in range(1, chunks)]
     exchange(0)
-    gate = gate_of(pair_act, centre, mean, after(ln_gain[None], *slabs), ln_bias[None], w_gate)
+
+    def base(n, *waits):
+        return jnp.pad(after(slabs[n], *waits) if waits else slabs[n], ((0, (half - 1) * step), (0, 0), (0, 0)))
+
+    bases = [base(n) for n in range(min(2, chunks))]
+    gate = gate_of(pair_act, centre, mean, after(ln_gain[None], *slabs, *bases), ln_bias[None], w_gate)
     token[:] = [gate]
     for n in range(chunks + 1):
-        waits = token + (exchanged[n][-1:] if n < chunks else []) + (moved[n - 3 : n - 2] if 3 <= n < chunks else [])
+        waits = token + (exchanged[n][-1:] if n < chunks else [])
+        if n >= 3:
+            waits = waits + moved[n - 3]
         if n + 1 < chunks:
             exchange(n + 1, *waits)
         if n < chunks:
-            payloads.append(jnp.concatenate([after(slabs[n], *waits)] + exchanged[n], axis=0))
+            payload = after(bases[n], *waits)
+            for p, piece in enumerate(exchanged[n]):
+                payload = lax.dynamic_update_slice_in_dim(payload, piece, (p + 1) * step, axis=0)
+            payloads.append(payload)
             firsts.append(first_step(payloads[n]))
         if n == 0:
             continue
         t = n - 1
         for s, found in enumerate(second_step(payloads[t], firsts[t], *waits)):
             spread[t, s] = found
+        if n + 1 < chunks:
+            bases.append(base(n + 1, *waits))
+            token.append(bases[-1])
         lefts.append(side([payloads[t]], 0, w_left))
         for s in shards:
             right_sent[t, s] = right_of((t, s), False)
         if t == chunks - 1:
             while len(own) < t - 1:
                 keep_own()
-        lefts[t] = after(lefts[t], *token)
-        made = product(waves[t], right_sent)
-        token[:] = [made]
-        waits = moved[t - 1 : t]
-        moved.append(lax.ppermute(after(made, *waits) if waits else made, "col", swap_half))
+        made = multiply(t, right_sent)
+        waits = moved[t - 1] if t else []
+        moved.append([lax.ppermute(after(x, *waits) if waits else x, "col", swap_half) for x in made])
         if t == chunks - 2:
             while len(own) < t // 2:
                 keep_own()
@@ -419,7 +435,9 @@
         keep_own()
     out = None
     for t in range(chunks):
-        out = finish(own[t], moved[t], gate, t, chunks, share, w_last, gain_out, bias_out, out)
+        for pairs, kept, came in zip(waves[t], own[t], moved[t]):
+            before = sum(j == t and i < t for i, j, _ in pairs)
+            out = finish(kept, came, gate, t, before, chunks, share, w_last, gain_out, bias_out, out)
     return out
 
 

time: 682 us -> 685 us (level)
  waiting for transfers between devices: 128 us -> 102 us
  Pallas kernels: 448 us -> 460 us
  other arithmetic: 16.3 us -> 24.9 us
    ppermute x6 -> x7, waiting for transfers between devices: 72.5 us -> 54.2 us  [on_device(): lax.ppermute(after(x, *waits) if waits else x, 'col', swap_half)]
    dynamic_update_slice x0 -> x6, local copies, waits for them, and re-layouts: none -> 12.3 us  [on_device(): lax.dynamic_update_slice_in_dim(payload, piece, (p + 1) * step, axis=0)]
    pad x0 -> x5, local copies, waits for them, and re-layouts: none -> 12 us  [base(): jnp.pad(after(slabs[n], *waits) if waits else slabs[n], ((0, (half - 1) *...]
    pallas_call x12 -> x14, Pallas kernels: 158 us -> 169 us  [triangle(): pl.pallas_call(functools.partial(triangle_kernel, len(lefts), n_sides, gr...]
    unnamed x45 -> x41, local copies, waits for them, and re-layouts: 15.8 us -> 5.48 us
    concatenate x6 -> x0, local copies, waits for them, and re-layouts: 8.61 us -> none  [on_device(): jnp.concatenate([after(slabs[n], *waits)] + exchanged[n], axis=0)]
    ppermute x6, waiting for transfers between devices: 55.8 us -> 47.7 us  [exchange(): lax.ppermute(block, 'col', [(c, c ^ o) for c in range(n_col)])]
    pallas_call x6 -> x7, Pallas kernels: 61.2 us -> 62.9 us  [finish(): pl.pallas_call(functools.partial(finish_kernel, group, hidden), grid=(pie...]
  transfers between devices with their start and end apart: 24 -> 25, of which waited for: 12 -> 9; matrix products, arithmetic and copies ran while one was open for 5% -> 6% of each run, Pallas kernels for 64% -> 67%
where the time goes in v8:
time: 685 us; the launch traced here: 674 us
  Pallas kernels  460 us (67%)
  waiting for transfers between devices  102 us (15%)
  local copies, waits for them, and re-layouts  43.7 us (6%)
  starting transfers between devices  42.7 us (6%)
  other arithmetic  24.9 us (4%)
    pallas_call x18, Pallas kernels, project(): pl.pallas_call(functools.partial(project_kernel, n_pieces, len(slabs)), g...  203 us
    pallas_call x14, Pallas kernels, triangle(): pl.pallas_call(functools.partial(triangle_kernel, len(lefts), n_sides, gr...  169 us
    pallas_call x7, Pallas kernels, finish(): pl.pallas_call(functools.partial(finish_kernel, group, hidden), grid=(pie...  62.9 us
    ppermute x7, waiting for transfers between devices, on_device(): lax.ppermute(after(x, *waits) if waits else x, 'col', swap_half)  54.2 us
    ppermute x6, waiting for transfers between devices, exchange(): lax.ppermute(block, 'col', [(c, c ^ o) for c in range(n_col)])  47.7 us
    pallas_call x1, Pallas kernels, gate_of(): pl.pallas_call(gate_kernel, grid=(count // rows,), in_specs=[block] + [wh...  25.2 us
    ppermute x6, starting transfers between devices, first_step(): return lax.ppermute(slab, axes, pairs)  24.9 us
    select_n x6, other arithmetic, second_step(): given = jnp.where(holder, slab, after(far, *waits))  21 us
  transfers between devices with their start and end apart: 25, of which 9 were waited for; matrix products, arithmetic and copies ran while one was open for 6% of the time, Pallas kernels for 67%

profile of v8, /device:TPU:0, one launch (start us, length us, event | category | flops | bytes accessed | tf_op | source)
XLA Modules:
  0.0 674.4 jit_solution(12113625705650002510)
XLA Ops:
  17.5 25.2 %gate.1 = bf16[192,192,128]{2,1,0:T(8,128)(2,1)} custom-call(bf16[192,192,128]{2,1,0:T(8,128)(2,1)} %pair.1, bf16[128,128]{1,0:T(8,128)(2,1)S(1)} %add_convert_fusion.centre.refs_3_.refs_7_, bf16[256,128]{1,0:T(8,128)(2,1)S(1)} %broadcast_in_dim.27.mean, f32[1,128]{1,0:T(1,128)S(1)} %bitcast.34, f32[1,128]{1,0:T(1,128)S(1)} %bitcast.35, ...), custom_call_target="tpu_custom_call" | custom-call | flops 4831838208 | bytes 18874368 | tf_op jit(solution)/shard_map/gate/pallas_call | solution.py:192
  48.2 36.3 %collective-permute-done.1 = bf16[32,192,128]{2,1,0:T(8,128)(2,1)} collective-permute-done((bf16[32,192,128]{2,1,0:T(8,128)(2,1)}, bf16[32,192,128]{2,1,0:T(8,128)(2,1)}, u32[]{:S(2)}, u32[]{:S(2)}) %collective-permute-start.1) | collective-permute-done | bytes 1572896 | tf_op jit(solution)/shard_map/ppermute | solution.py:389
  109.3 11.7 %project.19 = bf16[16,8,32,384]{3,2,1,0:T(8,128)(2,1)} custom-call(s32[1]{0:T(128)} %bitcast.4.which, bf16[64,192,128]{2,1,0:T(8,128)(2,1)} %constant_dynamic-update-slice_fusion.5.refs_0_.refs_1_, bf16[64,192,128]{2,1,0:T(8,128)(2,1)} %constant_dynamic-update-slice_fusion.5.refs_0_.refs_1_, bf16[64,192,128]{2,1,0:T(8,128)(2,1)} %collective-permute-done.3.refs_2_.refs_3_, ...), custom_call_target="tpu_custom_call" | custom-call | flops 1207959552 | bytes 3145728 | tf_op jit(solution)/shard_map/project/pallas_call | solution.py:102
  209.8 11.6 %project.23 = bf16[16,8,32,384]{3,2,1,0:T(8,128)(2,1)} custom-call(s32[1]{0:T(128)} %bitcast.4.which, bf16[64,192,128]{2,1,0:T(8,128)(2,1)} %constant_dynamic-update-slice_fusion.3.refs_0_.refs_1_, bf16[64,192,128]{2,1,0:T(8,128)(2,1)} %constant_dynamic-update-slice_fusion.3.refs_0_.refs_1_, bf16[64,192,128]{2,1,0:T(8,128)(2,1)} %collective-permute-done.10.refs_2_.refs_3_, ...), custom_call_target="tpu_custom_call" | custom-call | flops 1207959552 | bytes 3145728 | tf_op jit(solution)/shard_map/project/pallas_call | solution.py:102
  232.7 11.8 %collective-permute-done.12.sent = bf16[3,32,32,128]{3,2,1,0:T(8,128)(2,1)S(1)} collective-permute-done((bf16[3,32,32,128]{3,2,1,0:T(8,128)(2,1)S(1)}, bf16[3,32,32,128]{3,2,1,0:T(8,128)(2,1)S(1)}, u32[]{:S(2)}, u32[]{:S(2)}) %collective-permute-start.12) | collective-permute-done | bytes 786464 | tf_op jit(solution)/shard_map/ppermute | solution.py:430
  272.8 11.6 %project.25 = bf16[16,8,32,384]{3,2,1,0:T(8,128)(2,1)} custom-call(s32[1]{0:T(128)} %bitcast.4.which, bf16[64,192,128]{2,1,0:T(8,128)(2,1)} %copy-done.12, bf16[64,192,128]{2,1,0:T(8,128)(2,1)} %copy-done.12, bf16[64,192,128]{2,1,0:T(8,128)(2,1)} %collective-permute-done.14.refs_2_.refs_3_, bf16[64,192,128]{2,1,0:T(8,128)(2,1)} %collective-permute-done.14.refs_2_.refs_3_, ...), custom_call_target="tpu_custom_call" | custom-call | flops 1207959552 | bytes 3145728 | tf_op jit(solution)/shard_map/project/pallas_call | solution.py:102
  284.4 15.4 %triangle.17 = bf16[7,32,32,128]{3,2,1,0:T(8,128)(2,1)} custom-call(s32[1]{0:T(128)} %constant.33.clone.1.which, bf16[128,32,384]{2,1,0:T(8,128)(2,1)} %bitcast.39, bf16[128,32,384]{2,1,0:T(8,128)(2,1)} %bitcast.50, bf16[128,32,384]{2,1,0:T(8,128)(2,1)} %bitcast.59, bf16[128,32,384]{2,1,0:T(8,128)(2,1)} %bitcast.78, bf16[128,32,384]{2,1,0:T(8,128)(2,1)} %bitcast.69, ...), custom_call_target="tpu_custom_call" | custom-call | flops 704643072 | bytes 27000832 | tf_op jit(solution)/shard_map/triangle/pallas_call | solution.py:154
  299.8 21.8 %collective-permute-done.17.sent = bf16[5,32,32,128]{3,2,1,0:T(8,128)(2,1)} collective-permute-done((bf16[5,32,32,128]{3,2,1,0:T(8,128)(2,1)S(1)}, bf16[5,32,32,128]{3,2,1,0:T(8,128)(2,1)}, u32[]{:S(2)}, u32[]{:S(2)}) %collective-permute-start.17) | collective-permute-done | bytes 1310752 | tf_op jit(solution)/shard_map/ppermute | solution.py:430
  346.4 11.7 %project.27 = bf16[16,8,32,384]{3,2,1,0:T(8,128)(2,1)} custom-call(s32[1]{0:T(128)} %bitcast.4.which, bf16[64,192,128]{2,1,0:T(8,128)(2,1)} %constant_dynamic-update-slice_fusion.1.refs_0_.refs_1_, bf16[64,192,128]{2,1,0:T(8,128)(2,1)} %constant_dynamic-update-slice_fusion.1.refs_0_.refs_1_, bf16[64,192,128]{2,1,0:T(8,128)(2,1)} %collective-permute-done.18.refs_2_.refs_3_, ...), custom_call_target="tpu_custom_call" | custom-call | flops 1207959552 | bytes 3145728 | tf_op jit(solution)/shard_map/project/pallas_call | solution.py:102
  358.1 17.9 %triangle.18 = bf16[9,32,32,128]{3,2,1,0:T(8,128)(2,1)} custom-call(s32[1]{0:T(128)} %constant.33.clone.1.which, bf16[128,32,384]{2,1,0:T(8,128)(2,1)} %bitcast.40, bf16[128,32,384]{2,1,0:T(8,128)(2,1)} %bitcast.51, bf16[128,32,384]{2,1,0:T(8,128)(2,1)} %bitcast.60, bf16[128,32,384]{2,1,0:T(8,128)(2,1)} %bitcast.79, bf16[128,32,384]{2,1,0:T(8,128)(2,1)} %bitcast.102, ...), custom_call_target="tpu_custom_call" | custom-call | flops 905969664 | bytes 33816576 | tf_op jit(solution)/shard_map/triangle/pallas_call | solution.py:154
  376.0 11.6 %project.28 = bf16[16,8,32,384]{3,2,1,0:T(8,128)(2,1)} custom-call(s32[1]{0:T(128)} %bitcast.6.which, bf16[64,192,128]{2,1,0:T(8,128)(2,1)} %constant_dynamic-update-slice_fusion.5.refs_0_.refs_1_, bf16[64,192,128]{2,1,0:T(8,128)(2,1)} %constant_dynamic-update-slice_fusion.5.refs_0_.refs_1_, bf16[64,192,128]{2,1,0:T(8,128)(2,1)} %collective-permute-done.3.refs_2_.refs_3_, ...), custom_call_target="tpu_custom_call" | custom-call | flops 1207959552 | bytes 3145728 | tf_op jit(solution)/shard_map/project/pallas_call | solution.py:102
  393.6 11.7 %project.29 = bf16[16,8,32,384]{3,2,1,0:T(8,128)(2,1)} custom-call(s32[1]{0:T(128)} %bitcast.6.which, bf16[64,192,128]{2,1,0:T(8,128)(2,1)} %constant_dynamic-update-slice_fusion.4.refs_0_.refs_1_, bf16[64,192,128]{2,1,0:T(8,128)(2,1)} %constant_dynamic-update-slice_fusion.4.refs_0_.refs_1_, bf16[64,192,128]{2,1,0:T(8,128)(2,1)} %collective-permute-done.6.refs_2_.refs_3_, ...), custom_call_target="tpu_custom_call" | custom-call | flops 1207959552 | bytes 3145728 | tf_op jit(solution)/shard_map/project/pallas_call | solution.py:102
  441.1 11.8 %project.32 = bf16[16,8,32,384]{3,2,1,0:T(8,128)(2,1)} custom-call(s32[1]{0:T(128)} %bitcast.6.which, bf16[64,192,128]{2,1,0:T(8,128)(2,1)} %constant_dynamic-update-slice_fusion.3.refs_0_.refs_1_, bf16[64,192,128]{2,1,0:T(8,128)(2,1)} %constant_dynamic-update-slice_fusion.3.refs_0_.refs_1_, bf16[64,192,128]{2,1,0:T(8,128)(2,1)} %collective-permute-done.10.refs_2_.refs_3_, ...), custom_call_target="tpu_custom_call" | custom-call | flops 1207959552 | bytes 3145728 | tf_op jit(solution)/shard_map/project/pallas_call | solution.py:102
  465.4 11.6 %project.33 = bf16[16,8,32,384]{3,2,1,0:T(8,128)(2,1)} custom-call(s32[1]{0:T(128)} %bitcast.6.which, bf16[64,192,128]{2,1,0:T(8,128)(2,1)} %copy-done.12, bf16[64,192,128]{2,1,0:T(8,128)(2,1)} %copy-done.12, bf16[64,192,128]{2,1,0:T(8,128)(2,1)} %collective-permute-done.14.refs_2_.refs_3_, bf16[64,192,128]{2,1,0:T(8,128)(2,1)} %collective-permute-done.14.refs_2_.refs_3_, ...), custom_call_target="tpu_custom_call" | custom-call | flops 1207959552 | bytes 3145728 | tf_op jit(solution)/shard_map/project/pallas_call | solution.py:102
  477.0 14.6 %triangle.25.own = bf16[7,32,32,128]{3,2,1,0:T(8,128)(2,1)S(1)} custom-call(s32[1]{0:T(128)} %constant.33.clone.1.which, bf16[128,32,384]{2,1,0:T(8,128)(2,1)} %bitcast.44, bf16[128,32,384]{2,1,0:T(8,128)(2,1)} %bitcast.54, bf16[128,32,384]{2,1,0:T(8,128)(2,1)} %bitcast.62, bf16[128,32,384]{2,1,0:T(8,128)(2,1)} %bitcast.80, bf16[128,32,384]{2,1,0:T(8,128)(2,1)} %bitcast.75, ...), custom_call_target="tpu_custom_call" | custom-call | flops 704643072 | bytes 27000832 | tf_op jit(solution)/shard_map/triangle/pallas_call | solution.py:154
  491.6 14.3 %triangle.26 = bf16[6,32,32,128]{3,2,1,0:T(8,128)(2,1)} custom-call(s32[1]{0:T(128)} %constant.33.clone.1.which, bf16[128,32,384]{2,1,0:T(8,128)(2,1)} %bitcast.116, bf16[128,32,384]{2,1,0:T(8,128)(2,1)} %bitcast.71, bf16[128,32,384]{2,1,0:T(8,128)(2,1)} %bitcast.88, bf16[128,32,384]{2,1,0:T(8,128)(2,1)} %bitcast.97, bf16[128,32,384]{2,1,0:T(8,128)(2,1)} %bitcast.108, ...), custom_call_target="tpu_custom_call" | custom-call | flops 603979776 | bytes 23592960 | tf_op jit(solution)/shard_map/triangle/pallas_call | solution.py:154
  505.8 14.6 %collective-permute-done.22.sent = bf16[9,32,32,128]{3,2,1,0:T(8,128)(2,1)} collective-permute-done((bf16[9,32,32,128]{3,2,1,0:T(8,128)(2,1)}, bf16[9,32,32,128]{3,2,1,0:T(8,128)(2,1)}, u32[]{:S(2)}, u32[]{:S(2)}) %collective-permute-start.22) | collective-permute-done | bytes 2359328 | tf_op jit(solution)/shard_map/ppermute | solution.py:430
  520.5 12.1 %triangle.22 = bf16[5,32,32,128]{3,2,1,0:T(8,128)(2,1)} custom-call(s32[1]{0:T(128)} %constant.33.clone.1.which, bf16[128,32,384]{2,1,0:T(8,128)(2,1)} %bitcast.45, bf16[128,32,384]{2,1,0:T(8,128)(2,1)} %bitcast.55, bf16[128,32,384]{2,1,0:T(8,128)(2,1)} %bitcast.63, bf16[128,32,384]{2,1,0:T(8,128)(2,1)} %bitcast.81, bf16[128,32,384]{2,1,0:T(8,128)(2,1)} %bitcast.103, ...), custom_call_target="tpu_custom_call" | custom-call | flops 503316480 | bytes 20185088 | tf_op jit(solution)/shard_map/triangle/pallas_call | solution.py:154
  553.9 11.6 %project.34 = bf16[16,8,32,384]{3,2,1,0:T(8,128)(2,1)} custom-call(s32[1]{0:T(128)} %bitcast.6.which, bf16[64,192,128]{2,1,0:T(8,128)(2,1)} %constant_dynamic-update-slice_fusion.1.refs_0_.refs_1_, bf16[64,192,128]{2,1,0:T(8,128)(2,1)} %constant_dynamic-update-slice_fusion.1.refs_0_.refs_1_, bf16[64,192,128]{2,1,0:T(8,128)(2,1)} %collective-permute-done.18.refs_2_.refs_3_, ...), custom_call_target="tpu_custom_call" | custom-call | flops 1207959552 | bytes 3145728 | tf_op jit(solution)/shard_map/project/pallas_call | solution.py:102
  565.5 18.1 %triangle.23.own = bf16[9,32,32,128]{3,2,1,0:T(8,128)(2,1)} custom-call(s32[1]{0:T(128)} %constant.33.clone.1.which, bf16[128,32,384]{2,1,0:T(8,128)(2,1)} %bitcast.46, bf16[128,32,384]{2,1,0:T(8,128)(2,1)} %bitcast.56, bf16[128,32,384]{2,1,0:T(8,128)(2,1)} %bitcast.64, bf16[128,32,384]{2,1,0:T(8,128)(2,1)} %bitcast.82, bf16[128,32,384]{2,1,0:T(8,128)(2,1)} %bitcast.104, ...), custom_call_target="tpu_custom_call" | custom-call | flops 905969664 | bytes 33816576 | tf_op jit(solution)/shard_map/triangle/pallas_call | solution.py:154
  583.6 11.7 %project.35 = bf16[16,8,32,384]{3,2,1,0:T(8,128)(2,1)} custom-call(s32[1]{0:T(128)} %bitcast.6.which, bf16[64,192,128]{2,1,0:T(8,128)(2,1)} %constant_dynamic-update-slice_fusion.refs_0_.refs_1_, bf16[64,192,128]{2,1,0:T(8,128)(2,1)} %constant_dynamic-update-slice_fusion.refs_0_.refs_1_, bf16[64,192,128]{2,1,0:T(8,128)(2,1)} %copy-done.14, ...), custom_call_target="tpu_custom_call" | custom-call | flops 1207959552 | bytes 3145728 | tf_op jit(solution)/shard_map/project/pallas_call | solution.py:102
  604.1 11.6 %finish.10.refs_0_ = bf16[192,192,128]{2,1,0:T(8,128)(2,1)} custom-call(bf16[7,32,32,128]{3,2,1,0:T(8,128)(2,1)S(1)} %triangle.25.own, bf16[7,32,32,128]{3,2,1,0:T(8,128)(2,1)} %collective-permute-done.20.sent, bf16[192,192,128]{2,1,0:T(8,128)(2,1)} %gate.1, bf16[128,128]{1,0:T(8,128)(2,1)S(1)} %bitcast.30, ...), custom_call_target="tpu_custom_call", output_to_operand_aliasing={{}: (6, {})} | custom-call | flops 234881024 | bytes 3670016 | tf_op jit(solution)/shard_map/finish/pallas_call | solution.py:249
  615.7 14.5 %finish.11.refs_0_ = bf16[192,192,128]{2,1,0:T(8,128)(2,1)} custom-call(bf16[9,32,32,128]{3,2,1,0:T(8,128)(2,1)} %triangle.23.own, bf16[9,32,32,128]{3,2,1,0:T(8,128)(2,1)} %collective-permute-done.22.sent, bf16[192,192,128]{2,1,0:T(8,128)(2,1)} %gate.1, bf16[128,128]{1,0:T(8,128)(2,1)S(1)} %bitcast.31, ...), custom_call_target="tpu_custom_call", output_to_operand_aliasing={{}: (6, {})} | custom-call | flops 301989888 | bytes 4718592 | tf_op jit(solution)/shard_map/finish/pallas_call | solution.py:249
  641.5 13.5 %triangle.27.own = bf16[6,32,32,128]{3,2,1,0:T(8,128)(2,1)S(1)} custom-call(s32[1]{0:T(128)} %constant.33.clone.1.which, bf16[128,32,384]{2,1,0:T(8,128)(2,1)} %bitcast.117, bf16[128,32,384]{2,1,0:T(8,128)(2,1)} %bitcast.77, bf16[128,32,384]{2,1,0:T(8,128)(2,1)} %bitcast.93, bf16[128,32,384]{2,1,0:T(8,128)(2,1)} %bitcast.101, ...), custom_call_target="tpu_custom_call" | custom-call | flops 603979776 | bytes 23592960 | tf_op jit(solution)/shard_map/triangle/pallas_call | solution.py:154
  (139 shorter events, 315.2 us)
Async XLA Ops:
  1.5 41.2 %collective-permute-start = (bf16[32,192,128]{2,1,0:T(8,128)(2,1)S(1)}, bf16[32,192,128]{2,1,0:T(8,128)(2,1)S(1)}, u32[]{:S(2)}, u32[]{:S(2)}) collective-permute-start(bf16[32,192,128]{2,1,0:T(8,128)(2,1)S(1)} %slice.28), channel_id=1, source_target_pairs={{0,1},{1,0},{2,3},{3,2},{4,5},{5,4},{6,7},{7,6},{8,9},{9,8},{10,11... | collective-permute-start | bytes 4718600 | tf_op jit(solution)/shard_map/ppermute | solution.py:389
  44.0 40.5 %collective-permute-start.2 = (bf16[64,192,128]{2,1,0:T(8,128)(2,1)}, bf16[64,192,128]{2,1,0:T(8,128)(2,1)}, u32[]{:S(2)}, u32[]{:S(2)}) collective-permute-start(bf16[64,192,128]{2,1,0:T(8,128)(2,1)} %constant_dynamic-update-slice_fusion.5.refs_0_.refs_1_), channel_id=1, source_target_pairs={{0,12},{2,14},{5,9},{7,11},{8,4},{10,6},{13,1},{15,3},{16,28},{18,... | collective-permute-start | bytes 9437192 | tf_op jit(solution)/shard_map/ppermute | solution.py:332
  48.2 36.3 %collective-permute-start.1 = (bf16[32,192,128]{2,1,0:T(8,128)(2,1)}, bf16[32,192,128]{2,1,0:T(8,128)(2,1)}, u32[]{:S(2)}, u32[]{:S(2)}) collective-permute-start(bf16[32,192,128]{2,1,0:T(8,128)(2,1)} %get-tuple-element.64), channel_id=1, source_target_pairs={{0,1},{1,0},{2,3},{3,2},{4,5},{5,4},{6,7},{7,6},{8,9},{9,8},{10,11... | collective-permute-start | bytes 4718600 | tf_op jit(solution)/shard_map/ppermute | solution.py:389
  88.4 20.9 %collective-permute-start.3 = (bf16[64,192,128]{2,1,0:T(8,128)(2,1)}, bf16[64,192,128]{2,1,0:T(8,128)(2,1)}, u32[]{:S(2)}, u32[]{:S(2)}) collective-permute-start(bf16[64,192,128]{2,1,0:T(8,128)(2,1)} %broadcast_select_fusion.5), channel_id=1, source_target_pairs={{0,4},{4,0},{8,12},{12,8},{1,5},{5,1},{9,13},{13,9},{2,6},{6,2},{1... | collective-permute-start | bytes 9437192 | tf_op jit(solution)/shard_map/ppermute | solution.py:340
  91.1 40.4 %collective-permute-start.5 = (bf16[64,192,128]{2,1,0:T(8,128)(2,1)}, bf16[64,192,128]{2,1,0:T(8,128)(2,1)}, u32[]{:S(2)}, u32[]{:S(2)}) collective-permute-start(bf16[64,192,128]{2,1,0:T(8,128)(2,1)} %constant_dynamic-update-slice_fusion.4.refs_0_.refs_1_), channel_id=1, source_target_pairs={{0,12},{2,14},{5,9},{7,11},{8,4},{10,6},{13,1},{15,3},{16,28},{18,... | collective-permute-start | bytes 9437192 | tf_op jit(solution)/shard_map/ppermute | solution.py:332
  94.7 36.7 %collective-permute-start.4 = (bf16[32,192,128]{2,1,0:T(8,128)(2,1)}, bf16[32,192,128]{2,1,0:T(8,128)(2,1)}, u32[]{:S(2)}, u32[]{:S(2)}) collective-permute-start(bf16[32,192,128]{2,1,0:T(8,128)(2,1)} %get-tuple-element.65), channel_id=1, source_target_pairs={{0,1},{1,0},{2,3},{3,2},{4,5},{5,4},{6,7},{7,6},{8,9},{9,8},{10,11... | collective-permute-start | bytes 4718600 | tf_op jit(solution)/shard_map/ppermute | solution.py:389
  135.3 21.2 %collective-permute-start.6 = (bf16[64,192,128]{2,1,0:T(8,128)(2,1)}, bf16[64,192,128]{2,1,0:T(8,128)(2,1)}, u32[]{:S(2)}, u32[]{:S(2)}) collective-permute-start(bf16[64,192,128]{2,1,0:T(8,128)(2,1)} %broadcast_select_fusion.4), channel_id=1, source_target_pairs={{0,4},{4,0},{8,12},{12,8},{1,5},{5,1},{9,13},{13,9},{2,6},{6,2},{1... | collective-permute-start | bytes 9437192 | tf_op jit(solution)/shard_map/ppermute | solution.py:340
  138.1 46.7 %collective-permute-start.9 = (bf16[64,192,128]{2,1,0:T(8,128)(2,1)}, bf16[64,192,128]{2,1,0:T(8,128)(2,1)}, u32[]{:S(2)}, u32[]{:S(2)}) collective-permute-start(bf16[64,192,128]{2,1,0:T(8,128)(2,1)} %constant_dynamic-update-slice_fusion.3.refs_0_.refs_1_), channel_id=1, source_target_pairs={{0,12},{2,14},{5,9},{7,11},{8,4},{10,6},{13,1},{15,3},{16,28},{18,... | collective-permute-start | bytes 9437192 | tf_op jit(solution)/shard_map/ppermute | solution.py:332
  142.8 41.9 %collective-permute-start.7 = (bf16[32,192,128]{2,1,0:T(8,128)(2,1)S(1)}, bf16[32,192,128]{2,1,0:T(8,128)(2,1)}, u32[]{:S(2)}, u32[]{:S(2)}) collective-permute-start(bf16[32,192,128]{2,1,0:T(8,128)(2,1)S(1)} %copy-done.16), channel_id=1, source_target_pairs={{0,1},{1,0},{2,3},{3,2},{4,5},{5,4},{6,7},{7,6},{8,9},{9,8},{10,11... | collective-permute-start | bytes 4718600 | tf_op jit(solution)/shard_map/ppermute | solution.py:389
  142.8 39.8 %collective-permute-start.8 = (bf16[1,32,32,128]{3,2,1,0:T(8,128)(2,1)S(1)}, bf16[1,32,32,128]{3,2,1,0:T(8,128)(2,1)S(1)}, u32[]{:S(2)}, u32[]{:S(2)}) collective-permute-start(bf16[1,32,32,128]{3,2,1,0:T(8,128)(2,1)S(1)} %triangle.14), channel_id=1, source_target_pairs={{0,2},{1,3},{2,0},{3,1},{4,6},{5,7},{6,4},{7,5},{8,10},{9,11},{10,... | collective-permute-start | bytes 786440 | tf_op jit(solution)/shard_map/ppermute | solution.py:430
  188.7 21.1 %collective-permute-start.10 = (bf16[64,192,128]{2,1,0:T(8,128)(2,1)}, bf16[64,192,128]{2,1,0:T(8,128)(2,1)}, u32[]{:S(2)}, u32[]{:S(2)}) collective-permute-start(bf16[64,192,128]{2,1,0:T(8,128)(2,1)} %broadcast_select_fusion.3), channel_id=1, source_target_pairs={{0,4},{4,0},{8,12},{12,8},{1,5},{5,1},{9,13},{13,9},{2,6},{6,2},{1... | collective-permute-start | bytes 9437192 | tf_op jit(solution)/shard_map/ppermute | solution.py:340
  190.4 57.5 %collective-permute-start.13 = (bf16[64,192,128]{2,1,0:T(8,128)(2,1)S(1)}, bf16[64,192,128]{2,1,0:T(8,128)(2,1)}, u32[]{:S(2)}, u32[]{:S(2)}) collective-permute-start(bf16[64,192,128]{2,1,0:T(8,128)(2,1)S(1)} %constant_dynamic-update-slice_fusion.2.refs_0_.refs_1_), channel_id=1, source_target_pairs={{0,12},{2,14},{5,9},{7,11},{8,4},{10,6},{13,1},{15,3},{16,28},{18,... | collective-permute-start | bytes 9437192 | tf_op jit(solution)/shard_map/ppermute | solution.py:332
  194.3 53.7 %collective-permute-start.11 = (bf16[32,192,128]{2,1,0:T(8,128)(2,1)S(1)}, bf16[32,192,128]{2,1,0:T(8,128)(2,1)}, u32[]{:S(2)}, u32[]{:S(2)}) collective-permute-start(bf16[32,192,128]{2,1,0:T(8,128)(2,1)S(1)} %copy-done.15), channel_id=1, source_target_pairs={{0,1},{1,0},{2,3},{3,2},{4,5},{5,4},{6,7},{7,6},{8,9},{9,8},{10,11... | collective-permute-start | bytes 4718600 | tf_op jit(solution)/shard_map/ppermute | solution.py:389
  194.9 49.7 %collective-permute-start.12 = (bf16[3,32,32,128]{3,2,1,0:T(8,128)(2,1)S(1)}, bf16[3,32,32,128]{3,2,1,0:T(8,128)(2,1)S(1)}, u32[]{:S(2)}, u32[]{:S(2)}) collective-permute-start(bf16[3,32,32,128]{3,2,1,0:T(8,128)(2,1)S(1)} %triangle.15), channel_id=1, source_target_pairs={{0,2},{1,3},{2,0},{3,1},{4,6},{5,7},{6,4},{7,5},{8,10},{9,11},{10,... | collective-permute-start | bytes 2359304 | tf_op jit(solution)/shard_map/ppermute | solution.py:430
  250.0 22.8 %collective-permute-start.14 = (bf16[64,192,128]{2,1,0:T(8,128)(2,1)}, bf16[64,192,128]{2,1,0:T(8,128)(2,1)}, u32[]{:S(2)}, u32[]{:S(2)}) collective-permute-start(bf16[64,192,128]{2,1,0:T(8,128)(2,1)} %broadcast_select_fusion.2), channel_id=1, source_target_pairs={{0,4},{4,0},{8,12},{12,8},{1,5},{5,1},{9,13},{13,9},{2,6},{6,2},{1... | collective-permute-start | bytes 9437192 | tf_op jit(solution)/shard_map/ppermute | solution.py:340
  254.9 68.3 %collective-permute-start.15 = (bf16[64,192,128]{2,1,0:T(8,128)(2,1)}, bf16[64,192,128]{2,1,0:T(8,128)(2,1)S(1)}, u32[]{:S(2)}, u32[]{:S(2)}) collective-permute-start(bf16[64,192,128]{2,1,0:T(8,128)(2,1)} %constant_dynamic-update-slice_fusion.1.refs_0_.refs_1_), channel_id=1, source_target_pairs={{0,12},{2,14},{5,9},{7,11},{8,4},{10,6},{13,1},{15,3},{16,28},{18,... | collective-permute-start | bytes 9437192 | tf_op jit(solution)/shard_map/ppermute | solution.py:332
  259.1 64.1 %collective-permute-start.16 = (bf16[32,192,128]{2,1,0:T(8,128)(2,1)S(1)}, bf16[32,192,128]{2,1,0:T(8,128)(2,1)S(1)}, u32[]{:S(2)}, u32[]{:S(2)}) collective-permute-start(bf16[32,192,128]{2,1,0:T(8,128)(2,1)S(1)} %get-tuple-element.84), channel_id=1, source_target_pairs={{0,1},{1,0},{2,3},{3,2},{4,5},{5,4},{6,7},{7,6},{8,9},{9,8},{10,11... | collective-permute-start | bytes 4718600 | tf_op jit(solution)/shard_map/ppermute | solution.py:389
  259.2 62.5 %collective-permute-start.17 = (bf16[5,32,32,128]{3,2,1,0:T(8,128)(2,1)S(1)}, bf16[5,32,32,128]{3,2,1,0:T(8,128)(2,1)}, u32[]{:S(2)}, u32[]{:S(2)}) collective-permute-start(bf16[5,32,32,128]{3,2,1,0:T(8,128)(2,1)S(1)} %triangle.16), channel_id=1, source_target_pairs={{0,2},{1,3},{2,0},{3,1},{4,6},{5,7},{6,4},{7,5},{8,10},{9,11},{10,... | collective-permute-start | bytes 3932168 | tf_op jit(solution)/shard_map/ppermute | solution.py:430
  328.4 18.1 %collective-permute-start.18 = (bf16[64,192,128]{2,1,0:T(8,128)(2,1)}, bf16[64,192,128]{2,1,0:T(8,128)(2,1)}, u32[]{:S(2)}, u32[]{:S(2)}) collective-permute-start(bf16[64,192,128]{2,1,0:T(8,128)(2,1)} %broadcast_select_fusion.1), channel_id=1, source_target_pairs={{0,4},{4,0},{8,12},{12,8},{1,5},{5,1},{9,13},{13,9},{2,6},{6,2},{1... | collective-permute-start | bytes 9437192 | tf_op jit(solution)/shard_map/ppermute | solution.py:340
  329.6 84.4 %collective-permute-start.19 = (bf16[64,192,128]{2,1,0:T(8,128)(2,1)}, bf16[64,192,128]{2,1,0:T(8,128)(2,1)}, u32[]{:S(2)}, u32[]{:S(2)}) collective-permute-start(bf16[64,192,128]{2,1,0:T(8,128)(2,1)} %constant_dynamic-update-slice_fusion.refs_0_.refs_1_), channel_id=1, source_target_pairs={{0,12},{2,14},{5,9},{7,11},{8,4},{10,6},{13,1},{15,3},{16,28},{18,... | collective-permute-start | bytes 9437192 | tf_op jit(solution)/shard_map/ppermute | solution.py:332
  333.9 80.1 %collective-permute-start.20 = (bf16[7,32,32,128]{3,2,1,0:T(8,128)(2,1)}, bf16[7,32,32,128]{3,2,1,0:T(8,128)(2,1)}, u32[]{:S(2)}, u32[]{:S(2)}) collective-permute-start(bf16[7,32,32,128]{3,2,1,0:T(8,128)(2,1)} %triangle.17), channel_id=1, source_target_pairs={{0,2},{1,3},{2,0},{3,1},{4,6},{5,7},{6,4},{7,5},{8,10},{9,11},{10,... | collective-permute-start | bytes 5505032 | tf_op jit(solution)/shard_map/ppermute | solution.py:430
  416.4 104.1 %collective-permute-start.22 = (bf16[9,32,32,128]{3,2,1,0:T(8,128)(2,1)}, bf16[9,32,32,128]{3,2,1,0:T(8,128)(2,1)}, u32[]{:S(2)}, u32[]{:S(2)}) collective-permute-start(bf16[9,32,32,128]{3,2,1,0:T(8,128)(2,1)} %triangle.18), channel_id=1, source_target_pairs={{0,2},{1,3},{2,0},{3,1},{4,6},{5,7},{6,4},{7,5},{8,10},{9,11},{10,... | collective-permute-start | bytes 7077896 | tf_op jit(solution)/shard_map/ppermute | solution.py:430
  520.5 134.5 %collective-permute-start.24 = (bf16[6,32,32,128]{3,2,1,0:T(8,128)(2,1)}, bf16[6,32,32,128]{3,2,1,0:T(8,128)(2,1)}, u32[]{:S(2)}, u32[]{:S(2)}) collective-permute-start(bf16[6,32,32,128]{3,2,1,0:T(8,128)(2,1)} %triangle.26), channel_id=1, source_target_pairs={{0,2},{1,3},{2,0},{3,1},{4,6},{5,7},{6,4},{7,5},{8,10},{9,11},{10,... | collective-permute-start | bytes 4718600 | tf_op jit(solution)/shard_map/ppermute | solution.py:430
  532.6 132.6 %collective-permute-start.23 = (bf16[5,32,32,128]{3,2,1,0:T(8,128)(2,1)}, bf16[5,32,32,128]{3,2,1,0:T(8,128)(2,1)}, u32[]{:S(2)}, u32[]{:S(2)}) collective-permute-start(bf16[5,32,32,128]{3,2,1,0:T(8,128)(2,1)} %triangle.22), channel_id=1, source_target_pairs={{0,2},{1,3},{2,0},{3,1},{4,6},{5,7},{6,4},{7,5},{8,10},{9,11},{10,... | collective-permute-start | bytes 3932168 | tf_op jit(solution)/shard_map/ppermute | solution.py:430
  (21 other events, 182.1 us)

commit v9 on v8

--- a/solution.py
+++ b/solution.py
@@ -120,14 +120,30 @@
 def triangle_kernel(n_left, n_sides, group, pairs, which, *refs):
     lefts, out = refs[:n_left], refs[-1]
     sides = refs[n_left:-1]
-    step = lefts[0].shape[0]
+    step, rows, _ = lefts[0].shape
+    columns = sides[0].shape[1]
 
     def go(choice):
+        def pieces_of(h):
+            found = {}
+            for j in sorted({j for _, j in pairs}):
+                same = [n for n, pair in enumerate(pairs) if pair[1] == j]
+                if len(same) > 1:
+                    rows_of = jnp.concatenate([lefts[pairs[n][0]][h] for n in same], axis=0)
+                    made = contract(rows_of, sides[j * n_sides + choice][h], 1, 1)
+                    found.update({n: made[p * rows : (p + 1) * rows] for p, n in enumerate(same)})
+            for i in sorted({i for i, _ in pairs}):
+                same = [n for n, pair in enumerate(pairs) if pair[0] == i and n not in found]
+                if same:
+                    columns_of = jnp.concatenate([sides[pairs[n][1] * n_sides + choice][h] for n in same], axis=0)
+                    made = contract(lefts[i][h], columns_of, 1, 1)
+                    found.update({n: made[:, p * columns : (p + 1) * columns] for p, n in enumerate(same)})
+            return found
+
         def one_group(g, carry):
-            for n, (i, j) in enumerate(pairs):
-                side = sides[j * n_sides + choice]
-                parts = [contract(lefts[i][g * group + h], side[g * group + h], 1, 1) for h in range(group)]
-                out[n, g] = jnp.concatenate(parts, axis=-1).astype(BF16)
+            found = [pieces_of(g * group + h) for h in range(group)]
+            for n in range(len(pairs)):
+                out[n, g] = jnp.concatenate([x[n] for x in found], axis=-1).astype(BF16)
             return carry
 
         lax.fori_loop(0, step // group, one_group, 0, unroll=2)
@@ -221,11 +237,16 @@
     scale = lax.rsqrt(over_hidden(centred * centred) + EPS)
     normed = centred * scale[None] * gain[...] + bias[...]
     rows_of[...] = normed.reshape(packed * rows, lanes)
-    for i in range(rows):
-        held = rows_of[pl.ds(i, packed, stride=rows), :]
-        parts = [held[:, g * columns : (g + 1) * columns] for g in range(group)]
+    batch = max(1, 128 // columns)
+    for first in range(0, rows, batch):
+        held = [rows_of[pl.ds(first + i, packed, stride=rows), :] for i in range(batch)]
+        parts = [
+            jnp.concatenate([x[:, g * columns : (g + 1) * columns] for x in held], axis=1) for g in range(group)
+        ]
         result = contract(jnp.concatenate(parts, axis=0).astype(BF16), weights[...], 0, 0)
-        out[i] = (result * gate[i].astype(F32)).astype(BF16)
+        for i in range(batch):
+            gated = result[i * columns : (i + 1) * columns] * gate[first + i].astype(F32)
+            out[first + i] = gated.astype(BF16)
 
 
 def finish(own, sent, gate, t, before, chunks, share, weights, gain, bias, held):

time: 685 us -> 671 us (0.980)
  Pallas kernels: 460 us -> 442 us
    pallas_call x14, Pallas kernels: 169 us -> 159 us  [triangle(): pl.pallas_call(functools.partial(triangle_kernel, len(lefts), n_sides, gr...]
    pallas_call x7, Pallas kernels: 62.9 us -> 53.6 us  [finish(): pl.pallas_call(functools.partial(finish_kernel, group, hidden), grid=(pie...]
  transfers between devices with their start and end apart: 25 -> 25, of which waited for: 9 -> 10; matrix products, arithmetic and copies ran while one was open for 6% -> 6% of each run, Pallas kernels for 67% -> 66%
where the time goes in v9:
time: 671 us; the launch traced here: 661 us
  Pallas kernels  442 us (66%)
  waiting for transfers between devices  107 us (16%)
  local copies, waits for them, and re-layouts  43.7 us (7%)
  starting transfers between devices  42.2 us (6%)
  other arithmetic  24.9 us (4%)
    pallas_call x18, Pallas kernels, project(): pl.pallas_call(functools.partial(project_kernel, n_pieces, len(slabs)), g...  203 us
    pallas_call x14, Pallas kernels, triangle(): pl.pallas_call(functools.partial(triangle_kernel, len(lefts), n_sides, gr...  159 us
    ppermute x7, waiting for transfers between devices, on_device(): lax.ppermute(after(x, *waits) if waits else x, 'col', swap_half)  59.6 us
    pallas_call x7, Pallas kernels, finish(): pl.pallas_call(functools.partial(finish_kernel, group, hidden), grid=(pie...  53.6 us
    ppermute x6, waiting for transfers between devices, exchange(): lax.ppermute(block, 'col', [(c, c ^ o) for c in range(n_col)])  47.7 us
    pallas_call x1, Pallas kernels, gate_of(): pl.pallas_call(gate_kernel, grid=(count // rows,), in_specs=[block] + [wh...  25.2 us
    ppermute x6, starting transfers between devices, first_step(): return lax.ppermute(slab, axes, pairs)  24.9 us
    select_n x6, other arithmetic, second_step(): given = jnp.where(holder, slab, after(far, *waits))  21 us
  transfers between devices with their start and end apart: 25, of which 10 were waited for; matrix products, arithmetic and copies ran while one was open for 6% of the time, Pallas kernels for 66%

profile of v9, /device:TPU:0, one launch (start us, length us, event | category | flops | bytes accessed | tf_op | source)
XLA Modules:
  0.0 660.6 jit_solution(2121699124951250508)
XLA Ops:
  17.5 25.2 %gate.1 = bf16[192,192,128]{2,1,0:T(8,128)(2,1)} custom-call(bf16[192,192,128]{2,1,0:T(8,128)(2,1)} %pair.1, bf16[128,128]{1,0:T(8,128)(2,1)S(1)} %add_convert_fusion.centre.refs_3_.refs_7_, bf16[256,128]{1,0:T(8,128)(2,1)S(1)} %broadcast_in_dim.27.mean, f32[1,128]{1,0:T(1,128)S(1)} %bitcast.34, f32[1,128]{1,0:T(1,128)S(1)} %bitcast.35, ...), custom_call_target="tpu_custom_call" | custom-call | flops 4831838208 | bytes 18874368 | tf_op jit(solution)/shard_map/gate/pallas_call | solution.py:208
  48.2 36.3 %collective-permute-done.1 = bf16[32,192,128]{2,1,0:T(8,128)(2,1)} collective-permute-done((bf16[32,192,128]{2,1,0:T(8,128)(2,1)}, bf16[32,192,128]{2,1,0:T(8,128)(2,1)}, u32[]{:S(2)}, u32[]{:S(2)}) %collective-permute-start.1) | collective-permute-done | bytes 1572896 | tf_op jit(solution)/shard_map/ppermute | solution.py:410
  109.3 11.7 %project.19 = bf16[16,8,32,384]{3,2,1,0:T(8,128)(2,1)} custom-call(s32[1]{0:T(128)} %bitcast.4.which, bf16[64,192,128]{2,1,0:T(8,128)(2,1)} %constant_dynamic-update-slice_fusion.5.refs_0_.refs_1_, bf16[64,192,128]{2,1,0:T(8,128)(2,1)} %constant_dynamic-update-slice_fusion.5.refs_0_.refs_1_, bf16[64,192,128]{2,1,0:T(8,128)(2,1)} %collective-permute-done.3.refs_2_.refs_3_, ...), custom_call_target="tpu_custom_call" | custom-call | flops 1207959552 | bytes 3145728 | tf_op jit(solution)/shard_map/project/pallas_call | solution.py:102
  156.5 11.6 %project.21 = bf16[16,8,32,384]{3,2,1,0:T(8,128)(2,1)} custom-call(s32[1]{0:T(128)} %bitcast.4.which, bf16[64,192,128]{2,1,0:T(8,128)(2,1)} %constant_dynamic-update-slice_fusion.4.refs_0_.refs_1_, bf16[64,192,128]{2,1,0:T(8,128)(2,1)} %constant_dynamic-update-slice_fusion.4.refs_0_.refs_1_, bf16[64,192,128]{2,1,0:T(8,128)(2,1)} %collective-permute-done.6.refs_2_.refs_3_, ...), custom_call_target="tpu_custom_call" | custom-call | flops 1207959552 | bytes 3145728 | tf_op jit(solution)/shard_map/project/pallas_call | solution.py:102
  209.8 11.6 %project.23 = bf16[16,8,32,384]{3,2,1,0:T(8,128)(2,1)} custom-call(s32[1]{0:T(128)} %bitcast.4.which, bf16[64,192,128]{2,1,0:T(8,128)(2,1)} %constant_dynamic-update-slice_fusion.3.refs_0_.refs_1_, bf16[64,192,128]{2,1,0:T(8,128)(2,1)} %constant_dynamic-update-slice_fusion.3.refs_0_.refs_1_, bf16[64,192,128]{2,1,0:T(8,128)(2,1)} %collective-permute-done.10.refs_2_.refs_3_, ...), custom_call_target="tpu_custom_call" | custom-call | flops 1207959552 | bytes 3145728 | tf_op jit(solution)/shard_map/project/pallas_call | solution.py:102
  231.8 12.8 %collective-permute-done.12.sent = bf16[3,32,32,128]{3,2,1,0:T(8,128)(2,1)S(1)} collective-permute-done((bf16[3,32,32,128]{3,2,1,0:T(8,128)(2,1)S(1)}, bf16[3,32,32,128]{3,2,1,0:T(8,128)(2,1)S(1)}, u32[]{:S(2)}, u32[]{:S(2)}) %collective-permute-start.12) | collective-permute-done | bytes 786464 | tf_op jit(solution)/shard_map/ppermute | solution.py:451
  272.8 11.6 %project.25 = bf16[16,8,32,384]{3,2,1,0:T(8,128)(2,1)} custom-call(s32[1]{0:T(128)} %bitcast.4.which, bf16[64,192,128]{2,1,0:T(8,128)(2,1)} %copy-done.12, bf16[64,192,128]{2,1,0:T(8,128)(2,1)} %copy-done.12, bf16[64,192,128]{2,1,0:T(8,128)(2,1)} %collective-permute-done.14.refs_2_.refs_3_, bf16[64,192,128]{2,1,0:T(8,128)(2,1)} %collective-permute-done.14.refs_2_.refs_3_, ...), custom_call_target="tpu_custom_call" | custom-call | flops 1207959552 | bytes 3145728 | tf_op jit(solution)/shard_map/project/pallas_call | solution.py:102
  284.4 14.2 %triangle.17 = bf16[7,32,32,128]{3,2,1,0:T(8,128)(2,1)} custom-call(s32[1]{0:T(128)} %constant.33.clone.1.which, bf16[128,32,384]{2,1,0:T(8,128)(2,1)} %bitcast.39, bf16[128,32,384]{2,1,0:T(8,128)(2,1)} %bitcast.50, bf16[128,32,384]{2,1,0:T(8,128)(2,1)} %bitcast.59, bf16[128,32,384]{2,1,0:T(8,128)(2,1)} %bitcast.78, bf16[128,32,384]{2,1,0:T(8,128)(2,1)} %bitcast.69, ...), custom_call_target="tpu_custom_call" | custom-call | flops 704643072 | bytes 27000832 | tf_op jit(solution)/shard_map/triangle/pallas_call | solution.py:170
  298.6 23.1 %collective-permute-done.17.sent = bf16[5,32,32,128]{3,2,1,0:T(8,128)(2,1)} collective-permute-done((bf16[5,32,32,128]{3,2,1,0:T(8,128)(2,1)S(1)}, bf16[5,32,32,128]{3,2,1,0:T(8,128)(2,1)}, u32[]{:S(2)}, u32[]{:S(2)}) %collective-permute-start.17) | collective-permute-done | bytes 1310752 | tf_op jit(solution)/shard_map/ppermute | solution.py:451
  346.4 11.7 %project.27 = bf16[16,8,32,384]{3,2,1,0:T(8,128)(2,1)} custom-call(s32[1]{0:T(128)} %bitcast.4.which, bf16[64,192,128]{2,1,0:T(8,128)(2,1)} %constant_dynamic-update-slice_fusion.1.refs_0_.refs_1_, bf16[64,192,128]{2,1,0:T(8,128)(2,1)} %constant_dynamic-update-slice_fusion.1.refs_0_.refs_1_, bf16[64,192,128]{2,1,0:T(8,128)(2,1)} %collective-permute-done.18.refs_2_.refs_3_, ...), custom_call_target="tpu_custom_call" | custom-call | flops 1207959552 | bytes 3145728 | tf_op jit(solution)/shard_map/project/pallas_call | solution.py:102
  358.1 15.9 %triangle.18 = bf16[9,32,32,128]{3,2,1,0:T(8,128)(2,1)} custom-call(s32[1]{0:T(128)} %constant.33.clone.1.which, bf16[128,32,384]{2,1,0:T(8,128)(2,1)} %bitcast.40, bf16[128,32,384]{2,1,0:T(8,128)(2,1)} %bitcast.51, bf16[128,32,384]{2,1,0:T(8,128)(2,1)} %bitcast.60, bf16[128,32,384]{2,1,0:T(8,128)(2,1)} %bitcast.79, bf16[128,32,384]{2,1,0:T(8,128)(2,1)} %bitcast.102, ...), custom_call_target="tpu_custom_call" | custom-call | flops 905969664 | bytes 33816576 | tf_op jit(solution)/shard_map/triangle/pallas_call | solution.py:170
  374.0 11.6 %project.28 = bf16[16,8,32,384]{3,2,1,0:T(8,128)(2,1)} custom-call(s32[1]{0:T(128)} %bitcast.6.which, bf16[64,192,128]{2,1,0:T(8,128)(2,1)} %constant_dynamic-update-slice_fusion.5.refs_0_.refs_1_, bf16[64,192,128]{2,1,0:T(8,128)(2,1)} %constant_dynamic-update-slice_fusion.5.refs_0_.refs_1_, bf16[64,192,128]{2,1,0:T(8,128)(2,1)} %collective-permute-done.3.refs_2_.refs_3_, ...), custom_call_target="tpu_custom_call" | custom-call | flops 1207959552 | bytes 3145728 | tf_op jit(solution)/shard_map/project/pallas_call | solution.py:102
  391.7 11.7 %project.29 = bf16[16,8,32,384]{3,2,1,0:T(8,128)(2,1)} custom-call(s32[1]{0:T(128)} %bitcast.6.which, bf16[64,192,128]{2,1,0:T(8,128)(2,1)} %constant_dynamic-update-slice_fusion.4.refs_0_.refs_1_, bf16[64,192,128]{2,1,0:T(8,128)(2,1)} %constant_dynamic-update-slice_fusion.4.refs_0_.refs_1_, bf16[64,192,128]{2,1,0:T(8,128)(2,1)} %collective-permute-done.6.refs_2_.refs_3_, ...), custom_call_target="tpu_custom_call" | custom-call | flops 1207959552 | bytes 3145728 | tf_op jit(solution)/shard_map/project/pallas_call | solution.py:102
  427.4 11.5 %project.31 = bf16[16,8,32,384]{3,2,1,0:T(8,128)(2,1)} custom-call(s32[1]{0:T(128)} %bitcast.4.which, bf16[64,192,128]{2,1,0:T(8,128)(2,1)} %constant_dynamic-update-slice_fusion.refs_0_.refs_1_, bf16[64,192,128]{2,1,0:T(8,128)(2,1)} %constant_dynamic-update-slice_fusion.refs_0_.refs_1_, bf16[64,192,128]{2,1,0:T(8,128)(2,1)} %copy-done.14, ...), custom_call_target="tpu_custom_call" | custom-call | flops 1207959552 | bytes 3145728 | tf_op jit(solution)/shard_map/project/pallas_call | solution.py:102
  438.9 11.8 %project.32 = bf16[16,8,32,384]{3,2,1,0:T(8,128)(2,1)} custom-call(s32[1]{0:T(128)} %bitcast.6.which, bf16[64,192,128]{2,1,0:T(8,128)(2,1)} %constant_dynamic-update-slice_fusion.3.refs_0_.refs_1_, bf16[64,192,128]{2,1,0:T(8,128)(2,1)} %constant_dynamic-update-slice_fusion.3.refs_0_.refs_1_, bf16[64,192,128]{2,1,0:T(8,128)(2,1)} %collective-permute-done.10.refs_2_.refs_3_, ...), custom_call_target="tpu_custom_call" | custom-call | flops 1207959552 | bytes 3145728 | tf_op jit(solution)/shard_map/project/pallas_call | solution.py:102
  462.2 11.6 %project.33 = bf16[16,8,32,384]{3,2,1,0:T(8,128)(2,1)} custom-call(s32[1]{0:T(128)} %bitcast.6.which, bf16[64,192,128]{2,1,0:T(8,128)(2,1)} %copy-done.12, bf16[64,192,128]{2,1,0:T(8,128)(2,1)} %copy-done.12, bf16[64,192,128]{2,1,0:T(8,128)(2,1)} %collective-permute-done.14.refs_2_.refs_3_, bf16[64,192,128]{2,1,0:T(8,128)(2,1)} %collective-permute-done.14.refs_2_.refs_3_, ...), custom_call_target="tpu_custom_call" | custom-call | flops 1207959552 | bytes 3145728 | tf_op jit(solution)/shard_map/project/pallas_call | solution.py:102
  473.8 13.3 %triangle.25.own = bf16[7,32,32,128]{3,2,1,0:T(8,128)(2,1)S(1)} custom-call(s32[1]{0:T(128)} %constant.33.clone.1.which, bf16[128,32,384]{2,1,0:T(8,128)(2,1)} %bitcast.44, bf16[128,32,384]{2,1,0:T(8,128)(2,1)} %bitcast.54, bf16[128,32,384]{2,1,0:T(8,128)(2,1)} %bitcast.62, bf16[128,32,384]{2,1,0:T(8,128)(2,1)} %bitcast.80, bf16[128,32,384]{2,1,0:T(8,128)(2,1)} %bitcast.75, ...), custom_call_target="tpu_custom_call" | custom-call | flops 704643072 | bytes 27000832 | tf_op jit(solution)/shard_map/triangle/pallas_call | solution.py:170
  487.1 14.8 %triangle.26 = bf16[6,32,32,128]{3,2,1,0:T(8,128)(2,1)} custom-call(s32[1]{0:T(128)} %constant.33.clone.1.which, bf16[128,32,384]{2,1,0:T(8,128)(2,1)} %bitcast.116, bf16[128,32,384]{2,1,0:T(8,128)(2,1)} %bitcast.71, bf16[128,32,384]{2,1,0:T(8,128)(2,1)} %bitcast.88, bf16[128,32,384]{2,1,0:T(8,128)(2,1)} %bitcast.97, bf16[128,32,384]{2,1,0:T(8,128)(2,1)} %bitcast.108, ...), custom_call_target="tpu_custom_call" | custom-call | flops 603979776 | bytes 23592960 | tf_op jit(solution)/shard_map/triangle/pallas_call | solution.py:170
  501.9 17.1 %collective-permute-done.22.sent = bf16[9,32,32,128]{3,2,1,0:T(8,128)(2,1)} collective-permute-done((bf16[9,32,32,128]{3,2,1,0:T(8,128)(2,1)}, bf16[9,32,32,128]{3,2,1,0:T(8,128)(2,1)}, u32[]{:S(2)}, u32[]{:S(2)}) %collective-permute-start.22) | collective-permute-done | bytes 2359328 | tf_op jit(solution)/shard_map/ppermute | solution.py:451
  550.6 11.6 %project.34 = bf16[16,8,32,384]{3,2,1,0:T(8,128)(2,1)} custom-call(s32[1]{0:T(128)} %bitcast.6.which, bf16[64,192,128]{2,1,0:T(8,128)(2,1)} %constant_dynamic-update-slice_fusion.1.refs_0_.refs_1_, bf16[64,192,128]{2,1,0:T(8,128)(2,1)} %constant_dynamic-update-slice_fusion.1.refs_0_.refs_1_, bf16[64,192,128]{2,1,0:T(8,128)(2,1)} %collective-permute-done.18.refs_2_.refs_3_, ...), custom_call_target="tpu_custom_call" | custom-call | flops 1207959552 | bytes 3145728 | tf_op jit(solution)/shard_map/project/pallas_call | solution.py:102
  562.2 15.9 %triangle.23.own = bf16[9,32,32,128]{3,2,1,0:T(8,128)(2,1)} custom-call(s32[1]{0:T(128)} %constant.33.clone.1.which, bf16[128,32,384]{2,1,0:T(8,128)(2,1)} %bitcast.46, bf16[128,32,384]{2,1,0:T(8,128)(2,1)} %bitcast.56, bf16[128,32,384]{2,1,0:T(8,128)(2,1)} %bitcast.64, bf16[128,32,384]{2,1,0:T(8,128)(2,1)} %bitcast.82, bf16[128,32,384]{2,1,0:T(8,128)(2,1)} %bitcast.104, ...), custom_call_target="tpu_custom_call" | custom-call | flops 905969664 | bytes 33816576 | tf_op jit(solution)/shard_map/triangle/pallas_call | solution.py:170
  578.1 12.0 %project.35 = bf16[16,8,32,384]{3,2,1,0:T(8,128)(2,1)} custom-call(s32[1]{0:T(128)} %bitcast.6.which, bf16[64,192,128]{2,1,0:T(8,128)(2,1)} %constant_dynamic-update-slice_fusion.refs_0_.refs_1_, bf16[64,192,128]{2,1,0:T(8,128)(2,1)} %constant_dynamic-update-slice_fusion.refs_0_.refs_1_, bf16[64,192,128]{2,1,0:T(8,128)(2,1)} %copy-done.14, ...), custom_call_target="tpu_custom_call" | custom-call | flops 1207959552 | bytes 3145728 | tf_op jit(solution)/shard_map/project/pallas_call | solution.py:102
  607.3 12.3 %finish.11.refs_0_ = bf16[192,192,128]{2,1,0:T(8,128)(2,1)} custom-call(bf16[9,32,32,128]{3,2,1,0:T(8,128)(2,1)} %triangle.23.own, bf16[9,32,32,128]{3,2,1,0:T(8,128)(2,1)} %collective-permute-done.22.sent, bf16[192,192,128]{2,1,0:T(8,128)(2,1)} %gate.1, bf16[128,128]{1,0:T(8,128)(2,1)S(1)} %bitcast.31, ...), custom_call_target="tpu_custom_call", output_to_operand_aliasing={{}: (6, {})} | custom-call | flops 301989888 | bytes 4718592 | tf_op jit(solution)/shard_map/finish/pallas_call | solution.py:270
  630.0 14.0 %triangle.27.own = bf16[6,32,32,128]{3,2,1,0:T(8,128)(2,1)S(1)} custom-call(s32[1]{0:T(128)} %constant.33.clone.1.which, bf16[128,32,384]{2,1,0:T(8,128)(2,1)} %bitcast.117, bf16[128,32,384]{2,1,0:T(8,128)(2,1)} %bitcast.77, bf16[128,32,384]{2,1,0:T(8,128)(2,1)} %bitcast.93, bf16[128,32,384]{2,1,0:T(8,128)(2,1)} %bitcast.101, ...), custom_call_target="tpu_custom_call" | custom-call | flops 603979776 | bytes 23592960 | tf_op jit(solution)/shard_map/triangle/pallas_call | solution.py:170
  (139 shorter events, 304.9 us)
Async XLA Ops:
  1.5 41.2 %collective-permute-start = (bf16[32,192,128]{2,1,0:T(8,128)(2,1)S(1)}, bf16[32,192,128]{2,1,0:T(8,128)(2,1)S(1)}, u32[]{:S(2)}, u32[]{:S(2)}) collective-permute-start(bf16[32,192,128]{2,1,0:T(8,128)(2,1)S(1)} %slice.28), channel_id=1, source_target_pairs={{0,1},{1,0},{2,3},{3,2},{4,5},{5,4},{6,7},{7,6},{8,9},{9,8},{10,11... | collective-permute-start | bytes 4718600 | tf_op jit(solution)/shard_map/ppermute | solution.py:410
  44.0 40.5 %collective-permute-start.2 = (bf16[64,192,128]{2,1,0:T(8,128)(2,1)}, bf16[64,192,128]{2,1,0:T(8,128)(2,1)}, u32[]{:S(2)}, u32[]{:S(2)}) collective-permute-start(bf16[64,192,128]{2,1,0:T(8,128)(2,1)} %constant_dynamic-update-slice_fusion.5.refs_0_.refs_1_), channel_id=1, source_target_pairs={{0,12},{2,14},{5,9},{7,11},{8,4},{10,6},{13,1},{15,3},{16,28},{18,... | collective-permute-start | bytes 9437192 | tf_op jit(solution)/shard_map/ppermute | solution.py:353
  48.2 36.3 %collective-permute-start.1 = (bf16[32,192,128]{2,1,0:T(8,128)(2,1)}, bf16[32,192,128]{2,1,0:T(8,128)(2,1)}, u32[]{:S(2)}, u32[]{:S(2)}) collective-permute-start(bf16[32,192,128]{2,1,0:T(8,128)(2,1)} %get-tuple-element.64), channel_id=1, source_target_pairs={{0,1},{1,0},{2,3},{3,2},{4,5},{5,4},{6,7},{7,6},{8,9},{9,8},{10,11... | collective-permute-start | bytes 4718600 | tf_op jit(solution)/shard_map/ppermute | solution.py:410
  88.4 20.9 %collective-permute-start.3 = (bf16[64,192,128]{2,1,0:T(8,128)(2,1)}, bf16[64,192,128]{2,1,0:T(8,128)(2,1)}, u32[]{:S(2)}, u32[]{:S(2)}) collective-permute-start(bf16[64,192,128]{2,1,0:T(8,128)(2,1)} %broadcast_select_fusion.5), channel_id=1, source_target_pairs={{0,4},{4,0},{8,12},{12,8},{1,5},{5,1},{9,13},{13,9},{2,6},{6,2},{1... | collective-permute-start | bytes 9437192 | tf_op jit(solution)/shard_map/ppermute | solution.py:361
  91.1 40.4 %collective-permute-start.5 = (bf16[64,192,128]{2,1,0:T(8,128)(2,1)}, bf16[64,192,128]{2,1,0:T(8,128)(2,1)}, u32[]{:S(2)}, u32[]{:S(2)}) collective-permute-start(bf16[64,192,128]{2,1,0:T(8,128)(2,1)} %constant_dynamic-update-slice_fusion.4.refs_0_.refs_1_), channel_id=1, source_target_pairs={{0,12},{2,14},{5,9},{7,11},{8,4},{10,6},{13,1},{15,3},{16,28},{18,... | collective-permute-start | bytes 9437192 | tf_op jit(solution)/shard_map/ppermute | solution.py:353
  94.7 36.7 %collective-permute-start.4 = (bf16[32,192,128]{2,1,0:T(8,128)(2,1)}, bf16[32,192,128]{2,1,0:T(8,128)(2,1)}, u32[]{:S(2)}, u32[]{:S(2)}) collective-permute-start(bf16[32,192,128]{2,1,0:T(8,128)(2,1)} %get-tuple-element.65), channel_id=1, source_target_pairs={{0,1},{1,0},{2,3},{3,2},{4,5},{5,4},{6,7},{7,6},{8,9},{9,8},{10,11... | collective-permute-start | bytes 4718600 | tf_op jit(solution)/shard_map/ppermute | solution.py:410
  135.3 21.2 %collective-permute-start.6 = (bf16[64,192,128]{2,1,0:T(8,128)(2,1)}, bf16[64,192,128]{2,1,0:T(8,128)(2,1)}, u32[]{:S(2)}, u32[]{:S(2)}) collective-permute-start(bf16[64,192,128]{2,1,0:T(8,128)(2,1)} %broadcast_select_fusion.4), channel_id=1, source_target_pairs={{0,4},{4,0},{8,12},{12,8},{1,5},{5,1},{9,13},{13,9},{2,6},{6,2},{1... | collective-permute-start | bytes 9437192 | tf_op jit(solution)/shard_map/ppermute | solution.py:361
  138.1 46.7 %collective-permute-start.9 = (bf16[64,192,128]{2,1,0:T(8,128)(2,1)}, bf16[64,192,128]{2,1,0:T(8,128)(2,1)}, u32[]{:S(2)}, u32[]{:S(2)}) collective-permute-start(bf16[64,192,128]{2,1,0:T(8,128)(2,1)} %constant_dynamic-update-slice_fusion.3.refs_0_.refs_1_), channel_id=1, source_target_pairs={{0,12},{2,14},{5,9},{7,11},{8,4},{10,6},{13,1},{15,3},{16,28},{18,... | collective-permute-start | bytes 9437192 | tf_op jit(solution)/shard_map/ppermute | solution.py:353
  142.8 41.9 %collective-permute-start.7 = (bf16[32,192,128]{2,1,0:T(8,128)(2,1)S(1)}, bf16[32,192,128]{2,1,0:T(8,128)(2,1)}, u32[]{:S(2)}, u32[]{:S(2)}) collective-permute-start(bf16[32,192,128]{2,1,0:T(8,128)(2,1)S(1)} %copy-done.16), channel_id=1, source_target_pairs={{0,1},{1,0},{2,3},{3,2},{4,5},{5,4},{6,7},{7,6},{8,9},{9,8},{10,11... | collective-permute-start | bytes 4718600 | tf_op jit(solution)/shard_map/ppermute | solution.py:410
  142.8 39.8 %collective-permute-start.8 = (bf16[1,32,32,128]{3,2,1,0:T(8,128)(2,1)S(1)}, bf16[1,32,32,128]{3,2,1,0:T(8,128)(2,1)S(1)}, u32[]{:S(2)}, u32[]{:S(2)}) collective-permute-start(bf16[1,32,32,128]{3,2,1,0:T(8,128)(2,1)S(1)} %triangle.14), channel_id=1, source_target_pairs={{0,2},{1,3},{2,0},{3,1},{4,6},{5,7},{6,4},{7,5},{8,10},{9,11},{10,... | collective-permute-start | bytes 786440 | tf_op jit(solution)/shard_map/ppermute | solution.py:451
  188.7 21.1 %collective-permute-start.10 = (bf16[64,192,128]{2,1,0:T(8,128)(2,1)}, bf16[64,192,128]{2,1,0:T(8,128)(2,1)}, u32[]{:S(2)}, u32[]{:S(2)}) collective-permute-start(bf16[64,192,128]{2,1,0:T(8,128)(2,1)} %broadcast_select_fusion.3), channel_id=1, source_target_pairs={{0,4},{4,0},{8,12},{12,8},{1,5},{5,1},{9,13},{13,9},{2,6},{6,2},{1... | collective-permute-start | bytes 9437192 | tf_op jit(solution)/shard_map/ppermute | solution.py:361
  190.4 57.5 %collective-permute-start.13 = (bf16[64,192,128]{2,1,0:T(8,128)(2,1)S(1)}, bf16[64,192,128]{2,1,0:T(8,128)(2,1)}, u32[]{:S(2)}, u32[]{:S(2)}) collective-permute-start(bf16[64,192,128]{2,1,0:T(8,128)(2,1)S(1)} %constant_dynamic-update-slice_fusion.2.refs_0_.refs_1_), channel_id=1, source_target_pairs={{0,12},{2,14},{5,9},{7,11},{8,4},{10,6},{13,1},{15,3},{16,28},{18,... | collective-permute-start | bytes 9437192 | tf_op jit(solution)/shard_map/ppermute | solution.py:353
  194.3 53.7 %collective-permute-start.11 = (bf16[32,192,128]{2,1,0:T(8,128)(2,1)S(1)}, bf16[32,192,128]{2,1,0:T(8,128)(2,1)}, u32[]{:S(2)}, u32[]{:S(2)}) collective-permute-start(bf16[32,192,128]{2,1,0:T(8,128)(2,1)S(1)} %copy-done.15), channel_id=1, source_target_pairs={{0,1},{1,0},{2,3},{3,2},{4,5},{5,4},{6,7},{7,6},{8,9},{9,8},{10,11... | collective-permute-start | bytes 4718600 | tf_op jit(solution)/shard_map/ppermute | solution.py:410
  194.9 49.7 %collective-permute-start.12 = (bf16[3,32,32,128]{3,2,1,0:T(8,128)(2,1)S(1)}, bf16[3,32,32,128]{3,2,1,0:T(8,128)(2,1)S(1)}, u32[]{:S(2)}, u32[]{:S(2)}) collective-permute-start(bf16[3,32,32,128]{3,2,1,0:T(8,128)(2,1)S(1)} %triangle.15), channel_id=1, source_target_pairs={{0,2},{1,3},{2,0},{3,1},{4,6},{5,7},{6,4},{7,5},{8,10},{9,11},{10,... | collective-permute-start | bytes 2359304 | tf_op jit(solution)/shard_map/ppermute | solution.py:451
  250.0 22.8 %collective-permute-start.14 = (bf16[64,192,128]{2,1,0:T(8,128)(2,1)}, bf16[64,192,128]{2,1,0:T(8,128)(2,1)}, u32[]{:S(2)}, u32[]{:S(2)}) collective-permute-start(bf16[64,192,128]{2,1,0:T(8,128)(2,1)} %broadcast_select_fusion.2), channel_id=1, source_target_pairs={{0,4},{4,0},{8,12},{12,8},{1,5},{5,1},{9,13},{13,9},{2,6},{6,2},{1... | collective-permute-start | bytes 9437192 | tf_op jit(solution)/shard_map/ppermute | solution.py:361
  254.9 68.3 %collective-permute-start.15 = (bf16[64,192,128]{2,1,0:T(8,128)(2,1)}, bf16[64,192,128]{2,1,0:T(8,128)(2,1)S(1)}, u32[]{:S(2)}, u32[]{:S(2)}) collective-permute-start(bf16[64,192,128]{2,1,0:T(8,128)(2,1)} %constant_dynamic-update-slice_fusion.1.refs_0_.refs_1_), channel_id=1, source_target_pairs={{0,12},{2,14},{5,9},{7,11},{8,4},{10,6},{13,1},{15,3},{16,28},{18,... | collective-permute-start | bytes 9437192 | tf_op jit(solution)/shard_map/ppermute | solution.py:353
  259.1 64.1 %collective-permute-start.16 = (bf16[32,192,128]{2,1,0:T(8,128)(2,1)S(1)}, bf16[32,192,128]{2,1,0:T(8,128)(2,1)S(1)}, u32[]{:S(2)}, u32[]{:S(2)}) collective-permute-start(bf16[32,192,128]{2,1,0:T(8,128)(2,1)S(1)} %get-tuple-element.84), channel_id=1, source_target_pairs={{0,1},{1,0},{2,3},{3,2},{4,5},{5,4},{6,7},{7,6},{8,9},{9,8},{10,11... | collective-permute-start | bytes 4718600 | tf_op jit(solution)/shard_map/ppermute | solution.py:410
  259.2 62.5 %collective-permute-start.17 = (bf16[5,32,32,128]{3,2,1,0:T(8,128)(2,1)S(1)}, bf16[5,32,32,128]{3,2,1,0:T(8,128)(2,1)}, u32[]{:S(2)}, u32[]{:S(2)}) collective-permute-start(bf16[5,32,32,128]{3,2,1,0:T(8,128)(2,1)S(1)} %triangle.16), channel_id=1, source_target_pairs={{0,2},{1,3},{2,0},{3,1},{4,6},{5,7},{6,4},{7,5},{8,10},{9,11},{10,... | collective-permute-start | bytes 3932168 | tf_op jit(solution)/shard_map/ppermute | solution.py:451
  328.4 18.1 %collective-permute-start.18 = (bf16[64,192,128]{2,1,0:T(8,128)(2,1)}, bf16[64,192,128]{2,1,0:T(8,128)(2,1)}, u32[]{:S(2)}, u32[]{:S(2)}) collective-permute-start(bf16[64,192,128]{2,1,0:T(8,128)(2,1)} %broadcast_select_fusion.1), channel_id=1, source_target_pairs={{0,4},{4,0},{8,12},{12,8},{1,5},{5,1},{9,13},{13,9},{2,6},{6,2},{1... | collective-permute-start | bytes 9437192 | tf_op jit(solution)/shard_map/ppermute | solution.py:361
  329.6 82.7 %collective-permute-start.19 = (bf16[64,192,128]{2,1,0:T(8,128)(2,1)}, bf16[64,192,128]{2,1,0:T(8,128)(2,1)}, u32[]{:S(2)}, u32[]{:S(2)}) collective-permute-start(bf16[64,192,128]{2,1,0:T(8,128)(2,1)} %constant_dynamic-update-slice_fusion.refs_0_.refs_1_), channel_id=1, source_target_pairs={{0,12},{2,14},{5,9},{7,11},{8,4},{10,6},{13,1},{15,3},{16,28},{18,... | collective-permute-start | bytes 9437192 | tf_op jit(solution)/shard_map/ppermute | solution.py:353
  333.9 78.4 %collective-permute-start.20 = (bf16[7,32,32,128]{3,2,1,0:T(8,128)(2,1)}, bf16[7,32,32,128]{3,2,1,0:T(8,128)(2,1)}, u32[]{:S(2)}, u32[]{:S(2)}) collective-permute-start(bf16[7,32,32,128]{3,2,1,0:T(8,128)(2,1)} %triangle.17), channel_id=1, source_target_pairs={{0,2},{1,3},{2,0},{3,1},{4,6},{5,7},{6,4},{7,5},{8,10},{9,11},{10,... | collective-permute-start | bytes 5505032 | tf_op jit(solution)/shard_map/ppermute | solution.py:451
  414.6 104.4 %collective-permute-start.22 = (bf16[9,32,32,128]{3,2,1,0:T(8,128)(2,1)}, bf16[9,32,32,128]{3,2,1,0:T(8,128)(2,1)}, u32[]{:S(2)}, u32[]{:S(2)}) collective-permute-start(bf16[9,32,32,128]{3,2,1,0:T(8,128)(2,1)} %triangle.18), channel_id=1, source_target_pairs={{0,2},{1,3},{2,0},{3,1},{4,6},{5,7},{6,4},{7,5},{8,10},{9,11},{10,... | collective-permute-start | bytes 7077896 | tf_op jit(solution)/shard_map/ppermute | solution.py:451
  519.1 125.0 %collective-permute-start.24 = (bf16[6,32,32,128]{3,2,1,0:T(8,128)(2,1)}, bf16[6,32,32,128]{3,2,1,0:T(8,128)(2,1)}, u32[]{:S(2)}, u32[]{:S(2)}) collective-permute-start(bf16[6,32,32,128]{3,2,1,0:T(8,128)(2,1)} %triangle.26), channel_id=1, source_target_pairs={{0,2},{1,3},{2,0},{3,1},{4,6},{5,7},{6,4},{7,5},{8,10},{9,11},{10,... | collective-permute-start | bytes 4718600 | tf_op jit(solution)/shard_map/ppermute | solution.py:451
  530.3 122.4 %collective-permute-start.23 = (bf16[5,32,32,128]{3,2,1,0:T(8,128)(2,1)}, bf16[5,32,32,128]{3,2,1,0:T(8,128)(2,1)}, u32[]{:S(2)}, u32[]{:S(2)}) collective-permute-start(bf16[5,32,32,128]{3,2,1,0:T(8,128)(2,1)} %triangle.22), channel_id=1, source_target_pairs={{0,2},{1,3},{2,0},{3,1},{4,6},{5,7},{6,4},{7,5},{8,10},{9,11},{10,... | collective-permute-start | bytes 3932168 | tf_op jit(solution)/shard_map/ppermute | solution.py:451
  (21 other events, 183.2 us)

commit v10 on v9

--- a/solution.py
+++ b/solution.py
@@ -399,11 +399,14 @@
             token[:] = made[-1:]
         return made
 
-    def keep_own():
-        t = len(own)
-        for s in shards:
-            right_own[t, s] = right_of((t, s), True)
-        own.append(multiply(t, right_own))
+    def keep_own(steps):
+        for _ in range(steps):
+            t = len(own)
+            missing = [s for s in shards if (t, s) not in right_own]
+            if t < chunks and missing:
+                right_own[t, missing[0]] = right_of((t, missing[0]), True)
+            elif t < chunks:
+                own.append(multiply(t, right_own))
 
     def exchange(n, *waits):
         block = after(slabs[n], *waits) if waits else slabs[n]
@@ -418,8 +421,7 @@
         return jnp.pad(after(slabs[n], *waits) if waits else slabs[n], ((0, (half - 1) * step), (0, 0), (0, 0)))
 
     bases = [base(n) for n in range(min(2, chunks))]
-    gate = gate_of(pair_act, centre, mean, after(ln_gain[None], *slabs, *bases), ln_bias[None], w_gate)
-    token[:] = [gate]
+    token[:] = slabs + bases
     for n in range(chunks + 1):
         waits = token + (exchanged[n][-1:] if n < chunks else [])
         if n >= 3:
@@ -433,6 +435,9 @@
             payloads.append(payload)
             firsts.append(first_step(payloads[n]))
         if n == 0:
+            early = after(ln_gain[None], *waits, gain_out, bias_out, w_last)
+            gate = gate_of(pair_act, centre, mean, early, ln_bias[None], w_gate)
+            token[:] = [gate]
             continue
         t = n - 1
         for s, found in enumerate(second_step(payloads[t], firsts[t], *waits)):
@@ -444,16 +449,12 @@
         for s in shards:
             right_sent[t, s] = right_of((t, s), False)
         if t == chunks - 1:
-            while len(own) < t - 1:
-                keep_own()
+            keep_own(2)
         made = multiply(t, right_sent)
         waits = moved[t - 1] if t else []
         moved.append([lax.ppermute(after(x, *waits) if waits else x, "col", swap_half) for x in made])
-        if t == chunks - 2:
-            while len(own) < t // 2:
-                keep_own()
-    while len(own) < chunks:
-        keep_own()
+        keep_own({chunks - 4: 1, chunks - 3: 2, chunks - 2: 4}.get(t, 0))
+    keep_own(chunks * (share + 1))
     out = None
     for t in range(chunks):
         for pairs, kept, came in zip(waves[t], own[t], moved[t]):

time: 671 us -> 663 us (0.988)
  transfers between devices with their start and end apart: 25 -> 25, of which waited for: 10 -> 11; matrix products, arithmetic and copies ran while one was open for 6% -> 5% of each run, Pallas kernels for 66% -> 66%
where the time goes in v10:
time: 663 us; the launch traced here: 654 us
  Pallas kernels  439 us (66%)
  waiting for transfers between devices  112 us (17%)
  starting transfers between devices  41.4 us (6%)
  local copies, waits for them, and re-layouts  39.5 us (6%)
  other arithmetic  21.9 us (3%)
    pallas_call x18, Pallas kernels, project(): pl.pallas_call(functools.partial(project_kernel, n_pieces, len(slabs)), g...  203 us
    pallas_call x14, Pallas kernels, triangle(): pl.pallas_call(functools.partial(triangle_kernel, len(lefts), n_sides, gr...  157 us
    ppermute x7, waiting for transfers between devices, on_device(): lax.ppermute(after(x, *waits) if waits else x, 'col', swap_half)  65.8 us
    pallas_call x7, Pallas kernels, finish(): pl.pallas_call(functools.partial(finish_kernel, group, hidden), grid=(pie...  53.5 us
    ppermute x6, waiting for transfers between devices, exchange(): lax.ppermute(block, 'col', [(c, c ^ o) for c in range(n_col)])  45.9 us
    ppermute x6, starting transfers between devices, first_step(): return lax.ppermute(slab, axes, pairs)  25.7 us
    pallas_call x1, Pallas kernels, gate_of(): pl.pallas_call(gate_kernel, grid=(count // rows,), in_specs=[block] + [wh...  25.3 us
    select_n x6, other arithmetic, second_step(): given = jnp.where(holder, slab, after(far, *waits))  18.1 us
  transfers between devices with their start and end apart: 25, of which 11 were waited for; matrix products, arithmetic and copies ran while one was open for 5% of the time, Pallas kernels for 66%

profile of v10, /device:TPU:0, one launch (start us, length us, event | category | flops | bytes accessed | tf_op | source)
XLA Modules:
  0.0 654.5 jit_solution(12275015268153732583)
XLA Ops:
  19.2 21.2 %collective-permute-done = bf16[32,192,128]{2,1,0:T(8,128)(2,1)} collective-permute-done((bf16[32,192,128]{2,1,0:T(8,128)(2,1)}, bf16[32,192,128]{2,1,0:T(8,128)(2,1)}, u32[]{:S(2)}, u32[]{:S(2)}) %collective-permute-start) | collective-permute-done | bytes 1572896 | tf_op jit(solution)/shard_map/ppermute | solution.py:413
  47.0 25.3 %gate.1 = bf16[192,192,128]{2,1,0:T(8,128)(2,1)} custom-call(bf16[192,192,128]{2,1,0:T(8,128)(2,1)} %pair.1, bf16[128,128]{1,0:T(8,128)(2,1)S(1)} %add_convert_fusion.centre.refs_3_.refs_7_, bf16[256,128]{1,0:T(8,128)(2,1)S(1)} %broadcast_in_dim.28.mean, f32[1,128]{1,0:T(1,128)S(1)} %bitcast.34, f32[1,128]{1,0:T(1,128)S(1)} %bitcast.35, ...), custom_call_target="tpu_custom_call" | custom-call | flops 4831838208 | bytes 18874368 | tf_op jit(solution)/shard_map/gate/pallas_call | solution.py:208
  72.3 11.9 %collective-permute-done.1 = bf16[32,192,128]{2,1,0:T(8,128)(2,1)} collective-permute-done((bf16[32,192,128]{2,1,0:T(8,128)(2,1)}, bf16[32,192,128]{2,1,0:T(8,128)(2,1)}, u32[]{:S(2)}, u32[]{:S(2)}) %collective-permute-start.1) | collective-permute-done | bytes 1572896 | tf_op jit(solution)/shard_map/ppermute | solution.py:413
  107.1 11.7 %project.19 = bf16[16,8,32,384]{3,2,1,0:T(8,128)(2,1)} custom-call(s32[1]{0:T(128)} %bitcast.7.which, bf16[64,192,128]{2,1,0:T(8,128)(2,1)} %constant_dynamic-update-slice_fusion.5.refs_0_.refs_1_, bf16[64,192,128]{2,1,0:T(8,128)(2,1)} %constant_dynamic-update-slice_fusion.5.refs_0_.refs_1_, bf16[64,192,128]{2,1,0:T(8,128)(2,1)} %collective-permute-done.3.refs_2_.refs_3_, ...), custom_call_target="tpu_custom_call" | custom-call | flops 1207959552 | bytes 3145728 | tf_op jit(solution)/shard_map/project/pallas_call | solution.py:102
  156.5 11.6 %project.21 = bf16[16,8,32,384]{3,2,1,0:T(8,128)(2,1)} custom-call(s32[1]{0:T(128)} %bitcast.7.which, bf16[64,192,128]{2,1,0:T(8,128)(2,1)} %constant_dynamic-update-slice_fusion.4.refs_0_.refs_1_, bf16[64,192,128]{2,1,0:T(8,128)(2,1)} %constant_dynamic-update-slice_fusion.4.refs_0_.refs_1_, bf16[64,192,128]{2,1,0:T(8,128)(2,1)} %collective-permute-done.6.refs_2_.refs_3_, ...), custom_call_target="tpu_custom_call" | custom-call | flops 1207959552 | bytes 3145728 | tf_op jit(solution)/shard_map/project/pallas_call | solution.py:102
  204.1 11.7 %project.23 = bf16[16,8,32,384]{3,2,1,0:T(8,128)(2,1)} custom-call(s32[1]{0:T(128)} %bitcast.7.which, bf16[64,192,128]{2,1,0:T(8,128)(2,1)} %copy-done.4, bf16[64,192,128]{2,1,0:T(8,128)(2,1)} %copy-done.4, bf16[64,192,128]{2,1,0:T(8,128)(2,1)} %collective-permute-done.10.refs_2_.refs_3_, bf16[64,192,128]{2,1,0:T(8,128)(2,1)} %collective-permute-done.10.refs_2_.refs_3_, ...), custom_call_target="tpu_custom_call" | custom-call | flops 1207959552 | bytes 3145728 | tf_op jit(solution)/shard_map/project/pallas_call | solution.py:102
  226.1 11.7 %project.24 = bf16[16,8,32,384]{3,2,1,0:T(8,128)(2,1)} custom-call(s32[1]{0:T(128)} %bitcast.13.which, bf16[64,192,128]{2,1,0:T(8,128)(2,1)} %constant_dynamic-update-slice_fusion.5.refs_0_.refs_1_, bf16[64,192,128]{2,1,0:T(8,128)(2,1)} %constant_dynamic-update-slice_fusion.5.refs_0_.refs_1_, bf16[64,192,128]{2,1,0:T(8,128)(2,1)} %collective-permute-done.3.refs_2_.refs_3_, ...), custom_call_target="tpu_custom_call" | custom-call | flops 1207959552 | bytes 3145728 | tf_op jit(solution)/shard_map/project/pallas_call | solution.py:102
  268.2 11.6 %project.26 = bf16[16,8,32,384]{3,2,1,0:T(8,128)(2,1)} custom-call(s32[1]{0:T(128)} %bitcast.7.which, bf16[64,192,128]{2,1,0:T(8,128)(2,1)} %constant_dynamic-update-slice_fusion.2.refs_0_.refs_1_, bf16[64,192,128]{2,1,0:T(8,128)(2,1)} %constant_dynamic-update-slice_fusion.2.refs_0_.refs_1_, bf16[64,192,128]{2,1,0:T(8,128)(2,1)} %collective-permute-done.14.refs_2_.refs_3_, ...), custom_call_target="tpu_custom_call" | custom-call | flops 1207959552 | bytes 3145728 | tf_op jit(solution)/shard_map/project/pallas_call | solution.py:102
  279.8 13.3 %triangle.17 = bf16[7,32,32,128]{3,2,1,0:T(8,128)(2,1)S(1)} custom-call(s32[1]{0:T(128)} %constant.33.clone.1.which, bf16[128,32,384]{2,1,0:T(8,128)(2,1)} %bitcast.39, bf16[128,32,384]{2,1,0:T(8,128)(2,1)} %bitcast.50, bf16[128,32,384]{2,1,0:T(8,128)(2,1)} %bitcast.59, bf16[128,32,384]{2,1,0:T(8,128)(2,1)} %bitcast.78, bf16[128,32,384]{2,1,0:T(8,128)(2,1)} %bitcast.69, ...), custom_call_target="tpu_custom_call" | custom-call | flops 704643072 | bytes 27000832 | tf_op jit(solution)/shard_map/triangle/pallas_call | solution.py:170
  299.1 11.7 %project.27 = bf16[16,8,32,384]{3,2,1,0:T(8,128)(2,1)} custom-call(s32[1]{0:T(128)} %bitcast.13.which, bf16[64,192,128]{2,1,0:T(8,128)(2,1)} %constant_dynamic-update-slice_fusion.4.refs_0_.refs_1_, bf16[64,192,128]{2,1,0:T(8,128)(2,1)} %constant_dynamic-update-slice_fusion.4.refs_0_.refs_1_, bf16[64,192,128]{2,1,0:T(8,128)(2,1)} %collective-permute-done.6.refs_2_.refs_3_, ...), custom_call_target="tpu_custom_call" | custom-call | flops 1207959552 | bytes 3145728 | tf_op jit(solution)/shard_map/project/pallas_call | solution.py:102
  344.7 11.6 %project.29 = bf16[16,8,32,384]{3,2,1,0:T(8,128)(2,1)} custom-call(s32[1]{0:T(128)} %bitcast.7.which, bf16[64,192,128]{2,1,0:T(8,128)(2,1)} %copy-done.3, bf16[64,192,128]{2,1,0:T(8,128)(2,1)} %copy-done.3, bf16[64,192,128]{2,1,0:T(8,128)(2,1)} %copy-done.6, bf16[64,192,128]{2,1,0:T(8,128)(2,1)} %copy-done.6, ...), custom_call_target="tpu_custom_call" | custom-call | flops 1207959552 | bytes 3145728 | tf_op jit(solution)/shard_map/project/pallas_call | solution.py:102
  356.3 15.9 %triangle.19 = bf16[9,32,32,128]{3,2,1,0:T(8,128)(2,1)} custom-call(s32[1]{0:T(128)} %constant.33.clone.1.which, bf16[128,32,384]{2,1,0:T(8,128)(2,1)} %bitcast.41, bf16[128,32,384]{2,1,0:T(8,128)(2,1)} %bitcast.51, bf16[128,32,384]{2,1,0:T(8,128)(2,1)} %bitcast.60, bf16[128,32,384]{2,1,0:T(8,128)(2,1)} %bitcast.79, bf16[128,32,384]{2,1,0:T(8,128)(2,1)} %bitcast.102, ...), custom_call_target="tpu_custom_call" | custom-call | flops 905969664 | bytes 33816576 | tf_op jit(solution)/shard_map/triangle/pallas_call | solution.py:170
  380.6 11.7 %project.30 = bf16[16,8,32,384]{3,2,1,0:T(8,128)(2,1)} custom-call(s32[1]{0:T(128)} %bitcast.13.which, bf16[64,192,128]{2,1,0:T(8,128)(2,1)} %copy-done.4, bf16[64,192,128]{2,1,0:T(8,128)(2,1)} %copy-done.4, bf16[64,192,128]{2,1,0:T(8,128)(2,1)} %collective-permute-done.10.refs_2_.refs_3_, bf16[64,192,128]{2,1,0:T(8,128)(2,1)} %collective-permute-done.10.refs_2_.refs_3_, ...), custom_call_target="tpu_custom_call" | custom-call | flops 1207959552 | bytes 3145728 | tf_op jit(solution)/shard_map/project/pallas_call | solution.py:102
  402.6 11.6 %project.31 = bf16[16,8,32,384]{3,2,1,0:T(8,128)(2,1)} custom-call(s32[1]{0:T(128)} %bitcast.13.which, bf16[64,192,128]{2,1,0:T(8,128)(2,1)} %constant_dynamic-update-slice_fusion.2.refs_0_.refs_1_, bf16[64,192,128]{2,1,0:T(8,128)(2,1)} %constant_dynamic-update-slice_fusion.2.refs_0_.refs_1_, bf16[64,192,128]{2,1,0:T(8,128)(2,1)} %collective-permute-done.14.refs_2_.refs_3_, ...), custom_call_target="tpu_custom_call" | custom-call | flops 1207959552 | bytes 3145728 | tf_op jit(solution)/shard_map/project/pallas_call | solution.py:102
  428.9 11.6 %project.33 = bf16[16,8,32,384]{3,2,1,0:T(8,128)(2,1)} custom-call(s32[1]{0:T(128)} %bitcast.7.which, bf16[64,192,128]{2,1,0:T(8,128)(2,1)} %constant_dynamic-update-slice_fusion.refs_0_.refs_1_, bf16[64,192,128]{2,1,0:T(8,128)(2,1)} %constant_dynamic-update-slice_fusion.refs_0_.refs_1_, bf16[64,192,128]{2,1,0:T(8,128)(2,1)} %copy-done.7, ...), custom_call_target="tpu_custom_call" | custom-call | flops 1207959552 | bytes 3145728 | tf_op jit(solution)/shard_map/project/pallas_call | solution.py:102
  440.5 13.6 %triangle.23.own = bf16[7,32,32,128]{3,2,1,0:T(8,128)(2,1)S(1)} custom-call(s32[1]{0:T(128)} %constant.33.clone.1.which, bf16[128,32,384]{2,1,0:T(8,128)(2,1)} %bitcast.44, bf16[128,32,384]{2,1,0:T(8,128)(2,1)} %bitcast.54, bf16[128,32,384]{2,1,0:T(8,128)(2,1)} %bitcast.62, bf16[128,32,384]{2,1,0:T(8,128)(2,1)} %bitcast.80, bf16[128,32,384]{2,1,0:T(8,128)(2,1)} %bitcast.75, ...), custom_call_target="tpu_custom_call" | custom-call | flops 704643072 | bytes 27000832 | tf_op jit(solution)/shard_map/triangle/pallas_call | solution.py:170
  454.0 11.6 %project.34 = bf16[16,8,32,384]{3,2,1,0:T(8,128)(2,1)} custom-call(s32[1]{0:T(128)} %bitcast.13.which, bf16[64,192,128]{2,1,0:T(8,128)(2,1)} %copy-done.3, bf16[64,192,128]{2,1,0:T(8,128)(2,1)} %copy-done.3, bf16[64,192,128]{2,1,0:T(8,128)(2,1)} %copy-done.6, bf16[64,192,128]{2,1,0:T(8,128)(2,1)} %copy-done.6, ...), custom_call_target="tpu_custom_call" | custom-call | flops 1207959552 | bytes 3145728 | tf_op jit(solution)/shard_map/project/pallas_call | solution.py:102
  465.6 14.0 %triangle.26 = bf16[6,32,32,128]{3,2,1,0:T(8,128)(2,1)S(1)} custom-call(s32[1]{0:T(128)} %constant.33.clone.1.which, bf16[128,32,384]{2,1,0:T(8,128)(2,1)} %bitcast.116, bf16[128,32,384]{2,1,0:T(8,128)(2,1)} %bitcast.71, bf16[128,32,384]{2,1,0:T(8,128)(2,1)} %bitcast.88, bf16[128,32,384]{2,1,0:T(8,128)(2,1)} %bitcast.97, bf16[128,32,384]{2,1,0:T(8,128)(2,1)} %bitcast.111, ...), custom_call_target="tpu_custom_call" | custom-call | flops 603979776 | bytes 23592960 | tf_op jit(solution)/shard_map/triangle/pallas_call | solution.py:170
  479.7 40.6 %collective-permute-done.22.sent = bf16[9,32,32,128]{3,2,1,0:T(8,128)(2,1)} collective-permute-done((bf16[9,32,32,128]{3,2,1,0:T(8,128)(2,1)}, bf16[9,32,32,128]{3,2,1,0:T(8,128)(2,1)}, u32[]{:S(2)}, u32[]{:S(2)}) %collective-permute-start.22) | collective-permute-done | bytes 2359328 | tf_op jit(solution)/shard_map/ppermute | solution.py:455
  549.1 15.9 %triangle.24.own = bf16[9,32,32,128]{3,2,1,0:T(8,128)(2,1)} custom-call(s32[1]{0:T(128)} %constant.33.clone.1.which, bf16[128,32,384]{2,1,0:T(8,128)(2,1)} %bitcast.46, bf16[128,32,384]{2,1,0:T(8,128)(2,1)} %bitcast.56, bf16[128,32,384]{2,1,0:T(8,128)(2,1)} %bitcast.64, bf16[128,32,384]{2,1,0:T(8,128)(2,1)} %bitcast.82, bf16[128,32,384]{2,1,0:T(8,128)(2,1)} %bitcast.104, ...), custom_call_target="tpu_custom_call" | custom-call | flops 905969664 | bytes 33816576 | tf_op jit(solution)/shard_map/triangle/pallas_call | solution.py:170
  564.9 11.7 %project.35 = bf16[16,8,32,384]{3,2,1,0:T(8,128)(2,1)} custom-call(s32[1]{0:T(128)} %bitcast.13.which, bf16[64,192,128]{2,1,0:T(8,128)(2,1)} %constant_dynamic-update-slice_fusion.refs_0_.refs_1_, bf16[64,192,128]{2,1,0:T(8,128)(2,1)} %constant_dynamic-update-slice_fusion.refs_0_.refs_1_, bf16[64,192,128]{2,1,0:T(8,128)(2,1)} %copy-done.7, ...), custom_call_target="tpu_custom_call" | custom-call | flops 1207959552 | bytes 3145728 | tf_op jit(solution)/shard_map/project/pallas_call | solution.py:102
  586.4 12.3 %finish.11.refs_0_ = bf16[192,192,128]{2,1,0:T(8,128)(2,1)} custom-call(bf16[9,32,32,128]{3,2,1,0:T(8,128)(2,1)} %triangle.24.own, bf16[9,32,32,128]{3,2,1,0:T(8,128)(2,1)} %collective-permute-done.22.sent, bf16[192,192,128]{2,1,0:T(8,128)(2,1)} %gate.1, bf16[128,128]{1,0:T(8,128)(2,1)S(1)} %bitcast.31, ...), custom_call_target="tpu_custom_call", output_to_operand_aliasing={{}: (6, {})} | custom-call | flops 301989888 | bytes 4718592 | tf_op jit(solution)/shard_map/finish/pallas_call | solution.py:270
  609.2 14.0 %triangle.27.own = bf16[6,32,32,128]{3,2,1,0:T(8,128)(2,1)S(1)} custom-call(s32[1]{0:T(128)} %constant.33.clone.1.which, bf16[128,32,384]{2,1,0:T(8,128)(2,1)} %bitcast.117, bf16[128,32,384]{2,1,0:T(8,128)(2,1)} %bitcast.77, bf16[128,32,384]{2,1,0:T(8,128)(2,1)} %bitcast.93, bf16[128,32,384]{2,1,0:T(8,128)(2,1)} %bitcast.101, ...), custom_call_target="tpu_custom_call" | custom-call | flops 603979776 | bytes 23592960 | tf_op jit(solution)/shard_map/triangle/pallas_call | solution.py:170
  632.9 12.6 %collective-permute-done.23.sent = bf16[5,32,32,128]{3,2,1,0:T(8,128)(2,1)S(1)} collective-permute-done((bf16[5,32,32,128]{3,2,1,0:T(8,128)(2,1)S(1)}, bf16[5,32,32,128]{3,2,1,0:T(8,128)(2,1)S(1)}, u32[]{:S(2)}, u32[]{:S(2)}) %collective-permute-start.23) | collective-permute-done | bytes 1310752 | tf_op jit(solution)/shard_map/ppermute | solution.py:455
  (133 shorter events, 303.3 us)
Async XLA Ops:
  2.7 37.7 %collective-permute-start = (bf16[32,192,128]{2,1,0:T(8,128)(2,1)}, bf16[32,192,128]{2,1,0:T(8,128)(2,1)}, u32[]{:S(2)}, u32[]{:S(2)}) collective-permute-start(bf16[32,192,128]{2,1,0:T(8,128)(2,1)} %slice.28), channel_id=1, source_target_pairs={{0,1},{1,0},{2,3},{3,2},{4,5},{5,4},{6,7},{7,6},{8,9},{9,8},{10,11... | collective-permute-start | bytes 4718600 | tf_op jit(solution)/shard_map/ppermute | solution.py:413
  43.1 41.1 %collective-permute-start.2 = (bf16[64,192,128]{2,1,0:T(8,128)(2,1)}, bf16[64,192,128]{2,1,0:T(8,128)(2,1)}, u32[]{:S(2)}, u32[]{:S(2)}) collective-permute-start(bf16[64,192,128]{2,1,0:T(8,128)(2,1)} %constant_dynamic-update-slice_fusion.5.refs_0_.refs_1_), channel_id=1, source_target_pairs={{0,12},{2,14},{5,9},{7,11},{8,4},{10,6},{13,1},{15,3},{16,28},{18,... | collective-permute-start | bytes 9437192 | tf_op jit(solution)/shard_map/ppermute | solution.py:353
  46.9 37.3 %collective-permute-start.1 = (bf16[32,192,128]{2,1,0:T(8,128)(2,1)}, bf16[32,192,128]{2,1,0:T(8,128)(2,1)}, u32[]{:S(2)}, u32[]{:S(2)}) collective-permute-start(bf16[32,192,128]{2,1,0:T(8,128)(2,1)} %get-tuple-element.64), channel_id=1, source_target_pairs={{0,1},{1,0},{2,3},{3,2},{4,5},{5,4},{6,7},{7,6},{8,9},{9,8},{10,11... | collective-permute-start | bytes 4718600 | tf_op jit(solution)/shard_map/ppermute | solution.py:413
  88.1 19.0 %collective-permute-start.3 = (bf16[64,192,128]{2,1,0:T(8,128)(2,1)}, bf16[64,192,128]{2,1,0:T(8,128)(2,1)}, u32[]{:S(2)}, u32[]{:S(2)}) collective-permute-start(bf16[64,192,128]{2,1,0:T(8,128)(2,1)} %broadcast_select_fusion.5), channel_id=1, source_target_pairs={{0,4},{4,0},{8,12},{12,8},{1,5},{5,1},{9,13},{13,9},{2,6},{6,2},{1... | collective-permute-start | bytes 9437192 | tf_op jit(solution)/shard_map/ppermute | solution.py:361
  90.9 39.5 %collective-permute-start.5 = (bf16[64,192,128]{2,1,0:T(8,128)(2,1)}, bf16[64,192,128]{2,1,0:T(8,128)(2,1)}, u32[]{:S(2)}, u32[]{:S(2)}) collective-permute-start(bf16[64,192,128]{2,1,0:T(8,128)(2,1)} %constant_dynamic-update-slice_fusion.4.refs_0_.refs_1_), channel_id=1, source_target_pairs={{0,12},{2,14},{5,9},{7,11},{8,4},{10,6},{13,1},{15,3},{16,28},{18,... | collective-permute-start | bytes 9437192 | tf_op jit(solution)/shard_map/ppermute | solution.py:353
  95.6 34.8 %collective-permute-start.4 = (bf16[32,192,128]{2,1,0:T(8,128)(2,1)S(1)}, bf16[32,192,128]{2,1,0:T(8,128)(2,1)}, u32[]{:S(2)}, u32[]{:S(2)}) collective-permute-start(bf16[32,192,128]{2,1,0:T(8,128)(2,1)S(1)} %get-tuple-element.65), channel_id=1, source_target_pairs={{0,1},{1,0},{2,3},{3,2},{4,5},{5,4},{6,7},{7,6},{8,9},{9,8},{10,11... | collective-permute-start | bytes 4718600 | tf_op jit(solution)/shard_map/ppermute | solution.py:413
  134.2 22.3 %collective-permute-start.6 = (bf16[64,192,128]{2,1,0:T(8,128)(2,1)}, bf16[64,192,128]{2,1,0:T(8,128)(2,1)}, u32[]{:S(2)}, u32[]{:S(2)}) collective-permute-start(bf16[64,192,128]{2,1,0:T(8,128)(2,1)} %broadcast_select_fusion.4), channel_id=1, source_target_pairs={{0,4},{4,0},{8,12},{12,8},{1,5},{5,1},{9,13},{13,9},{2,6},{6,2},{1... | collective-permute-start | bytes 9437192 | tf_op jit(solution)/shard_map/ppermute | solution.py:361
  135.9 45.8 %collective-permute-start.9 = (bf16[64,192,128]{2,1,0:T(8,128)(2,1)S(1)}, bf16[64,192,128]{2,1,0:T(8,128)(2,1)S(1)}, u32[]{:S(2)}, u32[]{:S(2)}) collective-permute-start(bf16[64,192,128]{2,1,0:T(8,128)(2,1)S(1)} %constant_dynamic-update-slice_fusion.3.refs_0_.refs_1_), channel_id=1, source_target_pairs={{0,12},{2,14},{5,9},{7,11},{8,4},{10,6},{13,1},{15,3},{16,28},{18,... | collective-permute-start | bytes 9437192 | tf_op jit(solution)/shard_map/ppermute | solution.py:353
  139.6 42.2 %collective-permute-start.7 = (bf16[32,192,128]{2,1,0:T(8,128)(2,1)}, bf16[32,192,128]{2,1,0:T(8,128)(2,1)S(1)}, u32[]{:S(2)}, u32[]{:S(2)}) collective-permute-start(bf16[32,192,128]{2,1,0:T(8,128)(2,1)} %get-tuple-element.71), channel_id=1, source_target_pairs={{0,1},{1,0},{2,3},{3,2},{4,5},{5,4},{6,7},{7,6},{8,9},{9,8},{10,11... | collective-permute-start | bytes 4718600 | tf_op jit(solution)/shard_map/ppermute | solution.py:413
  139.6 39.9 %collective-permute-start.8 = (bf16[1,32,32,128]{3,2,1,0:T(8,128)(2,1)S(1)}, bf16[1,32,32,128]{3,2,1,0:T(8,128)(2,1)S(1)}, u32[]{:S(2)}, u32[]{:S(2)}) collective-permute-start(bf16[1,32,32,128]{3,2,1,0:T(8,128)(2,1)S(1)} %triangle.14), channel_id=1, source_target_pairs={{0,2},{1,3},{2,0},{3,1},{4,6},{5,7},{6,4},{7,5},{8,10},{9,11},{10,... | collective-permute-start | bytes 786440 | tf_op jit(solution)/shard_map/ppermute | solution.py:455
  184.4 19.7 %collective-permute-start.10 = (bf16[64,192,128]{2,1,0:T(8,128)(2,1)}, bf16[64,192,128]{2,1,0:T(8,128)(2,1)}, u32[]{:S(2)}, u32[]{:S(2)}) collective-permute-start(bf16[64,192,128]{2,1,0:T(8,128)(2,1)} %broadcast_select_fusion.3), channel_id=1, source_target_pairs={{0,4},{4,0},{8,12},{12,8},{1,5},{5,1},{9,13},{13,9},{2,6},{6,2},{1... | collective-permute-start | bytes 9437192 | tf_op jit(solution)/shard_map/ppermute | solution.py:361
  185.6 59.1 %collective-permute-start.13 = (bf16[64,192,128]{2,1,0:T(8,128)(2,1)}, bf16[64,192,128]{2,1,0:T(8,128)(2,1)}, u32[]{:S(2)}, u32[]{:S(2)}) collective-permute-start(bf16[64,192,128]{2,1,0:T(8,128)(2,1)} %constant_dynamic-update-slice_fusion.2.refs_0_.refs_1_), channel_id=1, source_target_pairs={{0,12},{2,14},{5,9},{7,11},{8,4},{10,6},{13,1},{15,3},{16,28},{18,... | collective-permute-start | bytes 9437192 | tf_op jit(solution)/shard_map/ppermute | solution.py:353
  190.4 54.3 %collective-permute-start.11 = (bf16[32,192,128]{2,1,0:T(8,128)(2,1)}, bf16[32,192,128]{2,1,0:T(8,128)(2,1)}, u32[]{:S(2)}, u32[]{:S(2)}) collective-permute-start(bf16[32,192,128]{2,1,0:T(8,128)(2,1)} %get-tuple-element.77), channel_id=1, source_target_pairs={{0,1},{1,0},{2,3},{3,2},{4,5},{5,4},{6,7},{7,6},{8,9},{9,8},{10,11... | collective-permute-start | bytes 4718600 | tf_op jit(solution)/shard_map/ppermute | solution.py:413
  190.4 50.2 %collective-permute-start.12 = (bf16[3,32,32,128]{3,2,1,0:T(8,128)(2,1)S(1)}, bf16[3,32,32,128]{3,2,1,0:T(8,128)(2,1)S(1)}, u32[]{:S(2)}, u32[]{:S(2)}) collective-permute-start(bf16[3,32,32,128]{3,2,1,0:T(8,128)(2,1)S(1)} %triangle.15), channel_id=1, source_target_pairs={{0,2},{1,3},{2,0},{3,1},{4,6},{5,7},{6,4},{7,5},{8,10},{9,11},{10,... | collective-permute-start | bytes 2359304 | tf_op jit(solution)/shard_map/ppermute | solution.py:455
  248.5 19.7 %collective-permute-start.14 = (bf16[64,192,128]{2,1,0:T(8,128)(2,1)}, bf16[64,192,128]{2,1,0:T(8,128)(2,1)}, u32[]{:S(2)}, u32[]{:S(2)}) collective-permute-start(bf16[64,192,128]{2,1,0:T(8,128)(2,1)} %broadcast_select_fusion.2), channel_id=1, source_target_pairs={{0,4},{4,0},{8,12},{12,8},{1,5},{5,1},{9,13},{13,9},{2,6},{6,2},{1... | collective-permute-start | bytes 9437192 | tf_op jit(solution)/shard_map/ppermute | solution.py:361
  250.3 68.4 %collective-permute-start.15 = (bf16[64,192,128]{2,1,0:T(8,128)(2,1)S(1)}, bf16[64,192,128]{2,1,0:T(8,128)(2,1)}, u32[]{:S(2)}, u32[]{:S(2)}) collective-permute-start(bf16[64,192,128]{2,1,0:T(8,128)(2,1)S(1)} %constant_dynamic-update-slice_fusion.1.refs_0_.refs_1_), channel_id=1, source_target_pairs={{0,12},{2,14},{5,9},{7,11},{8,4},{10,6},{13,1},{15,3},{16,28},{18,... | collective-permute-start | bytes 9437192 | tf_op jit(solution)/shard_map/ppermute | solution.py:353
  255.0 63.6 %collective-permute-start.16 = (bf16[32,192,128]{2,1,0:T(8,128)(2,1)S(1)}, bf16[32,192,128]{2,1,0:T(8,128)(2,1)}, u32[]{:S(2)}, u32[]{:S(2)}) collective-permute-start(bf16[32,192,128]{2,1,0:T(8,128)(2,1)S(1)} %copy-done.8), channel_id=1, source_target_pairs={{0,1},{1,0},{2,3},{3,2},{4,5},{5,4},{6,7},{7,6},{8,9},{9,8},{10,11... | collective-permute-start | bytes 4718600 | tf_op jit(solution)/shard_map/ppermute | solution.py:413
  255.1 62.7 %collective-permute-start.17 = (bf16[5,32,32,128]{3,2,1,0:T(8,128)(2,1)S(1)}, bf16[5,32,32,128]{3,2,1,0:T(8,128)(2,1)S(1)}, u32[]{:S(2)}, u32[]{:S(2)}) collective-permute-start(bf16[5,32,32,128]{3,2,1,0:T(8,128)(2,1)S(1)} %triangle.16), channel_id=1, source_target_pairs={{0,2},{1,3},{2,0},{3,1},{4,6},{5,7},{6,4},{7,5},{8,10},{9,11},{10,... | collective-permute-start | bytes 3932168 | tf_op jit(solution)/shard_map/ppermute | solution.py:455
  320.7 22.4 %collective-permute-start.18 = (bf16[64,192,128]{2,1,0:T(8,128)(2,1)}, bf16[64,192,128]{2,1,0:T(8,128)(2,1)S(1)}, u32[]{:S(2)}, u32[]{:S(2)}) collective-permute-start(bf16[64,192,128]{2,1,0:T(8,128)(2,1)} %broadcast_select_fusion.1), channel_id=1, source_target_pairs={{0,4},{4,0},{8,12},{12,8},{1,5},{5,1},{9,13},{13,9},{2,6},{6,2},{1... | collective-permute-start | bytes 9437192 | tf_op jit(solution)/shard_map/ppermute | solution.py:361
  324.8 89.4 %collective-permute-start.19 = (bf16[64,192,128]{2,1,0:T(8,128)(2,1)}, bf16[64,192,128]{2,1,0:T(8,128)(2,1)}, u32[]{:S(2)}, u32[]{:S(2)}) collective-permute-start(bf16[64,192,128]{2,1,0:T(8,128)(2,1)} %constant_dynamic-update-slice_fusion.refs_0_.refs_1_), channel_id=1, source_target_pairs={{0,12},{2,14},{5,9},{7,11},{8,4},{10,6},{13,1},{15,3},{16,28},{18,... | collective-permute-start | bytes 9437192 | tf_op jit(solution)/shard_map/ppermute | solution.py:353
  329.0 85.3 %collective-permute-start.20 = (bf16[7,32,32,128]{3,2,1,0:T(8,128)(2,1)S(1)}, bf16[7,32,32,128]{3,2,1,0:T(8,128)(2,1)}, u32[]{:S(2)}, u32[]{:S(2)}) collective-permute-start(bf16[7,32,32,128]{3,2,1,0:T(8,128)(2,1)S(1)} %triangle.17), channel_id=1, source_target_pairs={{0,2},{1,3},{2,0},{3,1},{4,6},{5,7},{6,4},{7,5},{8,10},{9,11},{10,... | collective-permute-start | bytes 5505032 | tf_op jit(solution)/shard_map/ppermute | solution.py:455
  416.6 103.7 %collective-permute-start.22 = (bf16[9,32,32,128]{3,2,1,0:T(8,128)(2,1)}, bf16[9,32,32,128]{3,2,1,0:T(8,128)(2,1)}, u32[]{:S(2)}, u32[]{:S(2)}) collective-permute-start(bf16[9,32,32,128]{3,2,1,0:T(8,128)(2,1)} %triangle.19), channel_id=1, source_target_pairs={{0,2},{1,3},{2,0},{3,1},{4,6},{5,7},{6,4},{7,5},{8,10},{9,11},{10,... | collective-permute-start | bytes 7077896 | tf_op jit(solution)/shard_map/ppermute | solution.py:455
  520.3 102.9 %collective-permute-start.24 = (bf16[6,32,32,128]{3,2,1,0:T(8,128)(2,1)S(1)}, bf16[6,32,32,128]{3,2,1,0:T(8,128)(2,1)S(1)}, u32[]{:S(2)}, u32[]{:S(2)}) collective-permute-start(bf16[6,32,32,128]{3,2,1,0:T(8,128)(2,1)S(1)} %triangle.26), channel_id=1, source_target_pairs={{0,2},{1,3},{2,0},{3,1},{4,6},{5,7},{6,4},{7,5},{8,10},{9,11},{10,... | collective-permute-start | bytes 4718600 | tf_op jit(solution)/shard_map/ppermute | solution.py:455
  530.7 114.8 %collective-permute-start.23 = (bf16[5,32,32,128]{3,2,1,0:T(8,128)(2,1)S(1)}, bf16[5,32,32,128]{3,2,1,0:T(8,128)(2,1)S(1)}, u32[]{:S(2)}, u32[]{:S(2)}) collective-permute-start(bf16[5,32,32,128]{3,2,1,0:T(8,128)(2,1)S(1)} %triangle.22), channel_id=1, source_target_pairs={{0,2},{1,3},{2,0},{3,1},{4,6},{5,7},{6,4},{7,5},{8,10},{9,11},{10,... | collective-permute-start | bytes 3932168 | tf_op jit(solution)/shard_map/ppermute | solution.py:455
  (18 other events, 254.1 us)

commit v11 on v10

--- a/solution.py
+++ b/solution.py
@@ -423,13 +423,14 @@
     bases = [base(n) for n in range(min(2, chunks))]
     token[:] = slabs + bases
     for n in range(chunks + 1):
-        waits = token + (exchanged[n][-1:] if n < chunks else [])
+        steps = list(token)
+        waits = steps + (exchanged[n][-1:] if n < chunks else [])
         if n >= 3:
             waits = waits + moved[n - 3]
         if n + 1 < chunks:
             exchange(n + 1, *waits)
         if n < chunks:
-            payload = after(bases[n], *waits)
+            payload = after(bases[n], *(waits if n >= 3 else steps))
             for p, piece in enumerate(exchanged[n]):
                 payload = lax.dynamic_update_slice_in_dim(payload, piece, (p + 1) * step, axis=0)
             payloads.append(payload)
@@ -440,7 +441,7 @@
             token[:] = [gate]
             continue
         t = n - 1
-        for s, found in enumerate(second_step(payloads[t], firsts[t], *waits)):
+        for s, found in enumerate(second_step(payloads[t], firsts[t], *steps)):
             spread[t, s] = found
         if n + 1 < chunks:
             bases.append(base(n + 1, *waits))

time: 663 us -> 648 us (0.977)
  waiting for transfers between devices: 112 us -> 90.9 us
  starting transfers between devices: 41.4 us -> 48.9 us
    ppermute x6, waiting for transfers between devices: 45.9 us -> 23.3 us  [exchange(): lax.ppermute(block, 'col', [(c, c ^ o) for c in range(n_col)])]
    ppermute x6, waiting for transfers between devices: 0.02 us -> 12.3 us  [first_step(): return lax.ppermute(slab, axes, pairs)]
    ppermute x7, waiting for transfers between devices: 65.8 us -> 55.3 us  [on_device(): lax.ppermute(after(x, *waits) if waits else x, 'col', swap_half)]
  transfers between devices with their start and end apart: 25 -> 25, of which waited for: 11 -> 8; matrix products, arithmetic and copies ran while one was open for 5% -> 8% of each run, Pallas kernels for 66% -> 67%
where the time goes in v11:
time: 648 us; the launch traced here: 640 us
  Pallas kernels  439 us (68%)
  waiting for transfers between devices  90.9 us (14%)
  starting transfers between devices  48.9 us (8%)
  local copies, waits for them, and re-layouts  37.1 us (6%)
  other arithmetic  23.7 us (4%)
    pallas_call x18, Pallas kernels, project(): pl.pallas_call(functools.partial(project_kernel, n_pieces, len(slabs)), g...  203 us
    pallas_call x14, Pallas kernels, triangle(): pl.pallas_call(functools.partial(triangle_kernel, len(lefts), n_sides, gr...  157 us
    ppermute x7, waiting for transfers between devices, on_device(): lax.ppermute(after(x, *waits) if waits else x, 'col', swap_half)  55.3 us
    pallas_call x7, Pallas kernels, finish(): pl.pallas_call(functools.partial(finish_kernel, group, hidden), grid=(pie...  53.5 us
    pallas_call x1, Pallas kernels, gate_of(): pl.pallas_call(gate_kernel, grid=(count // rows,), in_specs=[block] + [wh...  25.3 us
    ppermute x6, starting transfers between devices, first_step(): return lax.ppermute(slab, axes, pairs)  25.2 us
    ppermute x6, waiting for transfers between devices, exchange(): lax.ppermute(block, 'col', [(c, c ^ o) for c in range(n_col)])  23.3 us
    select_n x6, other arithmetic, second_step(): given = jnp.where(holder, slab, after(far, *waits))  19.8 us
  transfers between devices with their start and end apart: 25, of which 8 were waited for; matrix products, arithmetic and copies ran while one was open for 8% of the time, Pallas kernels for 67%

profile of v11, /device:TPU:0, one launch (start us, length us, event | category | flops | bytes accessed | tf_op | source)
XLA Modules:
  0.0 640.1 jit_solution(10160095361256317165)
XLA Ops:
  19.3 21.1 %collective-permute-done = bf16[32,192,128]{2,1,0:T(8,128)(2,1)} collective-permute-done((bf16[32,192,128]{2,1,0:T(8,128)(2,1)}, bf16[32,192,128]{2,1,0:T(8,128)(2,1)}, u32[]{:S(2)}, u32[]{:S(2)}) %collective-permute-start) | collective-permute-done | bytes 1572896 | tf_op jit(solution)/shard_map/ppermute | solution.py:413
  47.1 25.3 %gate.1 = bf16[192,192,128]{2,1,0:T(8,128)(2,1)} custom-call(bf16[192,192,128]{2,1,0:T(8,128)(2,1)} %pair.1, bf16[128,128]{1,0:T(8,128)(2,1)S(1)} %add_convert_fusion.centre.refs_3_.refs_7_, bf16[256,128]{1,0:T(8,128)(2,1)S(1)} %broadcast_in_dim.28.mean, f32[1,128]{1,0:T(1,128)S(1)} %bitcast.34, f32[1,128]{1,0:T(1,128)S(1)} %bitcast.35, ...), custom_call_target="tpu_custom_call" | custom-call | flops 4831838208 | bytes 18874368 | tf_op jit(solution)/shard_map/gate/pallas_call | solution.py:208
  104.2 11.6 %project.19 = bf16[16,8,32,384]{3,2,1,0:T(8,128)(2,1)} custom-call(s32[1]{0:T(128)} %bitcast.7.which, bf16[64,192,128]{2,1,0:T(8,128)(2,1)} %constant_dynamic-update-slice_fusion.5.refs_0_.refs_1_, bf16[64,192,128]{2,1,0:T(8,128)(2,1)} %constant_dynamic-update-slice_fusion.5.refs_0_.refs_1_, bf16[64,192,128]{2,1,0:T(8,128)(2,1)} %collective-permute-done.3.refs_2_.refs_3_, ...), custom_call_target="tpu_custom_call" | custom-call | flops 1207959552 | bytes 3145728 | tf_op jit(solution)/shard_map/project/pallas_call | solution.py:102
  153.4 11.6 %project.21 = bf16[16,8,32,384]{3,2,1,0:T(8,128)(2,1)} custom-call(s32[1]{0:T(128)} %bitcast.7.which, bf16[64,192,128]{2,1,0:T(8,128)(2,1)} %constant_dynamic-update-slice_fusion.4.refs_0_.refs_1_, bf16[64,192,128]{2,1,0:T(8,128)(2,1)} %constant_dynamic-update-slice_fusion.4.refs_0_.refs_1_, bf16[64,192,128]{2,1,0:T(8,128)(2,1)} %collective-permute-done.6.refs_2_.refs_3_, ...), custom_call_target="tpu_custom_call" | custom-call | flops 1207959552 | bytes 3145728 | tf_op jit(solution)/shard_map/project/pallas_call | solution.py:102
  199.0 11.6 %project.23 = bf16[16,8,32,384]{3,2,1,0:T(8,128)(2,1)} custom-call(s32[1]{0:T(128)} %bitcast.7.which, bf16[64,192,128]{2,1,0:T(8,128)(2,1)} %copy-done.4, bf16[64,192,128]{2,1,0:T(8,128)(2,1)} %copy-done.4, bf16[64,192,128]{2,1,0:T(8,128)(2,1)} %collective-permute-done.10.refs_2_.refs_3_, bf16[64,192,128]{2,1,0:T(8,128)(2,1)} %collective-permute-done.10.refs_2_.refs_3_, ...), custom_call_target="tpu_custom_call" | custom-call | flops 1207959552 | bytes 3145728 | tf_op jit(solution)/shard_map/project/pallas_call | solution.py:102
  220.9 11.6 %project.24 = bf16[16,8,32,384]{3,2,1,0:T(8,128)(2,1)} custom-call(s32[1]{0:T(128)} %bitcast.13.which, bf16[64,192,128]{2,1,0:T(8,128)(2,1)} %constant_dynamic-update-slice_fusion.5.refs_0_.refs_1_, bf16[64,192,128]{2,1,0:T(8,128)(2,1)} %constant_dynamic-update-slice_fusion.5.refs_0_.refs_1_, bf16[64,192,128]{2,1,0:T(8,128)(2,1)} %collective-permute-done.3.refs_2_.refs_3_, ...), custom_call_target="tpu_custom_call" | custom-call | flops 1207959552 | bytes 3145728 | tf_op jit(solution)/shard_map/project/pallas_call | solution.py:102
  259.5 11.6 %project.26 = bf16[16,8,32,384]{3,2,1,0:T(8,128)(2,1)} custom-call(s32[1]{0:T(128)} %bitcast.7.which, bf16[64,192,128]{2,1,0:T(8,128)(2,1)} %constant_dynamic-update-slice_fusion.2.refs_0_.refs_1_, bf16[64,192,128]{2,1,0:T(8,128)(2,1)} %constant_dynamic-update-slice_fusion.2.refs_0_.refs_1_, bf16[64,192,128]{2,1,0:T(8,128)(2,1)} %collective-permute-done.14.refs_2_.refs_3_, ...), custom_call_target="tpu_custom_call" | custom-call | flops 1207959552 | bytes 3145728 | tf_op jit(solution)/shard_map/project/pallas_call | solution.py:102
  271.1 13.3 %triangle.17 = bf16[7,32,32,128]{3,2,1,0:T(8,128)(2,1)S(1)} custom-call(s32[1]{0:T(128)} %constant.33.clone.1.which, bf16[128,32,384]{2,1,0:T(8,128)(2,1)} %bitcast.39, bf16[128,32,384]{2,1,0:T(8,128)(2,1)} %bitcast.50, bf16[128,32,384]{2,1,0:T(8,128)(2,1)} %bitcast.59, bf16[128,32,384]{2,1,0:T(8,128)(2,1)} %bitcast.78, bf16[128,32,384]{2,1,0:T(8,128)(2,1)} %bitcast.69, ...), custom_call_target="tpu_custom_call" | custom-call | flops 704643072 | bytes 27000832 | tf_op jit(solution)/shard_map/triangle/pallas_call | solution.py:170
  290.4 11.6 %project.27 = bf16[16,8,32,384]{3,2,1,0:T(8,128)(2,1)} custom-call(s32[1]{0:T(128)} %bitcast.13.which, bf16[64,192,128]{2,1,0:T(8,128)(2,1)} %constant_dynamic-update-slice_fusion.4.refs_0_.refs_1_, bf16[64,192,128]{2,1,0:T(8,128)(2,1)} %constant_dynamic-update-slice_fusion.4.refs_0_.refs_1_, bf16[64,192,128]{2,1,0:T(8,128)(2,1)} %collective-permute-done.6.refs_2_.refs_3_, ...), custom_call_target="tpu_custom_call" | custom-call | flops 1207959552 | bytes 3145728 | tf_op jit(solution)/shard_map/project/pallas_call | solution.py:102
  316.1 10.8 %project.28 = bf16[16,8,32,384]{3,2,1,0:T(8,128)(2,1)} custom-call(s32[1]{0:T(128)} %constant.33.clone.1.which, bf16[64,192,128]{2,1,0:T(8,128)(2,1)} %copy-done.3, bf16[64,192,128]{2,1,0:T(8,128)(2,1)} %copy-done.3, bf16[256,128]{1,0:T(8,128)(2,1)S(1)} %get-tuple-element.123.refs_2_, bf16[128,128]{1,0:T(8,128)(2,1)S(1)} %add_convert_fusion.centre.refs_3_.refs_7_, ...), custom_call_target="tpu_custom_call" | custom-call | flops 1207959552 | bytes 3145728 | tf_op jit(solution)/shard_map/project/pallas_call | solution.py:102
  328.5 11.6 %project.29 = bf16[16,8,32,384]{3,2,1,0:T(8,128)(2,1)} custom-call(s32[1]{0:T(128)} %bitcast.7.which, bf16[64,192,128]{2,1,0:T(8,128)(2,1)} %copy-done.3, bf16[64,192,128]{2,1,0:T(8,128)(2,1)} %copy-done.3, bf16[64,192,128]{2,1,0:T(8,128)(2,1)} %copy-done.6, bf16[64,192,128]{2,1,0:T(8,128)(2,1)} %copy-done.6, ...), custom_call_target="tpu_custom_call" | custom-call | flops 1207959552 | bytes 3145728 | tf_op jit(solution)/shard_map/project/pallas_call | solution.py:102
  340.1 15.9 %triangle.19 = bf16[9,32,32,128]{3,2,1,0:T(8,128)(2,1)} custom-call(s32[1]{0:T(128)} %constant.33.clone.1.which, bf16[128,32,384]{2,1,0:T(8,128)(2,1)} %bitcast.41, bf16[128,32,384]{2,1,0:T(8,128)(2,1)} %bitcast.51, bf16[128,32,384]{2,1,0:T(8,128)(2,1)} %bitcast.60, bf16[128,32,384]{2,1,0:T(8,128)(2,1)} %bitcast.79, bf16[128,32,384]{2,1,0:T(8,128)(2,1)} %bitcast.102, ...), custom_call_target="tpu_custom_call" | custom-call | flops 905969664 | bytes 33816576 | tf_op jit(solution)/shard_map/triangle/pallas_call | solution.py:170
  364.4 11.7 %project.30 = bf16[16,8,32,384]{3,2,1,0:T(8,128)(2,1)} custom-call(s32[1]{0:T(128)} %bitcast.13.which, bf16[64,192,128]{2,1,0:T(8,128)(2,1)} %copy-done.4, bf16[64,192,128]{2,1,0:T(8,128)(2,1)} %copy-done.4, bf16[64,192,128]{2,1,0:T(8,128)(2,1)} %collective-permute-done.10.refs_2_.refs_3_, bf16[64,192,128]{2,1,0:T(8,128)(2,1)} %collective-permute-done.10.refs_2_.refs_3_, ...), custom_call_target="tpu_custom_call" | custom-call | flops 1207959552 | bytes 3145728 | tf_op jit(solution)/shard_map/project/pallas_call | solution.py:102
  386.4 11.6 %project.31 = bf16[16,8,32,384]{3,2,1,0:T(8,128)(2,1)} custom-call(s32[1]{0:T(128)} %bitcast.13.which, bf16[64,192,128]{2,1,0:T(8,128)(2,1)} %constant_dynamic-update-slice_fusion.2.refs_0_.refs_1_, bf16[64,192,128]{2,1,0:T(8,128)(2,1)} %constant_dynamic-update-slice_fusion.2.refs_0_.refs_1_, bf16[64,192,128]{2,1,0:T(8,128)(2,1)} %collective-permute-done.14.refs_2_.refs_3_, ...), custom_call_target="tpu_custom_call" | custom-call | flops 1207959552 | bytes 3145728 | tf_op jit(solution)/shard_map/project/pallas_call | solution.py:102
  415.3 11.6 %project.33 = bf16[16,8,32,384]{3,2,1,0:T(8,128)(2,1)} custom-call(s32[1]{0:T(128)} %bitcast.7.which, bf16[64,192,128]{2,1,0:T(8,128)(2,1)} %constant_dynamic-update-slice_fusion.refs_0_.refs_1_, bf16[64,192,128]{2,1,0:T(8,128)(2,1)} %constant_dynamic-update-slice_fusion.refs_0_.refs_1_, bf16[64,192,128]{2,1,0:T(8,128)(2,1)} %copy-done.7, ...), custom_call_target="tpu_custom_call" | custom-call | flops 1207959552 | bytes 3145728 | tf_op jit(solution)/shard_map/project/pallas_call | solution.py:102
  426.8 13.5 %triangle.23.own = bf16[7,32,32,128]{3,2,1,0:T(8,128)(2,1)S(1)} custom-call(s32[1]{0:T(128)} %constant.33.clone.1.which, bf16[128,32,384]{2,1,0:T(8,128)(2,1)} %bitcast.44, bf16[128,32,384]{2,1,0:T(8,128)(2,1)} %bitcast.54, bf16[128,32,384]{2,1,0:T(8,128)(2,1)} %bitcast.62, bf16[128,32,384]{2,1,0:T(8,128)(2,1)} %bitcast.80, bf16[128,32,384]{2,1,0:T(8,128)(2,1)} %bitcast.75, ...), custom_call_target="tpu_custom_call" | custom-call | flops 704643072 | bytes 27000832 | tf_op jit(solution)/shard_map/triangle/pallas_call | solution.py:170
  440.4 11.6 %project.34 = bf16[16,8,32,384]{3,2,1,0:T(8,128)(2,1)} custom-call(s32[1]{0:T(128)} %bitcast.13.which, bf16[64,192,128]{2,1,0:T(8,128)(2,1)} %copy-done.3, bf16[64,192,128]{2,1,0:T(8,128)(2,1)} %copy-done.3, bf16[64,192,128]{2,1,0:T(8,128)(2,1)} %copy-done.6, bf16[64,192,128]{2,1,0:T(8,128)(2,1)} %copy-done.6, ...), custom_call_target="tpu_custom_call" | custom-call | flops 1207959552 | bytes 3145728 | tf_op jit(solution)/shard_map/project/pallas_call | solution.py:102
  452.0 14.0 %triangle.26 = bf16[6,32,32,128]{3,2,1,0:T(8,128)(2,1)S(1)} custom-call(s32[1]{0:T(128)} %constant.33.clone.1.which, bf16[128,32,384]{2,1,0:T(8,128)(2,1)} %bitcast.116, bf16[128,32,384]{2,1,0:T(8,128)(2,1)} %bitcast.71, bf16[128,32,384]{2,1,0:T(8,128)(2,1)} %bitcast.88, bf16[128,32,384]{2,1,0:T(8,128)(2,1)} %bitcast.97, bf16[128,32,384]{2,1,0:T(8,128)(2,1)} %bitcast.111, ...), custom_call_target="tpu_custom_call" | custom-call | flops 603979776 | bytes 23592960 | tf_op jit(solution)/shard_map/triangle/pallas_call | solution.py:170
  466.0 41.1 %collective-permute-done.22.sent = bf16[9,32,32,128]{3,2,1,0:T(8,128)(2,1)} collective-permute-done((bf16[9,32,32,128]{3,2,1,0:T(8,128)(2,1)}, bf16[9,32,32,128]{3,2,1,0:T(8,128)(2,1)}, u32[]{:S(2)}, u32[]{:S(2)}) %collective-permute-start.22) | collective-permute-done | bytes 2359328 | tf_op jit(solution)/shard_map/ppermute | solution.py:456
  535.9 15.9 %triangle.24.own = bf16[9,32,32,128]{3,2,1,0:T(8,128)(2,1)} custom-call(s32[1]{0:T(128)} %constant.33.clone.1.which, bf16[128,32,384]{2,1,0:T(8,128)(2,1)} %bitcast.46, bf16[128,32,384]{2,1,0:T(8,128)(2,1)} %bitcast.56, bf16[128,32,384]{2,1,0:T(8,128)(2,1)} %bitcast.64, bf16[128,32,384]{2,1,0:T(8,128)(2,1)} %bitcast.82, bf16[128,32,384]{2,1,0:T(8,128)(2,1)} %bitcast.104, ...), custom_call_target="tpu_custom_call" | custom-call | flops 905969664 | bytes 33816576 | tf_op jit(solution)/shard_map/triangle/pallas_call | solution.py:170
  551.8 11.6 %project.35 = bf16[16,8,32,384]{3,2,1,0:T(8,128)(2,1)} custom-call(s32[1]{0:T(128)} %bitcast.13.which, bf16[64,192,128]{2,1,0:T(8,128)(2,1)} %constant_dynamic-update-slice_fusion.refs_0_.refs_1_, bf16[64,192,128]{2,1,0:T(8,128)(2,1)} %constant_dynamic-update-slice_fusion.refs_0_.refs_1_, bf16[64,192,128]{2,1,0:T(8,128)(2,1)} %copy-done.7, ...), custom_call_target="tpu_custom_call" | custom-call | flops 1207959552 | bytes 3145728 | tf_op jit(solution)/shard_map/project/pallas_call | solution.py:102
  573.2 12.3 %finish.11.refs_0_ = bf16[192,192,128]{2,1,0:T(8,128)(2,1)} custom-call(bf16[9,32,32,128]{3,2,1,0:T(8,128)(2,1)} %triangle.24.own, bf16[9,32,32,128]{3,2,1,0:T(8,128)(2,1)} %collective-permute-done.22.sent, bf16[192,192,128]{2,1,0:T(8,128)(2,1)} %gate.1, bf16[128,128]{1,0:T(8,128)(2,1)S(1)} %bitcast.31, ...), custom_call_target="tpu_custom_call", output_to_operand_aliasing={{}: (6, {})} | custom-call | flops 301989888 | bytes 4718592 | tf_op jit(solution)/shard_map/finish/pallas_call | solution.py:270
  595.9 14.0 %triangle.27.own = bf16[6,32,32,128]{3,2,1,0:T(8,128)(2,1)S(1)} custom-call(s32[1]{0:T(128)} %constant.33.clone.1.which, bf16[128,32,384]{2,1,0:T(8,128)(2,1)} %bitcast.117, bf16[128,32,384]{2,1,0:T(8,128)(2,1)} %bitcast.77, bf16[128,32,384]{2,1,0:T(8,128)(2,1)} %bitcast.93, bf16[128,32,384]{2,1,0:T(8,128)(2,1)} %bitcast.101, ...), custom_call_target="tpu_custom_call" | custom-call | flops 603979776 | bytes 23592960 | tf_op jit(solution)/shard_map/triangle/pallas_call | solution.py:170
  619.7 12.5 %collective-permute-done.23.sent = bf16[5,32,32,128]{3,2,1,0:T(8,128)(2,1)} collective-permute-done((bf16[5,32,32,128]{3,2,1,0:T(8,128)(2,1)S(1)}, bf16[5,32,32,128]{3,2,1,0:T(8,128)(2,1)}, u32[]{:S(2)}, u32[]{:S(2)}) %collective-permute-start.23) | collective-permute-done | bytes 1310752 | tf_op jit(solution)/shard_map/ppermute | solution.py:456
  (131 shorter events, 290.1 us)
Async XLA Ops:
  2.7 37.7 %collective-permute-start = (bf16[32,192,128]{2,1,0:T(8,128)(2,1)}, bf16[32,192,128]{2,1,0:T(8,128)(2,1)}, u32[]{:S(2)}, u32[]{:S(2)}) collective-permute-start(bf16[32,192,128]{2,1,0:T(8,128)(2,1)} %slice.28), channel_id=1, source_target_pairs={{0,1},{1,0},{2,3},{3,2},{4,5},{5,4},{6,7},{7,6},{8,9},{9,8},{10,11... | collective-permute-start | bytes 4718600 | tf_op jit(solution)/shard_map/ppermute | solution.py:413
  43.1 37.2 %collective-permute-start.2 = (bf16[64,192,128]{2,1,0:T(8,128)(2,1)}, bf16[64,192,128]{2,1,0:T(8,128)(2,1)}, u32[]{:S(2)}, u32[]{:S(2)}) collective-permute-start(bf16[64,192,128]{2,1,0:T(8,128)(2,1)} %constant_dynamic-update-slice_fusion.5.refs_0_.refs_1_), channel_id=1, source_target_pairs={{0,12},{2,14},{5,9},{7,11},{8,4},{10,6},{13,1},{15,3},{16,28},{18,... | collective-permute-start | bytes 9437192 | tf_op jit(solution)/shard_map/ppermute | solution.py:353
  47.0 38.6 %collective-permute-start.1 = (bf16[32,192,128]{2,1,0:T(8,128)(2,1)}, bf16[32,192,128]{2,1,0:T(8,128)(2,1)}, u32[]{:S(2)}, u32[]{:S(2)}) collective-permute-start(bf16[32,192,128]{2,1,0:T(8,128)(2,1)} %get-tuple-element.64), channel_id=1, source_target_pairs={{0,1},{1,0},{2,3},{3,2},{4,5},{5,4},{6,7},{7,6},{8,9},{9,8},{10,11... | collective-permute-start | bytes 4718600 | tf_op jit(solution)/shard_map/ppermute | solution.py:413
  84.3 19.9 %collective-permute-start.3 = (bf16[64,192,128]{2,1,0:T(8,128)(2,1)}, bf16[64,192,128]{2,1,0:T(8,128)(2,1)}, u32[]{:S(2)}, u32[]{:S(2)}) collective-permute-start(bf16[64,192,128]{2,1,0:T(8,128)(2,1)} %broadcast_select_fusion.5), channel_id=1, source_target_pairs={{0,4},{4,0},{8,12},{12,8},{1,5},{5,1},{9,13},{13,9},{2,6},{6,2},{1... | collective-permute-start | bytes 9437192 | tf_op jit(solution)/shard_map/ppermute | solution.py:361
  88.3 37.8 %collective-permute-start.5 = (bf16[64,192,128]{2,1,0:T(8,128)(2,1)}, bf16[64,192,128]{2,1,0:T(8,128)(2,1)}, u32[]{:S(2)}, u32[]{:S(2)}) collective-permute-start(bf16[64,192,128]{2,1,0:T(8,128)(2,1)} %constant_dynamic-update-slice_fusion.4.refs_0_.refs_1_), channel_id=1, source_target_pairs={{0,12},{2,14},{5,9},{7,11},{8,4},{10,6},{13,1},{15,3},{16,28},{18,... | collective-permute-start | bytes 9437192 | tf_op jit(solution)/shard_map/ppermute | solution.py:353
  92.7 38.7 %collective-permute-start.4 = (bf16[32,192,128]{2,1,0:T(8,128)(2,1)S(1)}, bf16[32,192,128]{2,1,0:T(8,128)(2,1)}, u32[]{:S(2)}, u32[]{:S(2)}) collective-permute-start(bf16[32,192,128]{2,1,0:T(8,128)(2,1)S(1)} %get-tuple-element.65), channel_id=1, source_target_pairs={{0,1},{1,0},{2,3},{3,2},{4,5},{5,4},{6,7},{7,6},{8,9},{9,8},{10,11... | collective-permute-start | bytes 4718600 | tf_op jit(solution)/shard_map/ppermute | solution.py:413
  130.0 23.4 %collective-permute-start.6 = (bf16[64,192,128]{2,1,0:T(8,128)(2,1)}, bf16[64,192,128]{2,1,0:T(8,128)(2,1)}, u32[]{:S(2)}, u32[]{:S(2)}) collective-permute-start(bf16[64,192,128]{2,1,0:T(8,128)(2,1)} %broadcast_select_fusion.4), channel_id=1, source_target_pairs={{0,4},{4,0},{8,12},{12,8},{1,5},{5,1},{9,13},{13,9},{2,6},{6,2},{1... | collective-permute-start | bytes 9437192 | tf_op jit(solution)/shard_map/ppermute | solution.py:361
  133.1 40.4 %collective-permute-start.9 = (bf16[64,192,128]{2,1,0:T(8,128)(2,1)S(1)}, bf16[64,192,128]{2,1,0:T(8,128)(2,1)S(1)}, u32[]{:S(2)}, u32[]{:S(2)}) collective-permute-start(bf16[64,192,128]{2,1,0:T(8,128)(2,1)S(1)} %constant_dynamic-update-slice_fusion.3.refs_0_.refs_1_), channel_id=1, source_target_pairs={{0,12},{2,14},{5,9},{7,11},{8,4},{10,6},{13,1},{15,3},{16,28},{18,... | collective-permute-start | bytes 9437192 | tf_op jit(solution)/shard_map/ppermute | solution.py:353
  136.4 43.0 %collective-permute-start.7 = (bf16[32,192,128]{2,1,0:T(8,128)(2,1)}, bf16[32,192,128]{2,1,0:T(8,128)(2,1)S(1)}, u32[]{:S(2)}, u32[]{:S(2)}) collective-permute-start(bf16[32,192,128]{2,1,0:T(8,128)(2,1)} %get-tuple-element.71), channel_id=1, source_target_pairs={{0,1},{1,0},{2,3},{3,2},{4,5},{5,4},{6,7},{7,6},{8,9},{9,8},{10,11... | collective-permute-start | bytes 4718600 | tf_op jit(solution)/shard_map/ppermute | solution.py:413
  136.6 41.4 %collective-permute-start.8 = (bf16[1,32,32,128]{3,2,1,0:T(8,128)(2,1)S(1)}, bf16[1,32,32,128]{3,2,1,0:T(8,128)(2,1)S(1)}, u32[]{:S(2)}, u32[]{:S(2)}) collective-permute-start(bf16[1,32,32,128]{3,2,1,0:T(8,128)(2,1)S(1)} %triangle.14), channel_id=1, source_target_pairs={{0,2},{1,3},{2,0},{3,1},{4,6},{5,7},{6,4},{7,5},{8,10},{9,11},{10,... | collective-permute-start | bytes 786440 | tf_op jit(solution)/shard_map/ppermute | solution.py:456
  176.1 22.9 %collective-permute-start.10 = (bf16[64,192,128]{2,1,0:T(8,128)(2,1)}, bf16[64,192,128]{2,1,0:T(8,128)(2,1)}, u32[]{:S(2)}, u32[]{:S(2)}) collective-permute-start(bf16[64,192,128]{2,1,0:T(8,128)(2,1)} %broadcast_select_fusion.3), channel_id=1, source_target_pairs={{0,4},{4,0},{8,12},{12,8},{1,5},{5,1},{9,13},{13,9},{2,6},{6,2},{1... | collective-permute-start | bytes 9437192 | tf_op jit(solution)/shard_map/ppermute | solution.py:361
  180.7 51.9 %collective-permute-start.13 = (bf16[64,192,128]{2,1,0:T(8,128)(2,1)}, bf16[64,192,128]{2,1,0:T(8,128)(2,1)}, u32[]{:S(2)}, u32[]{:S(2)}) collective-permute-start(bf16[64,192,128]{2,1,0:T(8,128)(2,1)} %constant_dynamic-update-slice_fusion.2.refs_0_.refs_1_), channel_id=1, source_target_pairs={{0,12},{2,14},{5,9},{7,11},{8,4},{10,6},{13,1},{15,3},{16,28},{18,... | collective-permute-start | bytes 9437192 | tf_op jit(solution)/shard_map/ppermute | solution.py:353
  184.1 53.8 %collective-permute-start.11 = (bf16[32,192,128]{2,1,0:T(8,128)(2,1)}, bf16[32,192,128]{2,1,0:T(8,128)(2,1)}, u32[]{:S(2)}, u32[]{:S(2)}) collective-permute-start(bf16[32,192,128]{2,1,0:T(8,128)(2,1)} %get-tuple-element.77), channel_id=1, source_target_pairs={{0,1},{1,0},{2,3},{3,2},{4,5},{5,4},{6,7},{7,6},{8,9},{9,8},{10,11... | collective-permute-start | bytes 4718600 | tf_op jit(solution)/shard_map/ppermute | solution.py:413
  186.6 51.3 %collective-permute-start.12 = (bf16[3,32,32,128]{3,2,1,0:T(8,128)(2,1)S(1)}, bf16[3,32,32,128]{3,2,1,0:T(8,128)(2,1)S(1)}, u32[]{:S(2)}, u32[]{:S(2)}) collective-permute-start(bf16[3,32,32,128]{3,2,1,0:T(8,128)(2,1)S(1)} %triangle.15), channel_id=1, source_target_pairs={{0,2},{1,3},{2,0},{3,1},{4,6},{5,7},{6,4},{7,5},{8,10},{9,11},{10,... | collective-permute-start | bytes 2359304 | tf_op jit(solution)/shard_map/ppermute | solution.py:456
  236.5 23.0 %collective-permute-start.14 = (bf16[64,192,128]{2,1,0:T(8,128)(2,1)}, bf16[64,192,128]{2,1,0:T(8,128)(2,1)}, u32[]{:S(2)}, u32[]{:S(2)}) collective-permute-start(bf16[64,192,128]{2,1,0:T(8,128)(2,1)} %broadcast_select_fusion.2), channel_id=1, source_target_pairs={{0,4},{4,0},{8,12},{12,8},{1,5},{5,1},{9,13},{13,9},{2,6},{6,2},{1... | collective-permute-start | bytes 9437192 | tf_op jit(solution)/shard_map/ppermute | solution.py:361
  239.5 62.5 %collective-permute-start.15 = (bf16[64,192,128]{2,1,0:T(8,128)(2,1)S(1)}, bf16[64,192,128]{2,1,0:T(8,128)(2,1)}, u32[]{:S(2)}, u32[]{:S(2)}) collective-permute-start(bf16[64,192,128]{2,1,0:T(8,128)(2,1)S(1)} %constant_dynamic-update-slice_fusion.1.refs_0_.refs_1_), channel_id=1, source_target_pairs={{0,12},{2,14},{5,9},{7,11},{8,4},{10,6},{13,1},{15,3},{16,28},{18,... | collective-permute-start | bytes 9437192 | tf_op jit(solution)/shard_map/ppermute | solution.py:353
  245.1 63.3 %collective-permute-start.17 = (bf16[32,192,128]{2,1,0:T(8,128)(2,1)S(1)}, bf16[32,192,128]{2,1,0:T(8,128)(2,1)S(1)}, u32[]{:S(2)}, u32[]{:S(2)}) collective-permute-start(bf16[32,192,128]{2,1,0:T(8,128)(2,1)S(1)} %copy-done.8), channel_id=1, source_target_pairs={{0,1},{1,0},{2,3},{3,2},{4,5},{5,4},{6,7},{7,6},{8,9},{9,8},{10,11... | collective-permute-start | bytes 4718600 | tf_op jit(solution)/shard_map/ppermute | solution.py:413
  245.1 62.5 %collective-permute-start.18 = (bf16[5,32,32,128]{3,2,1,0:T(8,128)(2,1)S(1)}, bf16[5,32,32,128]{3,2,1,0:T(8,128)(2,1)}, u32[]{:S(2)}, u32[]{:S(2)}) collective-permute-start(bf16[5,32,32,128]{3,2,1,0:T(8,128)(2,1)S(1)} %triangle.16), channel_id=1, source_target_pairs={{0,2},{1,3},{2,0},{3,1},{4,6},{5,7},{6,4},{7,5},{8,10},{9,11},{10,... | collective-permute-start | bytes 3932168 | tf_op jit(solution)/shard_map/ppermute | solution.py:456
  304.1 22.7 %collective-permute-start.16 = (bf16[64,192,128]{2,1,0:T(8,128)(2,1)}, bf16[64,192,128]{2,1,0:T(8,128)(2,1)S(1)}, u32[]{:S(2)}, u32[]{:S(2)}) collective-permute-start(bf16[64,192,128]{2,1,0:T(8,128)(2,1)} %broadcast_select_fusion.1), channel_id=1, source_target_pairs={{0,4},{4,0},{8,12},{12,8},{1,5},{5,1},{9,13},{13,9},{2,6},{6,2},{1... | collective-permute-start | bytes 9437192 | tf_op jit(solution)/shard_map/ppermute | solution.py:361
  309.6 88.4 %collective-permute-start.19 = (bf16[64,192,128]{2,1,0:T(8,128)(2,1)}, bf16[64,192,128]{2,1,0:T(8,128)(2,1)}, u32[]{:S(2)}, u32[]{:S(2)}) collective-permute-start(bf16[64,192,128]{2,1,0:T(8,128)(2,1)} %constant_dynamic-update-slice_fusion.refs_0_.refs_1_), channel_id=1, source_target_pairs={{0,12},{2,14},{5,9},{7,11},{8,4},{10,6},{13,1},{15,3},{16,28},{18,... | collective-permute-start | bytes 9437192 | tf_op jit(solution)/shard_map/ppermute | solution.py:353
  314.2 87.7 %collective-permute-start.21 = (bf16[7,32,32,128]{3,2,1,0:T(8,128)(2,1)S(1)}, bf16[7,32,32,128]{3,2,1,0:T(8,128)(2,1)S(1)}, u32[]{:S(2)}, u32[]{:S(2)}) collective-permute-start(bf16[7,32,32,128]{3,2,1,0:T(8,128)(2,1)S(1)} %triangle.17), channel_id=1, source_target_pairs={{0,2},{1,3},{2,0},{3,1},{4,6},{5,7},{6,4},{7,5},{8,10},{9,11},{10,... | collective-permute-start | bytes 5505032 | tf_op jit(solution)/shard_map/ppermute | solution.py:456
  401.9 105.2 %collective-permute-start.22 = (bf16[9,32,32,128]{3,2,1,0:T(8,128)(2,1)}, bf16[9,32,32,128]{3,2,1,0:T(8,128)(2,1)}, u32[]{:S(2)}, u32[]{:S(2)}) collective-permute-start(bf16[9,32,32,128]{3,2,1,0:T(8,128)(2,1)} %triangle.19), channel_id=1, source_target_pairs={{0,2},{1,3},{2,0},{3,1},{4,6},{5,7},{6,4},{7,5},{8,10},{9,11},{10,... | collective-permute-start | bytes 7077896 | tf_op jit(solution)/shard_map/ppermute | solution.py:456
  507.2 102.8 %collective-permute-start.24 = (bf16[6,32,32,128]{3,2,1,0:T(8,128)(2,1)S(1)}, bf16[6,32,32,128]{3,2,1,0:T(8,128)(2,1)S(1)}, u32[]{:S(2)}, u32[]{:S(2)}) collective-permute-start(bf16[6,32,32,128]{3,2,1,0:T(8,128)(2,1)S(1)} %triangle.26), channel_id=1, source_target_pairs={{0,2},{1,3},{2,0},{3,1},{4,6},{5,7},{6,4},{7,5},{8,10},{9,11},{10,... | collective-permute-start | bytes 4718600 | tf_op jit(solution)/shard_map/ppermute | solution.py:456
  517.6 114.6 %collective-permute-start.23 = (bf16[5,32,32,128]{3,2,1,0:T(8,128)(2,1)S(1)}, bf16[5,32,32,128]{3,2,1,0:T(8,128)(2,1)}, u32[]{:S(2)}, u32[]{:S(2)}) collective-permute-start(bf16[5,32,32,128]{3,2,1,0:T(8,128)(2,1)S(1)} %triangle.22), channel_id=1, source_target_pairs={{0,2},{1,3},{2,0},{3,1},{4,6},{5,7},{6,4},{7,5},{8,10},{9,11},{10,... | collective-permute-start | bytes 3932168 | tf_op jit(solution)/shard_map/ppermute | solution.py:456
  (17 other events, 255.1 us)
